TPU v7x, 128 devices: a whole 4x4x4 slice. The times are simulated.
128 devices in a mesh: row: 16 (over z, x_lo, core), col: 8 (over y, x_hi).
Axes of the slice: x: 4 (x_hi: 2, x_lo: 2; x = x_hi * 2 + x_lo), y: 4, z: 4, core: 2. Of those that a mesh axis runs over, the one named last changes fastest.
Arguments:
- cube: bfloat16 [8, 424, 512, 256], P(None, 'col', 'row'), may hold values from -6 to 6
- library_t: bfloat16 [64, 424], replicated, may hold values from -0.3125 to 0.3125
- inverse: float32 [64, 64], replicated, as said below
- weight_h: int32 [512, 2048], P('row', 'col'), may hold values from 0 to 255
- weight_v: int32 [512, 2048], P('row', 'col'), may hold values from 0 to 255
Outputs:
- abundances: float32 [64, 512, 2048], P(None, 'row', 'col')
Inputs may be any that keep to these rules, and one draw needn't show every extreme that they name: `inverse`: an order-one matrix of independent entries with a diagonal between 0.6 and 1.4.
All inputs are finite; a program needn't handle non-finite values.
Results may differ from a plain program's by a relative error of at most 0.0003.
Values may be sent and summed in bfloat16 or wider, within the bound.
No kernel may reach another device: no remote copies, remote signals or barrier semaphores. Data moves between devices by JAX's collectives and lax.ppermute only.
A program may use at most 128 MiB of HBM per device.

v0:
```python
import jax
import jax.numpy as jnp
from jax import lax
from jax.sharding import PartitionSpec as P

ITERS = 2
STEPS = 2


KAPPA = 0.24
PENALTY = 0.5
EDGE_SCALE = 1.0 / 255.0


def extended(block, sides, width):
    for axis, dim in sides:
        count = lax.axis_size(axis)
        forward = [(i, i + 1) for i in range(count - 1)]
        backward = [(target, source) for source, target in forward]
        low = lax.ppermute(
            lax.slice_in_dim(block, block.shape[dim] - width, None, axis=dim), axis, forward
        )
        high = lax.ppermute(lax.slice_in_dim(block, 0, width, axis=dim), axis, backward)
        block = jnp.concatenate([low, block, high], axis=dim)
    return block


def shifted(x, axis, by):
    count = lax.axis_size(axis)
    pairs = [(i, i + by) for i in range(count) if 0 <= i + by < count]
    return lax.ppermute(x, axis, pairs)


def diffuse(padded, wh_pad, wv_pad):
    center = padded[:, 1:-1, 1:-1]
    right = padded[:, 1:-1, 2:] - center
    left = center - padded[:, 1:-1, :-2]
    down = padded[:, 2:, 1:-1] - center
    upper = center - padded[:, :-2, 1:-1]
    flux = (
        wh_pad[1:-1, 1:-1] * right
        - wh_pad[1:-1, :-2] * left
        + wv_pad[1:-1, 1:-1] * down
        - wv_pad[:-2, 1:-1] * upper
    )
    return center + KAPPA * flux


def smooth(field, wh_wide, wv_wide):
    for step in range(STEPS):
        padded = extended(field, (("row", 1), ("col", 2)), 1)
        field = diffuse(padded, wh_wide, wv_wide)
    return field


def per_device(cube, library_t, inverse, weight_h, weight_v):
    col_count = lax.axis_size("col")
    row_count = lax.axis_size("row")
    tile_h, tile_w = weight_h.shape
    count = library_t.shape[0]
    row_start = lax.axis_index("row") * tile_h
    col_start = lax.axis_index("col") * tile_w
    rows = row_start + lax.broadcasted_iota(jnp.int32, (tile_h, tile_w), 0)
    cols = col_start + lax.broadcasted_iota(jnp.int32, (tile_h, tile_w), 1)
    wh = jnp.where(
        cols < tile_w * col_count - 1, weight_h.astype(jnp.float32) * EDGE_SCALE, jnp.float32(0.0)
    )
    wv = jnp.where(
        rows < tile_h * row_count - 1, weight_v.astype(jnp.float32) * EDGE_SCALE, jnp.float32(0.0)
    )
    left_column = shifted(wh[:, tile_w - 1 :], "col", 1)
    upper_row = shifted(wv[tile_h - 1 :, :], "row", 1)
    wh_wide = jnp.pad(jnp.concatenate([left_column, wh], 1), ((1, 1), (0, 1)))
    wv_wide = jnp.pad(jnp.concatenate([upper_row, wv], 0), ((0, 1), (1, 1)))
    projected_tile = jnp.einsum(
        "eb,cbhw->ehw",
        library_t,
        lax.all_to_all(cube, "col", split_axis=0, concat_axis=1, tiled=True),
        preferred_element_type=jnp.float32,
    )
    local_shape = projected_tile.shape[1:]
    projected = projected_tile.reshape(count, -1)
    kept = jnp.zeros_like(projected)
    dual = jnp.zeros_like(projected)
    result = None
    for it in range(ITERS):
        mixed = jnp.dot(
            inverse, projected + PENALTY * (kept - dual), precision=lax.Precision.HIGHEST
        )
        field = (mixed + dual).reshape((count,) + local_shape)
        field = smooth(field, wh_wide, wv_wide)
        result = jnp.maximum(field, jnp.float32(0.0))
        if it + 1 < ITERS:
            kept = result.reshape(count, -1)
            dual = mixed - kept
    return result


def solution(mesh):
    return jax.shard_map(
        per_device,
        mesh=mesh,
        in_specs=(P(None, "col", "row", None), P(), P(), P("row", "col"), P("row", "col")),
        out_specs=P(None, "row", "col"),
        check_vma=False,
    )
```

profile of v0, /device:TPU:39, one launch (start us, length us, event | category | flops | bytes accessed | tf_op | source)
XLA Modules:
  0.0 251.4 jit_solution(2837653638061818132)
XLA Ops:
  0.0 7.0 %all-to-all-start = ((bf16[8,53,32,256]{3,2,1,0:T(8,128)(2,1)}), bf16[8,53,32,256]{3,2,1,0:T(8,128)(2,1)}, u32[]{:S(2)}, u32[]{:S(2)}) async-start(bf16[8,53,32,256]{3,2,1,0:T(8,128)(2,1)} %param.5), calls=%async_computation | async-start | bytes 13893632 | tf_op jit(solution)/shard_map/all_to_all | solution.py:78
  7.1 0.1 slice.180
  7.1 3.1 %collective-permute-start.3 = (f32[32,1]{1,0:T(8,128)S(1)}, f32[32,1]{1,0:T(8,128)S(1)}, u32[]{:S(2)}, u32[]{:S(2)}) collective-permute-start(f32[32,1]{1,0:T(8,128)S(1)} %slice.180), channel_id=1, source_target_pairs={{0,1},{1,2},{2,3},{3,4},{4,5},{5,6},{6,7},{8,9},{9,10},{10,11},{11... | collective-permute-start | bytes 392 | tf_op jit(solution)/shard_map/ppermute | solution.py:31
  10.3 0.1 multiply_select_fusion
  10.3 5.2 %collective-permute-start.5 = (f32[1,256]{1,0:T(1,128)S(1)}, f32[1,256]{1,0:T(1,128)S(1)}, u32[]{:S(2)}, u32[]{:S(2)}) collective-permute-start(f32[1,256]{1,0:T(1,128)S(1)} %slice.181), channel_id=1, source_target_pairs={{0,8},{8,16},{16,24},{24,32},{32,40},{40,48},{48,56},{56,64},{64,7... | collective-permute-start | bytes 3080 | tf_op jit(solution)/shard_map/ppermute | solution.py:31
  15.5 68.7 %all-to-all-done = bf16[8,53,32,256]{3,2,1,0:T(8,128)(2,1)} async-done(((bf16[8,53,32,256]{3,2,1,0:T(8,128)(2,1)}), bf16[8,53,32,256]{3,2,1,0:T(8,128)(2,1)}, u32[]{:S(2)}, u32[]{:S(2)}) %all-to-all-start) | async-done | bytes 6946848 | tf_op jit(solution)/shard_map/all_to_all | solution.py:78
  84.2 11.1 %copy.31 = bf16[53,8,32,256]{3,1,2,0:T(8,128)(2,1)S(1)} copy(bf16[53,8,32,256]{3,2,1,0:T(8,128)(2,1)} %bitcast.9) | data formatting | bytes 13893632
  95.3 0.0 copy-start.3
  95.4 1.5 fusion.65
  96.9 3.3 %convolution_bitcast_fusion.1 = f32[64,8192]{1,0:T(8,128)} fusion(f32[64,8192]{1,0:T(8,128)S(1)} %fusion.65, f32[64,64]{1,0:T(8,128)S(1)} %copy-done.3), kind=kOutput, calls=%fused_computation.2 | convolution fusion | flops 402653184 | bytes 4210688 | tf_op jit(solution)/shard_map/dot_general | solution.py:87
  100.2 3.8 %copy.29 = f32[64,8192]{0,1:T(8,128)} copy(f32[64,8192]{1,0:T(8,128)} %convolution_bitcast_fusion.1) | data formatting | bytes 4194304 | tf_op jit(solution)/shard_map/reshape | solution.py:90
  104.0 1.1 fusion.64
  105.1 5.7 %collective-permute-start = (f32[64,1,256]{0,2,1:T(8,128)S(1)}, f32[64,1,256]{0,2,1:T(8,128)S(1)}, u32[]{:S(2)}, u32[]{:S(2)}) collective-permute-start(f32[64,1,256]{0,2,1:T(8,128)S(1)} %get-tuple-element.20), channel_id=1, source_target_pairs={{0,8},{8,16},{16,24},{24,32},{32,40},{40,48},{48,56},{56,64},{64,7... | collective-permute-start | bytes 196616 | tf_op jit(solution)/shard_map/ppermute | solution.py:20
  110.8 1.9 collective-permute-start.1
  112.8 0.1 pad_maximum_fusion.33
  112.9 5.2 %collective-permute-done.1 = f32[64,1,256]{0,2,1:T(8,128)S(1)} collective-permute-done((f32[64,1,256]{0,2,1:T(8,128)S(1)}, f32[64,1,256]{0,2,1:T(8,128)S(1)}, u32[]{:S(2)}, u32[]{:S(2)}) %collective-permute-start.1) | collective-permute-done | bytes 65568 | tf_op jit(solution)/shard_map/ppermute | solution.py:23
  118.0 1.0 pad_maximum_fusion.45
  119.0 5.0 %collective-permute-start.2 = (f32[64,34,1]{0,2,1:T(1,128)S(1)}, f32[64,34,1]{0,2,1:T(1,128)S(1)}, u32[]{:S(2)}, u32[]{:S(2)}) collective-permute-start(f32[64,34,1]{0,2,1:T(1,128)S(1)} %get-tuple-element.11), channel_id=1, source_target_pairs={{1,0},{2,1},{3,2},{4,3},{5,4},{6,5},{7,6},{9,8},{10,9},{11,10},{12... | collective-permute-start | bytes 26120 | tf_op jit(solution)/shard_map/ppermute | solution.py:23
  124.0 2.7 %collective-permute-start.4 = (f32[64,34,1]{0,2,1:T(1,128)S(1)}, f32[64,34,1]{0,2,1:T(1,128)S(1)}, u32[]{:S(2)}, u32[]{:S(2)}) collective-permute-start(f32[64,34,1]{0,2,1:T(1,128)S(1)} %get-tuple-element.12), channel_id=1, source_target_pairs={{0,1},{1,2},{2,3},{3,4},{4,5},{5,6},{6,7},{8,9},{9,10},{10,11},{11... | collective-permute-start | bytes 26120 | tf_op jit(solution)/shard_map/ppermute | solution.py:20
  126.8 3.2 %collective-permute-done.4 = f32[64,34,1]{0,2,1:T(1,128)S(1)} collective-permute-done((f32[64,34,1]{0,2,1:T(1,128)S(1)}, f32[64,34,1]{0,2,1:T(1,128)S(1)}, u32[]{:S(2)}, u32[]{:S(2)}) %collective-permute-start.4) | collective-permute-done | bytes 8736 | tf_op jit(solution)/shard_map/ppermute | solution.py:20
  130.0 10.2 %fusion.46 = f32[64,32,256]{0,2,1:T(8,128)S(1)} fusion(f32[64,32,256]{0,2,1:T(8,128)S(1)} %bitcast.23, f32[64,1,256]{0,2,1:T(8,128)S(1)} %collective-permute-done, f32[64,1,256]{0,2,1:T(8,128)S(1)} %collective-permute-done.1, f32[64,34,1]{0,2,1:T(1,128)S(1)} %collective-permute-done.4, f32[64,34,1]{0,2,1:T(1,128)S(1)} %collective-permute-done.2, ...), kind=kLoop, calls=%fused_computation.73 | loop fusion | flops 11010048 | bytes 4473856 | tf_op jit(solution)/shard_map/add | solution.py:46
  140.2 2.6 %collective-permute-start.6 = (f32[64,1,256]{0,2,1:T(8,128)S(1)}, f32[64,1,256]{0,2,1:T(8,128)S(1)}, u32[]{:S(2)}, u32[]{:S(2)}) collective-permute-start(f32[64,1,256]{0,2,1:T(8,128)S(1)} %get-tuple-element.18), channel_id=1, source_target_pairs={{0,8},{8,16},{16,24},{24,32},{32,40},{40,48},{48,56},{56,64},{64,7... | collective-permute-start | bytes 196616 | tf_op jit(solution)/shard_map/ppermute | solution.py:20
  142.8 1.9 collective-permute-start.7
  144.8 5.2 %collective-permute-done.7 = f32[64,1,256]{0,2,1:T(8,128)S(1)} collective-permute-done((f32[64,1,256]{0,2,1:T(8,128)S(1)}, f32[64,1,256]{0,2,1:T(8,128)S(1)}, u32[]{:S(2)}, u32[]{:S(2)}) %collective-permute-start.7) | collective-permute-done | bytes 65568 | tf_op jit(solution)/shard_map/ppermute | solution.py:23
  150.1 2.0 collective-permute-start.8
  152.0 5.7 %collective-permute-start.9 = (f32[64,34,1]{0,2,1:T(1,128)S(1)}, f32[64,34,1]{0,2,1:T(1,128)S(1)}, u32[]{:S(2)}, u32[]{:S(2)}) collective-permute-start(f32[64,34,1]{0,2,1:T(1,128)S(1)} %get-tuple-element.10), channel_id=1, source_target_pairs={{0,1},{1,2},{2,3},{3,4},{4,5},{5,6},{6,7},{8,9},{9,10},{10,11},{11... | collective-permute-start | bytes 26120 | tf_op jit(solution)/shard_map/ppermute | solution.py:20
  157.8 0.8 collective-permute-done.9
  158.6 11.2 %fusion.33 = f32[64,32,256]{0,2,1:T(8,128)} fusion(f32[64,32,256]{0,2,1:T(8,128)S(1)} %fusion.46, f32[64,1,256]{0,2,1:T(8,128)S(1)} %collective-permute-done.6, f32[64,1,256]{0,2,1:T(8,128)S(1)} %collective-permute-done.7, f32[64,34,1]{0,2,1:T(1,128)S(1)} %collective-permute-done.9, f32[64,34,1]{0,2,1:T(1,128)S(1)} %collective-permute-done.8, ...), kind=kLoop, calls=%fused_computation.52 | loop fusion | flops 11534336 | bytes 4473856 | tf_op jit(solution)/shard_map/max | solution.py:92
  169.8 3.8 %copy.28 = f32[64,8192]{1,0:T(8,128)} copy(f32[64,8192]{0,1:T(8,128)} %bitcast.28) | data formatting | bytes 4194304 | tf_op jit(solution)/shard_map/reshape | solution.py:94
  173.7 7.3 %fusion = f32[64,8192]{1,0:T(8,128)} fusion(f32[64,64]{1,0:T(8,128)S(1)} %copy-done.3, f32[64,8192]{1,0:T(8,128)S(1)} %fusion.65, f32[64,8192]{1,0:T(8,128)} %copy.28, f32[64,8192]{1,0:T(8,128)} %convolution_bitcast_fusion.1), kind=kOutput, calls=%fused_computation.1 | convolution fusion | flops 405798912 | bytes 8404992 | tf_op jit(solution)/shard_map/dot_general | solution.py:87
  180.9 3.8 %copy.30 = f32[64,8192]{0,1:T(8,128)} copy(f32[64,8192]{1,0:T(8,128)} %fusion) | data formatting | bytes 4194304 | tf_op jit(solution)/shard_map/reshape | solution.py:90
  184.7 1.1 fusion.62
  185.8 3.0 %collective-permute-start.10 = (f32[64,1,256]{0,2,1:T(8,128)S(1)}, f32[64,1,256]{0,2,1:T(8,128)S(1)}, u32[]{:S(2)}, u32[]{:S(2)}) collective-permute-start(f32[64,1,256]{0,2,1:T(8,128)S(1)} %get-tuple-element.16), channel_id=1, source_target_pairs={{0,8},{8,16},{16,24},{24,32},{32,40},{40,48},{48,56},{56,64},{64,7... | collective-permute-start | bytes 196616 | tf_op jit(solution)/shard_map/ppermute | solution.py:20
  188.9 1.9 collective-permute-start.11
  190.8 5.2 %collective-permute-done.11 = f32[64,1,256]{0,2,1:T(8,128)S(1)} collective-permute-done((f32[64,1,256]{0,2,1:T(8,128)S(1)}, f32[64,1,256]{0,2,1:T(8,128)S(1)}, u32[]{:S(2)}, u32[]{:S(2)}) %collective-permute-start.11) | collective-permute-done | bytes 65568 | tf_op jit(solution)/shard_map/ppermute | solution.py:23
  196.1 1.0 pad_maximum_fusion.39
  197.1 1.9 collective-permute-start.12
  199.0 6.9 %collective-permute-start.13 = (f32[64,34,1]{0,2,1:T(1,128)S(1)}, f32[64,34,1]{0,2,1:T(1,128)S(1)}, u32[]{:S(2)}, u32[]{:S(2)}) collective-permute-start(f32[64,34,1]{0,2,1:T(1,128)S(1)} %get-tuple-element.8), channel_id=1, source_target_pairs={{0,1},{1,2},{2,3},{3,4},{4,5},{5,6},{6,7},{8,9},{9,10},{10,11},{11... | collective-permute-start | bytes 26120 | tf_op jit(solution)/shard_map/ppermute | solution.py:20
  206.0 0.8 collective-permute-done.13
  206.8 10.2 %fusion.19 = f32[64,32,256]{0,2,1:T(8,128)S(1)} fusion(f32[64,32,256]{0,2,1:T(8,128)S(1)} %bitcast.26, f32[64,1,256]{0,2,1:T(8,128)S(1)} %collective-permute-done.10, f32[64,1,256]{0,2,1:T(8,128)S(1)} %collective-permute-done.11, f32[64,34,1]{0,2,1:T(1,128)S(1)} %collective-permute-done.13, f32[64,34,1]{0,2,1:T(1,128)S(1)} %collective-permute-done.12, ...), kind=kLoop, calls=%fused_computation.30 | loop fusion | flops 11010048 | bytes 4473856 | tf_op jit(solution)/shard_map/add | solution.py:46
  217.0 2.0 collective-permute-start.14
  219.1 2.3 collective-permute-start.15
  221.4 4.9 %collective-permute-done.15 = f32[64,1,256]{0,2,1:T(8,128)S(1)} collective-permute-done((f32[64,1,256]{0,2,1:T(8,128)S(1)}, f32[64,1,256]{0,2,1:T(8,128)S(1)}, u32[]{:S(2)}, u32[]{:S(2)}) %collective-permute-start.15) | collective-permute-done | bytes 65568 | tf_op jit(solution)/shard_map/ppermute | solution.py:23
  226.3 1.9 collective-permute-start.16
  228.2 6.9 %collective-permute-start.17 = (f32[64,34,1]{0,2,1:T(1,128)S(1)}, f32[64,34,1]{0,2,1:T(1,128)S(1)}, u32[]{:S(2)}, u32[]{:S(2)}) collective-permute-start(f32[64,34,1]{0,2,1:T(1,128)S(1)} %get-tuple-element.6), channel_id=1, source_target_pairs={{0,1},{1,2},{2,3},{3,4},{4,5},{5,6},{6,7},{8,9},{9,10},{10,11},{11... | collective-permute-start | bytes 26120 | tf_op jit(solution)/shard_map/ppermute | solution.py:20
  235.2 0.8 collective-permute-done.17
  236.0 11.2 %fusion.6 = f32[64,32,256]{0,2,1:T(8,128)} fusion(f32[64,32,256]{0,2,1:T(8,128)S(1)} %fusion.19, f32[64,1,256]{0,2,1:T(8,128)S(1)} %collective-permute-done.14, f32[64,1,256]{0,2,1:T(8,128)S(1)} %collective-permute-done.15, f32[64,34,1]{0,2,1:T(1,128)S(1)} %collective-permute-done.17, f32[64,34,1]{0,2,1:T(1,128)S(1)} %collective-permute-done.16, ...), kind=kLoop, calls=%fused_computation.9 | loop fusion | flops 11534336 | bytes 4473856 | tf_op jit(solution)/shard_map/max | solution.py:92
  247.2 4.2 %copy.27 = f32[64,32,256]{2,1,0:T(8,128)} copy(f32[64,32,256]{0,2,1:T(8,128)} %fusion.6) | data formatting | bytes 4194304 | tf_op jit(solution)/shard_map/max | solution.py:92
  (30 shorter events, 0.2 us)
Async XLA Ops:
  0.0 95.3 %copy-start = (bf16[64,424]{1,0:T(8,128)(2,1)S(1)}, bf16[64,424]{1,0:T(8,128)(2,1)}, u32[]{:S(2)}) copy-start(bf16[64,424]{1,0:T(8,128)(2,1)} %param.6) | copy-start | bytes 162820
  0.0 7.0 %copy-start.4 = (s32[32,256]{1,0:T(8,128)S(1)}, s32[32,256]{1,0:T(8,128)}, u32[]{:S(2)}) copy-start(s32[32,256]{1,0:T(8,128)} %param.8) | copy-start | bytes 98308
  0.0 10.2 %copy-start.5 = (s32[32,256]{1,0:T(8,128)S(1)}, s32[32,256]{1,0:T(8,128)}, u32[]{:S(2)}) copy-start(s32[32,256]{1,0:T(8,128)} %param.9) | copy-start | bytes 98308
  0.0 84.2 %all-to-all-start = ((bf16[8,53,32,256]{3,2,1,0:T(8,128)(2,1)}), bf16[8,53,32,256]{3,2,1,0:T(8,128)(2,1)}, u32[]{:S(2)}, u32[]{:S(2)}) async-start(bf16[8,53,32,256]{3,2,1,0:T(8,128)(2,1)} %param.5), calls=%async_computation | async-start | bytes 13893632 | tf_op jit(solution)/shard_map/all_to_all | solution.py:78
  7.1 105.6 %collective-permute-start.3 = (f32[32,1]{1,0:T(8,128)S(1)}, f32[32,1]{1,0:T(8,128)S(1)}, u32[]{:S(2)}, u32[]{:S(2)}) collective-permute-start(f32[32,1]{1,0:T(8,128)S(1)} %slice.180), channel_id=1, source_target_pairs={{0,1},{1,2},{2,3},{3,4},{4,5},{5,6},{6,7},{8,9},{9,10},{10,11},{11... | collective-permute-start | bytes 392 | tf_op jit(solution)/shard_map/ppermute | solution.py:31
  10.3 116.4 %collective-permute-start.5 = (f32[1,256]{1,0:T(1,128)S(1)}, f32[1,256]{1,0:T(1,128)S(1)}, u32[]{:S(2)}, u32[]{:S(2)}) collective-permute-start(f32[1,256]{1,0:T(1,128)S(1)} %slice.181), channel_id=1, source_target_pairs={{0,8},{8,16},{16,24},{24,32},{32,40},{40,48},{48,56},{56,64},{64,7... | collective-permute-start | bytes 3080 | tf_op jit(solution)/shard_map/ppermute | solution.py:31
  95.3 1.5 copy-start.3
  104.0 26.0 %copy-start.1 = (f32[64,8192]{0,1:T(8,128)S(1)}, f32[64,8192]{0,1:T(8,128)}, u32[]{:S(2)}) copy-start(f32[64,8192]{0,1:T(8,128)} %copy.29) | copy-start | bytes 6291460
  105.1 7.7 %collective-permute-start = (f32[64,1,256]{0,2,1:T(8,128)S(1)}, f32[64,1,256]{0,2,1:T(8,128)S(1)}, u32[]{:S(2)}, u32[]{:S(2)}) collective-permute-start(f32[64,1,256]{0,2,1:T(8,128)S(1)} %get-tuple-element.20), channel_id=1, source_target_pairs={{0,8},{8,16},{16,24},{24,32},{32,40},{40,48},{48,56},{56,64},{64,7... | collective-permute-start | bytes 196616 | tf_op jit(solution)/shard_map/ppermute | solution.py:20
  110.8 7.2 %collective-permute-start.1 = (f32[64,1,256]{0,2,1:T(8,128)S(1)}, f32[64,1,256]{0,2,1:T(8,128)S(1)}, u32[]{:S(2)}, u32[]{:S(2)}) collective-permute-start(f32[64,1,256]{0,2,1:T(8,128)S(1)} %get-tuple-element.19), channel_id=1, source_target_pairs={{8,0},{16,8},{24,16},{32,24},{40,32},{48,40},{56,48},{64,56},{72,6... | collective-permute-start | bytes 196616 | tf_op jit(solution)/shard_map/ppermute | solution.py:23
  119.0 7.7 %collective-permute-start.2 = (f32[64,34,1]{0,2,1:T(1,128)S(1)}, f32[64,34,1]{0,2,1:T(1,128)S(1)}, u32[]{:S(2)}, u32[]{:S(2)}) collective-permute-start(f32[64,34,1]{0,2,1:T(1,128)S(1)} %get-tuple-element.11), channel_id=1, source_target_pairs={{1,0},{2,1},{3,2},{4,3},{5,4},{6,5},{7,6},{9,8},{10,9},{11,10},{12... | collective-permute-start | bytes 26120 | tf_op jit(solution)/shard_map/ppermute | solution.py:23
  124.0 6.0 %collective-permute-start.4 = (f32[64,34,1]{0,2,1:T(1,128)S(1)}, f32[64,34,1]{0,2,1:T(1,128)S(1)}, u32[]{:S(2)}, u32[]{:S(2)}) collective-permute-start(f32[64,34,1]{0,2,1:T(1,128)S(1)} %get-tuple-element.12), channel_id=1, source_target_pairs={{0,1},{1,2},{2,3},{3,4},{4,5},{5,6},{6,7},{8,9},{9,10},{10,11},{11... | collective-permute-start | bytes 26120 | tf_op jit(solution)/shard_map/ppermute | solution.py:20
  140.2 4.5 %collective-permute-start.6 = (f32[64,1,256]{0,2,1:T(8,128)S(1)}, f32[64,1,256]{0,2,1:T(8,128)S(1)}, u32[]{:S(2)}, u32[]{:S(2)}) collective-permute-start(f32[64,1,256]{0,2,1:T(8,128)S(1)} %get-tuple-element.18), channel_id=1, source_target_pairs={{0,8},{8,16},{16,24},{24,32},{32,40},{40,48},{48,56},{56,64},{64,7... | collective-permute-start | bytes 196616 | tf_op jit(solution)/shard_map/ppermute | solution.py:20
  142.8 7.2 %collective-permute-start.7 = (f32[64,1,256]{0,2,1:T(8,128)S(1)}, f32[64,1,256]{0,2,1:T(8,128)S(1)}, u32[]{:S(2)}, u32[]{:S(2)}) collective-permute-start(f32[64,1,256]{0,2,1:T(8,128)S(1)} %get-tuple-element.17), channel_id=1, source_target_pairs={{8,0},{16,8},{24,16},{32,24},{40,32},{48,40},{56,48},{64,56},{72,6... | collective-permute-start | bytes 196616 | tf_op jit(solution)/shard_map/ppermute | solution.py:23
  150.1 7.7 %collective-permute-start.8 = (f32[64,34,1]{0,2,1:T(1,128)S(1)}, f32[64,34,1]{0,2,1:T(1,128)S(1)}, u32[]{:S(2)}, u32[]{:S(2)}) collective-permute-start(f32[64,34,1]{0,2,1:T(1,128)S(1)} %get-tuple-element.9), channel_id=1, source_target_pairs={{1,0},{2,1},{3,2},{4,3},{5,4},{6,5},{7,6},{9,8},{10,9},{11,10},{12... | collective-permute-start | bytes 26120 | tf_op jit(solution)/shard_map/ppermute | solution.py:23
  152.0 6.6 %collective-permute-start.9 = (f32[64,34,1]{0,2,1:T(1,128)S(1)}, f32[64,34,1]{0,2,1:T(1,128)S(1)}, u32[]{:S(2)}, u32[]{:S(2)}) collective-permute-start(f32[64,34,1]{0,2,1:T(1,128)S(1)} %get-tuple-element.10), channel_id=1, source_target_pairs={{0,1},{1,2},{2,3},{3,4},{4,5},{5,6},{6,7},{8,9},{9,10},{10,11},{11... | collective-permute-start | bytes 26120 | tf_op jit(solution)/shard_map/ppermute | solution.py:20
  184.7 22.1 %copy-start.2 = (f32[64,8192]{0,1:T(8,128)S(1)}, f32[64,8192]{0,1:T(8,128)}, u32[]{:S(2)}) copy-start(f32[64,8192]{0,1:T(8,128)} %copy.30) | copy-start | bytes 6291460
  185.8 5.0 %collective-permute-start.10 = (f32[64,1,256]{0,2,1:T(8,128)S(1)}, f32[64,1,256]{0,2,1:T(8,128)S(1)}, u32[]{:S(2)}, u32[]{:S(2)}) collective-permute-start(f32[64,1,256]{0,2,1:T(8,128)S(1)} %get-tuple-element.16), channel_id=1, source_target_pairs={{0,8},{8,16},{16,24},{24,32},{32,40},{40,48},{48,56},{56,64},{64,7... | collective-permute-start | bytes 196616 | tf_op jit(solution)/shard_map/ppermute | solution.py:20
  188.9 7.2 %collective-permute-start.11 = (f32[64,1,256]{0,2,1:T(8,128)S(1)}, f32[64,1,256]{0,2,1:T(8,128)S(1)}, u32[]{:S(2)}, u32[]{:S(2)}) collective-permute-start(f32[64,1,256]{0,2,1:T(8,128)S(1)} %get-tuple-element.15), channel_id=1, source_target_pairs={{8,0},{16,8},{24,16},{32,24},{40,32},{48,40},{56,48},{64,56},{72,6... | collective-permute-start | bytes 196616 | tf_op jit(solution)/shard_map/ppermute | solution.py:23
  197.1 8.9 %collective-permute-start.12 = (f32[64,34,1]{0,2,1:T(1,128)S(1)}, f32[64,34,1]{0,2,1:T(1,128)S(1)}, u32[]{:S(2)}, u32[]{:S(2)}) collective-permute-start(f32[64,34,1]{0,2,1:T(1,128)S(1)} %get-tuple-element.7), channel_id=1, source_target_pairs={{1,0},{2,1},{3,2},{4,3},{5,4},{6,5},{7,6},{9,8},{10,9},{11,10},{12... | collective-permute-start | bytes 26120 | tf_op jit(solution)/shard_map/ppermute | solution.py:23
  199.0 7.8 %collective-permute-start.13 = (f32[64,34,1]{0,2,1:T(1,128)S(1)}, f32[64,34,1]{0,2,1:T(1,128)S(1)}, u32[]{:S(2)}, u32[]{:S(2)}) collective-permute-start(f32[64,34,1]{0,2,1:T(1,128)S(1)} %get-tuple-element.8), channel_id=1, source_target_pairs={{0,1},{1,2},{2,3},{3,4},{4,5},{5,6},{6,7},{8,9},{9,10},{10,11},{11... | collective-permute-start | bytes 26120 | tf_op jit(solution)/shard_map/ppermute | solution.py:20
  217.0 4.3 %collective-permute-start.14 = (f32[64,1,256]{0,2,1:T(8,128)S(1)}, f32[64,1,256]{0,2,1:T(8,128)S(1)}, u32[]{:S(2)}, u32[]{:S(2)}) collective-permute-start(f32[64,1,256]{0,2,1:T(8,128)S(1)} %get-tuple-element.14), channel_id=1, source_target_pairs={{0,8},{8,16},{16,24},{24,32},{32,40},{40,48},{48,56},{56,64},{64,7... | collective-permute-start | bytes 196616 | tf_op jit(solution)/shard_map/ppermute | solution.py:20
  219.1 7.2 %collective-permute-start.15 = (f32[64,1,256]{0,2,1:T(8,128)S(1)}, f32[64,1,256]{0,2,1:T(8,128)S(1)}, u32[]{:S(2)}, u32[]{:S(2)}) collective-permute-start(f32[64,1,256]{0,2,1:T(8,128)S(1)} %get-tuple-element.13), channel_id=1, source_target_pairs={{8,0},{16,8},{24,16},{32,24},{40,32},{48,40},{56,48},{64,56},{72,6... | collective-permute-start | bytes 196616 | tf_op jit(solution)/shard_map/ppermute | solution.py:23
  226.3 8.9 %collective-permute-start.16 = (f32[64,34,1]{0,2,1:T(1,128)S(1)}, f32[64,34,1]{0,2,1:T(1,128)S(1)}, u32[]{:S(2)}, u32[]{:S(2)}) collective-permute-start(f32[64,34,1]{0,2,1:T(1,128)S(1)} %get-tuple-element.5), channel_id=1, source_target_pairs={{1,0},{2,1},{3,2},{4,3},{5,4},{6,5},{7,6},{9,8},{10,9},{11,10},{12... | collective-permute-start | bytes 26120 | tf_op jit(solution)/shard_map/ppermute | solution.py:23
  228.2 7.8 %collective-permute-start.17 = (f32[64,34,1]{0,2,1:T(1,128)S(1)}, f32[64,34,1]{0,2,1:T(1,128)S(1)}, u32[]{:S(2)}, u32[]{:S(2)}) collective-permute-start(f32[64,34,1]{0,2,1:T(1,128)S(1)} %get-tuple-element.6), channel_id=1, source_target_pairs={{0,1},{1,2},{2,3},{3,4},{4,5},{5,6},{6,7},{8,9},{9,10},{10,11},{11... | collective-permute-start | bytes 26120 | tf_op jit(solution)/shard_map/ppermute | solution.py:20
where the time goes:
time: 256 us; the launch traced here: 251 us
  waiting for transfers between devices  95 us (37%)
  starting transfers between devices  69.8 us (27%)
  other arithmetic  45 us (18%)
  local copies, waits for them, and re-layouts  29.1 us (11%)
  matrix products  12.1 us (5%)
    all_to_all x1, waiting for transfers between devices, per_device(): lax.all_to_all(cube, 'col', split_axis=0, concat_axis=1, tiled=True)  68.7 us
    ppermute x8, starting transfers between devices, extended(): lax.ppermute(lax.slice_in_dim(block, block.shape[dim] - width, None, axis...  35.7 us
    max x2, other arithmetic, per_device(): result = jnp.maximum(field, jnp.float32(0.0))  22.4 us
    ppermute x8, waiting for transfers between devices, extended(): lax.ppermute(lax.slice_in_dim(block, 0, width, axis=dim), axis, backward)  20.5 us
    add x2, other arithmetic, diffuse(): return center + KAPPA * flux  20.4 us
    ppermute x8, starting transfers between devices, extended(): lax.ppermute(lax.slice_in_dim(block, 0, width, axis=dim), axis, backward)  18.8 us
    unnamed x13, local copies, waits for them, and re-layouts  11.1 us
    dot_general x2, matrix products, per_device(): jnp.dot(inverse, projected + PENALTY * (kept - dual), precision=lax.Preci...  10.6 us
  transfers between devices with their start and end apart: 19, of which 9 were waited for; matrix products, arithmetic and copies ran while one was open for 9% of the time, Pallas kernels for 0%

commit v1 on v0

v1 whole, which is shorter than its diff:
```python
import functools

import jax
import jax.numpy as jnp
from jax import lax
from jax.experimental import pallas as pl
from jax.experimental.pallas import tpu as pltpu
from jax.sharding import PartitionSpec as P

KAPPA = 0.24
EDGE_SCALE = 1.0 / 255.0
HALO = 4
LANES = 384


def neighbours(axis, low_part, high_part):
    count = lax.axis_size(axis)
    forward = [(i, i + 1) for i in range(count - 1)]
    backward = [(i + 1, i) for i in range(count - 1)]
    return lax.ppermute(high_part, axis, forward), lax.ppermute(low_part, axis, backward)


def ring_lanes(block):
    width = block.shape[-1]
    left, right = neighbours("col", block[..., :HALO], block[..., width - HALO :])
    gap = jnp.zeros(block.shape[:-1] + (LANES - width - 2 * HALO,), block.dtype)
    return jnp.concatenate([right, gap, left], axis=-1)


def split3(x):
    hi = x.astype(jnp.bfloat16)
    lo = (x - hi.astype(jnp.float32)).astype(jnp.bfloat16)
    return jnp.concatenate([hi, hi, lo], axis=0)


def admm_kernel(inv_ref, p_ref, side_ref, top_ref, bottom_ref, wh_ref, wv_ref, out_ref, mixed, z):
    rows, count, width = p_ref.shape
    total = rows + 2 * HALO
    inv = inv_ref[...]

    def mix(x):
        return jnp.dot(inv, split3(x), preferred_element_type=jnp.float32)

    for i in range(HALO):
        mixed[i] = mix(top_ref[i])
        mixed[total - HALO + i] = mix(bottom_ref[i])

    def first(i, _):
        x = jnp.concatenate([p_ref[i], side_ref[i]], axis=1)
        mixed[i + HALO] = mix(x)
        return 0

    lax.fori_loop(0, rows, first, 0, unroll=2)

    def weight(ref, i):
        return jnp.broadcast_to(ref[pl.ds(i, 1), :], (count, LANES))

    def diffuse(src, begin, end, store):
        def body(i, carry):
            here, above = carry
            below = src[i + 1]
            down = weight(wv_ref, i) * (below - here)
            across = weight(wh_ref, i) * (pltpu.roll(here, LANES - 1, 1) - here)
            store(i, here + (across - pltpu.roll(across, 1, 1)) + (down - above))
            return below, down

        here = src[begin]
        above = weight(wv_ref, begin - 1) * (here - src[begin - 1])
        lax.fori_loop(begin, end, body, (here, above))

    def to_z(i, value):
        z[i] = value

    def second(i, smoothed):
        kept = jnp.maximum(smoothed, 0.0)
        before = mixed[i]
        z[i] = mix(kept - 0.5 * before) + (2.0 * before - kept)

    def emit(i, smoothed):
        out_ref[i - HALO] = jnp.maximum(smoothed[:, :width], 0.0)

    diffuse(mixed, 1, total - 1, to_z)
    diffuse(z, 2, total - 2, second)
    diffuse(z, 3, total - 3, to_z)
    diffuse(z, 4, total - 4, emit)


def admm(inv3, projected, side, top, bottom, wh, wv):
    rows, count, width = projected.shape
    total = rows + 2 * HALO
    vmem = pl.BlockSpec(memory_space=pltpu.VMEM)
    out = pl.pallas_call(
        admm_kernel,
        out_shape=jax.ShapeDtypeStruct((rows, count, width), jnp.float32),
        in_specs=[vmem] * 7,
        out_specs=vmem,
        scratch_shapes=[
            pltpu.VMEM((total, count, LANES), jnp.float32),
            pltpu.VMEM((total, count, LANES), jnp.float32),
        ],
        compiler_params=pltpu.CompilerParams(vmem_limit_bytes=40 * 2**20),
    )(inv3, projected, side, top, bottom, wh, wv)
    return jnp.transpose(out, (1, 0, 2))


def per_device(cube, library_t, inverse, weight_h, weight_v):
    col_count = lax.axis_size("col")
    row_count = lax.axis_size("row")
    tile_h, tile_w = weight_h.shape
    rows = lax.axis_index("row") * tile_h + lax.broadcasted_iota(jnp.int32, (tile_h, tile_w), 0)
    cols = lax.axis_index("col") * tile_w + lax.broadcasted_iota(jnp.int32, (tile_h, tile_w), 1)
    wh = jnp.where(cols < tile_w * col_count - 1, weight_h.astype(jnp.float32), 0.0)
    wv = jnp.where(rows < tile_h * row_count - 1, weight_v.astype(jnp.float32), 0.0)
    weights = jnp.stack([wh, wv], axis=1) * (KAPPA * EDGE_SCALE)
    weights = jnp.concatenate([weights, ring_lanes(weights)], axis=-1)
    above, below = neighbours("row", weights[:HALO], weights[tile_h - HALO :])
    weights = jnp.concatenate([above, weights, below], axis=0)

    received = lax.all_to_all(cube, "col", split_axis=0, concat_axis=1, tiled=True)
    projected = jnp.einsum(
        "eb,cbhw->hew", library_t, received, preferred_element_type=jnp.float32
    )
    side = ring_lanes(projected)
    top, bottom = neighbours(
        "row",
        jnp.concatenate([projected[:HALO], side[:HALO]], axis=-1),
        jnp.concatenate([projected[tile_h - HALO :], side[tile_h - HALO :]], axis=-1),
    )
    inv_hi = lax.reduce_precision(inverse, 8, 7)
    inv3 = jnp.concatenate([inv_hi, inverse - inv_hi, inv_hi], axis=1).astype(jnp.bfloat16)
    return admm(inv3, projected, side, top, bottom, weights[:, 0], weights[:, 1])


def solution(mesh):
    return jax.shard_map(
        per_device,
        mesh=mesh,
        in_specs=(P(None, "col", "row", None), P(), P(), P("row", "col"), P("row", "col")),
        out_specs=P(None, "row", "col"),
        check_vma=False,
    )
```

time: 256 us -> 177 us (0.69); the launches traced: 251 us -> 176 us
  other arithmetic: 45 us -> 5.74 us
  Pallas kernels: 0 us -> 34 us
  starting transfers between devices: 69.8 us -> 37.5 us
  local copies, waits for them, and re-layouts: 29.1 us -> 12 us
  waiting for transfers between devices: 95 us -> 79 us
  matrix products: 12.1 us -> 7.09 us
    all_to_all x1, waiting for transfers between devices: 68.7 us -> 0.01 us  [per_device(): lax.all_to_all(cube, 'col', split_axis=0, concat_axis=1, tiled=True)]
    ppermute x18 -> x8, waiting for transfers between devices: 26.3 us -> 79 us  [the longest x4 75.8 us: neighbours(): lax.ppermute(low_part, axis, backward)]
    pallas_call x0 -> x1, Pallas kernels: none -> 34 us  [admm(): pl.pallas_call(admm_kernel, out_shape=jax.ShapeDtypeStruct((rows, count,...]
    ppermute x18 -> x8, starting transfers between devices: 62.8 us -> 30.5 us  [the longest x4 22.8 us: neighbours(): lax.ppermute(high_part, axis, forward)]
    max x2 -> x0, other arithmetic: 22.4 us -> none  [per_device(): result = jnp.maximum(field, jnp.float32(0.0))]
    add x2 -> x0, other arithmetic: 20.4 us -> none  [diffuse(): return center + KAPPA * flux]
    reshape x3 -> x0, local copies, waits for them, and re-layouts: 11.4 us -> none  [the longest x2 7.59 us: per_device(): field = (mixed + dual).reshape((count,) + local_shape)]
    unnamed x13 -> x14, local copies, waits for them, and re-layouts: 11.1 us -> 0.65 us
  transfers between devices with their start and end apart: 19 -> 9, of which waited for: 9 -> 4; matrix products, arithmetic and copies ran while one was open for 9% -> 12% of each run, Pallas kernels for 0% -> 0%
where the time goes in v1:
time: 177 us; the launch traced here: 176 us
  waiting for transfers between devices  79 us (45%)
  starting transfers between devices  37.5 us (21%)
  Pallas kernels  34 us (19%)
  local copies, waits for them, and re-layouts  12 us (7%)
  matrix products  7.09 us (4%)
  other arithmetic  5.74 us (3%)
    ppermute x4, waiting for transfers between devices, neighbours(): lax.ppermute(low_part, axis, backward)  75.8 us
    pallas_call x1, Pallas kernels, admm(): pl.pallas_call(admm_kernel, out_shape=jax.ShapeDtypeStruct((rows, count,...  34 us
    ppermute x4, starting transfers between devices, neighbours(): lax.ppermute(high_part, axis, forward)  22.8 us
    ppermute x4, starting transfers between devices, neighbours(): lax.ppermute(low_part, axis, backward)  7.68 us
    dot_general x1, matrix products, per_device(): jnp.einsum('eb,cbhw->hew', library_t, received, preferred_element_type=jn...  7.09 us
    all_to_all x1, starting transfers between devices, per_device(): lax.all_to_all(cube, 'col', split_axis=0, concat_axis=1, tiled=True)  7.02 us
  transfers between devices with their start and end apart: 9, of which 4 were waited for; matrix products, arithmetic and copies ran while one was open for 12% of the time, Pallas kernels for 0%

profile of v1, /device:TPU:39, one launch (start us, length us, event | category | flops | bytes accessed | tf_op | source)
XLA Modules:
  0.0 175.6 jit_solution(7778991240141464635)
XLA Ops:
  0.0 0.0 copy-start
  0.0 0.0 copy-start.5
  0.0 0.0 copy-start.6
  0.0 0.0 copy-start.4
  0.0 7.0 %all-to-all-start = ((bf16[8,53,32,256]{3,2,1,0:T(8,128)(2,1)}), bf16[8,53,32,256]{3,2,1,0:T(8,128)(2,1)}, u32[]{:S(2)}, u32[]{:S(2)}) async-start(bf16[8,53,32,256]{3,2,1,0:T(8,128)(2,1)} %param.5), calls=%async_computation | async-start | bytes 13893632 | tf_op jit(solution)/shard_map/all_to_all | solution.py:119
  7.1 0.0 copy-done.5
  7.1 0.0 copy-done.6
  7.1 0.1 select_bitcast_fusion
  7.2 0.1 fusion.10
  7.2 1.9 %collective-permute-start.4 = (f32[32,2,4]{2,0,1:T(8,128)S(1)}, f32[32,2,4]{2,0,1:T(8,128)S(1)}, u32[]{:S(2)}, u32[]{:S(2)}) collective-permute-start(f32[32,2,4]{2,0,1:T(8,128)S(1)} %get-tuple-element.15), channel_id=1, source_target_pairs={{1,0},{2,1},{3,2},{4,3},{5,4},{6,5},{7,6},{9,8},{10,9},{11,10},{12... | collective-permute-start | bytes 3080 | tf_op jit(solution)/shard_map/ppermute | solution.py:20
  9.2 5.8 %collective-permute-start.5 = (f32[32,2,4]{2,0,1:T(8,128)S(1)}, f32[32,2,4]{2,0,1:T(8,128)S(1)}, u32[]{:S(2)}, u32[]{:S(2)}) collective-permute-start(f32[32,2,4]{2,0,1:T(8,128)S(1)} %get-tuple-element.16), channel_id=1, source_target_pairs={{0,1},{1,2},{2,3},{3,4},{4,5},{5,6},{6,7},{8,9},{9,10},{10,11},{11... | collective-permute-start | bytes 3080 | tf_op jit(solution)/shard_map/ppermute | solution.py:20
  14.9 0.0 copy-done.4
  14.9 0.6 fusion.6
  15.6 0.6 pad.17.clone
  16.1 67.0 %collective-permute-done.4 = f32[32,2,4]{2,0,1:T(8,128)S(1)} collective-permute-done((f32[32,2,4]{2,0,1:T(8,128)S(1)}, f32[32,2,4]{2,0,1:T(8,128)S(1)}, u32[]{:S(2)}, u32[]{:S(2)}) %collective-permute-start.4) | collective-permute-done | bytes 1056 | tf_op jit(solution)/shard_map/ppermute | solution.py:20
  83.1 0.0 collective-permute-done.5
  83.1 0.0 copy-start.1
  83.2 0.6 copy-done.1
  83.8 0.7 pad_maximum_fusion.8
  84.5 0.0 copy-done.2
  84.5 0.0 copy-done.3
  84.5 6.2 %collective-permute-start.6 = (f32[4,2,384]{2,0,1:T(4,128)}, f32[4,2,384]{2,0,1:T(4,128)}, u32[]{:S(2)}, u32[]{:S(2)}) collective-permute-start(f32[4,2,384]{2,0,1:T(4,128)} %get-tuple-element.11), channel_id=1, source_target_pairs={{0,8},{8,16},{16,24},{24,32},{32,40},{40,48},{48,56},{56,64},{64,7... | collective-permute-start | bytes 36872 | tf_op jit(solution)/shard_map/ppermute | solution.py:20
  90.7 1.9 %collective-permute-start.7 = (f32[4,2,384]{2,0,1:T(4,128)}, f32[4,2,384]{2,0,1:T(4,128)}, u32[]{:S(2)}, u32[]{:S(2)}) collective-permute-start(f32[4,2,384]{2,0,1:T(4,128)} %get-tuple-element.12), channel_id=1, source_target_pairs={{8,0},{16,8},{24,16},{32,24},{40,32},{48,40},{56,48},{64,56},{72,6... | collective-permute-start | bytes 36872 | tf_op jit(solution)/shard_map/ppermute | solution.py:20
  92.6 0.0 all-to-all-done
  92.6 0.0 copy-done
  92.6 7.1 %fusion.2.p_ref = f32[32,64,256]{2,1,0:T(8,128)S(1)} fusion(bf16[424,32,256]{2,1,0:T(8,128)(2,1)} %bitcast, bf16[64,424]{1,0:T(8,128)(2,1)S(1)} %copy-done), kind=kOutput, calls=%fused_computation.2 | convolution fusion | flops 444596224 | bytes 9098240 | tf_op jit(solution)/shard_map/eb,cbhw->hew/dot_general | solution.py:120
  99.7 1.3 fusion.8
  101.1 1.6 copy.11
  102.7 1.0 copy.12
  103.7 6.4 %collective-permute-start.1 = (f32[32,64,4]{1,0,2:T(8,128)}, f32[32,64,4]{1,0,2:T(8,128)}, u32[]{:S(2)}, u32[]{:S(2)}) collective-permute-start(f32[32,64,4]{1,0,2:T(8,128)} %copy.12), channel_id=1, source_target_pairs={{0,1},{1,2},{2,3},{3,4},{4,5},{5,6},{6,7},{8,9},{9,10},{10,11},{11... | collective-permute-start | bytes 98312 | tf_op jit(solution)/shard_map/ppermute | solution.py:20
  110.0 1.9 %collective-permute-start = (f32[32,64,4]{1,0,2:T(8,128)S(1)}, f32[32,64,4]{1,0,2:T(8,128)}, u32[]{:S(2)}, u32[]{:S(2)}) collective-permute-start(f32[32,64,4]{1,0,2:T(8,128)S(1)} %copy.11), channel_id=1, source_target_pairs={{1,0},{2,1},{3,2},{4,3},{5,4},{6,5},{7,6},{9,8},{10,9},{11,10},{12... | collective-permute-start | bytes 98312 | tf_op jit(solution)/shard_map/ppermute | solution.py:20
  112.0 0.8 fusion.7
  112.7 5.7 %collective-permute-done = f32[32,64,4]{1,0,2:T(8,128)} collective-permute-done((f32[32,64,4]{1,0,2:T(8,128)S(1)}, f32[32,64,4]{1,0,2:T(8,128)}, u32[]{:S(2)}, u32[]{:S(2)}) %collective-permute-start) | collective-permute-done | bytes 32800 | tf_op jit(solution)/shard_map/ppermute | solution.py:20
  118.5 1.2 copy.13
  119.7 0.0 collective-permute-done.1
  119.7 2.2 %copy.14 = f32[32,64,4]{2,1,0:T(8,128)} copy(f32[32,64,4]{1,0,2:T(8,128)} %collective-permute-done.1) | data formatting | bytes 65536 | tf_op jit(solution)/shard_map/ppermute | solution.py:20
  121.9 1.6 pad_maximum_fusion.side_ref
  123.5 1.0 pad_maximum_fusion.1
  124.5 4.5 %collective-permute-start.2 = (f32[4,64,384]{2,1,0:T(8,128)S(1)}, f32[4,64,384]{2,1,0:T(8,128)S(1)}, u32[]{:S(2)}, u32[]{:S(2)}) collective-permute-start(f32[4,64,384]{2,1,0:T(8,128)S(1)} %pad_maximum_fusion.1), channel_id=1, source_target_pairs={{0,8},{8,16},{16,24},{24,32},{32,40},{40,48},{48,56},{56,64},{64,7... | collective-permute-start | bytes 1179656 | tf_op jit(solution)/shard_map/ppermute | solution.py:20
  129.0 1.9 %collective-permute-start.3 = (f32[4,64,384]{2,1,0:T(8,128)S(1)}, f32[4,64,384]{2,1,0:T(8,128)S(1)}, u32[]{:S(2)}, u32[]{:S(2)}) collective-permute-start(f32[4,64,384]{2,1,0:T(8,128)S(1)} %pad_maximum_fusion.2), channel_id=1, source_target_pairs={{8,0},{16,8},{24,16},{32,24},{40,32},{48,40},{56,48},{64,56},{72,6... | collective-permute-start | bytes 1179656 | tf_op jit(solution)/shard_map/ppermute | solution.py:20
  130.9 0.9 pad_maximum_fusion.4.inv_ref
  131.8 0.0 collective-permute-done.6
  131.8 0.0 collective-permute-done.7
  131.8 0.9 pad_maximum_fusion.3
  132.8 3.2 %collective-permute-done.2.top_ref = f32[4,64,384]{2,1,0:T(8,128)S(1)} collective-permute-done((f32[4,64,384]{2,1,0:T(8,128)S(1)}, f32[4,64,384]{2,1,0:T(8,128)S(1)}, u32[]{:S(2)}, u32[]{:S(2)}) %collective-permute-start.2) | collective-permute-done | bytes 393248 | tf_op jit(solution)/shard_map/ppermute | solution.py:20
  136.0 3.0 %collective-permute-done.3.bottom_ref = f32[4,64,384]{2,1,0:T(8,128)S(1)} collective-permute-done((f32[4,64,384]{2,1,0:T(8,128)S(1)}, f32[4,64,384]{2,1,0:T(8,128)S(1)}, u32[]{:S(2)}, u32[]{:S(2)}) %collective-permute-start.3) | collective-permute-done | bytes 393248 | tf_op jit(solution)/shard_map/ppermute | solution.py:20
  139.0 34.0 %shard_map.55 = f32[32,64,256]{2,1,0:T(8,128)S(1)} custom-call(bf16[64,192]{1,0:T(8,128)(2,1)S(1)} %pad_maximum_fusion.4.inv_ref, f32[32,64,256]{2,1,0:T(8,128)S(1)} %fusion.2.p_ref, f32[32,64,128]{2,1,0:T(8,128)S(1)} %pad_maximum_fusion.side_ref, f32[4,64,384]{2,1,0:T(8,128)S(1)} %collective-permute-done.2.top_ref, ...), custom_call_target="tpu_custom_call" | custom-call | tf_op jit(solution)/shard_map/pallas_call | solution.py:92
  173.0 2.5 %copy.15 = f32[64,32,256]{2,1,0:T(8,128)} copy(f32[64,32,256]{2,0,1:T(8,128)S(1)} %bitcast.15) | data formatting | bytes 4194304 | tf_op jit(solution)/shard_map/transpose | solution.py:103
  (10 shorter events, 0.1 us)
Async XLA Ops:
  0.0 92.6 %copy-start = (bf16[64,424]{1,0:T(8,128)(2,1)S(1)}, bf16[64,424]{1,0:T(8,128)(2,1)}, u32[]{:S(2)}) copy-start(bf16[64,424]{1,0:T(8,128)(2,1)} %param.6) | copy-start | bytes 162820
  0.0 7.1 %copy-start.5 = (s32[32,256]{1,0:T(8,128)S(1)}, s32[32,256]{1,0:T(8,128)}, u32[]{:S(2)}) copy-start(s32[32,256]{1,0:T(8,128)} %param.9) | copy-start | bytes 98308
  0.0 7.1 %copy-start.6 = (s32[32,256]{1,0:T(8,128)S(1)}, s32[32,256]{1,0:T(8,128)}, u32[]{:S(2)}) copy-start(s32[32,256]{1,0:T(8,128)} %param.8) | copy-start | bytes 98308
  0.0 14.9 %copy-start.4 = (f32[64,64]{1,0:T(8,128)S(1)}, f32[64,64]{1,0:T(8,128)}, u32[]{:S(2)}) copy-start(f32[64,64]{1,0:T(8,128)} %param.7) | copy-start | bytes 49156
  0.0 92.6 %all-to-all-start = ((bf16[8,53,32,256]{3,2,1,0:T(8,128)(2,1)}), bf16[8,53,32,256]{3,2,1,0:T(8,128)(2,1)}, u32[]{:S(2)}, u32[]{:S(2)}) async-start(bf16[8,53,32,256]{3,2,1,0:T(8,128)(2,1)} %param.5), calls=%async_computation | async-start | bytes 13893632 | tf_op jit(solution)/shard_map/all_to_all | solution.py:119
  7.2 75.9 %collective-permute-start.4 = (f32[32,2,4]{2,0,1:T(8,128)S(1)}, f32[32,2,4]{2,0,1:T(8,128)S(1)}, u32[]{:S(2)}, u32[]{:S(2)}) collective-permute-start(f32[32,2,4]{2,0,1:T(8,128)S(1)} %get-tuple-element.15), channel_id=1, source_target_pairs={{1,0},{2,1},{3,2},{4,3},{5,4},{6,5},{7,6},{9,8},{10,9},{11,10},{12... | collective-permute-start | bytes 3080 | tf_op jit(solution)/shard_map/ppermute | solution.py:20
  9.2 74.0 %collective-permute-start.5 = (f32[32,2,4]{2,0,1:T(8,128)S(1)}, f32[32,2,4]{2,0,1:T(8,128)S(1)}, u32[]{:S(2)}, u32[]{:S(2)}) collective-permute-start(f32[32,2,4]{2,0,1:T(8,128)S(1)} %get-tuple-element.16), channel_id=1, source_target_pairs={{0,1},{1,2},{2,3},{3,4},{4,5},{5,6},{6,7},{8,9},{9,10},{10,11},{11... | collective-permute-start | bytes 3080 | tf_op jit(solution)/shard_map/ppermute | solution.py:20
  83.1 1.3 copy-start.2
  83.1 1.3 copy-start.3
  83.1 0.6 copy-start.1
  84.5 47.4 %collective-permute-start.6 = (f32[4,2,384]{2,0,1:T(4,128)}, f32[4,2,384]{2,0,1:T(4,128)}, u32[]{:S(2)}, u32[]{:S(2)}) collective-permute-start(f32[4,2,384]{2,0,1:T(4,128)} %get-tuple-element.11), channel_id=1, source_target_pairs={{0,8},{8,16},{16,24},{24,32},{32,40},{40,48},{48,56},{56,64},{64,7... | collective-permute-start | bytes 36872 | tf_op jit(solution)/shard_map/ppermute | solution.py:20
  90.7 41.2 %collective-permute-start.7 = (f32[4,2,384]{2,0,1:T(4,128)}, f32[4,2,384]{2,0,1:T(4,128)}, u32[]{:S(2)}, u32[]{:S(2)}) collective-permute-start(f32[4,2,384]{2,0,1:T(4,128)} %get-tuple-element.12), channel_id=1, source_target_pairs={{8,0},{16,8},{24,16},{32,24},{40,32},{48,40},{56,48},{64,56},{72,6... | collective-permute-start | bytes 36872 | tf_op jit(solution)/shard_map/ppermute | solution.py:20
  103.7 16.1 %collective-permute-start.1 = (f32[32,64,4]{1,0,2:T(8,128)}, f32[32,64,4]{1,0,2:T(8,128)}, u32[]{:S(2)}, u32[]{:S(2)}) collective-permute-start(f32[32,64,4]{1,0,2:T(8,128)} %copy.12), channel_id=1, source_target_pairs={{0,1},{1,2},{2,3},{3,4},{4,5},{5,6},{6,7},{8,9},{9,10},{10,11},{11... | collective-permute-start | bytes 98312 | tf_op jit(solution)/shard_map/ppermute | solution.py:20
  110.0 8.4 %collective-permute-start = (f32[32,64,4]{1,0,2:T(8,128)S(1)}, f32[32,64,4]{1,0,2:T(8,128)}, u32[]{:S(2)}, u32[]{:S(2)}) collective-permute-start(f32[32,64,4]{1,0,2:T(8,128)S(1)} %copy.11), channel_id=1, source_target_pairs={{1,0},{2,1},{3,2},{4,3},{5,4},{6,5},{7,6},{9,8},{10,9},{11,10},{12... | collective-permute-start | bytes 98312 | tf_op jit(solution)/shard_map/ppermute | solution.py:20
  124.5 11.5 %collective-permute-start.2 = (f32[4,64,384]{2,1,0:T(8,128)S(1)}, f32[4,64,384]{2,1,0:T(8,128)S(1)}, u32[]{:S(2)}, u32[]{:S(2)}) collective-permute-start(f32[4,64,384]{2,1,0:T(8,128)S(1)} %pad_maximum_fusion.1), channel_id=1, source_target_pairs={{0,8},{8,16},{16,24},{24,32},{32,40},{40,48},{48,56},{56,64},{64,7... | collective-permute-start | bytes 1179656 | tf_op jit(solution)/shard_map/ppermute | solution.py:20
  129.0 10.0 %collective-permute-start.3 = (f32[4,64,384]{2,1,0:T(8,128)S(1)}, f32[4,64,384]{2,1,0:T(8,128)S(1)}, u32[]{:S(2)}, u32[]{:S(2)}) collective-permute-start(f32[4,64,384]{2,1,0:T(8,128)S(1)} %pad_maximum_fusion.2), channel_id=1, source_target_pairs={{8,0},{16,8},{24,16},{32,24},{40,32},{48,40},{56,48},{64,56},{72,6... | collective-permute-start | bytes 1179656 | tf_op jit(solution)/shard_map/ppermute | solution.py:20

commit v2 on v1

v2 whole, which is shorter than its diff:
```python
import jax
import jax.numpy as jnp
from jax import lax
from jax.experimental import pallas as pl
from jax.experimental.pallas import tpu as pltpu
from jax.sharding import PartitionSpec as P

KAPPA = 0.24
EDGE_SCALE = 1.0 / 255.0
HALO = 4
LEAD = 16
SPAN = 288
GROUP = 16


def parts3(x, axis):
    hi = x.astype(jnp.bfloat16)
    lo = (x - hi.astype(jnp.float32)).astype(jnp.bfloat16)
    return jnp.concatenate([hi, hi, lo], axis=axis)


def admm_kernel(
    inv_ref, invt_ref, outer_ref, inner_ref, side_ref, top_ref, bottom_ref, wh_ref, wv_ref,
    out_ref, mixed, y, z, turned,
):
    _, count, width = inner_ref.shape
    half = inner_ref.shape[0]
    quarter = half // 2
    deep = half + 2 * HALO
    inv = inv_ref[...]

    def mix_pairs(pairs, slot):
        cat = jnp.concatenate([parts3(x, 0) for pair in pairs for x in pair], axis=1)
        m = jnp.dot(inv, cat, preferred_element_type=jnp.float32)
        for k in range(len(pairs)):
            a = m[:, 2 * k * width : (2 * k + 1) * width]
            b = m[:, (2 * k + 1) * width : (2 * k + 2) * width]
            mixed[slot + k, LEAD : LEAD + width, :] = jnp.transpose(jnp.concatenate([a, b], 0))

    mix_pairs([(top_ref[k], inner_ref[quarter - HALO + k]) for k in range(HALO)], 0)
    mix_pairs([(inner_ref[quarter + k], bottom_ref[k]) for k in range(HALO)], deep - HALO)

    @pl.loop(0, quarter // 2)
    def _(g):
        r = g * 2
        mix_pairs([(outer_ref[r + k], inner_ref[r + k + quarter]) for k in range(2)], r + HALO)
        mix_pairs(
            [(inner_ref[r + k], outer_ref[r + k + quarter]) for k in range(2)],
            r + HALO + quarter,
        )

    side = jnp.dot(inv, parts3(side_ref[...], 0), preferred_element_type=jnp.float32)
    side = jnp.transpose(jnp.concatenate([side[:, :256], side[:, 128:]], axis=0))
    for r in range(deep):
        mixed[r, LEAD - 8 : LEAD, :] = side[8 * r : 8 * r + 8]
        mixed[r, LEAD + width : LEAD + width + 8, :] = side[8 * r : 8 * r + 8]

    def diffuse(src, dst, begin, end):
        @pl.loop(0, (width + 16) // GROUP)
        def _(g):
            c = pl.multiple_of(LEAD - 8 + g * GROUP, 8)
            at, after, before = pl.ds(c, GROUP), pl.ds(c + 1, GROUP), pl.ds(c - 1, GROUP)
            here = src[begin, at]
            above = wv_ref[begin - 1, at] * (here - src[begin - 1, at])
            for i in range(begin, end):
                below = src[i + 1, at]
                down = wv_ref[i, at] * (below - here)
                right = wh_ref[i, at] * (src[i, after] - here)
                left = wh_ref[i, before] * (here - src[i, before])
                dst[i, at] = here + (right - left) + (down - above)
                here, above = below, down

    diffuse(mixed, z, 1, deep - 1)
    diffuse(z, y, 2, deep - 2)
    invt = invt_ref[...]
    used = pl.ds(LEAD - 8, width + 16)

    @pl.loop(2, deep - 2, step=2)
    def _(first):
        for k in range(2):
            kept = jnp.maximum(y[first + k, used], 0.0)
            before = mixed[first + k, used]
            u = parts3(kept - 0.5 * before, 1)
            m = jnp.dot(u, invt, preferred_element_type=jnp.float32)
            z[first + k, used] = m + (2.0 * before - kept)

    diffuse(z, y, 3, deep - 3)
    diffuse(y, z, 4, deep - 4)

    @pl.loop(0, half // 2)
    def _(g):
        for k in range(2):
            r = g * 2 + k
            v = jnp.transpose(jnp.maximum(z[r + HALO, LEAD : LEAD + width], 0.0))
            for h in range(2):
                for t in range(width // 128):
                    turned[t, pl.ds(r + h * half, count, stride=2 * half), :] = v[
                        h * count : (h + 1) * count, t * 128 : (t + 1) * 128
                    ]

    @pl.loop(0, count // 8)
    def _(g):
        for k in range(8):
            e = g * 8 + k
            for t in range(width // 128):
                out_ref[e, :, t * 128 : (t + 1) * 128] = turned[t, pl.ds(e * 2 * half, 2 * half), :]


def admm(inv3, inv3t, outer, inner, side, top, bottom, wh, wv):
    half, count, width = inner.shape
    vmem = pl.BlockSpec(memory_space=pltpu.VMEM)
    field = pltpu.VMEM((half + 2 * HALO, SPAN, 2 * count), jnp.float32)
    return pl.pallas_call(
        admm_kernel,
        out_shape=jax.ShapeDtypeStruct((count, 2 * half, width), jnp.float32),
        in_specs=[vmem] * 9,
        out_specs=vmem,
        scratch_shapes=[
            field,
            field,
            field,
            pltpu.VMEM((width // 128, count * 2 * half, 128), jnp.float32),
        ],
        compiler_params=pltpu.CompilerParams(vmem_limit_bytes=32 * 2**20),
    )(inv3, inv3t, outer, inner, side, top, bottom, wh, wv)


def neighbours(axis, low_part, high_part):
    count = lax.axis_size(axis)
    forward = [(i, i + 1) for i in range(count - 1)]
    backward = [(i + 1, i) for i in range(count - 1)]
    return lax.ppermute(high_part, axis, forward), lax.ppermute(low_part, axis, backward)


def scaled_weights(weight_h, weight_v):
    col_count = lax.axis_size("col")
    row_count = lax.axis_size("row")
    tile_h, tile_w = weight_h.shape
    rows = lax.axis_index("row") * tile_h + lax.broadcasted_iota(jnp.int32, (tile_h, tile_w), 0)
    cols = lax.axis_index("col") * tile_w + lax.broadcasted_iota(jnp.int32, (tile_h, tile_w), 1)
    wh = jnp.where(cols < tile_w * col_count - 1, weight_h.astype(jnp.float32), 0.0)
    wv = jnp.where(rows < tile_h * row_count - 1, weight_v.astype(jnp.float32), 0.0)
    weights = jnp.stack([wh, wv]) * (KAPPA * EDGE_SCALE)
    above, below = neighbours("row", weights[:, :HALO], weights[:, tile_h - HALO :])
    return jnp.concatenate([above, weights, below], axis=1)


def widened(weights):
    left, right = neighbours("col", weights[..., :HALO], weights[..., -HALO:])
    tile_w = weights.shape[2]
    gap = jnp.zeros(weights.shape[:2] + (LEAD - HALO,), jnp.float32)
    tail = jnp.zeros(weights.shape[:2] + (SPAN - LEAD - HALO - tile_w,), jnp.float32)
    return jnp.concatenate([gap, left, weights, right, tail], axis=2)


def held_weights(weights, count, half):
    halves = [weights[:, : half + 2 * HALO, :, None], weights[:, half:, :, None]]
    spread = [jnp.broadcast_to(x, x.shape[:3] + (count,)) for x in halves]
    both = jnp.concatenate(spread, axis=3)
    return both[0], both[1]


def per_device(cube, library_t, inverse, weight_h, weight_v):
    strips, bands, tile_h, tile_w = cube.shape
    count = library_t.shape[0]
    quarter = tile_h // 4
    half = tile_h // 2

    def to_owner(x):
        return lax.all_to_all(x, "col", split_axis=0, concat_axis=0, tiled=True)

    def project(x):
        x = x.reshape(strips * bands, half, tile_w)
        return jnp.einsum("eb,bhw->hew", library_t, x, preferred_element_type=jnp.float32)

    outer = jnp.concatenate([cube[:, :, :quarter], cube[:, :, 3 * quarter :]], axis=2)
    weights = scaled_weights(weight_h, weight_v)
    outer, weights = lax.optimization_barrier((outer, weights))
    outer = to_owner(outer)
    edge = ((0, 0), (0, 0), (0, 0))
    from_right = jnp.pad(cube[1:, :, :, :HALO], ((0, 1),) + edge)
    from_left = jnp.pad(cube[:-1, :, :, tile_w - HALO :], ((1, 0),) + edge)
    border = jnp.concatenate([from_right, from_left], axis=3).reshape(strips, bands, tile_w)
    border = jnp.pad(border, ((0, 0), (0, -bands % 8), (0, 0)))
    inner = cube[:, :, quarter : 3 * quarter].reshape(strips, bands * half, tile_w)
    inner = jnp.concatenate([inner, border], axis=1)
    weights = widened(weights)
    inner, outer, weights = lax.optimization_barrier((inner, outer, weights))
    inner = to_owner(inner)

    wh, wv = held_weights(weights, count, half)
    outer = project(outer)
    top, bottom = neighbours("row", outer[:HALO], outer[half - HALO :])
    border = inner[:, bands * half : bands * half + bands].reshape(strips * bands, tile_w)
    side = jnp.dot(library_t, border, preferred_element_type=jnp.float32)
    ahead = 2 * HALO * HALO
    side_top, side_bottom = neighbours("row", side[:, :ahead], side[:, side.shape[1] - ahead :])
    side = jnp.concatenate([side_top, side, side_bottom, jnp.zeros_like(side[:, : 2 * ahead])], 1)
    inner = project(inner[:, : bands * half])

    inv_hi = lax.reduce_precision(inverse, 8, 7)
    inv_lo = inverse - inv_hi
    inv3 = jnp.concatenate([inv_hi, inv_lo, inv_hi], axis=1).astype(jnp.bfloat16)
    twice = [jnp.kron(jnp.eye(2, dtype=jnp.float32), x.T) for x in (inv_hi, inv_lo, inv_hi)]
    inv3t = jnp.concatenate(twice, axis=0).astype(jnp.bfloat16)
    return admm(inv3, inv3t, outer, inner, side, top, bottom, wh, wv)


def solution(mesh):
    return jax.shard_map(
        per_device,
        mesh=mesh,
        in_specs=(P(None, "col", "row", None), P(), P(), P("row", "col"), P("row", "col")),
        out_specs=P(None, "row", "col"),
        check_vma=False,
    )
```

time: 177 us -> 144 us (0.81)
  the two profiles are of different devices: /device:TPU:39 before, /device:TPU:1 now
where the time goes in v2:
time: 144 us; the launch traced here: 143 us
  starting transfers between devices  38.6 us (27%)
  local copies, waits for them, and re-layouts  37.5 us (26%)
  waiting for transfers between devices  30.1 us (21%)
  other arithmetic  16.9 us (12%)
  Pallas kernels  15.3 us (11%)
  matrix products  4.59 us (3%)
    all_to_all x2, waiting for transfers between devices, to_owner(): return lax.all_to_all(x, 'col', split_axis=0, concat_axis=0, tiled=True)  21.4 us
    ppermute x4, starting transfers between devices, neighbours(): lax.ppermute(high_part, axis, forward)  20.5 us
    unnamed x15, local copies, waits for them, and re-layouts  16.5 us
    pallas_call x1, Pallas kernels, admm(): pl.pallas_call(admm_kernel, out_shape=jax.ShapeDtypeStruct((count, 2 * ha...  15.3 us
    all_to_all x2, starting transfers between devices, to_owner(): return lax.all_to_all(x, 'col', split_axis=0, concat_axis=0, tiled=True)  10.9 us
    ppermute x4, waiting for transfers between devices, neighbours(): lax.ppermute(low_part, axis, backward)  8.66 us
    squeeze x1, other arithmetic, held_weights(): return (both[0], both[1])  7.82 us
    ppermute x4, starting transfers between devices, neighbours(): lax.ppermute(low_part, axis, backward)  7.23 us
  transfers between devices with their start and end apart: 10, of which 2 were waited for; matrix products, arithmetic and copies ran while one was open for 39% of the time, Pallas kernels for 0%

profile of v2, /device:TPU:1, one launch (start us, length us, event | category | flops | bytes accessed | tf_op | source)
XLA Modules:
  0.0 143.2 jit_solution(2861431452523875927)
XLA Ops:
  0.0 0.9 select_bitcast_fusion
  0.9 4.5 %collective-permute-start = (f32[2,4,256]{2,1,0:T(4,128)S(1)}, f32[2,4,256]{2,1,0:T(4,128)S(1)}, u32[]{:S(2)}, u32[]{:S(2)}) collective-permute-start(f32[2,4,256]{2,1,0:T(4,128)S(1)} %get-tuple-element.29), channel_id=1, source_target_pairs={{0,8},{8,16},{16,24},{24,32},{32,40},{40,48},{48,56},{56,64},{64,7... | collective-permute-start | bytes 24584 | tf_op jit(solution)/shard_map/ppermute | solution.py:132
  5.4 1.9 %collective-permute-start.1 = (f32[2,4,256]{2,1,0:T(4,128)S(1)}, f32[2,4,256]{2,1,0:T(4,128)S(1)}, u32[]{:S(2)}, u32[]{:S(2)}) collective-permute-start(f32[2,4,256]{2,1,0:T(4,128)S(1)} %get-tuple-element.30), channel_id=1, source_target_pairs={{8,0},{16,8},{24,16},{32,24},{40,32},{48,40},{56,48},{64,56},{72,6... | collective-permute-start | bytes 24584 | tf_op jit(solution)/shard_map/ppermute | solution.py:132
  7.4 2.2 %fusion.23 = (bf16[8,53,8,256]{3,2,1,0:T(8,128)(2,1)S(1)}, bf16[8,53,8,256]{3,2,1,0:T(8,128)(2,1)S(1)}) fusion(bf16[8,53,32,256]{3,2,1,0:T(8,128)(2,1)} %param.5), kind=kLoop, calls=%fused_computation.42 | loop fusion | bytes 6946816 | tf_op jit(solution)/shard_map/slice | solution.py:176
  9.6 2.1 %pad_maximum_fusion.1 = bf16[8,53,16,256]{3,2,1,0:T(8,128)(2,1)} fusion(bf16[8,53,8,256]{3,2,1,0:T(8,128)(2,1)S(1)} %get-tuple-element.18, bf16[8,53,8,256]{3,2,1,0:T(8,128)(2,1)S(1)} %get-tuple-element.17), kind=kLoop, calls=%fused_computation.9 | loop fusion | flops 6946816 | bytes 6946816 | tf_op jit(solution)/shard_map/concatenate | solution.py:176
  11.6 0.0 collective-permute-done
  11.7 0.6 pad_maximum_fusion.3
  12.3 6.4 %all-to-all-start = ((bf16[8,53,16,256]{3,2,1,0:T(8,128)(2,1)}), bf16[8,53,16,256]{3,2,1,0:T(8,128)(2,1)}, u32[]{:S(2)}, u32[]{:S(2)}) async-start(bf16[8,53,16,256]{3,2,1,0:T(8,128)(2,1)} %pad_maximum_fusion.1), calls=%async_computation | async-start | bytes 6946816 | tf_op jit(solution)/shard_map/all_to_all | solution.py:170
  18.7 6.8 %fusion.24 = (bf16[7,53,32,4]{3,2,1,0:T(8,128)(2,1)}, bf16[7,53,32,4]{3,2,1,0:T(8,128)(2,1)}) fusion(bf16[8,53,32,256]{3,2,1,0:T(8,128)(2,1)} %param.5), kind=kLoop, calls=%fused_computation.43 | loop fusion | bytes 379904 | tf_op jit(solution)/shard_map/slice | solution.py:181
  25.4 6.3 %copy.22 = bf16[7,53,32,4]{1,3,2,0:T(4,128)(2,1)} copy(bf16[7,53,32,4]{3,2,1,0:T(8,128)(2,1)} %get-tuple-element.19) | data formatting | bytes 189952
  31.7 6.2 %copy.23 = bf16[7,53,32,4]{1,3,2,0:T(4,128)(2,1)} copy(bf16[7,53,32,4]{3,2,1,0:T(8,128)(2,1)} %get-tuple-element.20) | data formatting | bytes 189952
  37.9 2.2 %fusion.18 = bf16[8,53,256]{1,2,0:T(8,128)(2,1)} fusion(bf16[7,53,32,4]{1,3,2,0:T(4,128)(2,1)} %copy.23, bf16[7,53,32,4]{1,3,2,0:T(4,128)(2,1)} %copy.22), kind=kLoop, calls=%fused_computation.22 | loop fusion | flops 868352 | bytes 407040 | tf_op jit(solution)/shard_map/reshape | solution.py:183
  40.1 2.0 %copy.24 = bf16[8,53,256]{2,1,0:T(8,128)(2,1)} copy(bf16[8,53,256]{1,2,0:T(8,128)(2,1)} %fusion.18) | data formatting | bytes 434176
  42.1 0.9 fusion.27
  43.0 1.3 collective-permute-start.3
  44.3 5.5 %collective-permute-start.2 = (f32[2,40,4]{2,1,0:T(8,128)S(1)}, f32[2,40,4]{2,1,0:T(8,128)S(1)}, u32[]{:S(2)}, u32[]{:S(2)}) collective-permute-start(f32[2,40,4]{2,1,0:T(8,128)S(1)} %get-tuple-element.26), channel_id=1, source_target_pairs={{0,1},{1,2},{2,3},{3,4},{4,5},{5,6},{6,7},{8,9},{9,10},{10,11},{11... | collective-permute-start | bytes 3848 | tf_op jit(solution)/shard_map/ppermute | solution.py:132
  49.8 2.9 %fusion.1 = bf16[8,904,256]{2,1,0:T(8,128)(2,1)} fusion(bf16[8,53,256]{2,1,0:T(8,128)(2,1)} %copy.24, bf16[8,848,256]{2,1,0:T(8,128)(2,1)S(1)} %bitcast.30), kind=kLoop, calls=%fused_computation.4 | loop fusion | flops 11108352 | bytes 7393280 | tf_op jit(solution)/shard_map/concatenate | solution.py:186
  52.7 8.7 %collective-permute-done.3 = f32[2,40,4]{2,1,0:T(8,128)S(1)} collective-permute-done((f32[2,40,4]{2,1,0:T(8,128)S(1)}, f32[2,40,4]{2,1,0:T(8,128)S(1)}, u32[]{:S(2)}, u32[]{:S(2)}) %collective-permute-start.3) | collective-permute-done | bytes 1312 | tf_op jit(solution)/shard_map/ppermute | solution.py:132
  61.4 0.6 copy-done.3
  62.0 0.6 copy-done.4
  62.6 1.0 concatenate.35
  63.6 0.0 copy-start.5
  63.7 4.5 %all-to-all-start.1 = ((bf16[8,904,256]{2,1,0:T(8,128)(2,1)}), bf16[8,904,256]{2,1,0:T(8,128)(2,1)}, u32[]{:S(2)}, u32[]{:S(2)}) async-start(bf16[8,904,256]{2,1,0:T(8,128)(2,1)} %fusion.1), calls=%async_computation.1 | async-start | bytes 7405568 | tf_op jit(solution)/shard_map/all_to_all | solution.py:170
  68.2 0.1 copy.16
  68.3 0.1 copy.15
  68.4 0.2 multiply_convert_fusion
  68.5 0.1 mul.66
  68.6 0.1 reshape.43
  68.8 0.1 pad.20.clone
  68.8 0.1 pad_maximum_fusion.4.inv_ref
  68.9 3.2 %fusion.9.outer_ref = f32[16,64,256]{2,1,0:T(8,128)S(1)} fusion(bf16[424,16,256]{2,1,0:T(8,128)(2,1)} %bitcast.6, bf16[64,424]{1,0:T(8,128)(2,1)S(1)} %copy-done), kind=kOutput, calls=%fused_computation.14 | convolution fusion | flops 222298112 | bytes 4576256 | tf_op jit(solution)/shard_map/eb,bhw->hew/dot_general | solution.py:174
  72.2 1.9 %collective-permute-start.7 = (f32[4,64,256]{2,1,0:T(8,128)S(1)}, f32[4,64,256]{2,1,0:T(8,128)S(1)}, u32[]{:S(2)}, u32[]{:S(2)}) collective-permute-start(f32[4,64,256]{2,1,0:T(8,128)S(1)} %get-tuple-element.21), channel_id=1, source_target_pairs={{8,0},{16,8},{24,16},{32,24},{40,32},{48,40},{56,48},{64,56},{72,6... | collective-permute-start | bytes 786440 | tf_op jit(solution)/shard_map/ppermute | solution.py:132
  74.1 4.6 %collective-permute-start.6 = (f32[4,64,256]{2,1,0:T(8,128)S(1)}, f32[4,64,256]{2,1,0:T(8,128)S(1)}, u32[]{:S(2)}, u32[]{:S(2)}) collective-permute-start(f32[4,64,256]{2,1,0:T(8,128)S(1)} %get-tuple-element.22), channel_id=1, source_target_pairs={{0,8},{8,16},{16,24},{24,32},{32,40},{40,48},{48,56},{56,64},{64,7... | collective-permute-start | bytes 786440 | tf_op jit(solution)/shard_map/ppermute | solution.py:132
  78.8 2.0 %broadcast_in_dim.31 = f32[2,24,288,64]{3,2,1,0:T(8,128)S(1)} broadcast(f32[2,24,288]{2,1,0:T(8,128)S(1)} %get-tuple-element.23), dimensions={0,1,2} | broadcast | bytes 3594240 | tf_op jit(solution)/shard_map/broadcast_in_dim | solution.py:158
  80.8 4.2 %broadcast_in_dim.30 = f32[2,24,288,64]{3,2,1,0:T(8,128)} broadcast(f32[2,24,288]{2,1,0:T(8,128)S(1)} %get-tuple-element.24), dimensions={0,1,2} | broadcast | bytes 3594240 | tf_op jit(solution)/shard_map/broadcast_in_dim | solution.py:158
  84.9 7.8 %fusion.4 = (f32[24,288,128]{2,1,0:T(8,128)}, f32[24,288,128]{2,1,0:T(8,128)}) fusion(f32[2,24,288,64]{3,2,1,0:T(8,128)S(1)} %broadcast_in_dim.31, f32[2,24,288,64]{3,2,1,0:T(8,128)} %broadcast_in_dim.30), kind=kLoop, calls=%fused_computation.8 | loop fusion | flops 1769472 | bytes 14155776 | tf_op jit(solution)/shard_map/squeeze | solution.py:160
  92.7 21.4 %all-to-all-done.1 = bf16[8,904,256]{2,1,0:T(8,128)(2,1)} async-done(((bf16[8,904,256]{2,1,0:T(8,128)(2,1)}), bf16[8,904,256]{2,1,0:T(8,128)(2,1)}, u32[]{:S(2)}, u32[]{:S(2)}) %all-to-all-start.1) | async-done | bytes 3702816 | tf_op jit(solution)/shard_map/all_to_all | solution.py:170
  114.1 1.0 slice.79
  115.1 0.1 reshape.42
  115.2 0.2 convolution_bitcast_fusion
  115.4 0.1 fusion.28
  115.4 5.8 %collective-permute-start.4 = (f32[64,32]{1,0:T(8,128)S(1)}, f32[64,32]{1,0:T(8,128)S(1)}, u32[]{:S(2)}, u32[]{:S(2)}) collective-permute-start(f32[64,32]{1,0:T(8,128)S(1)} %get-tuple-element.27), channel_id=1, source_target_pairs={{0,8},{8,16},{16,24},{24,32},{32,40},{40,48},{48,56},{56,64},{64,7... | collective-permute-start | bytes 24584 | tf_op jit(solution)/shard_map/ppermute | solution.py:132
  121.3 2.1 %collective-permute-start.5 = (f32[64,32]{1,0:T(8,128)S(1)}, f32[64,32]{1,0:T(8,128)S(1)}, u32[]{:S(2)}, u32[]{:S(2)}) collective-permute-start(f32[64,32]{1,0:T(8,128)S(1)} %get-tuple-element.28), channel_id=1, source_target_pairs={{8,0},{16,8},{24,16},{32,24},{40,32},{48,40},{56,48},{64,56},{72,6... | collective-permute-start | bytes 24584 | tf_op jit(solution)/shard_map/ppermute | solution.py:132
  123.4 2.4 %slice.78 = bf16[8,848,256]{2,1,0:T(8,128)(2,1)S(1)} slice(bf16[8,904,256]{2,1,0:T(8,128)(2,1)} %all-to-all-done.1), slice={[0:8], [0:848], [0:256]} | slice | bytes 6946816 | tf_op jit(solution)/shard_map/slice | solution.py:199
  125.8 1.2 fusion.12.inner_ref
  127.0 0.1 maximum_maximum_fusion.side_ref
  127.1 0.8 copy-done.1
  127.9 15.3 %shard_map.55 = f32[64,32,256]{2,1,0:T(8,128)} custom-call(bf16[64,192]{1,0:T(8,128)(2,1)S(1)} %pad_maximum_fusion.4.inv_ref, bf16[384,128]{1,0:T(8,128)(2,1)S(1)} %pad_maximum_fusion.2.invt_ref, f32[16,64,256]{2,1,0:T(8,128)S(1)} %fusion.9.outer_ref, f32[16,64,256]{2,1,0:T(8,128)S(1)} %fusion.12.inner_ref, f32[64,384]{1,0:T(8,128)S(1)} %maximum_maximum_fusion.side_ref, ...), custom_call_target="tpu_custom_call" | custom-call | tf_op jit(solution)/shard_map/pallas_call | solution.py:113
  (28 shorter events, 0.2 us)
Async XLA Ops:
  0.0 68.9 %copy-start = (bf16[64,424]{1,0:T(8,128)(2,1)S(1)}, bf16[64,424]{1,0:T(8,128)(2,1)}, u32[]{:S(2)}) copy-start(bf16[64,424]{1,0:T(8,128)(2,1)} %param.6) | copy-start | bytes 162820
  0.9 10.7 %collective-permute-start = (f32[2,4,256]{2,1,0:T(4,128)S(1)}, f32[2,4,256]{2,1,0:T(4,128)S(1)}, u32[]{:S(2)}, u32[]{:S(2)}) collective-permute-start(f32[2,4,256]{2,1,0:T(4,128)S(1)} %get-tuple-element.29), channel_id=1, source_target_pairs={{0,8},{8,16},{16,24},{24,32},{32,40},{40,48},{48,56},{56,64},{64,7... | collective-permute-start | bytes 24584 | tf_op jit(solution)/shard_map/ppermute | solution.py:132
  5.4 6.2 %collective-permute-start.1 = (f32[2,4,256]{2,1,0:T(4,128)S(1)}, f32[2,4,256]{2,1,0:T(4,128)S(1)}, u32[]{:S(2)}, u32[]{:S(2)}) collective-permute-start(f32[2,4,256]{2,1,0:T(4,128)S(1)} %get-tuple-element.30), channel_id=1, source_target_pairs={{8,0},{16,8},{24,16},{32,24},{40,32},{48,40},{56,48},{64,56},{72,6... | collective-permute-start | bytes 24584 | tf_op jit(solution)/shard_map/ppermute | solution.py:132
  12.3 51.4 %all-to-all-start = ((bf16[8,53,16,256]{3,2,1,0:T(8,128)(2,1)}), bf16[8,53,16,256]{3,2,1,0:T(8,128)(2,1)}, u32[]{:S(2)}, u32[]{:S(2)}) async-start(bf16[8,53,16,256]{3,2,1,0:T(8,128)(2,1)} %pad_maximum_fusion.1), calls=%async_computation | async-start | bytes 6946816 | tf_op jit(solution)/shard_map/all_to_all | solution.py:170
  25.4 24.4 %slice-start = ((bf16[8,53,32,256]{3,2,1,0:T(8,128)(2,1)}), bf16[8,53,16,256]{3,2,1,0:T(8,128)(2,1)S(1)}, s32[]{:S(2)}) async-start(bf16[8,53,32,256]{3,2,1,0:T(8,128)(2,1)} %param.5), calls=%async_computation.2 | async-start | bytes 6946816 | tf_op jit(solution)/shard_map/slice | solution.py:185
  43.0 18.4 %collective-permute-start.3 = (f32[2,40,4]{2,1,0:T(8,128)S(1)}, f32[2,40,4]{2,1,0:T(8,128)S(1)}, u32[]{:S(2)}, u32[]{:S(2)}) collective-permute-start(f32[2,40,4]{2,1,0:T(8,128)S(1)} %get-tuple-element.25), channel_id=1, source_target_pairs={{1,0},{2,1},{3,2},{4,3},{5,4},{6,5},{7,6},{9,8},{10,9},{11,10},{12... | collective-permute-start | bytes 3848 | tf_op jit(solution)/shard_map/ppermute | solution.py:132
  44.3 17.1 %collective-permute-start.2 = (f32[2,40,4]{2,1,0:T(8,128)S(1)}, f32[2,40,4]{2,1,0:T(8,128)S(1)}, u32[]{:S(2)}, u32[]{:S(2)}) collective-permute-start(f32[2,40,4]{2,1,0:T(8,128)S(1)} %get-tuple-element.26), channel_id=1, source_target_pairs={{0,1},{1,2},{2,3},{3,4},{4,5},{5,6},{6,7},{8,9},{9,10},{10,11},{11... | collective-permute-start | bytes 3848 | tf_op jit(solution)/shard_map/ppermute | solution.py:132
  61.4 0.6 copy-start.3
  62.0 0.6 copy-start.4
  63.6 4.5 %copy-start.5 = (f32[64,64]{1,0:T(8,128)S(1)}, f32[64,64]{1,0:T(8,128)}, u32[]{:S(2)}) copy-start(f32[64,64]{1,0:T(8,128)} %param.7) | copy-start | bytes 49156
  63.7 50.5 %all-to-all-start.1 = ((bf16[8,904,256]{2,1,0:T(8,128)(2,1)}), bf16[8,904,256]{2,1,0:T(8,128)(2,1)}, u32[]{:S(2)}, u32[]{:S(2)}) async-start(bf16[8,904,256]{2,1,0:T(8,128)(2,1)} %fusion.1), calls=%async_computation.1 | async-start | bytes 7405568 | tf_op jit(solution)/shard_map/all_to_all | solution.py:170
  72.2 54.9 %collective-permute-start.7 = (f32[4,64,256]{2,1,0:T(8,128)S(1)}, f32[4,64,256]{2,1,0:T(8,128)S(1)}, u32[]{:S(2)}, u32[]{:S(2)}) collective-permute-start(f32[4,64,256]{2,1,0:T(8,128)S(1)} %get-tuple-element.21), channel_id=1, source_target_pairs={{8,0},{16,8},{24,16},{32,24},{40,32},{48,40},{56,48},{64,56},{72,6... | collective-permute-start | bytes 786440 | tf_op jit(solution)/shard_map/ppermute | solution.py:132
  74.1 53.0 %collective-permute-start.6 = (f32[4,64,256]{2,1,0:T(8,128)S(1)}, f32[4,64,256]{2,1,0:T(8,128)S(1)}, u32[]{:S(2)}, u32[]{:S(2)}) collective-permute-start(f32[4,64,256]{2,1,0:T(8,128)S(1)} %get-tuple-element.22), channel_id=1, source_target_pairs={{0,8},{8,16},{16,24},{24,32},{32,40},{40,48},{48,56},{56,64},{64,7... | collective-permute-start | bytes 786440 | tf_op jit(solution)/shard_map/ppermute | solution.py:132
  115.4 11.6 %collective-permute-start.4 = (f32[64,32]{1,0:T(8,128)S(1)}, f32[64,32]{1,0:T(8,128)S(1)}, u32[]{:S(2)}, u32[]{:S(2)}) collective-permute-start(f32[64,32]{1,0:T(8,128)S(1)} %get-tuple-element.27), channel_id=1, source_target_pairs={{0,8},{8,16},{16,24},{24,32},{32,40},{40,48},{48,56},{56,64},{64,7... | collective-permute-start | bytes 24584 | tf_op jit(solution)/shard_map/ppermute | solution.py:132
  121.3 5.7 %collective-permute-start.5 = (f32[64,32]{1,0:T(8,128)S(1)}, f32[64,32]{1,0:T(8,128)S(1)}, u32[]{:S(2)}, u32[]{:S(2)}) collective-permute-start(f32[64,32]{1,0:T(8,128)S(1)} %get-tuple-element.28), channel_id=1, source_target_pairs={{8,0},{16,8},{24,16},{32,24},{40,32},{48,40},{56,48},{64,56},{72,6... | collective-permute-start | bytes 24584 | tf_op jit(solution)/shard_map/ppermute | solution.py:132
  123.4 3.8 %copy-start.2 = (f32[24,288,128]{2,1,0:T(8,128)S(1)}, f32[24,288,128]{2,1,0:T(8,128)}, u32[]{:S(2)}) copy-start(f32[24,288,128]{2,1,0:T(8,128)} %get-tuple-element.16.wh_ref) | copy-start | bytes 10616836
  125.7 2.2 %copy-start.1 = (f32[24,288,128]{2,1,0:T(8,128)S(1)}, f32[24,288,128]{2,1,0:T(8,128)}, u32[]{:S(2)}) copy-start(f32[24,288,128]{2,1,0:T(8,128)} %get-tuple-element.15.wv_ref) | copy-start | bytes 10616836

commit v3 on v2

v3 whole, which is shorter than its diff:
```python
import jax
import jax.numpy as jnp
from jax import lax
from jax.experimental import pallas as pl
from jax.experimental.pallas import tpu as pltpu
from jax.sharding import PartitionSpec as P

KAPPA = 0.24
EDGE_SCALE = 1.0 / 255.0
HALO = 4
LEAD = 16
SPAN = 288
GROUP = 16
LEVELS = 256.0
STEPS_MAX = 32000.0


def parts3(x, axis):
    hi = x.astype(jnp.bfloat16)
    lo = (x - hi.astype(jnp.float32)).astype(jnp.bfloat16)
    return jnp.concatenate([hi, hi, lo], axis=axis)


def code_kernel(which_ref, x_ref, out_ref):
    blocks = out_ref.shape[0]
    _, rows, count, width = x_ref.shape
    slot = lax.broadcasted_iota(jnp.int32, (16, width), 0)
    for s in range(blocks):
        levels = jnp.zeros((16, width), jnp.float32)
        for r in range(rows):
            x = x_ref[which_ref[s], r]
            top = jnp.max(jnp.max(jnp.abs(x), axis=0, keepdims=True), axis=1, keepdims=True)
            level = jnp.ceil(jnp.log2(jnp.maximum(top, 1e-30)) * LEVELS)
            scale = STEPS_MAX * jnp.exp2(level * (-1.0 / LEVELS))
            q = jnp.round(x * scale).astype(jnp.int32).astype(jnp.int16)
            out_ref[s, r * count : (r + 1) * count] = q
            levels = jnp.where(slot == r, level, levels)
        out_ref[s, rows * count :] = levels.astype(jnp.int32).astype(jnp.int16)


def coded(x, which):
    _, rows, count, width = x.shape
    vmem = pl.BlockSpec(memory_space=pltpu.VMEM)
    return pl.pallas_call(
        code_kernel,
        out_shape=jax.ShapeDtypeStruct((which.shape[0], rows * count + 16, width), jnp.int16),
        in_specs=[pl.BlockSpec(memory_space=pltpu.SMEM), vmem],
        out_specs=vmem,
        compiler_params=pltpu.CompilerParams(vmem_limit_bytes=16 * 2**20),
    )(which, x)


def scales(levels):
    levels = levels.astype(jnp.int32).astype(jnp.float32)
    return jnp.exp2(levels * (1.0 / LEVELS)) * (1.0 / STEPS_MAX)


def finish_kernel(which_ref, own_ref, given_ref, out_ref, first_ref, last_ref, scale):
    rows, count, _ = out_ref.shape
    scale[...] = scales(given_ref[0, rows * count :])
    for r in range(rows):
        q = given_ref[0, r * count : (r + 1) * count].astype(jnp.int32).astype(jnp.float32)
        x = own_ref[which_ref[0], r] + q * scale[r : r + 1]
        out_ref[r] = x
        if r < HALO:
            first_ref[r] = x
        if r >= rows - HALO:
            last_ref[r - rows + HALO] = x


def finished(own, given, which):
    _, rows, count, width = own.shape
    vmem = pl.BlockSpec(memory_space=pltpu.VMEM)
    shapes = [(rows, count, width), (HALO, count, width), (HALO, count, width)]
    return pl.pallas_call(
        finish_kernel,
        out_shape=[jax.ShapeDtypeStruct(x, jnp.float32) for x in shapes],
        in_specs=[pl.BlockSpec(memory_space=pltpu.SMEM), vmem, vmem],
        out_specs=[vmem] * 3,
        scratch_shapes=[pltpu.VMEM((16, width), jnp.float32)],
        compiler_params=pltpu.CompilerParams(vmem_limit_bytes=16 * 2**20),
    )(which, own, given)


def mix_kernel(
    inv_ref, outer_ref, upper_ref, lower_ref, top_ref, bottom_ref,
    mixed_ref, low_ref, high_ref, scale,
):
    quarter, count = outer_ref.shape[0] // 2, outer_ref.shape[1]
    parts, _, width = upper_ref.shape
    deep = mixed_ref.shape[0]
    inv = inv_ref[...]
    for which, ref in enumerate((upper_ref, lower_ref)):
        for s in range(parts):
            scale[which, s] = scales(ref[s, quarter * count :])

    def row(which, r):
        ref = (upper_ref, lower_ref)[which]
        at = pl.ds(r * count, count)
        terms = [
            ref[s, at].astype(jnp.int32).astype(jnp.float32) * scale[which, s, pl.ds(r, 1)]
            for s in range(parts)
        ]
        return sum(terms[1:], terms[0])

    def mix_pairs(pairs, slot):
        cat = jnp.concatenate([parts3(x, 0) for pair in pairs for x in pair], axis=1)
        m = jnp.dot(inv, cat, preferred_element_type=jnp.float32)
        for k in range(len(pairs)):
            a = m[:, 2 * k * width : (2 * k + 1) * width]
            b = m[:, (2 * k + 1) * width : (2 * k + 2) * width]
            turned = jnp.transpose(jnp.concatenate([a, b], 0))
            mixed_ref[slot + k] = turned
            low_ref[slot + k] = turned[:8]
            high_ref[slot + k] = turned[width - 8 :]

    mix_pairs([(top_ref[k], row(0, quarter - HALO + k)) for k in range(HALO)], 0)
    mix_pairs([(row(1, k), bottom_ref[k]) for k in range(HALO)], deep - HALO)

    @pl.loop(0, quarter // 2)
    def _(g):
        r = g * 2
        mix_pairs([(outer_ref[r + k], row(1, r + k)) for k in range(2)], r + HALO)
        mix_pairs(
            [(row(0, r + k), outer_ref[r + k + quarter]) for k in range(2)], r + HALO + quarter
        )


def mix(inv3, outer, upper, lower, top, bottom):
    half, count, width = outer.shape
    deep = half + 2 * HALO
    vmem = pl.BlockSpec(memory_space=pltpu.VMEM)
    shapes = [(deep, width, 2 * count), (deep, 8, 2 * count), (deep, 8, 2 * count)]
    return pl.pallas_call(
        mix_kernel,
        out_shape=[jax.ShapeDtypeStruct(x, jnp.float32) for x in shapes],
        in_specs=[vmem] * 6,
        out_specs=[vmem] * 3,
        scratch_shapes=[pltpu.VMEM((2, upper.shape[0], 16, width), jnp.float32)],
        compiler_params=pltpu.CompilerParams(vmem_limit_bytes=16 * 2**20),
    )(inv3, outer, upper, lower, top, bottom)


def admm_kernel(
    invt_ref, mixed_ref, left_ref, right_ref, wh_ref, wv_ref, out_ref, mixed, y, z, turned
):
    deep, width, lanes = mixed_ref.shape
    count = lanes // 2
    half = deep - 2 * HALO

    @pl.loop(0, deep)
    def _(r):
        mixed[r, LEAD : LEAD + width] = mixed_ref[r]
        mixed[r, LEAD - 8 : LEAD] = left_ref[r]
        mixed[r, LEAD + width : LEAD + width + 8] = right_ref[r]

    def diffuse(src, dst, begin, end):
        @pl.loop(0, (width + 16) // GROUP)
        def _(g):
            c = pl.multiple_of(LEAD - 8 + g * GROUP, 8)
            at, after, before = pl.ds(c, GROUP), pl.ds(c + 1, GROUP), pl.ds(c - 1, GROUP)
            here = src[begin, at]
            above = wv_ref[begin - 1, at] * (here - src[begin - 1, at])
            for i in range(begin, end):
                below = src[i + 1, at]
                down = wv_ref[i, at] * (below - here)
                right = wh_ref[i, at] * (src[i, after] - here)
                left = wh_ref[i, before] * (here - src[i, before])
                dst[i, at] = here + (right - left) + (down - above)
                here, above = below, down

    diffuse(mixed, z, 1, deep - 1)
    diffuse(z, y, 2, deep - 2)
    invt = invt_ref[...]
    used = pl.ds(LEAD - 8, width + 16)

    @pl.loop(2, deep - 2, step=2)
    def _(first):
        for k in range(2):
            kept = jnp.maximum(y[first + k, used], 0.0)
            before = mixed[first + k, used]
            u = parts3(kept - 0.5 * before, 1)
            m = jnp.dot(u, invt, preferred_element_type=jnp.float32)
            z[first + k, used] = m + (2.0 * before - kept)

    diffuse(z, y, 3, deep - 3)
    diffuse(y, z, 4, deep - 4)

    @pl.loop(0, half // 2)
    def _(g):
        for k in range(2):
            r = g * 2 + k
            v = jnp.transpose(jnp.maximum(z[r + HALO, LEAD : LEAD + width], 0.0))
            for h in range(2):
                for t in range(width // 128):
                    turned[t, pl.ds(r + h * half, count, stride=2 * half), :] = v[
                        h * count : (h + 1) * count, t * 128 : (t + 1) * 128
                    ]

    @pl.loop(0, count // 8)
    def _(g):
        for k in range(8):
            e = g * 8 + k
            for t in range(width // 128):
                out_ref[e, :, t * 128 : (t + 1) * 128] = turned[t, pl.ds(e * 2 * half, 2 * half), :]


def admm(inv3t, mixed, left, right, wh, wv):
    deep, width, lanes = mixed.shape
    half = deep - 2 * HALO
    vmem = pl.BlockSpec(memory_space=pltpu.VMEM)
    field = pltpu.VMEM((deep, SPAN, lanes), jnp.float32)
    return pl.pallas_call(
        admm_kernel,
        out_shape=jax.ShapeDtypeStruct((lanes // 2, 2 * half, width), jnp.float32),
        in_specs=[vmem] * 6,
        out_specs=vmem,
        scratch_shapes=[
            field,
            field,
            field,
            pltpu.VMEM((width // 128, lanes * half, 128), jnp.float32),
        ],
        compiler_params=pltpu.CompilerParams(vmem_limit_bytes=32 * 2**20),
    )(inv3t, mixed, left, right, wh, wv)


def neighbours(axis, low_part, high_part):
    count = lax.axis_size(axis)
    forward = [(i, i + 1) for i in range(count - 1)]
    backward = [(i + 1, i) for i in range(count - 1)]
    return lax.ppermute(high_part, axis, forward), lax.ppermute(low_part, axis, backward)


def raw_weights(weight_h, weight_v):
    col_count = lax.axis_size("col")
    row_count = lax.axis_size("row")
    tile_h, tile_w = weight_h.shape
    rows = lax.axis_index("row") * tile_h + lax.broadcasted_iota(jnp.int32, (tile_h, tile_w), 0)
    cols = lax.axis_index("col") * tile_w + lax.broadcasted_iota(jnp.int32, (tile_h, tile_w), 1)
    wh = jnp.where(cols < tile_w * col_count - 1, weight_h, 0)
    wv = jnp.where(rows < tile_h * row_count - 1, weight_v, 0)
    weights = jnp.stack([wh, wv]).astype(jnp.float32)
    above, below = neighbours("row", weights[:, :HALO], weights[:, tile_h - HALO :])
    return jnp.concatenate([above, weights, below], axis=1)


def widened(weights):
    left, right = neighbours("col", weights[..., :HALO], weights[..., -HALO:])
    tile_w = weights.shape[2]
    gap = jnp.zeros(weights.shape[:2] + (LEAD - HALO,), jnp.float32)
    tail = jnp.zeros(weights.shape[:2] + (SPAN - LEAD - HALO - tile_w,), jnp.float32)
    return jnp.concatenate([gap, left, weights, right, tail], axis=2)


def held_weights(weights, count, half):
    deep = half + 2 * HALO
    pair = jnp.stack([weights[:, :deep], weights[:, half:]]).astype(jnp.bfloat16)
    lanes = lax.broadcasted_iota(jnp.int32, (2, 2 * count), 1) // count
    spread = (lanes == lax.broadcasted_iota(jnp.int32, (2, 2 * count), 0)).astype(jnp.bfloat16)
    scale = jnp.float32(KAPPA * EDGE_SCALE)
    return [
        scale * jnp.einsum("hrc,hl->rcl", x, spread, preferred_element_type=jnp.float32)
        for x in (pair[:, 0], pair[:, 1])
    ]


def per_device(cube, library_t, inverse, weight_h, weight_v):
    strips, bands, tile_h, tile_w = cube.shape
    count = library_t.shape[0]
    half, quarter = tile_h // 2, tile_h // 4
    ys = strips // 2
    y, x = lax.axis_index("col") // 2, lax.axis_index("col") % 2
    swap = [(c, c ^ 1) for c in range(strips)]
    groups = [list(range(k, strips, 2)) for k in range(2)]

    def over_y(block):
        return lax.all_to_all(
            block, "col", split_axis=0, concat_axis=0, axis_index_groups=groups, tiled=True
        )

    def project(library, block):
        return jnp.einsum("eb,bhw->hew", library, block, preferred_element_type=jnp.float32)

    by_y = cube.reshape(ys, 2, bands, tile_h, tile_w)
    library = library_t.reshape(count, ys, 2, bands)
    library_x = lax.dynamic_index_in_dim(library, x, 2, keepdims=False)
    library_other = lax.dynamic_index_in_dim(library, 1 - x, 2, keepdims=False)
    library_own = lax.dynamic_index_in_dim(library_x, y, 1, keepdims=False)
    library_pair = lax.dynamic_index_in_dim(library_other, y, 1, keepdims=False)
    library_two = jnp.concatenate([library_own, library_pair], axis=1)
    library_four = library_x.reshape(count, ys * bands)

    def strips_of(source, other, begin):
        rows = source[:, :, :, begin : begin + quarter]
        block = jnp.where((x == 0) ^ other, rows[:, 0], rows[:, 1])
        return jnp.transpose(block, (1, 0, 2, 3)).reshape(bands, ys * quarter, tile_w)

    barrier = lax.optimization_barrier
    upper = strips_of(by_y, True, quarter)
    upper, by_y = barrier((upper, by_y))
    outer = jnp.concatenate([by_y[..., :quarter, :], by_y[..., 3 * quarter :, :]], axis=3)
    outer = jnp.transpose(outer, (0, 2, 1, 3, 4)).reshape(ys, bands, 2 * half, tile_w)
    outer, by_y = barrier((outer, by_y))
    lower = strips_of(by_y, True, 2 * quarter)
    own = [strips_of(by_y, False, quarter), strips_of(by_y, False, 2 * quarter)]
    upper = lax.ppermute(upper, "col", swap)
    outer = over_y(outer)
    lower = lax.ppermute(lower, "col", swap)
    weights = raw_weights(weight_h, weight_v)

    def inner_part(own_rows, other_rows):
        both = jnp.concatenate([own_rows, other_rows], axis=0)
        part = project(library_two, both).reshape(ys, quarter, count, tile_w)
        return coded(part, jnp.arange(ys, dtype=jnp.int32))

    upper = inner_part(own[0], upper)
    upper, outer = barrier((upper, outer))
    upper = over_y(upper)
    outer = project(library_four, outer.reshape(ys * bands, 2 * half, tile_w))
    outer = outer.reshape(2, half, count, tile_w)
    given = coded(outer, jnp.reshape(1 - x, (1,)))
    given, lower, weights = barrier((given, lower, weights))
    given = lax.ppermute(given, "col", swap)
    lower = inner_part(own[1], lower)
    lower, weights = barrier((lower, weights))
    lower = over_y(lower)
    weights = widened(weights)
    outer, first, last = finished(outer, given, jnp.reshape(x, (1,)))
    top, bottom = neighbours("row", first, last)

    inv_hi = lax.reduce_precision(inverse, 8, 7)
    inv_lo = inverse - inv_hi
    inv3 = jnp.concatenate([inv_hi, inv_lo, inv_hi], axis=1).astype(jnp.bfloat16)
    twice = [jnp.kron(jnp.eye(2, dtype=jnp.float32), a.T) for a in (inv_hi, inv_lo, inv_hi)]
    inv3t = jnp.concatenate(twice, axis=0).astype(jnp.bfloat16)
    wh, wv = held_weights(weights, count, half)
    mixed, low, high = mix(inv3, outer, upper, lower, top, bottom)
    left, right = neighbours("col", low, high)
    return admm(inv3t, mixed, left, right, wh, wv)


def solution(mesh):
    return jax.shard_map(
        per_device,
        mesh=mesh,
        in_specs=(P(None, "col", "row", None), P(), P(), P("row", "col"), P("row", "col")),
        out_specs=P(None, "row", "col"),
        check_vma=False,
    )
```

time: 144 us -> 144 us (level)
  the two profiles are of different devices: /device:TPU:1 before, /device:TPU:39 now
where the time goes in v3:
time: 144 us; the launch traced here: 142 us
  starting transfers between devices  46.5 us (32%)
  local copies, waits for them, and re-layouts  29 us (20%)
  waiting for transfers between devices  24.8 us (17%)
  Pallas kernels  21.9 us (15%)
  other arithmetic  12.2 us (8%)
  matrix products  6.74 us (5%)
    ppermute x4, starting transfers between devices, neighbours(): lax.ppermute(high_part, axis, forward)  20.5 us
    pallas_call x1, Pallas kernels, admm(): pl.pallas_call(admm_kernel, out_shape=jax.ShapeDtypeStruct((lanes // 2, 2...  13.4 us
    all_to_all x3, starting transfers between devices, over_y(): lax.all_to_all(block, 'col', split_axis=0, concat_axis=0, axis_index_grou...  12.1 us
    unnamed x48, local copies, waits for them, and re-layouts  10.2 us
    ppermute x4, starting transfers between devices, neighbours(): lax.ppermute(low_part, axis, backward)  9.77 us
    ppermute x4, waiting for transfers between devices, neighbours(): lax.ppermute(low_part, axis, backward)  8.75 us
    ppermute x1, waiting for transfers between devices, per_device(): upper = lax.ppermute(upper, 'col', swap)  6.37 us
    all_to_all x3, waiting for transfers between devices, over_y(): lax.all_to_all(block, 'col', split_axis=0, concat_axis=0, axis_index_grou...  6.02 us
  transfers between devices with their start and end apart: 14, of which 6 were waited for; matrix products, arithmetic and copies ran while one was open for 21% of the time, Pallas kernels for 4%

profile of v3, /device:TPU:39, one launch (start us, length us, event | category | flops | bytes accessed | tf_op | source)
XLA Modules:
  0.0 141.6 jit_solution(17188388327454907549)
XLA Ops:
  0.0 2.6 %copy_bitcast_fusion.1 = bf16[53,32,256]{2,1,0:T(8,128)(2,1)} fusion(bf16[4,2,53,32,256]{4,3,2,1,0:T(8,128)(2,1)} %bitcast.80, pred[]{:T(512)S(6)} %xor.4), kind=kLoop, calls=%fused_computation.16 | loop fusion | flops 434176 | bytes 2605057 | tf_op jit(solution)/shard_map/reshape | solution.py:297
  2.6 2.2 %fusion.31 = (bf16[4,2,53,8,256]{4,3,2,1,0:T(8,128)(2,1)S(1)}, bf16[4,2,53,8,256]{4,3,2,1,0:T(8,128)(2,1)S(1)}) fusion(bf16[4,2,53,32,256]{4,3,2,1,0:T(8,128)(2,1)} %bitcast.81), kind=kLoop, calls=%fused_computation.69 | loop fusion | bytes 6946816 | tf_op jit(solution)/shard_map/slice | solution.py:302
  5.2 2.2 %copy.57 = bf16[4,53,2,16,256]{4,3,2,1,0:T(8,128)(2,1)} copy(bf16[4,53,2,16,256]{4,3,1,2,0:T(8,128)(2,1)S(1)} %maximum_bitcast_fusion) | data formatting | bytes 6946816 | tf_op jit(solution)/shard_map/transpose | solution.py:303
  7.3 4.3 %all-to-all-start = ((bf16[4,53,32,256]{3,2,1,0:T(8,128)(2,1)}), bf16[4,53,32,256]{3,2,1,0:T(8,128)(2,1)S(1)}, u32[]{:S(2)}, u32[]{:S(2)}) async-start(bf16[4,53,32,256]{3,2,1,0:T(8,128)(2,1)} %bitcast.79), calls=%async_computation | async-start | bytes 6946816 | tf_op jit(solution)/shard_map/all_to_all | solution.py:278
  12.4 4.6 %collective-permute-start.2 = (bf16[2,4,256]{2,1,0:T(4,128)(2,1)}, bf16[2,4,256]{2,1,0:T(4,128)(2,1)}, u32[]{:S(2)}, u32[]{:S(2)}) collective-permute-start(bf16[2,4,256]{2,1,0:T(4,128)(2,1)} %get-tuple-element.50), channel_id=1, source_target_pairs={{0,8},{8,16},{16,24},{24,32},{32,40},{40,48},{48,56},{56,64},{64,7... | collective-permute-start | bytes 12296 | tf_op jit(solution)/shard_map/ppermute | solution.py:232
  17.0 1.9 %collective-permute-start.3 = (bf16[2,4,256]{2,1,0:T(4,128)(2,1)}, bf16[2,4,256]{2,1,0:T(4,128)(2,1)}, u32[]{:S(2)}, u32[]{:S(2)}) collective-permute-start(bf16[2,4,256]{2,1,0:T(4,128)(2,1)} %get-tuple-element.51), channel_id=1, source_target_pairs={{8,0},{16,8},{24,16},{32,24},{40,32},{48,40},{56,48},{64,56},{72,6... | collective-permute-start | bytes 12296 | tf_op jit(solution)/shard_map/ppermute | solution.py:232
  19.0 0.9 collective-permute-start
  19.9 3.5 %select_bitcast_fusion = (bf16[53,4,8,256]{3,2,0,1:T(8,128)(2,1)}, bf16[53,4,8,256]{3,2,0,1:T(8,128)(2,1)S(1)}, bf16[53,4,8,256]{3,2,0,1:T(8,128)(2,1)}) fusion(pred[]{:T(512)S(6)} %eq.25, bf16[4,2,53,32,256]{4,3,2,1,0:T(8,128)(2,1)} %bitcast.82, pred[]{:T(512)S(6)} %xor.4), kind=kLoop, calls=%fused_computation.17 | loop fusion | flops 1302528 | bytes 6078466 | tf_op jit(solution)/shard_map/transpose | solution.py:297
  23.4 1.1 copy.78
  24.4 2.1 %collective-permute-start.1 = (bf16[53,32,256]{2,1,0:T(8,128)(2,1)}, bf16[53,32,256]{2,1,0:T(8,128)(2,1)}, u32[]{:S(2)}, u32[]{:S(2)}) collective-permute-start(bf16[53,32,256]{2,1,0:T(8,128)(2,1)} %bitcast.73), channel_id=1, source_target_pairs={{0,1},{1,0},{2,3},{3,2},{4,5},{5,4},{6,7},{7,6},{8,9},{9,8},{10,11... | collective-permute-start | bytes 2605064 | tf_op jit(solution)/shard_map/ppermute | solution.py:309
  28.6 1.6 %reshape.81 = bf16[64,4,2,53]{3,2,1,0:T(2,128)(2,1)} reshape(bf16[64,424]{1,0:T(8,128)(2,1)} %param.6) | data formatting | bytes 108544 | tf_op jit(solution)/shard_map/reshape | solution.py:286
  30.2 1.3 copy.58
  31.6 1.5 %pad_maximum_fusion.3.inv_ref = bf16[64,192]{1,0:T(8,128)(2,1)} fusion(bf16[64,64]{1,0:T(8,128)(2,1)} %get-tuple-element.53, bf16[64,64]{1,0:T(8,128)(2,1)S(1)} %get-tuple-element.52), kind=kLoop, calls=%fused_computation.38 | loop fusion | flops 73728 | bytes 40960 | tf_op jit(solution)/shard_map/concatenate | solution.py:334
  33.0 0.9 constant_dynamic-slice_fusion.1
  34.0 1.5 %multiply_convert_fusion = (bf16[2,64,2,64]{3,2,1,0:T(2,128)(2,1)}, bf16[2,64,2,64]{3,2,1,0:T(2,128)(2,1)S(1)}) fusion(f32[64,64]{1,0:T(8,128)} %copy.55, f32[2,2]{1,0:T(2,128)S(1)} %compare_convert_fusion, f32[64,64]{1,0:T(8,128)} %copy.54), kind=kLoop, calls=%fused_computation.21 | loop fusion | flops 65536 | bytes 98320 | tf_op jit(solution)/shard_map/convert.12
  35.5 6.4 %collective-permute-done = bf16[53,32,256]{2,1,0:T(8,128)(2,1)} collective-permute-done((bf16[53,32,256]{2,1,0:T(8,128)(2,1)}, bf16[53,32,256]{2,1,0:T(8,128)(2,1)}, u32[]{:S(2)}, u32[]{:S(2)}) %collective-permute-start) | collective-permute-done | bytes 868384 | tf_op jit(solution)/shard_map/ppermute | solution.py:307
  41.9 1.6 %copy.59 = bf16[53,32,256]{2,0,1:T(8,128)(2,1)S(1)} copy(bf16[53,32,256]{2,1,0:T(8,128)(2,1)} %collective-permute-done) | data formatting | bytes 1736704 | tf_op jit(solution)/shard_map/ppermute | solution.py:307
  44.0 1.9 %shard_map.55 = s16[4,528,256]{2,1,0:T(8,128)(2,1)} custom-call(s32[4]{0:T(128)S(1)} %iota.71.which_ref, f32[4,8,64,256]{3,2,1,0:T(8,128)S(1)} %bitcast.77), custom_call_target="tpu_custom_call" | custom-call | tf_op jit(solution)/shard_map/pallas_call | solution.py:44
  45.9 6.0 %all-to-all-done = bf16[4,53,32,256]{3,2,1,0:T(8,128)(2,1)S(1)} async-done(((bf16[4,53,32,256]{3,2,1,0:T(8,128)(2,1)}), bf16[4,53,32,256]{3,2,1,0:T(8,128)(2,1)S(1)}, u32[]{:S(2)}, u32[]{:S(2)}) %all-to-all-start) | async-done | bytes 3473440 | tf_op jit(solution)/shard_map/all_to_all | solution.py:278
  51.9 1.7 %copy-done.11 = bf16[4,53,32,256]{3,2,1,0:T(8,128)(2,1)} copy-done((bf16[4,53,32,256]{3,2,1,0:T(8,128)(2,1)}, bf16[4,53,32,256]{3,2,1,0:T(8,128)(2,1)S(1)}, u32[]{:S(2)}) %copy-start.11) | copy-done | bytes 3473432
  53.6 3.5 %all-to-all-start.1 = ((s16[4,528,256]{2,1,0:T(8,128)(2,1)}), s16[4,528,256]{2,1,0:T(8,128)(2,1)S(1)}, u32[]{:S(2)}, u32[]{:S(2)}) async-start(s16[4,528,256]{2,1,0:T(8,128)(2,1)} %shard_map.55), calls=%async_computation.1 | async-start | bytes 2162688 | tf_op jit(solution)/shard_map/all_to_all | solution.py:278
  57.8 0.9 mul.66
  59.5 1.4 dynamic-slice_reduce_fusion
  60.9 1.3 copy.66
  63.1 4.1 %fusion = f32[32,256,64]{1,2,0:T(8,128)S(1)} fusion(bf16[64,212,1]{1,0,2:T(8,128)(2,1)S(1)} %reshape.92, bf16[212,32,256]{2,1,0:T(8,128)(2,1)} %bitcast.78), kind=kOutput, calls=%fused_computation | convolution fusion | flops 222298112 | bytes 5597696 | tf_op jit(solution)/shard_map/eb,bhw->hew/dot_general | solution.py:283
  67.2 1.0 shard_map.56
  68.3 1.0 collective-permute-start.4
  69.3 1.6 %copy.67 = bf16[53,32,256]{2,0,1:T(8,128)(2,1)S(1)} copy(bf16[53,32,256]{2,1,0:T(8,128)(2,1)} %collective-permute-done.1) | data formatting | bytes 1736704 | tf_op jit(solution)/shard_map/optimization_barrier | solution.py:323
  72.3 1.0 copy-done.2
  73.3 4.3 %all-to-all-start.2 = ((s16[4,528,256]{2,1,0:T(8,128)(2,1)}), s16[4,528,256]{2,1,0:T(8,128)(2,1)}, u32[]{:S(2)}, u32[]{:S(2)}) async-start(s16[4,528,256]{2,1,0:T(8,128)(2,1)} %copy-done.2), calls=%async_computation.2 | async-start | bytes 2162688 | tf_op jit(solution)/shard_map/all_to_all | solution.py:278
  77.7 3.8 %collective-permute-start.10 = (bf16[2,40,4]{2,1,0:T(8,128)(2,1)S(1)}, bf16[2,40,4]{2,1,0:T(8,128)(2,1)S(1)}, u32[]{:S(2)}, u32[]{:S(2)}) collective-permute-start(bf16[2,40,4]{2,1,0:T(8,128)(2,1)S(1)} %get-tuple-element.48), channel_id=1, source_target_pairs={{1,0},{2,1},{3,2},{4,3},{5,4},{6,5},{7,6},{9,8},{10,9},{11,10},{12... | collective-permute-start | bytes 1928 | tf_op jit(solution)/shard_map/ppermute | solution.py:232
  81.5 3.8 %collective-permute-start.9 = (bf16[2,40,4]{2,1,0:T(8,128)(2,1)S(1)}, bf16[2,40,4]{2,1,0:T(8,128)(2,1)S(1)}, u32[]{:S(2)}, u32[]{:S(2)}) collective-permute-start(bf16[2,40,4]{2,1,0:T(8,128)(2,1)S(1)} %get-tuple-element.49), channel_id=1, source_target_pairs={{0,1},{1,2},{2,3},{3,4},{4,5},{5,6},{6,7},{8,9},{9,10},{10,11},{11... | collective-permute-start | bytes 1928 | tf_op jit(solution)/shard_map/ppermute | solution.py:232
  85.4 2.5 %collective-permute-done.9 = bf16[2,40,4]{2,1,0:T(8,128)(2,1)S(1)} collective-permute-done((bf16[2,40,4]{2,1,0:T(8,128)(2,1)S(1)}, bf16[2,40,4]{2,1,0:T(8,128)(2,1)S(1)}, u32[]{:S(2)}, u32[]{:S(2)}) %collective-permute-start.9) | collective-permute-done | bytes 672 | tf_op jit(solution)/shard_map/ppermute | solution.py:232
  88.2 1.2 shard_map.57
  89.4 1.0 copy-done.3
  90.4 7.4 %collective-permute-start.5 = (f32[4,64,256]{2,1,0:T(8,128)S(1)}, f32[4,64,256]{2,1,0:T(8,128)S(1)}, u32[]{:S(2)}, u32[]{:S(2)}) collective-permute-start(f32[4,64,256]{2,1,0:T(8,128)S(1)} %get-tuple-element.33), channel_id=1, source_target_pairs={{0,8},{8,16},{16,24},{24,32},{32,40},{40,48},{48,56},{56,64},{64,7... | collective-permute-start | bytes 786440 | tf_op jit(solution)/shard_map/ppermute | solution.py:232
  97.7 1.9 %collective-permute-start.6 = (f32[4,64,256]{2,1,0:T(8,128)S(1)}, f32[4,64,256]{2,1,0:T(8,128)S(1)}, u32[]{:S(2)}, u32[]{:S(2)}) collective-permute-start(f32[4,64,256]{2,1,0:T(8,128)S(1)} %get-tuple-element.34), channel_id=1, source_target_pairs={{8,0},{16,8},{24,16},{32,24},{40,32},{48,40},{56,48},{64,56},{72,6... | collective-permute-start | bytes 786440 | tf_op jit(solution)/shard_map/ppermute | solution.py:232
  100.5 1.2 collective-permute-done.5.top_ref
  102.4 3.9 %collective-permute-done.6.bottom_ref = f32[4,64,256]{2,1,0:T(8,128)S(1)} collective-permute-done((f32[4,64,256]{2,1,0:T(8,128)S(1)}, f32[4,64,256]{2,1,0:T(8,128)S(1)}, u32[]{:S(2)}, u32[]{:S(2)}) %collective-permute-start.6) | collective-permute-done | bytes 262176 | tf_op jit(solution)/shard_map/ppermute | solution.py:232
  107.0 1.2 copy-done.1
  108.3 1.2 copy-done.4
  109.5 0.9 copy-done.7
  110.5 0.9 copy-done.9
  112.2 3.5 %shard_map.59 = (f32[24,256,128]{2,1,0:T(8,128)S(1)}, f32[24,8,128]{2,1,0:T(8,128)S(1)}, f32[24,8,128]{2,1,0:T(8,128)S(1)}) custom-call(bf16[64,192]{1,0:T(8,128)(2,1)S(1)} %copy-done.10, f32[16,64,256]{2,1,0:T(8,128)S(1)} %copy-done.4, s16[4,528,256]{2,1,0:T(8,128)(2,1)S(1)} %copy-done.1, s16[4,528,256]{2,1,0:T(8,128)(2,1)} %all-to-all-done.2.lower_ref, ...), custom_call_target="tpu_custom_call" | custom-call | tf_op jit(solution)/shard_map/pallas_call | solution.py:134
  115.7 4.7 %collective-permute-start.7 = (f32[24,8,128]{2,1,0:T(8,128)S(1)}, f32[24,8,128]{2,1,0:T(8,128)S(1)}, u32[]{:S(2)}, u32[]{:S(2)}) collective-permute-start(f32[24,8,128]{2,1,0:T(8,128)S(1)} %get-tuple-element.36), channel_id=1, source_target_pairs={{0,1},{1,2},{2,3},{3,4},{4,5},{5,6},{6,7},{8,9},{9,10},{10,11},{11... | collective-permute-start | bytes 294920 | tf_op jit(solution)/shard_map/ppermute | solution.py:232
  120.4 2.1 %collective-permute-start.8 = (f32[24,8,128]{2,1,0:T(8,128)S(1)}, f32[24,8,128]{2,1,0:T(8,128)S(1)}, u32[]{:S(2)}, u32[]{:S(2)}) collective-permute-start(f32[24,8,128]{2,1,0:T(8,128)S(1)} %get-tuple-element.37), channel_id=1, source_target_pairs={{1,0},{2,1},{3,2},{4,3},{5,4},{6,5},{7,6},{9,8},{10,9},{11,10},{12... | collective-permute-start | bytes 294920 | tf_op jit(solution)/shard_map/ppermute | solution.py:232
  123.4 4.8 %collective-permute-done.8.right_ref = f32[24,8,128]{2,1,0:T(8,128)S(1)} collective-permute-done((f32[24,8,128]{2,1,0:T(8,128)S(1)}, f32[24,8,128]{2,1,0:T(8,128)S(1)}, u32[]{:S(2)}, u32[]{:S(2)}) %collective-permute-start.8) | collective-permute-done | bytes 98336 | tf_op jit(solution)/shard_map/ppermute | solution.py:232
  128.2 13.4 %shard_map.60 = f32[64,32,256]{2,1,0:T(8,128)} custom-call(bf16[384,128]{1,0:T(8,128)(2,1)S(1)} %copy-done.5, f32[24,256,128]{2,1,0:T(8,128)S(1)} %get-tuple-element.35.mixed_ref, f32[24,8,128]{2,1,0:T(8,128)S(1)} %collective-permute-done.7.left_ref, f32[24,8,128]{2,1,0:T(8,128)S(1)} %collective-permute-done.8.right_ref, ...), custom_call_target="tpu_custom_call" | custom-call | tf_op jit(solution)/shard_map/pallas_call | solution.py:213
  (79 shorter events, 11.3 us)
Async XLA Ops:
  7.3 4.3 %copy-start.19 = (s32[32,256]{1,0:T(8,128)S(1)}, s32[32,256]{1,0:T(8,128)}, u32[]{:S(2)}) copy-start(s32[32,256]{1,0:T(8,128)} %param.9) | copy-start | bytes 98308
  7.3 4.3 %copy-start.20 = (s32[32,256]{1,0:T(8,128)S(1)}, s32[32,256]{1,0:T(8,128)}, u32[]{:S(2)}) copy-start(s32[32,256]{1,0:T(8,128)} %param.8) | copy-start | bytes 98308
  7.3 44.6 %all-to-all-start = ((bf16[4,53,32,256]{3,2,1,0:T(8,128)(2,1)}), bf16[4,53,32,256]{3,2,1,0:T(8,128)(2,1)S(1)}, u32[]{:S(2)}, u32[]{:S(2)}) async-start(bf16[4,53,32,256]{3,2,1,0:T(8,128)(2,1)} %bitcast.79), calls=%async_computation | async-start | bytes 6946816 | tf_op jit(solution)/shard_map/all_to_all | solution.py:278
  11.8 7.2 %copy-start.16 = (bf16[2,32,256]{2,1,0:T(8,128)(2,1)}, bf16[2,32,256]{2,1,0:T(8,128)(2,1)S(1)}, u32[]{:S(2)}) copy-start(bf16[2,32,256]{2,1,0:T(8,128)(2,1)S(1)} %add_convert_fusion) | copy-start | bytes 98308
  12.4 49.9 %collective-permute-start.2 = (bf16[2,4,256]{2,1,0:T(4,128)(2,1)}, bf16[2,4,256]{2,1,0:T(4,128)(2,1)}, u32[]{:S(2)}, u32[]{:S(2)}) collective-permute-start(bf16[2,4,256]{2,1,0:T(4,128)(2,1)} %get-tuple-element.50), channel_id=1, source_target_pairs={{0,8},{8,16},{16,24},{24,32},{32,40},{40,48},{48,56},{56,64},{64,7... | collective-permute-start | bytes 12296 | tf_op jit(solution)/shard_map/ppermute | solution.py:232
  17.0 9.5 %copy-start.21 = (f32[64,64]{1,0:T(8,128)S(1)}, f32[64,64]{1,0:T(8,128)}, u32[]{:S(2)}) copy-start(f32[64,64]{1,0:T(8,128)} %param.7) | copy-start | bytes 49156
  17.0 45.2 %collective-permute-start.3 = (bf16[2,4,256]{2,1,0:T(4,128)(2,1)}, bf16[2,4,256]{2,1,0:T(4,128)(2,1)}, u32[]{:S(2)}, u32[]{:S(2)}) collective-permute-start(bf16[2,4,256]{2,1,0:T(4,128)(2,1)} %get-tuple-element.51), channel_id=1, source_target_pairs={{8,0},{16,8},{24,16},{32,24},{40,32},{48,40},{56,48},{64,56},{72,6... | collective-permute-start | bytes 12296 | tf_op jit(solution)/shard_map/ppermute | solution.py:232
  19.0 22.9 %collective-permute-start = (bf16[53,32,256]{2,1,0:T(8,128)(2,1)}, bf16[53,32,256]{2,1,0:T(8,128)(2,1)}, u32[]{:S(2)}, u32[]{:S(2)}) collective-permute-start(bf16[53,32,256]{2,1,0:T(8,128)(2,1)} %copy_bitcast_fusion.1), channel_id=1, source_target_pairs={{0,1},{1,0},{2,3},{3,2},{4,5},{5,4},{6,7},{7,6},{8,9},{9,8},{10,11... | collective-permute-start | bytes 2605064 | tf_op jit(solution)/shard_map/ppermute | solution.py:307
  24.4 43.8 %collective-permute-start.1 = (bf16[53,32,256]{2,1,0:T(8,128)(2,1)}, bf16[53,32,256]{2,1,0:T(8,128)(2,1)}, u32[]{:S(2)}, u32[]{:S(2)}) collective-permute-start(bf16[53,32,256]{2,1,0:T(8,128)(2,1)} %bitcast.73), channel_id=1, source_target_pairs={{0,1},{1,0},{2,3},{3,2},{4,5},{5,4},{6,7},{7,6},{8,9},{9,8},{10,11... | collective-permute-start | bytes 2605064 | tf_op jit(solution)/shard_map/ppermute | solution.py:309
  34.0 10.1 %copy-start.17 = (bf16[64,53]{1,0:T(8,128)(2,1)}, bf16[64,53]{1,0:T(8,128)(2,1)S(1)}, u32[]{:S(2)}) copy-start(bf16[64,53]{1,0:T(8,128)(2,1)S(1)} %get-tuple-element.59) | copy-start | bytes 20356
  51.9 1.7 %copy-start.11 = (bf16[4,53,32,256]{3,2,1,0:T(8,128)(2,1)}, bf16[4,53,32,256]{3,2,1,0:T(8,128)(2,1)S(1)}, u32[]{:S(2)}) copy-start(bf16[4,53,32,256]{3,2,1,0:T(8,128)(2,1)S(1)} %all-to-all-done) | copy-start | bytes 10420228
  53.6 19.7 %all-to-all-start.1 = ((s16[4,528,256]{2,1,0:T(8,128)(2,1)}), s16[4,528,256]{2,1,0:T(8,128)(2,1)S(1)}, u32[]{:S(2)}, u32[]{:S(2)}) async-start(s16[4,528,256]{2,1,0:T(8,128)(2,1)} %shard_map.55), calls=%async_computation.1 | async-start | bytes 2162688 | tf_op jit(solution)/shard_map/all_to_all | solution.py:278
  67.2 3.7 %copy-start.18 = (bf16[64,53]{1,0:T(8,128)(2,1)S(1)}, bf16[64,53]{1,0:T(8,128)(2,1)}, u32[]{:S(2)}) copy-start(bf16[64,53]{1,0:T(8,128)(2,1)} %copy-done.17) | copy-start | bytes 20356
  68.3 19.9 %collective-permute-start.4 = (s16[1,1040,256]{2,1,0:T(8,128)(2,1)}, s16[1,1040,256]{2,1,0:T(8,128)(2,1)}, u32[]{:S(2)}, u32[]{:S(2)}) collective-permute-start(s16[1,1040,256]{2,1,0:T(8,128)(2,1)} %shard_map.56), channel_id=1, source_target_pairs={{0,1},{1,0},{2,3},{3,2},{4,5},{5,4},{6,7},{7,6},{8,9},{9,8},{10,11... | collective-permute-start | bytes 1597448 | tf_op jit(solution)/shard_map/ppermute | solution.py:324
  72.3 1.0 copy-start.2
  73.3 26.4 %copy-start.22 = (s32[128]{0:T(128)S(1)}, s32[128]{0:T(128)}, u32[]{:S(2)}) copy-start(s32[128]{0:T(128)} %get-tuple-element.62) | copy-start | bytes 1540
  73.3 26.4 %copy-start.23 = (s32[128]{0:T(128)S(1)}, s32[128]{0:T(128)}, u32[]{:S(2)}) copy-start(s32[128]{0:T(128)} %get-tuple-element.63) | copy-start | bytes 1540
  73.3 26.4 %copy-start = (s16[4,528,256]{2,1,0:T(8,128)(2,1)}, s16[4,528,256]{2,1,0:T(8,128)(2,1)S(1)}, u32[]{:S(2)}) copy-start(s16[4,528,256]{2,1,0:T(8,128)(2,1)S(1)} %all-to-all-done.1.upper_ref) | copy-start | bytes 3244036
  73.3 33.7 %all-to-all-start.2 = ((s16[4,528,256]{2,1,0:T(8,128)(2,1)}), s16[4,528,256]{2,1,0:T(8,128)(2,1)}, u32[]{:S(2)}, u32[]{:S(2)}) async-start(s16[4,528,256]{2,1,0:T(8,128)(2,1)} %copy-done.2), calls=%async_computation.2 | async-start | bytes 2162688 | tf_op jit(solution)/shard_map/all_to_all | solution.py:278
  77.7 7.7 %collective-permute-start.10 = (bf16[2,40,4]{2,1,0:T(8,128)(2,1)S(1)}, bf16[2,40,4]{2,1,0:T(8,128)(2,1)S(1)}, u32[]{:S(2)}, u32[]{:S(2)}) collective-permute-start(bf16[2,40,4]{2,1,0:T(8,128)(2,1)S(1)} %get-tuple-element.48), channel_id=1, source_target_pairs={{1,0},{2,1},{3,2},{4,3},{5,4},{6,5},{7,6},{9,8},{10,9},{11,10},{12... | collective-permute-start | bytes 1928 | tf_op jit(solution)/shard_map/ppermute | solution.py:232
  81.5 6.3 %collective-permute-start.9 = (bf16[2,40,4]{2,1,0:T(8,128)(2,1)S(1)}, bf16[2,40,4]{2,1,0:T(8,128)(2,1)S(1)}, u32[]{:S(2)}, u32[]{:S(2)}) collective-permute-start(bf16[2,40,4]{2,1,0:T(8,128)(2,1)S(1)} %get-tuple-element.49), channel_id=1, source_target_pairs={{0,1},{1,2},{2,3},{3,4},{4,5},{5,6},{6,7},{8,9},{9,10},{10,11},{11... | collective-permute-start | bytes 1928 | tf_op jit(solution)/shard_map/ppermute | solution.py:232
  88.1 13.7 %copy-start.12 = (bf16[1,2,24,288]{3,0,2,1:T(2,128)(2,1)}, bf16[1,2,24,288]{3,0,2,1:T(2,128)(2,1)S(1)}, u32[]{:S(2)}) copy-start(bf16[1,2,24,288]{3,0,2,1:T(2,128)(2,1)S(1)} %copy.69) | copy-start | bytes 82948
  88.2 13.6 %copy-start.14 = (bf16[1,2,24,288]{3,0,2,1:T(2,128)(2,1)}, bf16[1,2,24,288]{3,0,2,1:T(2,128)(2,1)S(1)}, u32[]{:S(2)}) copy-start(bf16[1,2,24,288]{3,0,2,1:T(2,128)(2,1)S(1)} %copy.68) | copy-start | bytes 82948
  89.4 1.0 copy-start.3
  90.4 11.3 %collective-permute-start.5 = (f32[4,64,256]{2,1,0:T(8,128)S(1)}, f32[4,64,256]{2,1,0:T(8,128)S(1)}, u32[]{:S(2)}, u32[]{:S(2)}) collective-permute-start(f32[4,64,256]{2,1,0:T(8,128)S(1)} %get-tuple-element.33), channel_id=1, source_target_pairs={{0,8},{8,16},{16,24},{24,32},{32,40},{40,48},{48,56},{56,64},{64,7... | collective-permute-start | bytes 786440 | tf_op jit(solution)/shard_map/ppermute | solution.py:232
  97.7 8.6 %collective-permute-start.6 = (f32[4,64,256]{2,1,0:T(8,128)S(1)}, f32[4,64,256]{2,1,0:T(8,128)S(1)}, u32[]{:S(2)}, u32[]{:S(2)}) collective-permute-start(f32[4,64,256]{2,1,0:T(8,128)S(1)} %get-tuple-element.34), channel_id=1, source_target_pairs={{8,0},{16,8},{24,16},{32,24},{40,32},{48,40},{56,48},{64,56},{72,6... | collective-permute-start | bytes 786440 | tf_op jit(solution)/shard_map/ppermute | solution.py:232
  101.7 0.7 copy-start.6
  106.3 0.7 copy-start.8
  107.0 1.2 copy-start.1
  108.3 1.2 copy-start.4
  109.5 0.9 copy-start.7
  110.5 0.9 copy-start.9
  111.4 0.8 copy-start.10
  112.2 10.4 %copy-start.13 = (bf16[1,2,24,288]{3,0,2,1:T(2,128)(2,1)S(1)}, bf16[1,2,24,288]{3,0,2,1:T(2,128)(2,1)}, u32[]{:S(2)}) copy-start(bf16[1,2,24,288]{3,0,2,1:T(2,128)(2,1)} %copy-done.12) | copy-start | bytes 82948
  112.2 10.4 %copy-start.15 = (bf16[1,2,24,288]{3,0,2,1:T(2,128)(2,1)S(1)}, bf16[1,2,24,288]{3,0,2,1:T(2,128)(2,1)}, u32[]{:S(2)}) copy-start(bf16[1,2,24,288]{3,0,2,1:T(2,128)(2,1)} %copy-done.14) | copy-start | bytes 82948
  112.2 16.0 %copy-start.5 = (bf16[384,128]{1,0:T(8,128)(2,1)S(1)}, bf16[384,128]{1,0:T(8,128)(2,1)}, u32[]{:S(2)}) copy-start(bf16[384,128]{1,0:T(8,128)(2,1)} %pad_maximum_fusion.invt_ref) | copy-start | bytes 294916
  115.7 7.6 %collective-permute-start.7 = (f32[24,8,128]{2,1,0:T(8,128)S(1)}, f32[24,8,128]{2,1,0:T(8,128)S(1)}, u32[]{:S(2)}, u32[]{:S(2)}) collective-permute-start(f32[24,8,128]{2,1,0:T(8,128)S(1)} %get-tuple-element.36), channel_id=1, source_target_pairs={{0,1},{1,2},{2,3},{3,4},{4,5},{5,6},{6,7},{8,9},{9,10},{10,11},{11... | collective-permute-start | bytes 294920 | tf_op jit(solution)/shard_map/ppermute | solution.py:232
  120.4 7.8 %collective-permute-start.8 = (f32[24,8,128]{2,1,0:T(8,128)S(1)}, f32[24,8,128]{2,1,0:T(8,128)S(1)}, u32[]{:S(2)}, u32[]{:S(2)}) collective-permute-start(f32[24,8,128]{2,1,0:T(8,128)S(1)} %get-tuple-element.37), channel_id=1, source_target_pairs={{1,0},{2,1},{3,2},{4,3},{5,4},{6,5},{7,6},{9,8},{10,9},{11,10},{12... | collective-permute-start | bytes 294920 | tf_op jit(solution)/shard_map/ppermute | solution.py:232

commit v4 on v3

v4 whole, which is shorter than its diff:
```python
import functools

import jax
import jax.numpy as jnp
from jax import lax
from jax.experimental import pallas as pl
from jax.experimental.pallas import tpu as pltpu
from jax.sharding import PartitionSpec as P

KAPPA = 0.24
EDGE_SCALE = 1.0 / 255.0
HALO = 4
LEAD = 16
SPAN = 288
GROUP = 16
LEVELS = 256.0
STEPS_MAX = 32000.0


def parts3(x, axis):
    hi = x.astype(jnp.bfloat16)
    lo = (x - hi.astype(jnp.float32)).astype(jnp.bfloat16)
    return jnp.concatenate([hi, hi, lo], axis=axis)


def code_kernel(which_ref, x_ref, *out_refs):
    _, rows, count, width = x_ref.shape
    slot = lax.broadcasted_iota(jnp.int32, (16, width), 0)
    for s, out_ref in enumerate(out_refs):
        levels = jnp.zeros((16, width), jnp.float32)
        for r in range(rows):
            x = x_ref[which_ref[s], r]
            top = jnp.max(jnp.max(jnp.abs(x), axis=0, keepdims=True), axis=1, keepdims=True)
            level = jnp.ceil(jnp.log2(jnp.maximum(top, 1e-30)) * LEVELS)
            scale = STEPS_MAX * jnp.exp2(level * (-1.0 / LEVELS))
            q = jnp.round(x * scale).astype(jnp.int32).astype(jnp.int16)
            out_ref[r * count : (r + 1) * count] = q
            levels = jnp.where(slot == r, level, levels)
        out_ref[rows * count :] = levels.astype(jnp.int32).astype(jnp.int16)


def coded(x, which):
    _, rows, count, width = x.shape
    vmem = pl.BlockSpec(memory_space=pltpu.VMEM)
    shape = jax.ShapeDtypeStruct((rows * count + 16, width), jnp.int16)
    return pl.pallas_call(
        code_kernel,
        out_shape=[shape] * len(which),
        in_specs=[pl.BlockSpec(memory_space=pltpu.SMEM), vmem],
        out_specs=[vmem] * len(which),
        compiler_params=pltpu.CompilerParams(vmem_limit_bytes=5 * 2**20),
    )(jnp.stack(which), x)


def scales(levels):
    levels = levels.astype(jnp.int32).astype(jnp.float32)
    return jnp.exp2(levels * (1.0 / LEVELS)) * (1.0 / STEPS_MAX)


def decoded_row(ref, scale, r, count):
    q = ref[pl.ds(r * count, count)].astype(jnp.int32).astype(jnp.float32)
    return q * scale[pl.ds(r, 1)]


def finish_kernel(keep_last, which_ref, own_ref, *refs):
    *part_refs, out_ref, edge_ref, scale = refs
    rows, count, _ = out_ref.shape
    for s, ref in enumerate(part_refs):
        scale[s] = scales(ref[rows * count :])
    for r in range(rows):
        x = own_ref[which_ref[0], r]
        for s, ref in enumerate(part_refs):
            x = x + decoded_row(ref, scale.at[s], r, count)
        out_ref[r] = x
        e = r - (rows - HALO) if keep_last else r
        if 0 <= e < HALO:
            edge_ref[e] = x


def finished(own, which, parts, keep_last):
    _, rows, count, width = own.shape
    vmem = pl.BlockSpec(memory_space=pltpu.VMEM)
    shapes = [(rows, count, width), (HALO, count, width)]
    return pl.pallas_call(
        functools.partial(finish_kernel, keep_last),
        out_shape=[jax.ShapeDtypeStruct(x, jnp.float32) for x in shapes],
        in_specs=[pl.BlockSpec(memory_space=pltpu.SMEM)] + [vmem] * (1 + len(parts)),
        out_specs=[vmem] * 2,
        scratch_shapes=[pltpu.VMEM((len(parts), 16, width), jnp.float32)],
        compiler_params=pltpu.CompilerParams(vmem_limit_bytes=6 * 2**20),
    )(jnp.reshape(which, (1,)), own, *parts)


def mix_kernel(
    which_ref, inv_ref, early_ref, late_ref, own_ref, a_ref, b_ref, c_ref, top_ref, bottom_ref,
    mixed_ref, low_ref, high_ref, scale,
):
    half, count, width = early_ref.shape
    quarter = half // 2
    deep = mixed_ref.shape[0]
    inv = inv_ref[...]
    parts = (a_ref, b_ref, c_ref)
    for s, ref in enumerate(parts):
        scale[s] = scales(ref[quarter * count :])

    def third(r):
        x = own_ref[which_ref[0], r]
        for s, ref in enumerate(parts):
            x = x + decoded_row(ref, scale.at[s], r, count)
        return x

    def mix_pairs(pairs, slot):
        cat = jnp.concatenate([parts3(x, 0) for pair in pairs for x in pair], axis=1)
        m = jnp.dot(inv, cat, preferred_element_type=jnp.float32)
        for k in range(len(pairs)):
            a = m[:, 2 * k * width : (2 * k + 1) * width]
            b = m[:, (2 * k + 1) * width : (2 * k + 2) * width]
            turned = jnp.transpose(jnp.concatenate([a, b], 0))
            mixed_ref[slot + k] = turned
            low_ref[slot + k] = turned[:8]
            high_ref[slot + k] = turned[width - 8 :]

    mix_pairs([(top_ref[k], early_ref[half - HALO + k]) for k in range(HALO)], 0)
    mix_pairs([(third(k), bottom_ref[k]) for k in range(HALO)], deep - HALO)

    @pl.loop(0, quarter // 2)
    def _(g):
        r = g * 2
        mix_pairs([(early_ref[r + k], third(r + k)) for k in range(2)], r + HALO)
        mix_pairs(
            [(early_ref[r + k + quarter], late_ref[r + k]) for k in range(2)], r + HALO + quarter
        )


def mix(which, inv3, early, late, own, parts, top, bottom):
    half, count, width = early.shape
    deep = half + 2 * HALO
    vmem = pl.BlockSpec(memory_space=pltpu.VMEM)
    shapes = [(deep, width, 2 * count), (deep, 8, 2 * count), (deep, 8, 2 * count)]
    return pl.pallas_call(
        mix_kernel,
        out_shape=[jax.ShapeDtypeStruct(x, jnp.float32) for x in shapes],
        in_specs=[pl.BlockSpec(memory_space=pltpu.SMEM)] + [vmem] * 9,
        out_specs=[vmem] * 3,
        scratch_shapes=[pltpu.VMEM((3, 16, width), jnp.float32)],
        compiler_params=pltpu.CompilerParams(vmem_limit_bytes=10 * 2**20),
    )(jnp.reshape(which, (1,)), inv3, early, late, own, *parts, top, bottom)


def admm_kernel(
    invt_ref, mixed_ref, left_ref, right_ref, wh_ref, wv_ref, out_ref, mixed, y, z, turned
):
    deep, width, lanes = mixed_ref.shape
    count = lanes // 2
    half = deep - 2 * HALO

    @pl.loop(0, deep)
    def _(r):
        mixed[r, LEAD : LEAD + width] = mixed_ref[r]
        mixed[r, LEAD - 8 : LEAD] = left_ref[r]
        mixed[r, LEAD + width : LEAD + width + 8] = right_ref[r]

    def diffuse(src, dst, begin, end):
        @pl.loop(0, (width + 16) // GROUP)
        def _(g):
            c = pl.multiple_of(LEAD - 8 + g * GROUP, 8)
            at, after, before = pl.ds(c, GROUP), pl.ds(c + 1, GROUP), pl.ds(c - 1, GROUP)
            here = src[begin, at]
            above = wv_ref[begin - 1, at] * (here - src[begin - 1, at])
            for i in range(begin, end):
                below = src[i + 1, at]
                down = wv_ref[i, at] * (below - here)
                right = wh_ref[i, at] * (src[i, after] - here)
                left = wh_ref[i, before] * (here - src[i, before])
                dst[i, at] = here + (right - left) + (down - above)
                here, above = below, down

    diffuse(mixed, z, 1, deep - 1)
    diffuse(z, y, 2, deep - 2)
    invt = invt_ref[...]
    used = pl.ds(LEAD - 8, width + 16)

    @pl.loop(2, deep - 2, step=2)
    def _(first):
        for k in range(2):
            kept = jnp.maximum(y[first + k, used], 0.0)
            before = mixed[first + k, used]
            u = parts3(kept - 0.5 * before, 1)
            m = jnp.dot(u, invt, preferred_element_type=jnp.float32)
            z[first + k, used] = m + (2.0 * before - kept)

    diffuse(z, y, 3, deep - 3)
    diffuse(y, z, 4, deep - 4)

    @pl.loop(0, half // 2)
    def _(g):
        for k in range(2):
            r = g * 2 + k
            v = jnp.transpose(jnp.maximum(z[r + HALO, LEAD : LEAD + width], 0.0))
            for h in range(2):
                for t in range(width // 128):
                    turned[t, pl.ds(r + h * half, count, stride=2 * half), :] = v[
                        h * count : (h + 1) * count, t * 128 : (t + 1) * 128
                    ]

    @pl.loop(0, count // 8)
    def _(g):
        for k in range(8):
            e = g * 8 + k
            for t in range(width // 128):
                out_ref[e, :, t * 128 : (t + 1) * 128] = turned[t, pl.ds(e * 2 * half, 2 * half), :]


def admm(inv3t, mixed, left, right, wh, wv):
    deep, width, lanes = mixed.shape
    half = deep - 2 * HALO
    vmem = pl.BlockSpec(memory_space=pltpu.VMEM)
    field = pltpu.VMEM((deep, SPAN, lanes), jnp.float32)
    return pl.pallas_call(
        admm_kernel,
        out_shape=jax.ShapeDtypeStruct((lanes // 2, 2 * half, width), jnp.float32),
        in_specs=[vmem] * 6,
        out_specs=vmem,
        scratch_shapes=[
            field,
            field,
            field,
            pltpu.VMEM((width // 128, lanes * half, 128), jnp.float32),
        ],
        compiler_params=pltpu.CompilerParams(vmem_limit_bytes=28 * 2**20),
    )(inv3t, mixed, left, right, wh, wv)


def neighbours(axis, low_part, high_part):
    count = lax.axis_size(axis)
    forward = [(i, i + 1) for i in range(count - 1)]
    backward = [(i + 1, i) for i in range(count - 1)]
    return lax.ppermute(high_part, axis, forward), lax.ppermute(low_part, axis, backward)


def raw_weights(weight_h, weight_v):
    col_count = lax.axis_size("col")
    row_count = lax.axis_size("row")
    tile_h, tile_w = weight_h.shape
    rows = lax.axis_index("row") * tile_h + lax.broadcasted_iota(jnp.int32, (tile_h, tile_w), 0)
    cols = lax.axis_index("col") * tile_w + lax.broadcasted_iota(jnp.int32, (tile_h, tile_w), 1)
    wh = jnp.where(cols < tile_w * col_count - 1, weight_h, 0)
    wv = jnp.where(rows < tile_h * row_count - 1, weight_v, 0)
    return jnp.stack([wh, wv]).astype(jnp.bfloat16)


def heightened(weights):
    tile_h = weights.shape[1]
    above, below = neighbours("row", weights[:, :HALO], weights[:, tile_h - HALO :])
    return jnp.concatenate([above, weights, below], axis=1)


def widened(weights):
    left, right = neighbours("col", weights[..., :HALO], weights[..., -HALO:])
    tile_w = weights.shape[2]
    gap = jnp.zeros(weights.shape[:2] + (LEAD - HALO,), weights.dtype)
    tail = jnp.zeros(weights.shape[:2] + (SPAN - LEAD - HALO - tile_w,), weights.dtype)
    return jnp.concatenate([gap, left, weights, right, tail], axis=2)


def held_weights(weights, count, half):
    deep = half + 2 * HALO
    pair = jnp.stack([weights[:, :deep], weights[:, half:]]).astype(jnp.bfloat16)
    lanes = lax.broadcasted_iota(jnp.int32, (2, 2 * count), 1) // count
    spread = (lanes == lax.broadcasted_iota(jnp.int32, (2, 2 * count), 0)).astype(jnp.bfloat16)
    scale = jnp.float32(KAPPA * EDGE_SCALE)
    return [
        scale * jnp.einsum("hrc,hl->rcl", x, spread, preferred_element_type=jnp.float32)
        for x in (pair[:, 0], pair[:, 1])
    ]


def per_device(cube, library_t, inverse, weight_h, weight_v):
    strips, bands, tile_h, tile_w = cube.shape
    count = library_t.shape[0]
    half, quarter = tile_h // 2, tile_h // 4
    ys = strips // 2
    col = lax.axis_index("col").astype(jnp.int32)
    y, x = lax.shift_right_logical(col, 1), lax.bitwise_and(col, 1)
    columns = [[c for c in range(strips) if c % 2 == k] for k in range(2)]
    swap = [(c, c ^ 1) for c in range(strips)]
    turns = [[(c, (c + 2 * k) % strips) for c in range(strips)] for k in range(ys)]
    barrier = lax.optimization_barrier

    def project(library, block, blocks, rows):
        block = block.reshape(-1, blocks * rows, tile_w)
        p = jnp.einsum("eb,bhw->hew", library, block, preferred_element_type=jnp.float32)
        return p.reshape(blocks, rows, count, tile_w)

    def rows_of(source, side, begin):
        rows = source[:, :, :, begin : begin + quarter]
        rows = jnp.where(side == 0, rows[:, 0], rows[:, 1])
        return jnp.transpose(rows, (1, 0, 2, 3)).reshape(bands, half * 2, tile_w)

    library_own = lax.dynamic_slice_in_dim(library_t, col * bands, bands, axis=1)
    library_pair = lax.dynamic_slice_in_dim(library_t, (col ^ 1) * bands, bands, axis=1)
    library_x = jnp.concatenate([library_own, library_pair], axis=1)
    split = [library_t[:, k * bands : (k + 1) * bands] for k in range(strips)]
    library_y = jnp.where(
        x == 0, jnp.concatenate(split[::2], axis=1), jnp.concatenate(split[1::2], axis=1)
    )

    by_y = cube.reshape(ys, 2, bands, tile_h, tile_w)
    early = jnp.transpose(by_y[..., :half, :], (0, 2, 1, 3, 4))
    early = early.reshape(ys, bands, 2 * half, tile_w)
    early, by_y = barrier((early, by_y))
    late = rows_of(by_y, 1 - x, 3 * quarter)
    late, by_y = barrier((late, by_y))
    third = rows_of(by_y, 1 - x, half)
    early = lax.all_to_all(
        early, "col", split_axis=0, concat_axis=0, axis_index_groups=columns, tiled=True
    )
    late = lax.ppermute(late, "col", swap)
    third, by_y, weight_h = barrier((third, by_y, weight_h))
    weights = heightened(raw_weights(weight_h, weight_v))
    late_own, third_own = rows_of(by_y, x, 3 * quarter), rows_of(by_y, x, half)
    order = [lax.bitwise_and(y + k, ys - 1) for k in range(1, ys)]

    def over_y(parts):
        return [lax.ppermute(p, "col", turns[k + 1]) for k, p in enumerate(parts)]

    third, late, weights = barrier((third, late, weights))
    third = lax.ppermute(third, "col", swap)
    late = project(library_x, jnp.concatenate([late_own, late], axis=0), ys, quarter)
    late_coded = coded(late, order)
    weights, _ = barrier((weights, late_coded))
    late_coded = over_y(late_coded)
    weights = widened(weights)
    early = project(library_y, early, 2, half)
    early_coded = coded(early, [1 - x])[0]
    third, late_coded, weights, _ = barrier((third, late_coded, weights, early_coded))
    early_coded = lax.ppermute(early_coded, "col", swap)
    third = project(library_x, jnp.concatenate([third_own, third], axis=0), ys, quarter)
    third_coded = coded(third, order)
    late_coded, _ = barrier((late_coded, third_coded))
    third_coded = over_y(third_coded)
    late, last = finished(late, y, late_coded, True)
    early, first = finished(early, x, [early_coded], False)
    top, bottom = neighbours("row", first, last)

    wh, wv = held_weights(weights, count, half)
    inv_hi = lax.reduce_precision(inverse, 8, 7)
    inv3 = jnp.concatenate([inv_hi, inverse - inv_hi, inv_hi], axis=1).astype(jnp.bfloat16)
    block = lax.broadcasted_iota(jnp.int32, (2 * count, 2 * count), 0) // count
    block = block == lax.broadcasted_iota(jnp.int32, (2 * count, 2 * count), 1) // count
    twice = jnp.where(block, jnp.tile(inverse.T, (2, 2)), 0.0)
    twice_hi = lax.reduce_precision(twice, 8, 7)
    inv3t = jnp.concatenate([twice_hi, twice - twice_hi, twice_hi], axis=0).astype(jnp.bfloat16)
    mixed, low, high = mix(y, inv3, early, late, third, third_coded, top, bottom)
    left, right = neighbours("col", low, high)
    return admm(inv3t, mixed, left, right, wh, wv)


def solution(mesh):
    return jax.shard_map(
        per_device,
        mesh=mesh,
        in_specs=(P(None, "col", "row", None), P(), P(), P("row", "col"), P("row", "col")),
        out_specs=P(None, "row", "col"),
        check_vma=False,
    )
```

time: 144 us -> 125 us (0.87); the launches traced: 142 us -> 124 us
  local copies, waits for them, and re-layouts: 29 us -> 20.6 us
  waiting for transfers between devices: 24.8 us -> 20.6 us
  other arithmetic: 12.2 us -> 9.14 us
  Pallas kernels: 21.9 us -> 19.5 us
    ppermute x3 -> x9, starting transfers between devices: 4.07 us -> 15.6 us  [the longest x6 11.7 us: over_y(): return [lax.ppermute(p, 'col', turns[k + 1]) for k, p in enumerate(parts)]]
    optimization_barrier x1 -> x3, local copies, waits for them, and re-layouts: 1.64 us -> 12.5 us  [the longest x1 10.2 us: per_device(): third, by_y, weight_h = barrier((third, by_y, weight_h))]
    all_to_all x3 -> x1, starting transfers between devices: 12.1 us -> 4.78 us  [per_device(): lax.all_to_all(early, 'col', split_axis=0, concat_axis=0, axis_index_grou...]
    transpose x6 -> x1, local copies, waits for them, and re-layouts: 7.29 us -> 0.07 us  [per_device(): twice = jnp.where(block, jnp.tile(inverse.T, (2, 2)), 0.0)]
    unnamed x48 -> x43, local copies, waits for them, and re-layouts: 10.2 us -> 3.67 us
    all_to_all x3 -> x1, waiting for transfers between devices: 6.02 us -> 0.01 us  [per_device(): lax.all_to_all(early, 'col', split_axis=0, concat_axis=0, axis_index_grou...]
    ppermute x4, waiting for transfers between devices: 3.68 us -> 8.94 us  [neighbours(): lax.ppermute(high_part, axis, forward)]
    ppermute x3 -> x9, waiting for transfers between devices: 6.38 us -> 1.49 us  [the longest x6 1.48 us: over_y(): return [lax.ppermute(p, 'col', turns[k + 1]) for k, p in enumerate(parts)]]
  transfers between devices with their start and end apart: 14 -> 18, of which waited for: 6 -> 6; matrix products, arithmetic and copies ran while one was open for 21% -> 26% of each run, Pallas kernels for 4% -> 3%
where the time goes in v4:
time: 125 us; the launch traced here: 124 us
  starting transfers between devices  46 us (37%)
  local copies, waits for them, and re-layouts  20.6 us (16%)
  waiting for transfers between devices  20.6 us (16%)
  Pallas kernels  19.5 us (16%)
  other arithmetic  9.14 us (7%)
  matrix products  7.97 us (6%)
    ppermute x4, starting transfers between devices, neighbours(): lax.ppermute(high_part, axis, forward)  17 us
    pallas_call x1, Pallas kernels, admm(): pl.pallas_call(admm_kernel, out_shape=jax.ShapeDtypeStruct((lanes // 2, 2...  13.3 us
    ppermute x6, starting transfers between devices, over_y(): return [lax.ppermute(p, 'col', turns[k + 1]) for k, p in enumerate(parts)]  11.7 us
    optimization_barrier x1, local copies, waits for them, and re-layouts, per_device(): third, by_y, weight_h = barrier((third, by_y, weight_h))  10.2 us
    ppermute x4, waiting for transfers between devices, neighbours(): lax.ppermute(low_part, axis, backward)  10.1 us
    ppermute x4, waiting for transfers between devices, neighbours(): lax.ppermute(high_part, axis, forward)  8.94 us
    ppermute x4, starting transfers between devices, neighbours(): lax.ppermute(low_part, axis, backward)  8.61 us
    dot_general x3, matrix products, project(): jnp.einsum('eb,bhw->hew', library, block, preferred_element_type=jnp.floa...  6.35 us
  transfers between devices with their start and end apart: 18, of which 6 were waited for; matrix products, arithmetic and copies ran while one was open for 26% of the time, Pallas kernels for 3%

profile of v4, /device:TPU:39, one launch (start us, length us, event | category | flops | bytes accessed | tf_op | source)
XLA Modules:
  0.0 124.2 jit_solution(9745656440973531474)
XLA Ops:
  0.0 2.3 %slice.112 = bf16[4,2,53,16,256]{4,3,2,1,0:T(8,128)(2,1)S(1)} slice(bf16[4,2,53,32,256]{4,3,2,1,0:T(8,128)(2,1)} %bitcast.75), slice={[0:4], [0:2], [0:53], [0:16], [0:256]} | slice | bytes 6946816 | tf_op jit(solution)/shard_map/slice | solution.py:309
  2.3 2.3 %copy.57 = bf16[4,2,53,16,256]{4,3,1,2,0:T(8,128)(2,1)} copy(bf16[4,2,53,16,256]{4,3,2,1,0:T(8,128)(2,1)S(1)} %slice.112) | data formatting | bytes 6946816
  4.6 4.8 %all-to-all-start = ((bf16[4,53,32,256]{3,2,1,0:T(8,128)(2,1)}), bf16[4,53,32,256]{3,2,1,0:T(8,128)(2,1)}, u32[]{:S(2)}, u32[]{:S(2)}) async-start(bf16[4,53,32,256]{3,2,1,0:T(8,128)(2,1)} %bitcast.79), calls=%async_computation | async-start | bytes 6946816 | tf_op jit(solution)/shard_map/all_to_all | solution.py:315
  9.4 1.7 %fusion.11 = bf16[53,32,256]{2,1,0:T(8,128)(2,1)S(1)} fusion(pred[]{:T(512)S(6)} %eq.19, bf16[4,2,53,32,256]{4,3,2,1,0:T(8,128)(2,1)} %bitcast.76), kind=kLoop, calls=%fused_computation.17 | loop fusion | flops 434176 | bytes 2605057 | tf_op jit(solution)/shard_map/reshape | solution.py:298
  11.1 1.2 collective-permute-start.1
  12.3 2.6 %fusion.10 = bf16[53,32,256]{2,1,0:T(8,128)(2,1)} fusion(pred[]{:T(512)S(6)} %eq.19, bf16[4,2,53,32,256]{4,3,2,1,0:T(8,128)(2,1)} %bitcast.77), kind=kLoop, calls=%fused_computation.15 | loop fusion | flops 434176 | bytes 2605057 | tf_op jit(solution)/shard_map/reshape | solution.py:298
  15.1 2.9 %collective-permute-start.3 = (bf16[2,4,256]{2,1,0:T(4,128)(2,1)S(1)}, bf16[2,4,256]{2,1,0:T(4,128)(2,1)S(1)}, u32[]{:S(2)}, u32[]{:S(2)}) collective-permute-start(bf16[2,4,256]{2,1,0:T(4,128)(2,1)S(1)} %get-tuple-element.88), channel_id=1, source_target_pairs={{8,0},{16,8},{24,16},{32,24},{40,32},{48,40},{56,48},{64,56},{72,6... | collective-permute-start | bytes 12296 | tf_op jit(solution)/shard_map/ppermute | solution.py:238
  18.0 3.6 %collective-permute-start.2 = (bf16[2,4,256]{2,1,0:T(4,128)(2,1)S(1)}, bf16[2,4,256]{2,1,0:T(4,128)(2,1)S(1)}, u32[]{:S(2)}, u32[]{:S(2)}) collective-permute-start(bf16[2,4,256]{2,1,0:T(4,128)(2,1)S(1)} %get-tuple-element.87), channel_id=1, source_target_pairs={{0,8},{8,16},{16,24},{24,32},{32,40},{40,48},{48,56},{56,64},{64,7... | collective-permute-start | bytes 12296 | tf_op jit(solution)/shard_map/ppermute | solution.py:238
  21.7 0.1 tile.10
  21.8 10.2 %copy.49 = bf16[4,2,53,32,256]{4,2,3,0,1:T(8,128)(2,1)} copy(bf16[4,2,53,32,256]{4,3,2,1,0:T(8,128)(2,1)} %bitcast.78) | data formatting | bytes 13893632 | tf_op jit(solution)/shard_map/optimization_barrier | solution.py:319
  32.1 0.8 fusion.12
  33.0 3.1 %slice_select_fusion = (bf16[4,1,53,8,256]{4,2,3,0,1:T(8,128)(2,1)}, bf16[4,1,53,8,256]{4,2,3,0,1:T(8,128)(2,1)S(1)}) fusion(bf16[4,2,53,32,256]{4,2,3,0,1:T(8,128)(2,1)} %copy.49, pred[]{:T(512)S(6)} %eq.18), kind=kLoop, calls=%fused_computation.12 | loop fusion | flops 868352 | bytes 5210113 | tf_op jit(solution)/shard_map/jit(_where)/select_n | solution.py:297
  36.3 0.5 copy.51
  36.8 2.6 %collective-permute-start.4 = (bf16[53,32,256]{2,1,0:T(8,128)(2,1)}, bf16[53,32,256]{2,1,0:T(8,128)(2,1)}, u32[]{:S(2)}, u32[]{:S(2)}) collective-permute-start(bf16[53,32,256]{2,1,0:T(8,128)(2,1)} %fusion.10), channel_id=1, source_target_pairs={{0,1},{1,0},{2,3},{3,2},{4,5},{5,4},{6,7},{7,6},{8,9},{9,8},{10,11... | collective-permute-start | bytes 2605064 | tf_op jit(solution)/shard_map/ppermute | solution.py:328
  39.5 0.5 fusion.2
  40.0 1.6 %shard_map.57 = (s16[528,256]{1,0:T(8,128)(2,1)}, s16[528,256]{1,0:T(8,128)(2,1)}, s16[528,256]{1,0:T(8,128)(2,1)}) custom-call(s32[3]{0:T(128)S(1)} %pad_add_fusion.which_ref, f32[4,8,64,256]{3,2,1,0:T(8,128)S(1)} %bitcast.71), custom_call_target="tpu_custom_call" | custom-call | tf_op jit(solution)/shard_map/pallas_call | solution.py:46
  41.6 1.3 %copy-done = f32[32,256,64]{1,2,0:T(8,128)} copy-done((f32[32,256,64]{1,2,0:T(8,128)}, f32[32,256,64]{1,2,0:T(8,128)S(1)}, u32[]{:S(2)}) %copy-start) | copy-done | bytes 2097176
  43.0 3.4 %collective-permute-start.8 = (bf16[2,40,4]{2,1,0:T(8,128)(2,1)S(1)}, bf16[2,40,4]{2,1,0:T(8,128)(2,1)S(1)}, u32[]{:S(2)}, u32[]{:S(2)}) collective-permute-start(bf16[2,40,4]{2,1,0:T(8,128)(2,1)S(1)} %get-tuple-element.86), channel_id=1, source_target_pairs={{0,1},{1,2},{2,3},{3,4},{4,5},{5,6},{6,7},{8,9},{9,10},{10,11},{11... | collective-permute-start | bytes 1928 | tf_op jit(solution)/shard_map/ppermute | solution.py:238
  46.4 1.3 %collective-permute-start.5 = (s16[528,256]{1,0:T(8,128)(2,1)}, s16[528,256]{1,0:T(8,128)(2,1)S(1)}, u32[]{:S(2)}, u32[]{:S(2)}) collective-permute-start(s16[528,256]{1,0:T(8,128)(2,1)} %get-tuple-element.47), channel_id=1, source_target_pairs={{0,2},{1,3},{2,4},{3,5},{4,6},{5,7},{6,0},{7,1},{8,10},{9,11},{10,... | collective-permute-start | bytes 811016 | tf_op jit(solution)/shard_map/ppermute | solution.py:325
  47.7 1.4 %collective-permute-start.6 = (s16[528,256]{1,0:T(8,128)(2,1)}, s16[528,256]{1,0:T(8,128)(2,1)}, u32[]{:S(2)}, u32[]{:S(2)}) collective-permute-start(s16[528,256]{1,0:T(8,128)(2,1)} %get-tuple-element.48), channel_id=1, source_target_pairs={{0,4},{1,5},{2,6},{3,7},{4,0},{5,1},{6,2},{7,3},{8,12},{9,13},{10,... | collective-permute-start | bytes 811016 | tf_op jit(solution)/shard_map/ppermute | solution.py:325
  49.0 2.0 %collective-permute-start.7 = (s16[528,256]{1,0:T(8,128)(2,1)}, s16[528,256]{1,0:T(8,128)(2,1)}, u32[]{:S(2)}, u32[]{:S(2)}) collective-permute-start(s16[528,256]{1,0:T(8,128)(2,1)} %get-tuple-element.49), channel_id=1, source_target_pairs={{0,6},{1,7},{2,0},{3,1},{4,2},{5,3},{6,4},{7,5},{8,14},{9,15},{10,... | collective-permute-start | bytes 811016 | tf_op jit(solution)/shard_map/ppermute | solution.py:325
  51.0 8.8 %collective-permute-done.8 = bf16[2,40,4]{2,1,0:T(8,128)(2,1)S(1)} collective-permute-done((bf16[2,40,4]{2,1,0:T(8,128)(2,1)S(1)}, bf16[2,40,4]{2,1,0:T(8,128)(2,1)S(1)}, u32[]{:S(2)}, u32[]{:S(2)}) %collective-permute-start.8) | collective-permute-done | bytes 672 | tf_op jit(solution)/shard_map/ppermute | solution.py:238
  59.8 1.9 %collective-permute-start.9 = (bf16[2,40,4]{2,1,0:T(8,128)(2,1)S(1)}, bf16[2,40,4]{2,1,0:T(8,128)(2,1)S(1)}, u32[]{:S(2)}, u32[]{:S(2)}) collective-permute-start(bf16[2,40,4]{2,1,0:T(8,128)(2,1)S(1)} %get-tuple-element.85), channel_id=1, source_target_pairs={{1,0},{2,1},{3,2},{4,3},{5,4},{6,5},{7,6},{9,8},{10,9},{11,10},{12... | collective-permute-start | bytes 1928 | tf_op jit(solution)/shard_map/ppermute | solution.py:238
  61.7 4.2 %fusion = f32[32,256,64]{1,2,0:T(8,128)S(1)} fusion(bf16[212,32,256]{2,1,0:T(8,128)(2,1)} %bitcast.6, bf16[64,53]{1,0:T(8,128)(2,1)S(1)} %get-tuple-element.78, bf16[64,53]{1,0:T(8,128)(2,1)S(1)} %get-tuple-element.79, bf16[64,53]{1,0:T(8,128)(2,1)S(1)} %get-tuple-element.80, bf16[64,53]{1,0:T(8,128)(2,1)S(1)} %get-tuple-element.81, ...), kind=kOutput, calls=%fused_computation | convolution fusion | flops 222528768 | bytes 5624833 | tf_op jit(solution)/shard_map/eb,bhw->hew/dot_general | solution.py:292
  65.9 0.2 shard_map.55
  66.1 1.0 collective-permute-done.9
  67.1 0.7 pad_maximum_fusion.3.inv_ref
  67.8 1.5 %concatenate.36 = bf16[2,40,288]{2,1,0:T(8,128)(2,1)} concatenate(bf16[2,40,12]{2,1,0:T(8,128)(2,1)S(1)} %broadcast.90, bf16[2,40,4]{2,1,0:T(8,128)(2,1)} %copy-done.13, bf16[2,40,256]{2,1,0:T(8,128)(2,1)} %copy-done.4, bf16[2,40,4]{2,1,0:T(8,128)(2,1)} %copy-done.14, bf16[2,40,12]{2,1,0:T(8,128)(2,1)S(1)} %broadcast.90), dimensions={2} | concatenate | bytes 92160 | tf_op jit(solution)/shard_map/concatenate | solution.py:263
  69.4 1.8 %copy.54 = bf16[53,32,256]{2,0,1:T(8,128)(2,1)S(1)} copy(bf16[53,32,256]{2,1,0:T(8,128)(2,1)} %collective-permute-done.4) | data formatting | bytes 1736704 | tf_op jit(solution)/shard_map/optimization_barrier | solution.py:336
  71.2 1.7 %fusion.6 = f32[32,256,64]{1,2,0:T(8,128)S(1)} fusion(bf16[53,32,256]{2,0,1:T(8,128)(2,1)S(1)} %copy.54, bf16[53,32,256]{2,0,1:T(8,128)(2,1)} %bitcast.80, bf16[64,53]{1,0:T(8,128)(2,1)} %copy-done.7, bf16[64,53]{1,0:T(8,128)(2,1)} %copy-done.6), kind=kOutput, calls=%fused_computation.8 | convolution fusion | flops 114649600 | bytes 3847424 | tf_op jit(solution)/shard_map/eb,bhw->hew/dot_general | solution.py:292
  72.9 0.8 shard_map.58
  73.7 3.5 %collective-permute-start.10 = (s16[528,256]{1,0:T(8,128)(2,1)S(1)}, s16[528,256]{1,0:T(8,128)(2,1)S(1)}, u32[]{:S(2)}, u32[]{:S(2)}) collective-permute-start(s16[528,256]{1,0:T(8,128)(2,1)S(1)} %get-tuple-element.56), channel_id=1, source_target_pairs={{0,2},{1,3},{2,4},{3,5},{4,6},{5,7},{6,0},{7,1},{8,10},{9,11},{10,... | collective-permute-start | bytes 811016 | tf_op jit(solution)/shard_map/ppermute | solution.py:325
  77.2 2.8 %collective-permute-start.11 = (s16[528,256]{1,0:T(8,128)(2,1)S(1)}, s16[528,256]{1,0:T(8,128)(2,1)S(1)}, u32[]{:S(2)}, u32[]{:S(2)}) collective-permute-start(s16[528,256]{1,0:T(8,128)(2,1)S(1)} %get-tuple-element.57), channel_id=1, source_target_pairs={{0,4},{1,5},{2,6},{3,7},{4,0},{5,1},{6,2},{7,3},{8,12},{9,13},{10,... | collective-permute-start | bytes 811016 | tf_op jit(solution)/shard_map/ppermute | solution.py:325
  80.0 0.9 collective-permute-start.12
  80.9 1.3 %shard_map.59 = (f32[8,64,256]{2,1,0:T(8,128)S(1)}, f32[4,64,256]{2,1,0:T(8,128)S(1)}) custom-call(s32[1]{0:T(128)} %bitcast.1.which_ref, f32[4,8,64,256]{3,2,1,0:T(8,128)S(1)} %bitcast.72, s16[528,256]{1,0:T(8,128)(2,1)S(1)} %collective-permute-done.5.refs_0_, s16[528,256]{1,0:T(8,128)(2,1)} %collective-permute-done.6.refs_1_, ...), custom_call_target="tpu_custom_call" | custom-call | tf_op jit(solution)/shard_map/pallas_call | solution.py:84
  82.2 4.5 %collective-permute-start.13 = (f32[4,64,256]{2,1,0:T(8,128)S(1)}, f32[4,64,256]{2,1,0:T(8,128)S(1)}, u32[]{:S(2)}, u32[]{:S(2)}) collective-permute-start(f32[4,64,256]{2,1,0:T(8,128)S(1)} %get-tuple-element.63), channel_id=1, source_target_pairs={{0,8},{8,16},{16,24},{24,32},{32,40},{40,48},{48,56},{56,64},{64,7... | collective-permute-start | bytes 786440 | tf_op jit(solution)/shard_map/ppermute | solution.py:238
  86.8 0.2 shard_map.56
  87.0 1.9 %collective-permute-start.14 = (f32[4,64,256]{2,1,0:T(8,128)S(1)}, f32[4,64,256]{2,1,0:T(8,128)S(1)}, u32[]{:S(2)}, u32[]{:S(2)}) collective-permute-start(f32[4,64,256]{2,1,0:T(8,128)S(1)} %get-tuple-element.64), channel_id=1, source_target_pairs={{8,0},{16,8},{24,16},{32,24},{40,32},{48,40},{56,48},{64,56},{72,6... | collective-permute-start | bytes 786440 | tf_op jit(solution)/shard_map/ppermute | solution.py:238
  89.0 0.8 convolution_multiply_fusion.1.wh_ref
  89.8 0.2 collective-permute-done.13.top_ref
  90.0 1.5 %collective-permute-done.11.b_ref = s16[528,256]{1,0:T(8,128)(2,1)S(1)} collective-permute-done((s16[528,256]{1,0:T(8,128)(2,1)S(1)}, s16[528,256]{1,0:T(8,128)(2,1)S(1)}, u32[]{:S(2)}, u32[]{:S(2)}) %collective-permute-start.11) | collective-permute-done | bytes 270368 | tf_op jit(solution)/shard_map/ppermute | solution.py:325
  91.4 4.2 %collective-permute-done.14.bottom_ref = f32[4,64,256]{2,1,0:T(8,128)S(1)} collective-permute-done((f32[4,64,256]{2,1,0:T(8,128)S(1)}, f32[4,64,256]{2,1,0:T(8,128)S(1)}, u32[]{:S(2)}, u32[]{:S(2)}) %collective-permute-start.14) | collective-permute-done | bytes 262176 | tf_op jit(solution)/shard_map/ppermute | solution.py:238
  95.6 2.1 %shard_map.60 = (f32[24,256,128]{2,1,0:T(8,128)S(1)}, f32[24,8,128]{2,1,0:T(8,128)S(1)}, f32[24,8,128]{2,1,0:T(8,128)S(1)}) custom-call(s32[1]{0:T(128)} %bitcast.1.which_ref, bf16[64,192]{1,0:T(8,128)(2,1)S(1)} %copy-done.2, f32[16,64,256]{2,1,0:T(8,128)S(1)} %get-tuple-element.38.early_ref, f32[8,64,256]{2,1,0:T(8,128)S(1)} %get-tuple-element.62.late_ref, ...), custom_call_target="tpu_custom_call" | custom-call | tf_op jit(solution)/shard_map/pallas_call | solution.py:140
  97.7 5.5 %collective-permute-start.15 = (f32[24,8,128]{2,1,0:T(8,128)S(1)}, f32[24,8,128]{2,1,0:T(8,128)S(1)}, u32[]{:S(2)}, u32[]{:S(2)}) collective-permute-start(f32[24,8,128]{2,1,0:T(8,128)S(1)} %get-tuple-element.66), channel_id=1, source_target_pairs={{0,1},{1,2},{2,3},{3,4},{4,5},{5,6},{6,7},{8,9},{9,10},{10,11},{11... | collective-permute-start | bytes 294920 | tf_op jit(solution)/shard_map/ppermute | solution.py:238
  103.2 1.9 %collective-permute-start.16 = (f32[24,8,128]{2,1,0:T(8,128)S(1)}, f32[24,8,128]{2,1,0:T(8,128)S(1)}, u32[]{:S(2)}, u32[]{:S(2)}) collective-permute-start(f32[24,8,128]{2,1,0:T(8,128)S(1)} %get-tuple-element.67), channel_id=1, source_target_pairs={{1,0},{2,1},{3,2},{4,3},{5,4},{6,5},{7,6},{9,8},{10,9},{11,10},{12... | collective-permute-start | bytes 294920 | tf_op jit(solution)/shard_map/ppermute | solution.py:238
  105.1 0.8 convolution_multiply_fusion.wv_ref
  105.9 5.0 %collective-permute-done.16.right_ref = f32[24,8,128]{2,1,0:T(8,128)S(1)} collective-permute-done((f32[24,8,128]{2,1,0:T(8,128)S(1)}, f32[24,8,128]{2,1,0:T(8,128)S(1)}, u32[]{:S(2)}, u32[]{:S(2)}) %collective-permute-start.16) | collective-permute-done | bytes 98336 | tf_op jit(solution)/shard_map/ppermute | solution.py:238
  110.9 13.3 %shard_map.61 = f32[64,32,256]{2,1,0:T(8,128)} custom-call(bf16[384,128]{1,0:T(8,128)(2,1)S(1)} %pad_maximum_fusion.invt_ref, f32[24,256,128]{2,1,0:T(8,128)S(1)} %get-tuple-element.65.mixed_ref, f32[24,8,128]{2,1,0:T(8,128)S(1)} %collective-permute-done.15.left_ref, f32[24,8,128]{2,1,0:T(8,128)S(1)} %collective-permute-done.16.right_ref, ...), custom_call_target="tpu_custom_call" | custom-call | tf_op jit(solution)/shard_map/pallas_call | solution.py:219
  (72 shorter events, 0.8 us)
Async XLA Ops:
  4.6 57.1 %all-to-all-start = ((bf16[4,53,32,256]{3,2,1,0:T(8,128)(2,1)}), bf16[4,53,32,256]{3,2,1,0:T(8,128)(2,1)}, u32[]{:S(2)}, u32[]{:S(2)}) async-start(bf16[4,53,32,256]{3,2,1,0:T(8,128)(2,1)} %bitcast.79), calls=%async_computation | async-start | bytes 6946816 | tf_op jit(solution)/shard_map/all_to_all | solution.py:315
  9.4 5.6 %copy-start.11 = (s32[32,256]{1,0:T(8,128)S(1)}, s32[32,256]{1,0:T(8,128)}, u32[]{:S(2)}) copy-start(s32[32,256]{1,0:T(8,128)} %param.8) | copy-start | bytes 98308
  9.4 5.6 %copy-start.12 = (s32[32,256]{1,0:T(8,128)S(1)}, s32[32,256]{1,0:T(8,128)}, u32[]{:S(2)}) copy-start(s32[32,256]{1,0:T(8,128)} %param.9) | copy-start | bytes 98308
  9.4 12.2 %copy-start.8 = (f32[64,64]{1,0:T(8,128)S(1)}, f32[64,64]{1,0:T(8,128)}, u32[]{:S(2)}) copy-start(f32[64,64]{1,0:T(8,128)} %param.7) | copy-start | bytes 49156
  11.1 25.2 %collective-permute-start.1 = (bf16[53,32,256]{2,1,0:T(8,128)(2,1)S(1)}, bf16[53,32,256]{2,1,0:T(8,128)(2,1)S(1)}, u32[]{:S(2)}, u32[]{:S(2)}) collective-permute-start(bf16[53,32,256]{2,1,0:T(8,128)(2,1)S(1)} %fusion.11), channel_id=1, source_target_pairs={{0,1},{1,0},{2,3},{3,2},{4,5},{5,4},{6,7},{7,6},{8,9},{9,8},{10,11... | collective-permute-start | bytes 2605064 | tf_op jit(solution)/shard_map/ppermute | solution.py:318
  15.1 21.2 %collective-permute-start.3 = (bf16[2,4,256]{2,1,0:T(4,128)(2,1)S(1)}, bf16[2,4,256]{2,1,0:T(4,128)(2,1)S(1)}, u32[]{:S(2)}, u32[]{:S(2)}) collective-permute-start(bf16[2,4,256]{2,1,0:T(4,128)(2,1)S(1)} %get-tuple-element.88), channel_id=1, source_target_pairs={{8,0},{16,8},{24,16},{32,24},{40,32},{48,40},{56,48},{64,56},{72,6... | collective-permute-start | bytes 12296 | tf_op jit(solution)/shard_map/ppermute | solution.py:238
  18.0 18.3 %collective-permute-start.2 = (bf16[2,4,256]{2,1,0:T(4,128)(2,1)S(1)}, bf16[2,4,256]{2,1,0:T(4,128)(2,1)S(1)}, u32[]{:S(2)}, u32[]{:S(2)}) collective-permute-start(bf16[2,4,256]{2,1,0:T(4,128)(2,1)S(1)} %get-tuple-element.87), channel_id=1, source_target_pairs={{0,8},{8,16},{16,24},{24,32},{32,40},{40,48},{48,56},{56,64},{64,7... | collective-permute-start | bytes 12296 | tf_op jit(solution)/shard_map/ppermute | solution.py:238
  21.8 11.0 %copy-start.3 = (bf16[64,424]{1,0:T(8,128)(2,1)S(1)}, bf16[64,424]{1,0:T(8,128)(2,1)}, u32[]{:S(2)}) copy-start(bf16[64,424]{1,0:T(8,128)(2,1)} %param.6) | copy-start | bytes 162820
  32.1 4.7 %copy-start.15 = (pred[128]{0:T(512)(128)(4,1)}, pred[128]{0:T(512)(128)(4,1)S(1)}, u32[]{:S(2)}) copy-start(pred[128]{0:T(512)(128)(4,1)S(1)} %compare_and_fusion) | copy-start | bytes 388
  32.1 4.7 %copy-start.17 = (s32[128]{0:T(128)}, s32[128]{0:T(128)S(1)}, u32[]{:S(2)}) copy-start(s32[128]{0:T(128)S(1)} %get-tuple-element.93) | copy-start | bytes 1540
  32.1 4.7 %copy-start.19 = (s32[128]{0:T(128)}, s32[128]{0:T(128)S(1)}, u32[]{:S(2)}) copy-start(s32[128]{0:T(128)S(1)} %get-tuple-element.94) | copy-start | bytes 1540
  33.0 6.5 %copy-start.6 = (bf16[64,53]{1,0:T(8,128)(2,1)}, bf16[64,53]{1,0:T(8,128)(2,1)S(1)}, u32[]{:S(2)}) copy-start(bf16[64,53]{1,0:T(8,128)(2,1)S(1)} %get-tuple-element.73) | copy-start | bytes 20356
  33.0 6.5 %copy-start.7 = (bf16[64,53]{1,0:T(8,128)(2,1)}, bf16[64,53]{1,0:T(8,128)(2,1)S(1)}, u32[]{:S(2)}) copy-start(bf16[64,53]{1,0:T(8,128)(2,1)S(1)} %get-tuple-element.82) | copy-start | bytes 20356
  36.3 6.6 %copy-start.4 = (bf16[2,40,256]{2,1,0:T(8,128)(2,1)}, bf16[2,40,256]{2,1,0:T(8,128)(2,1)S(1)}, u32[]{:S(2)}) copy-start(bf16[2,40,256]{2,1,0:T(8,128)(2,1)S(1)} %pad_maximum_fusion.1) | copy-start | bytes 122884
  36.8 32.6 %collective-permute-start.4 = (bf16[53,32,256]{2,1,0:T(8,128)(2,1)}, bf16[53,32,256]{2,1,0:T(8,128)(2,1)}, u32[]{:S(2)}, u32[]{:S(2)}) collective-permute-start(bf16[53,32,256]{2,1,0:T(8,128)(2,1)} %fusion.10), channel_id=1, source_target_pairs={{0,1},{1,0},{2,3},{3,2},{4,5},{5,4},{6,7},{7,6},{8,9},{9,8},{10,11... | collective-permute-start | bytes 2605064 | tf_op jit(solution)/shard_map/ppermute | solution.py:328
  41.6 1.3 %copy-start = (f32[32,256,64]{1,2,0:T(8,128)}, f32[32,256,64]{1,2,0:T(8,128)S(1)}, u32[]{:S(2)}) copy-start(f32[32,256,64]{1,2,0:T(8,128)S(1)} %fusion.2) | copy-start | bytes 6291460
  43.0 16.8 %collective-permute-start.8 = (bf16[2,40,4]{2,1,0:T(8,128)(2,1)S(1)}, bf16[2,40,4]{2,1,0:T(8,128)(2,1)S(1)}, u32[]{:S(2)}, u32[]{:S(2)}) collective-permute-start(bf16[2,40,4]{2,1,0:T(8,128)(2,1)S(1)} %get-tuple-element.86), channel_id=1, source_target_pairs={{0,1},{1,2},{2,3},{3,4},{4,5},{5,6},{6,7},{8,9},{9,10},{10,11},{11... | collective-permute-start | bytes 1928 | tf_op jit(solution)/shard_map/ppermute | solution.py:238
  46.4 22.9 %collective-permute-start.5 = (s16[528,256]{1,0:T(8,128)(2,1)}, s16[528,256]{1,0:T(8,128)(2,1)S(1)}, u32[]{:S(2)}, u32[]{:S(2)}) collective-permute-start(s16[528,256]{1,0:T(8,128)(2,1)} %get-tuple-element.47), channel_id=1, source_target_pairs={{0,2},{1,3},{2,4},{3,5},{4,6},{5,7},{6,0},{7,1},{8,10},{9,11},{10,... | collective-permute-start | bytes 811016 | tf_op jit(solution)/shard_map/ppermute | solution.py:325
  47.7 21.7 %collective-permute-start.6 = (s16[528,256]{1,0:T(8,128)(2,1)}, s16[528,256]{1,0:T(8,128)(2,1)}, u32[]{:S(2)}, u32[]{:S(2)}) collective-permute-start(s16[528,256]{1,0:T(8,128)(2,1)} %get-tuple-element.48), channel_id=1, source_target_pairs={{0,4},{1,5},{2,6},{3,7},{4,0},{5,1},{6,2},{7,3},{8,12},{9,13},{10,... | collective-permute-start | bytes 811016 | tf_op jit(solution)/shard_map/ppermute | solution.py:325
  49.0 20.3 %collective-permute-start.7 = (s16[528,256]{1,0:T(8,128)(2,1)}, s16[528,256]{1,0:T(8,128)(2,1)}, u32[]{:S(2)}, u32[]{:S(2)}) collective-permute-start(s16[528,256]{1,0:T(8,128)(2,1)} %get-tuple-element.49), channel_id=1, source_target_pairs={{0,6},{1,7},{2,0},{3,1},{4,2},{5,3},{6,4},{7,5},{8,14},{9,15},{10,... | collective-permute-start | bytes 811016 | tf_op jit(solution)/shard_map/ppermute | solution.py:325
  59.8 6.4 %copy-start.13 = (bf16[2,40,4]{2,1,0:T(8,128)(2,1)}, bf16[2,40,4]{2,1,0:T(8,128)(2,1)S(1)}, u32[]{:S(2)}) copy-start(bf16[2,40,4]{2,1,0:T(8,128)(2,1)S(1)} %collective-permute-done.8) | copy-start | bytes 1924
  59.8 7.4 %collective-permute-start.9 = (bf16[2,40,4]{2,1,0:T(8,128)(2,1)S(1)}, bf16[2,40,4]{2,1,0:T(8,128)(2,1)S(1)}, u32[]{:S(2)}, u32[]{:S(2)}) collective-permute-start(bf16[2,40,4]{2,1,0:T(8,128)(2,1)S(1)} %get-tuple-element.85), channel_id=1, source_target_pairs={{1,0},{2,1},{3,2},{4,3},{5,4},{6,5},{7,6},{9,8},{10,9},{11,10},{12... | collective-permute-start | bytes 1928 | tf_op jit(solution)/shard_map/ppermute | solution.py:238
  61.7 6.1 %copy-start.9 = (bf16[128,128]{1,0:T(8,128)(2,1)S(1)}, bf16[128,128]{1,0:T(8,128)(2,1)}, u32[]{:S(2)}) copy-start(bf16[128,128]{1,0:T(8,128)(2,1)} %get-tuple-element.71) | copy-start | bytes 98308
  61.7 6.1 %copy-start.10 = (bf16[128,128]{1,0:T(8,128)(2,1)S(1)}, bf16[128,128]{1,0:T(8,128)(2,1)}, u32[]{:S(2)}) copy-start(bf16[128,128]{1,0:T(8,128)(2,1)} %get-tuple-element.72) | copy-start | bytes 98308
  67.1 0.7 copy-start.14
  67.1 19.7 %collective-permute-start = (s16[1040,256]{1,0:T(8,128)(2,1)S(1)}, s16[1040,256]{1,0:T(8,128)(2,1)S(1)}, u32[]{:S(2)}, u32[]{:S(2)}) collective-permute-start(s16[1040,256]{1,0:T(8,128)(2,1)S(1)} %shard_map.55), channel_id=1, source_target_pairs={{0,1},{1,0},{2,3},{3,2},{4,5},{5,4},{6,7},{7,6},{8,9},{9,8},{10,11... | collective-permute-start | bytes 1597448 | tf_op jit(solution)/shard_map/ppermute | solution.py:337
  69.4 11.5 %copy-start.1 = (f32[32,256,64]{1,2,0:T(8,128)S(1)}, f32[32,256,64]{1,2,0:T(8,128)}, u32[]{:S(2)}) copy-start(f32[32,256,64]{1,2,0:T(8,128)} %copy-done) | copy-start | bytes 6291460
  71.2 15.5 %copy-start.5 = (bf16[2,40,288]{2,1,0:T(8,128)(2,1)S(1)}, bf16[2,40,288]{2,1,0:T(8,128)(2,1)}, u32[]{:S(2)}) copy-start(bf16[2,40,288]{2,1,0:T(8,128)(2,1)} %concatenate.36) | copy-start | bytes 138244
  72.9 16.1 %copy-start.16 = (pred[128]{0:T(512)(128)(4,1)S(1)}, pred[128]{0:T(512)(128)(4,1)}, u32[]{:S(2)}) copy-start(pred[128]{0:T(512)(128)(4,1)} %copy-done.15) | copy-start | bytes 388
  72.9 16.1 %copy-start.18 = (s32[128]{0:T(128)S(1)}, s32[128]{0:T(128)}, u32[]{:S(2)}) copy-start(s32[128]{0:T(128)} %copy-done.17) | copy-start | bytes 1540
  72.9 16.1 %copy-start.20 = (s32[128]{0:T(128)S(1)}, s32[128]{0:T(128)}, u32[]{:S(2)}) copy-start(s32[128]{0:T(128)} %copy-done.19) | copy-start | bytes 1540
  73.7 16.2 %collective-permute-start.10 = (s16[528,256]{1,0:T(8,128)(2,1)S(1)}, s16[528,256]{1,0:T(8,128)(2,1)S(1)}, u32[]{:S(2)}, u32[]{:S(2)}) collective-permute-start(s16[528,256]{1,0:T(8,128)(2,1)S(1)} %get-tuple-element.56), channel_id=1, source_target_pairs={{0,2},{1,3},{2,4},{3,5},{4,6},{5,7},{6,0},{7,1},{8,10},{9,11},{10,... | collective-permute-start | bytes 811016 | tf_op jit(solution)/shard_map/ppermute | solution.py:325
  77.2 14.2 %collective-permute-start.11 = (s16[528,256]{1,0:T(8,128)(2,1)S(1)}, s16[528,256]{1,0:T(8,128)(2,1)S(1)}, u32[]{:S(2)}, u32[]{:S(2)}) collective-permute-start(s16[528,256]{1,0:T(8,128)(2,1)S(1)} %get-tuple-element.57), channel_id=1, source_target_pairs={{0,4},{1,5},{2,6},{3,7},{4,0},{5,1},{6,2},{7,3},{8,12},{9,13},{10,... | collective-permute-start | bytes 811016 | tf_op jit(solution)/shard_map/ppermute | solution.py:325
  80.0 11.4 %collective-permute-start.12 = (s16[528,256]{1,0:T(8,128)(2,1)S(1)}, s16[528,256]{1,0:T(8,128)(2,1)S(1)}, u32[]{:S(2)}, u32[]{:S(2)}) collective-permute-start(s16[528,256]{1,0:T(8,128)(2,1)S(1)} %get-tuple-element.58), channel_id=1, source_target_pairs={{0,6},{1,7},{2,0},{3,1},{4,2},{5,3},{6,4},{7,5},{8,14},{9,15},{10,... | collective-permute-start | bytes 811016 | tf_op jit(solution)/shard_map/ppermute | solution.py:325
  82.1 13.4 %copy-start.2 = (bf16[64,192]{1,0:T(8,128)(2,1)S(1)}, bf16[64,192]{1,0:T(8,128)(2,1)}, u32[]{:S(2)}) copy-start(bf16[64,192]{1,0:T(8,128)(2,1)} %pad_maximum_fusion.3.inv_ref) | copy-start | bytes 73732
  82.2 7.8 %collective-permute-start.13 = (f32[4,64,256]{2,1,0:T(8,128)S(1)}, f32[4,64,256]{2,1,0:T(8,128)S(1)}, u32[]{:S(2)}, u32[]{:S(2)}) collective-permute-start(f32[4,64,256]{2,1,0:T(8,128)S(1)} %get-tuple-element.63), channel_id=1, source_target_pairs={{0,8},{8,16},{16,24},{24,32},{32,40},{40,48},{48,56},{56,64},{64,7... | collective-permute-start | bytes 786440 | tf_op jit(solution)/shard_map/ppermute | solution.py:238
  87.0 8.6 %collective-permute-start.14 = (f32[4,64,256]{2,1,0:T(8,128)S(1)}, f32[4,64,256]{2,1,0:T(8,128)S(1)}, u32[]{:S(2)}, u32[]{:S(2)}) collective-permute-start(f32[4,64,256]{2,1,0:T(8,128)S(1)} %get-tuple-element.64), channel_id=1, source_target_pairs={{8,0},{16,8},{24,16},{32,24},{40,32},{48,40},{56,48},{64,56},{72,6... | collective-permute-start | bytes 786440 | tf_op jit(solution)/shard_map/ppermute | solution.py:238
  97.7 8.2 %collective-permute-start.15 = (f32[24,8,128]{2,1,0:T(8,128)S(1)}, f32[24,8,128]{2,1,0:T(8,128)S(1)}, u32[]{:S(2)}, u32[]{:S(2)}) collective-permute-start(f32[24,8,128]{2,1,0:T(8,128)S(1)} %get-tuple-element.66), channel_id=1, source_target_pairs={{0,1},{1,2},{2,3},{3,4},{4,5},{5,6},{6,7},{8,9},{9,10},{10,11},{11... | collective-permute-start | bytes 294920 | tf_op jit(solution)/shard_map/ppermute | solution.py:238
  103.2 7.8 %collective-permute-start.16 = (f32[24,8,128]{2,1,0:T(8,128)S(1)}, f32[24,8,128]{2,1,0:T(8,128)S(1)}, u32[]{:S(2)}, u32[]{:S(2)}) collective-permute-start(f32[24,8,128]{2,1,0:T(8,128)S(1)} %get-tuple-element.67), channel_id=1, source_target_pairs={{1,0},{2,1},{3,2},{4,3},{5,4},{6,5},{7,6},{9,8},{10,9},{11,10},{12... | collective-permute-start | bytes 294920 | tf_op jit(solution)/shard_map/ppermute | solution.py:238

commit v5 on v4

--- a/solution.py
+++ b/solution.py
@@ -91,6 +91,12 @@
     )(jnp.reshape(which, (1,)), own, *parts)
 
 
+def clear_sides(ref):
+    for r in range(ref.shape[0]):
+        ref[r, :LEAD] = jnp.zeros((LEAD, ref.shape[2]), jnp.float32)
+        ref[r, SPAN - LEAD :] = jnp.zeros((LEAD, ref.shape[2]), jnp.float32)
+
+
 def mix_kernel(
     which_ref, inv_ref, early_ref, late_ref, own_ref, a_ref, b_ref, c_ref, top_ref, bottom_ref,
     mixed_ref, low_ref, high_ref, scale,
@@ -102,6 +108,7 @@
     parts = (a_ref, b_ref, c_ref)
     for s, ref in enumerate(parts):
         scale[s] = scales(ref[quarter * count :])
+    clear_sides(mixed_ref)
 
     def third(r):
         x = own_ref[which_ref[0], r]
@@ -116,7 +123,7 @@
             a = m[:, 2 * k * width : (2 * k + 1) * width]
             b = m[:, (2 * k + 1) * width : (2 * k + 2) * width]
             turned = jnp.transpose(jnp.concatenate([a, b], 0))
-            mixed_ref[slot + k] = turned
+            mixed_ref[slot + k, LEAD : LEAD + width] = turned
             low_ref[slot + k] = turned[:8]
             high_ref[slot + k] = turned[width - 8 :]
 
@@ -136,7 +143,7 @@
     half, count, width = early.shape
     deep = half + 2 * HALO
     vmem = pl.BlockSpec(memory_space=pltpu.VMEM)
-    shapes = [(deep, width, 2 * count), (deep, 8, 2 * count), (deep, 8, 2 * count)]
+    shapes = [(deep, SPAN, 2 * count), (deep, 8, 2 * count), (deep, 8, 2 * count)]
     return pl.pallas_call(
         mix_kernel,
         out_shape=[jax.ShapeDtypeStruct(x, jnp.float32) for x in shapes],
@@ -147,56 +154,110 @@
     )(jnp.reshape(which, (1,)), inv3, early, late, own, *parts, top, bottom)
 
 
-def admm_kernel(
-    invt_ref, mixed_ref, left_ref, right_ref, wh_ref, wv_ref, out_ref, mixed, y, z, turned
+def diffuse(src, wh_ref, wv_ref, rows, columns, group, store):
+    @pl.loop(0, (columns[1] - columns[0]) // group)
+    def _(g):
+        c = pl.multiple_of(columns[0] + g * group, 8)
+        at, after, before = pl.ds(c, group), pl.ds(c + 1, group), pl.ds(c - 1, group)
+        here = src[rows[0], at]
+        above = wv_ref[rows[0] - 1, at] * (here - src[rows[0] - 1, at])
+        for i in range(*rows):
+            below = src[i + 1, at]
+            down = wv_ref[i, at] * (below - here)
+            right = wh_ref[i, at] * (src[i, after] - here)
+            left = wh_ref[i, before] * (here - src[i, before])
+            store(i, c, here + (right - left) + (down - above))
+            here, above = below, down
+
+
+def iterate(mixed, y, z, wh_ref, wv_ref, invt_ref, columns, group, together, store):
+    deep, lanes = mixed.shape[0], mixed.shape[2]
+    length = columns[1] - columns[0]
+    used = pl.ds(columns[0], length)
+    invt = invt_ref[...]
+
+    def to(ref):
+        def put(i, c, value):
+            ref[i, pl.ds(c, group)] = value
+
+        return put
+
+    def step(src, rows, put):
+        diffuse(src, wh_ref, wv_ref, rows, columns, group, put)
+
+    step(mixed, (1, deep - 1), to(z))
+    step(z, (2, deep - 2), to(y))
+
+    @pl.loop(2, deep - 2, step=together)
+    def _(first):
+        rows = pl.ds(first, together)
+        kept = jnp.maximum(y[rows, used], 0.0).reshape(together * length, lanes)
+        before = mixed[rows, used].reshape(together * length, lanes)
+        u = parts3(kept - 0.5 * before, 1)
+        m = jnp.dot(u, invt, preferred_element_type=jnp.float32)
+        z[rows, used] = (m + (2.0 * before - kept)).reshape(together, length, lanes)
+
+    step(z, (3, deep - 3), to(y))
+    step(y, (4, deep - 4), store)
+
+
+def inside_kernel(invt_ref, mixed_ref, wh_ref, wv_ref, out_ref, y, z):
+    _, width, _ = out_ref.shape
+    clear_sides(y)
+    clear_sides(z)
+
+    def store(i, c, value):
+        out_ref[i - HALO, pl.ds(pl.multiple_of(c - LEAD, 8), GROUP)] = value
+
+    columns = (LEAD, LEAD + width)
+    iterate(mixed_ref, y, z, wh_ref, wv_ref, invt_ref, columns, GROUP, 2, store)
+
+
+def inside(inv3t, mixed, wh, wv, width):
+    deep, span, lanes = mixed.shape
+    vmem = pl.BlockSpec(memory_space=pltpu.VMEM)
+    field = pltpu.VMEM((deep, span, lanes), jnp.float32)
+    return pl.pallas_call(
+        inside_kernel,
+        out_shape=jax.ShapeDtypeStruct((deep - 2 * HALO, width, lanes), jnp.float32),
+        in_specs=[vmem] * 4,
+        out_specs=vmem,
+        scratch_shapes=[field, field],
+        compiler_params=pltpu.CompilerParams(vmem_limit_bytes=22 * 2**20),
+        cost_estimate=pl.CostEstimate(
+            flops=3 * 10**9, bytes_accessed=24 * 2**20, transcendentals=0
+        ),
+    )(inv3t, mixed, wh, wv)
+
+
+def sides_kernel(
+    invt_ref, left_ref, low_ref, high_ref, right_ref, wh_ref, wv_ref, inside_ref,
+    out_ref, mixed, y, z, turned,
 ):
-    deep, width, lanes = mixed_ref.shape
+    half, width, lanes = inside_ref.shape
     count = lanes // 2
-    half = deep - 2 * HALO
-
-    @pl.loop(0, deep)
-    def _(r):
-        mixed[r, LEAD : LEAD + width] = mixed_ref[r]
-        mixed[r, LEAD - 8 : LEAD] = left_ref[r]
-        mixed[r, LEAD + width : LEAD + width + 8] = right_ref[r]
-
-    def diffuse(src, dst, begin, end):
-        @pl.loop(0, (width + 16) // GROUP)
-        def _(g):
-            c = pl.multiple_of(LEAD - 8 + g * GROUP, 8)
-            at, after, before = pl.ds(c, GROUP), pl.ds(c + 1, GROUP), pl.ds(c - 1, GROUP)
-            here = src[begin, at]
-            above = wv_ref[begin - 1, at] * (here - src[begin - 1, at])
-            for i in range(begin, end):
-                below = src[i + 1, at]
-                down = wv_ref[i, at] * (below - here)
-                right = wh_ref[i, at] * (src[i, after] - here)
-                left = wh_ref[i, before] * (here - src[i, before])
-                dst[i, at] = here + (right - left) + (down - above)
-                here, above = below, down
-
-    diffuse(mixed, z, 1, deep - 1)
-    diffuse(z, y, 2, deep - 2)
-    invt = invt_ref[...]
-    used = pl.ds(LEAD - 8, width + 16)
-
-    @pl.loop(2, deep - 2, step=2)
-    def _(first):
-        for k in range(2):
-            kept = jnp.maximum(y[first + k, used], 0.0)
-            before = mixed[first + k, used]
-            u = parts3(kept - 0.5 * before, 1)
-            m = jnp.dot(u, invt, preferred_element_type=jnp.float32)
-            z[first + k, used] = m + (2.0 * before - kept)
-
-    diffuse(z, y, 3, deep - 3)
-    diffuse(y, z, 4, deep - 4)
+    deep, span, _ = mixed.shape
+    for ref in (mixed, y, z):
+        ref[...] = jnp.zeros(ref.shape, jnp.float32)
+    for at, ref in zip((8, 16, 32, 40), (left_ref, low_ref, high_ref, right_ref)):
+        mixed[:, at : at + 8] = ref[...]
+
+    def store(i, c, value):
+        z[i, pl.ds(c, span - 16)] = value
+
+    iterate(
+        mixed, y, z, wh_ref, wv_ref, invt_ref, (8, span - 8), span - 16, deep - 4, store
+    )
+    place = lax.broadcasted_iota(jnp.int32, (8, lanes), 0)
 
     @pl.loop(0, half // 2)
     def _(g):
         for k in range(2):
             r = g * 2 + k
-            v = jnp.transpose(jnp.maximum(z[r + HALO, LEAD : LEAD + width], 0.0))
+            first = jnp.where(place < HALO, z[r + HALO, 16:24], inside_ref[r, :8])
+            last = jnp.where(place < 8 - HALO, inside_ref[r, width - 8 :], z[r + HALO, 32:40])
+            whole = jnp.concatenate([first, inside_ref[r, 8 : width - 8], last], axis=0)
+            v = jnp.transpose(jnp.maximum(whole, 0.0))
             for h in range(2):
                 for t in range(width // 128):
                     turned[t, pl.ds(r + h * half, count, stride=2 * half), :] = v[
@@ -211,15 +272,14 @@
                 out_ref[e, :, t * 128 : (t + 1) * 128] = turned[t, pl.ds(e * 2 * half, 2 * half), :]
 
 
-def admm(inv3t, mixed, left, right, wh, wv):
-    deep, width, lanes = mixed.shape
-    half = deep - 2 * HALO
+def sides(inv3t, left, low, high, right, wh, wv, middle):
+    half, width, lanes = middle.shape
     vmem = pl.BlockSpec(memory_space=pltpu.VMEM)
-    field = pltpu.VMEM((deep, SPAN, lanes), jnp.float32)
-    return pl.pallas_call(
-        admm_kernel,
+    field = pltpu.VMEM(wh.shape, jnp.float32)
+    return pl.pallas_call(
+        sides_kernel,
         out_shape=jax.ShapeDtypeStruct((lanes // 2, 2 * half, width), jnp.float32),
-        in_specs=[vmem] * 6,
+        in_specs=[vmem] * 8,
         out_specs=vmem,
         scratch_shapes=[
             field,
@@ -227,8 +287,8 @@
             field,
             pltpu.VMEM((width // 128, lanes * half, 128), jnp.float32),
         ],
-        compiler_params=pltpu.CompilerParams(vmem_limit_bytes=28 * 2**20),
-    )(inv3t, mixed, left, right, wh, wv)
+        compiler_params=pltpu.CompilerParams(vmem_limit_bytes=14 * 2**20),
+    )(inv3t, left, low, high, right, wh, wv, middle)
 
 
 def neighbours(axis, low_part, high_part):
@@ -255,12 +315,38 @@
     return jnp.concatenate([above, weights, below], axis=1)
 
 
-def widened(weights):
-    left, right = neighbours("col", weights[..., :HALO], weights[..., -HALO:])
+def inside_weights(weights):
     tile_w = weights.shape[2]
-    gap = jnp.zeros(weights.shape[:2] + (LEAD - HALO,), weights.dtype)
-    tail = jnp.zeros(weights.shape[:2] + (SPAN - LEAD - HALO - tile_w,), weights.dtype)
-    return jnp.concatenate([gap, left, weights, right, tail], axis=2)
+    return jnp.pad(weights, ((0, 0), (0, 0), (LEAD, SPAN - LEAD - tile_w)))
+
+
+def side_parts(weights):
+    low, high = weights[..., :8], weights[..., -8:]
+    left, right = neighbours("col", low, high)
+    gap = jnp.zeros_like(low)
+    return [gap, left, low, gap, high, right, gap]
+
+
+def last_rows_kernel(which_ref, src_ref, out_ref):
+    del which_ref
+    out_ref[...] = src_ref[...].reshape(out_ref.shape)
+
+
+def last_rows(source, which, rows):
+    blocks, _, bands, height, width = source.shape
+    at = height // rows - 1
+    return pl.pallas_call(
+        last_rows_kernel,
+        grid_spec=pltpu.PrefetchScalarGridSpec(
+            num_scalar_prefetch=1,
+            grid=(blocks,),
+            in_specs=[
+                pl.BlockSpec((1, 1, bands, rows, width), lambda s, which: (s, which[0], 0, at, 0))
+            ],
+            out_specs=pl.BlockSpec((1, bands, rows, width), lambda s, which: (s, 0, 0, 0)),
+        ),
+        out_shape=jax.ShapeDtypeStruct((blocks, bands, rows, width), source.dtype),
+    )(jnp.reshape(which, (1,)), source)
 
 
 def held_weights(weights, count, half):
@@ -316,34 +402,42 @@
         early, "col", split_axis=0, concat_axis=0, axis_index_groups=columns, tiled=True
     )
     late = lax.ppermute(late, "col", swap)
-    third, by_y, weight_h = barrier((third, by_y, weight_h))
+    third, by_y = barrier((third, by_y))
+    own, weight_h, weight_v, _ = barrier((last_rows(by_y, x, half), weight_h, weight_v, third))
     weights = heightened(raw_weights(weight_h, weight_v))
-    late_own, third_own = rows_of(by_y, x, 3 * quarter), rows_of(by_y, x, half)
+    wh, wv = held_weights(inside_weights(weights), count, half)
+
+    def own_rows(begin):
+        rows = jnp.transpose(own[:, :, begin : begin + quarter], (1, 0, 2, 3))
+        return rows.reshape(bands, ys * quarter, tile_w)
+
+    third_own, late_own = own_rows(0), own_rows(quarter)
     order = [lax.bitwise_and(y + k, ys - 1) for k in range(1, ys)]
 
     def over_y(parts):
         return [lax.ppermute(p, "col", turns[k + 1]) for k, p in enumerate(parts)]
 
-    third, late, weights = barrier((third, late, weights))
+    third, late = barrier((third, late))
     third = lax.ppermute(third, "col", swap)
     late = project(library_x, jnp.concatenate([late_own, late], axis=0), ys, quarter)
     late_coded = coded(late, order)
-    weights, _ = barrier((weights, late_coded))
+    wh, wv, late_coded = barrier((wh, wv, late_coded))
     late_coded = over_y(late_coded)
-    weights = widened(weights)
     early = project(library_y, early, 2, half)
     early_coded = coded(early, [1 - x])[0]
-    third, late_coded, weights, _ = barrier((third, late_coded, weights, early_coded))
+    third, late_coded, _ = barrier((third, late_coded, early_coded))
     early_coded = lax.ppermute(early_coded, "col", swap)
     third = project(library_x, jnp.concatenate([third_own, third], axis=0), ys, quarter)
     third_coded = coded(third, order)
-    late_coded, _ = barrier((late_coded, third_coded))
+    late_coded, weights, _ = barrier((late_coded, weights, third_coded))
+    weights_side = side_parts(weights)
     third_coded = over_y(third_coded)
     late, last = finished(late, y, late_coded, True)
     early, first = finished(early, x, [early_coded], False)
     top, bottom = neighbours("row", first, last)
 
-    wh, wv = held_weights(weights, count, half)
+    weights_side, _, _ = barrier((weights_side, first, last))
+    wh_side, wv_side = held_weights(jnp.concatenate(weights_side, axis=2), count, half)
     inv_hi = lax.reduce_precision(inverse, 8, 7)
     inv3 = jnp.concatenate([inv_hi, inverse - inv_hi, inv_hi], axis=1).astype(jnp.bfloat16)
     block = lax.broadcasted_iota(jnp.int32, (2 * count, 2 * count), 0) // count
@@ -353,7 +447,8 @@
     inv3t = jnp.concatenate([twice_hi, twice - twice_hi, twice_hi], axis=0).astype(jnp.bfloat16)
     mixed, low, high = mix(y, inv3, early, late, third, third_coded, top, bottom)
     left, right = neighbours("col", low, high)
-    return admm(inv3t, mixed, left, right, wh, wv)
+    middle = inside(inv3t, mixed, wh, wv, tile_w)
+    return sides(inv3t, left, low, high, right, wh_side, wv_side, middle)
 
 
 def solution(mesh):

time: 125 us -> 122 us (0.976)
  waiting for transfers between devices: 20.6 us -> 15.1 us
  Pallas kernels: 19.5 us -> 24.5 us
  matrix products: 7.97 us -> 11 us
  other arithmetic: 9.14 us -> 6.31 us
  local copies, waits for them, and re-layouts: 20.6 us -> 18.9 us
    optimization_barrier x3 -> x2, local copies, waits for them, and re-layouts: 12.5 us -> 2.13 us  [the longest x1 1.64 us: per_device(): third, late_coded, _ = barrier((third, late_coded, early_coded))]
    ppermute x4, waiting for transfers between devices: 8.94 us -> 2.58 us  [neighbours(): lax.ppermute(high_part, axis, forward)]
    transpose x0 -> x3, local copies, waits for them, and re-layouts: none -> 6.13 us  [the longest x2 4.59 us: per_device(): early = jnp.transpose(by_y[..., :half, :], (0, 2, 1, 3, 4))]
    ppermute x6, waiting for transfers between devices: 1.48 us -> 6.33 us  [over_y(): return [lax.ppermute(p, 'col', turns[k + 1]) for k, p in enumerate(parts)]]
    dot_general x2 -> x4, matrix products: 1.62 us -> 5.8 us  [held_weights(): jnp.einsum('hrc,hl->rcl', x, spread, preferred_element_type=jnp.float32)]
    ppermute x4, waiting for transfers between devices: 10.1 us -> 6.15 us  [neighbours(): lax.ppermute(low_part, axis, backward)]
    pallas_call x1 -> x3, Pallas kernels: 13.3 us -> 16.8 us  [the longest x1 8.15 us: inside(): pl.pallas_call(inside_kernel, out_shape=jax.ShapeDtypeStruct((deep - 2 *...]
    ppermute x6, starting transfers between devices: 11.7 us -> 8.5 us  [over_y(): return [lax.ppermute(p, 'col', turns[k + 1]) for k, p in enumerate(parts)]]
  transfers between devices with their start and end apart: 18 -> 18, of which waited for: 6 -> 5; matrix products, arithmetic and copies ran while one was open for 26% -> 21% of each run, Pallas kernels for 3% -> 13%
where the time goes in v5:
time: 122 us; the launch traced here: 121 us
  starting transfers between devices  45.1 us (37%)
  Pallas kernels  24.5 us (20%)
  local copies, waits for them, and re-layouts  18.9 us (15%)
  waiting for transfers between devices  15.1 us (12%)
  matrix products  11 us (9%)
  other arithmetic  6.31 us (5%)
    ppermute x4, starting transfers between devices, neighbours(): lax.ppermute(high_part, axis, forward)  16.7 us
    ppermute x4, starting transfers between devices, neighbours(): lax.ppermute(low_part, axis, backward)  10.5 us
    ppermute x6, starting transfers between devices, over_y(): return [lax.ppermute(p, 'col', turns[k + 1]) for k, p in enumerate(parts)]  8.5 us
    pallas_call x1, Pallas kernels, inside(): pl.pallas_call(inside_kernel, out_shape=jax.ShapeDtypeStruct((deep - 2 *...  8.15 us
    ppermute x6, waiting for transfers between devices, over_y(): return [lax.ppermute(p, 'col', turns[k + 1]) for k, p in enumerate(parts)]  6.33 us
    ppermute x4, waiting for transfers between devices, neighbours(): lax.ppermute(low_part, axis, backward)  6.15 us
    dot_general x4, matrix products, held_weights(): jnp.einsum('hrc,hl->rcl', x, spread, preferred_element_type=jnp.float32)  5.8 us
    unnamed x36, local copies, waits for them, and re-layouts  5.71 us
  transfers between devices with their start and end apart: 18, of which 5 were waited for; matrix products, arithmetic and copies ran while one was open for 21% of the time, Pallas kernels for 13%

profile of v5, /device:TPU:39, one launch (start us, length us, event | category | flops | bytes accessed | tf_op | source)
XLA Modules:
  0.0 121.3 jit_solution(8903725169115080007)
XLA Ops:
  0.0 2.3 %slice_bitcast_fusion = bf16[4,53,2,16,256]{4,3,1,2,0:T(8,128)(2,1)S(1)} fusion(bf16[4,2,53,32,256]{4,3,2,1,0:T(8,128)(2,1)} %bitcast.89), kind=kLoop, calls=%fused_computation.2 | loop fusion | bytes 6946816 | tf_op jit(solution)/shard_map/transpose | solution.py:395
  2.3 2.3 %copy.68 = bf16[4,53,2,16,256]{4,3,2,1,0:T(8,128)(2,1)} copy(bf16[4,53,2,16,256]{4,3,1,2,0:T(8,128)(2,1)S(1)} %slice_bitcast_fusion) | data formatting | bytes 6946816 | tf_op jit(solution)/shard_map/transpose | solution.py:395
  4.6 4.8 %all-to-all-start = ((bf16[4,53,32,256]{3,2,1,0:T(8,128)(2,1)}), bf16[4,53,32,256]{3,2,1,0:T(8,128)(2,1)}, u32[]{:S(2)}, u32[]{:S(2)}) async-start(bf16[4,53,32,256]{3,2,1,0:T(8,128)(2,1)} %bitcast.5), calls=%async_computation | async-start | bytes 6946816 | tf_op jit(solution)/shard_map/all_to_all | solution.py:401
  9.4 2.6 %copy_bitcast_fusion.3 = bf16[53,32,256]{2,1,0:T(8,128)(2,1)} fusion(bf16[4,2,53,32,256]{4,3,2,1,0:T(8,128)(2,1)} %bitcast.90, pred[]{:T(512)S(6)} %eq.22), kind=kLoop, calls=%fused_computation.18 | loop fusion | flops 434176 | bytes 2605057 | tf_op jit(solution)/shard_map/reshape | solution.py:384
  12.0 1.1 collective-permute-start.1
  13.2 2.6 %copy_bitcast_fusion.2 = bf16[53,32,256]{2,1,0:T(8,128)(2,1)} fusion(bf16[4,2,53,32,256]{4,3,2,1,0:T(8,128)(2,1)} %bitcast.91, pred[]{:T(512)S(6)} %eq.22), kind=kLoop, calls=%fused_computation.17 | loop fusion | flops 434176 | bytes 2605057 | tf_op jit(solution)/shard_map/reshape | solution.py:384
  15.8 3.7 %shard_map.57 = bf16[4,53,16,256]{3,2,1,0:T(8,128)(2,1)} custom-call(s32[1]{0:T(128)} %bitcast.2.which_ref, bf16[4,2,53,32,256]{4,3,2,1,0:T(8,128)(2,1)} %bitcast.92), custom_call_target="tpu_custom_call" | custom-call | tf_op jit(solution)/shard_map/pallas_call | solution.py:338
  19.6 3.8 %collective-permute-start.3 = (bf16[2,4,256]{2,1,0:T(4,128)(2,1)S(1)}, bf16[2,4,256]{2,1,0:T(4,128)(2,1)S(1)}, u32[]{:S(2)}, u32[]{:S(2)}) collective-permute-start(bf16[2,4,256]{2,1,0:T(4,128)(2,1)S(1)} %get-tuple-element.111), channel_id=1, source_target_pairs={{0,8},{8,16},{16,24},{24,32},{32,40},{40,48},{48,56},{56,64},{64,7... | collective-permute-start | bytes 12296 | tf_op jit(solution)/shard_map/ppermute | solution.py:298
  23.4 1.9 %collective-permute-start.4 = (bf16[2,4,256]{2,1,0:T(4,128)(2,1)S(1)}, bf16[2,4,256]{2,1,0:T(4,128)(2,1)S(1)}, u32[]{:S(2)}, u32[]{:S(2)}) collective-permute-start(bf16[2,4,256]{2,1,0:T(4,128)(2,1)S(1)} %get-tuple-element.112), channel_id=1, source_target_pairs={{8,0},{16,8},{24,16},{32,24},{40,32},{48,40},{56,48},{64,56},{72,6... | collective-permute-start | bytes 12296 | tf_op jit(solution)/shard_map/ppermute | solution.py:298
  25.6 0.6 fusion.20
  26.5 1.5 %slice_bitcast_fusion.1 = (bf16[53,4,8,256]{3,2,0,1:T(8,128)(2,1)S(1)}, bf16[53,4,8,256]{3,2,0,1:T(8,128)(2,1)S(1)}) fusion(bf16[4,53,16,256]{3,2,1,0:T(8,128)(2,1)} %shard_map.57), kind=kLoop, calls=%fused_computation.19 | loop fusion | bytes 3473408 | tf_op jit(solution)/shard_map/transpose | solution.py:411
  28.9 2.6 %collective-permute-done.3 = bf16[2,4,256]{2,1,0:T(4,128)(2,1)S(1)} collective-permute-done((bf16[2,4,256]{2,1,0:T(4,128)(2,1)S(1)}, bf16[2,4,256]{2,1,0:T(4,128)(2,1)S(1)}, u32[]{:S(2)}, u32[]{:S(2)}) %collective-permute-start.3) | collective-permute-done | bytes 4128 | tf_op jit(solution)/shard_map/ppermute | solution.py:298
  31.4 3.0 %collective-permute-done.4 = bf16[2,4,256]{2,1,0:T(4,128)(2,1)S(1)} collective-permute-done((bf16[2,4,256]{2,1,0:T(4,128)(2,1)S(1)}, bf16[2,4,256]{2,1,0:T(4,128)(2,1)S(1)}, u32[]{:S(2)}, u32[]{:S(2)}) %collective-permute-start.4) | collective-permute-done | bytes 4128 | tf_op jit(solution)/shard_map/ppermute | solution.py:298
  34.7 2.6 %convolution_multiply_fusion.wv_ref = f32[24,288,128]{2,1,0:T(8,128)} fusion(bf16[1,2,24,288]{3,0,2,1:T(2,128)(2,1)S(1)} %copy.76, bf16[1,2,24,288]{3,0,2,1:T(2,128)(2,1)S(1)} %copy.75, pred[2,128]{1,0:T(4,128)(4,1)S(1)} %iota_compare_fusion), kind=kOutput, calls=%fused_computation.3 | convolution fusion | flops 4478976 | bytes 3594496 | tf_op jit(solution)/shard_map/hrc,hl->rcl/dot_general | solution.py:359
  37.2 3.3 %collective-permute-start.2 = (bf16[53,32,256]{2,1,0:T(8,128)(2,1)}, bf16[53,32,256]{2,1,0:T(8,128)(2,1)}, u32[]{:S(2)}, u32[]{:S(2)}) collective-permute-start(bf16[53,32,256]{2,1,0:T(8,128)(2,1)} %copy_bitcast_fusion.2), channel_id=1, source_target_pairs={{0,1},{1,0},{2,3},{3,2},{4,5},{5,4},{6,7},{7,6},{8,9},{9,8},{10,11... | collective-permute-start | bytes 2605064 | tf_op jit(solution)/shard_map/ppermute | solution.py:421
  40.6 2.6 %convolution_multiply_fusion.1.wh_ref = f32[24,288,128]{2,1,0:T(8,128)} fusion(bf16[1,2,24,288]{3,0,2,1:T(2,128)(2,1)S(1)} %copy.75, bf16[1,2,24,288]{3,0,2,1:T(2,128)(2,1)S(1)} %copy.76, pred[2,128]{1,0:T(4,128)(4,1)S(1)} %iota_compare_fusion), kind=kOutput, calls=%fused_computation.4 | convolution fusion | flops 4478976 | bytes 3594496 | tf_op jit(solution)/shard_map/hrc,hl->rcl/dot_general | solution.py:359
  44.2 0.8 shard_map.58
  45.0 1.3 %copy-done = f32[32,256,64]{1,2,0:T(8,128)} copy-done((f32[32,256,64]{1,2,0:T(8,128)}, f32[32,256,64]{1,2,0:T(8,128)S(1)}, u32[]{:S(2)}) %copy-start) | copy-done | bytes 2097176
  46.3 1.4 %collective-permute-start.5 = (s16[528,256]{1,0:T(8,128)(2,1)S(1)}, s16[528,256]{1,0:T(8,128)(2,1)S(1)}, u32[]{:S(2)}, u32[]{:S(2)}) collective-permute-start(s16[528,256]{1,0:T(8,128)(2,1)S(1)} %get-tuple-element.64), channel_id=1, source_target_pairs={{0,2},{1,3},{2,4},{3,5},{4,6},{5,7},{6,0},{7,1},{8,10},{9,11},{10,... | collective-permute-start | bytes 811016 | tf_op jit(solution)/shard_map/ppermute | solution.py:418
  47.7 2.4 %collective-permute-start.6 = (s16[528,256]{1,0:T(8,128)(2,1)S(1)}, s16[528,256]{1,0:T(8,128)(2,1)S(1)}, u32[]{:S(2)}, u32[]{:S(2)}) collective-permute-start(s16[528,256]{1,0:T(8,128)(2,1)S(1)} %get-tuple-element.65), channel_id=1, source_target_pairs={{0,4},{1,5},{2,6},{3,7},{4,0},{5,1},{6,2},{7,3},{8,12},{9,13},{10,... | collective-permute-start | bytes 811016 | tf_op jit(solution)/shard_map/ppermute | solution.py:418
  50.1 1.2 collective-permute-start.7
  51.3 4.2 %fusion = f32[32,256,64]{1,2,0:T(8,128)S(1)} fusion(bf16[212,32,256]{2,1,0:T(8,128)(2,1)} %bitcast.6, bf16[64,53]{1,0:T(8,128)(2,1)S(1)} %get-tuple-element.102, bf16[64,53]{1,0:T(8,128)(2,1)S(1)} %get-tuple-element.103, bf16[64,53]{1,0:T(8,128)(2,1)S(1)} %get-tuple-element.104, bf16[64,53]{1,0:T(8,128)(2,1)S(1)} %get-tuple-element.105, ...), kind=kOutput, calls=%fused_computation | convolution fusion | flops 222528768 | bytes 5624833 | tf_op jit(solution)/shard_map/eb,bhw->hew/dot_general | solution.py:378
  56.3 0.9 collective-permute-done.5.refs_0_
  57.2 5.4 %collective-permute-done.6.refs_1_ = s16[528,256]{1,0:T(8,128)(2,1)S(1)} collective-permute-done((s16[528,256]{1,0:T(8,128)(2,1)S(1)}, s16[528,256]{1,0:T(8,128)(2,1)S(1)}, u32[]{:S(2)}, u32[]{:S(2)}) %collective-permute-start.6) | collective-permute-done | bytes 270368 | tf_op jit(solution)/shard_map/ppermute | solution.py:418
  62.6 0.7 copy-done.6
  63.3 1.6 %copy.79 = bf16[53,32,256]{2,0,1:T(8,128)(2,1)S(1)} copy(bf16[53,32,256]{2,1,0:T(8,128)(2,1)} %collective-permute-done.2) | data formatting | bytes 1736704 | tf_op jit(solution)/shard_map/optimization_barrier | solution.py:428
  65.5 1.7 %shard_map.59 = (s16[528,256]{1,0:T(8,128)(2,1)}, s16[528,256]{1,0:T(8,128)(2,1)}, s16[528,256]{1,0:T(8,128)(2,1)}) custom-call(s32[3]{0:T(128)S(1)} %pad_add_fusion.which_ref, f32[4,8,64,256]{3,2,1,0:T(8,128)S(1)} %bitcast.85), custom_call_target="tpu_custom_call" | custom-call | tf_op jit(solution)/shard_map/pallas_call | solution.py:46
  67.3 2.3 %collective-permute-start.16 = (bf16[2,40,8]{2,1,0:T(8,128)(2,1)S(1)}, bf16[2,40,8]{2,1,0:T(8,128)(2,1)S(1)}, u32[]{:S(2)}, u32[]{:S(2)}) collective-permute-start(bf16[2,40,8]{2,1,0:T(8,128)(2,1)S(1)} %get-tuple-element.85), channel_id=1, source_target_pairs={{1,0},{2,1},{3,2},{4,3},{5,4},{6,5},{7,6},{9,8},{10,9},{11,10},{12... | collective-permute-start | bytes 3848 | tf_op jit(solution)/shard_map/ppermute | solution.py:298
  69.6 5.4 %collective-permute-start.15 = (bf16[2,40,8]{2,1,0:T(8,128)(2,1)S(1)}, bf16[2,40,8]{2,1,0:T(8,128)(2,1)S(1)}, u32[]{:S(2)}, u32[]{:S(2)}) collective-permute-start(bf16[2,40,8]{2,1,0:T(8,128)(2,1)S(1)} %get-tuple-element.87), channel_id=1, source_target_pairs={{0,1},{1,2},{2,3},{3,4},{4,5},{5,6},{6,7},{8,9},{9,10},{10,11},{11... | collective-permute-start | bytes 3848 | tf_op jit(solution)/shard_map/ppermute | solution.py:298
  75.1 0.6 collective-permute-start.8
  75.7 1.0 collective-permute-start.9
  76.7 0.9 shard_map.60
  77.6 2.0 %collective-permute-start.10 = (s16[528,256]{1,0:T(8,128)(2,1)}, s16[528,256]{1,0:T(8,128)(2,1)S(1)}, u32[]{:S(2)}, u32[]{:S(2)}) collective-permute-start(s16[528,256]{1,0:T(8,128)(2,1)} %get-tuple-element.73), channel_id=1, source_target_pairs={{0,6},{1,7},{2,0},{3,1},{4,2},{5,3},{6,4},{7,5},{8,14},{9,15},{10,... | collective-permute-start | bytes 811016 | tf_op jit(solution)/shard_map/ppermute | solution.py:418
  79.6 0.8 shard_map.56
  80.3 5.2 %collective-permute-start.11 = (f32[4,64,256]{2,1,0:T(8,128)}, f32[4,64,256]{2,1,0:T(8,128)}, u32[]{:S(2)}, u32[]{:S(2)}) collective-permute-start(f32[4,64,256]{2,1,0:T(8,128)} %get-tuple-element.78), channel_id=1, source_target_pairs={{0,8},{8,16},{16,24},{24,32},{32,40},{40,48},{48,56},{56,64},{64,7... | collective-permute-start | bytes 786440 | tf_op jit(solution)/shard_map/ppermute | solution.py:298
  85.6 0.6 copy-done.17
  86.2 1.9 %collective-permute-start.12 = (f32[4,64,256]{2,1,0:T(8,128)}, f32[4,64,256]{2,1,0:T(8,128)}, u32[]{:S(2)}, u32[]{:S(2)}) collective-permute-start(f32[4,64,256]{2,1,0:T(8,128)} %get-tuple-element.79), channel_id=1, source_target_pairs={{8,0},{16,8},{24,16},{32,24},{40,32},{48,40},{56,48},{64,56},{72,6... | collective-permute-start | bytes 786440 | tf_op jit(solution)/shard_map/ppermute | solution.py:298
  88.1 0.6 broadcast_in_dim.14
  88.7 1.6 %concatenate.37 = bf16[2,40,56]{2,1,0:T(8,128)(2,1)} concatenate(bf16[2,40,8]{2,1,0:T(8,128)(2,1)} %broadcast_in_dim.14, bf16[2,40,8]{2,1,0:T(8,128)(2,1)} %copy-done.17, bf16[2,40,8]{2,1,0:T(8,128)(2,1)} %copy-done.10, bf16[2,40,8]{2,1,0:T(8,128)(2,1)} %broadcast_in_dim.14, bf16[2,40,8]{2,1,0:T(8,128)(2,1)} %copy-done.11, bf16[2,40,8]{2,1,0:T(8,128)(2,1)} %copy-done.16, ...), dimensions={2} | concatenate | bytes 17920 | tf_op jit(solution)/shard_map/concatenate | solution.py:440
  90.3 0.9 slice_bitcast_fusion.3
  91.9 3.2 %collective-permute-done.12.bottom_ref = f32[4,64,256]{2,1,0:T(8,128)} collective-permute-done((f32[4,64,256]{2,1,0:T(8,128)}, f32[4,64,256]{2,1,0:T(8,128)}, u32[]{:S(2)}, u32[]{:S(2)}) %collective-permute-start.12) | collective-permute-done | bytes 262176 | tf_op jit(solution)/shard_map/ppermute | solution.py:298
  95.1 1.0 copy-done.5
  96.1 3.3 %shard_map.61 = (f32[24,288,128]{2,1,0:T(8,128)S(1)}, f32[24,8,128]{2,1,0:T(8,128)S(1)}, f32[24,8,128]{2,1,0:T(8,128)S(1)}) custom-call(s32[1]{0:T(128)} %bitcast.1.which_ref, bf16[64,192]{1,0:T(8,128)(2,1)S(1)} %pad_maximum_fusion.3.inv_ref, f32[16,64,256]{2,1,0:T(8,128)S(1)} %get-tuple-element.50.early_ref, f32[8,64,256]{2,1,0:T(8,128)S(1)} %copy-done.5, ...), custom_call_target="tpu_custom_call" | custom-call | tf_op jit(solution)/shard_map/pallas_call | solution.py:147
  99.4 2.4 %collective-permute-start.13 = (f32[24,8,128]{2,1,0:T(8,128)S(1)}, f32[24,8,128]{2,1,0:T(8,128)S(1)}, u32[]{:S(2)}, u32[]{:S(2)}) collective-permute-start(f32[24,8,128]{2,1,0:T(8,128)S(1)} %get-tuple-element.80.high_ref), channel_id=1, source_target_pairs={{0,1},{1,2},{2,3},{3,4},{4,5},{5,6},{6,7},{8,9},{9,10},{10,11},{11... | collective-permute-start | bytes 294920 | tf_op jit(solution)/shard_map/ppermute | solution.py:298
  101.8 4.4 %collective-permute-start.14 = (f32[24,8,128]{2,1,0:T(8,128)S(1)}, f32[24,8,128]{2,1,0:T(8,128)S(1)}, u32[]{:S(2)}, u32[]{:S(2)}) collective-permute-start(f32[24,8,128]{2,1,0:T(8,128)S(1)} %get-tuple-element.81.low_ref), channel_id=1, source_target_pairs={{1,0},{2,1},{3,2},{4,3},{5,4},{6,5},{7,6},{9,8},{10,9},{11,10},{12... | collective-permute-start | bytes 294920 | tf_op jit(solution)/shard_map/ppermute | solution.py:298
  106.2 2.0 %copy-done.3 = f32[24,288,128]{2,1,0:T(8,128)S(1)} copy-done((f32[24,288,128]{2,1,0:T(8,128)S(1)}, f32[24,288,128]{2,1,0:T(8,128)}, u32[]{:S(2)}) %copy-start.3) | copy-done | bytes 3538968
  108.2 8.1 %shard_map.62.inside_ref = f32[16,256,128]{2,1,0:T(8,128)S(1)} custom-call(bf16[384,128]{1,0:T(8,128)(2,1)S(1)} %pad_maximum_fusion.invt_ref, f32[24,288,128]{2,1,0:T(8,128)S(1)} %get-tuple-element.90.mixed_ref, f32[24,288,128]{2,1,0:T(8,128)S(1)} %copy-done.3, f32[24,288,128]{2,1,0:T(8,128)S(1)} %copy-done.2), custom_call_target="tpu_custom_call" | custom-call | flops 3000000000 | bytes 25165824 | tf_op jit(solution)/shard_map/pallas_call | solution.py:220
  116.4 5.0 %shard_map.63 = f32[64,32,256]{2,1,0:T(8,128)} custom-call(bf16[384,128]{1,0:T(8,128)(2,1)S(1)} %pad_maximum_fusion.invt_ref, f32[24,8,128]{2,1,0:T(8,128)S(1)} %collective-permute-done.13.left_ref, f32[24,8,128]{2,1,0:T(8,128)S(1)} %get-tuple-element.81.low_ref, f32[24,8,128]{2,1,0:T(8,128)S(1)} %get-tuple-element.80.high_ref, ...), custom_call_target="tpu_custom_call" | custom-call | tf_op jit(solution)/shard_map/pallas_call | solution.py:279
  (76 shorter events, 4.8 us)
Async XLA Ops:
  4.6 46.7 %all-to-all-start = ((bf16[4,53,32,256]{3,2,1,0:T(8,128)(2,1)}), bf16[4,53,32,256]{3,2,1,0:T(8,128)(2,1)}, u32[]{:S(2)}, u32[]{:S(2)}) async-start(bf16[4,53,32,256]{3,2,1,0:T(8,128)(2,1)} %bitcast.5), calls=%async_computation | async-start | bytes 6946816 | tf_op jit(solution)/shard_map/all_to_all | solution.py:401
  12.0 25.2 %collective-permute-start.1 = (bf16[53,32,256]{2,1,0:T(8,128)(2,1)}, bf16[53,32,256]{2,1,0:T(8,128)(2,1)S(1)}, u32[]{:S(2)}, u32[]{:S(2)}) collective-permute-start(bf16[53,32,256]{2,1,0:T(8,128)(2,1)} %copy_bitcast_fusion.3), channel_id=1, source_target_pairs={{0,1},{1,0},{2,3},{3,2},{4,5},{5,4},{6,7},{7,6},{8,9},{9,8},{10,11... | collective-permute-start | bytes 2605064 | tf_op jit(solution)/shard_map/ppermute | solution.py:404
  15.8 3.7 %copy-start.14 = (s32[32,256]{1,0:T(8,128)S(1)}, s32[32,256]{1,0:T(8,128)}, u32[]{:S(2)}) copy-start(s32[32,256]{1,0:T(8,128)} %param.8) | copy-start | bytes 98308
  15.8 3.7 %copy-start.15 = (s32[32,256]{1,0:T(8,128)S(1)}, s32[32,256]{1,0:T(8,128)}, u32[]{:S(2)}) copy-start(s32[32,256]{1,0:T(8,128)} %param.9) | copy-start | bytes 98308
  15.8 9.5 %copy-start.9 = (f32[64,64]{1,0:T(8,128)S(1)}, f32[64,64]{1,0:T(8,128)}, u32[]{:S(2)}) copy-start(f32[64,64]{1,0:T(8,128)} %param.7) | copy-start | bytes 49156
  15.8 10.6 %copy-start.8 = (bf16[64,424]{1,0:T(8,128)(2,1)S(1)}, bf16[64,424]{1,0:T(8,128)(2,1)}, u32[]{:S(2)}) copy-start(bf16[64,424]{1,0:T(8,128)(2,1)} %param.6) | copy-start | bytes 162820
  19.6 11.8 %collective-permute-start.3 = (bf16[2,4,256]{2,1,0:T(4,128)(2,1)S(1)}, bf16[2,4,256]{2,1,0:T(4,128)(2,1)S(1)}, u32[]{:S(2)}, u32[]{:S(2)}) collective-permute-start(bf16[2,4,256]{2,1,0:T(4,128)(2,1)S(1)} %get-tuple-element.111), channel_id=1, source_target_pairs={{0,8},{8,16},{16,24},{24,32},{32,40},{40,48},{48,56},{56,64},{64,7... | collective-permute-start | bytes 12296 | tf_op jit(solution)/shard_map/ppermute | solution.py:298
  23.4 11.0 %collective-permute-start.4 = (bf16[2,4,256]{2,1,0:T(4,128)(2,1)S(1)}, bf16[2,4,256]{2,1,0:T(4,128)(2,1)S(1)}, u32[]{:S(2)}, u32[]{:S(2)}) collective-permute-start(bf16[2,4,256]{2,1,0:T(4,128)(2,1)S(1)} %get-tuple-element.112), channel_id=1, source_target_pairs={{8,0},{16,8},{24,16},{32,24},{40,32},{48,40},{56,48},{64,56},{72,6... | collective-permute-start | bytes 12296 | tf_op jit(solution)/shard_map/ppermute | solution.py:298
  37.2 26.1 %collective-permute-start.2 = (bf16[53,32,256]{2,1,0:T(8,128)(2,1)}, bf16[53,32,256]{2,1,0:T(8,128)(2,1)}, u32[]{:S(2)}, u32[]{:S(2)}) collective-permute-start(bf16[53,32,256]{2,1,0:T(8,128)(2,1)} %copy_bitcast_fusion.2), channel_id=1, source_target_pairs={{0,1},{1,0},{2,3},{3,2},{4,5},{5,4},{6,7},{7,6},{8,9},{9,8},{10,11... | collective-permute-start | bytes 2605064 | tf_op jit(solution)/shard_map/ppermute | solution.py:421
  45.0 1.3 %copy-start = (f32[32,256,64]{1,2,0:T(8,128)}, f32[32,256,64]{1,2,0:T(8,128)S(1)}, u32[]{:S(2)}) copy-start(f32[32,256,64]{1,2,0:T(8,128)S(1)} %fusion.2) | copy-start | bytes 6291460
  46.3 10.9 %collective-permute-start.5 = (s16[528,256]{1,0:T(8,128)(2,1)S(1)}, s16[528,256]{1,0:T(8,128)(2,1)S(1)}, u32[]{:S(2)}, u32[]{:S(2)}) collective-permute-start(s16[528,256]{1,0:T(8,128)(2,1)S(1)} %get-tuple-element.64), channel_id=1, source_target_pairs={{0,2},{1,3},{2,4},{3,5},{4,6},{5,7},{6,0},{7,1},{8,10},{9,11},{10,... | collective-permute-start | bytes 811016 | tf_op jit(solution)/shard_map/ppermute | solution.py:418
  47.7 14.9 %collective-permute-start.6 = (s16[528,256]{1,0:T(8,128)(2,1)S(1)}, s16[528,256]{1,0:T(8,128)(2,1)S(1)}, u32[]{:S(2)}, u32[]{:S(2)}) collective-permute-start(s16[528,256]{1,0:T(8,128)(2,1)S(1)} %get-tuple-element.65), channel_id=1, source_target_pairs={{0,4},{1,5},{2,6},{3,7},{4,0},{5,1},{6,2},{7,3},{8,12},{9,13},{10,... | collective-permute-start | bytes 811016 | tf_op jit(solution)/shard_map/ppermute | solution.py:418
  50.1 12.5 %collective-permute-start.7 = (s16[528,256]{1,0:T(8,128)(2,1)S(1)}, s16[528,256]{1,0:T(8,128)(2,1)S(1)}, u32[]{:S(2)}, u32[]{:S(2)}) collective-permute-start(s16[528,256]{1,0:T(8,128)(2,1)S(1)} %get-tuple-element.66), channel_id=1, source_target_pairs={{0,6},{1,7},{2,0},{3,1},{4,2},{5,3},{6,4},{7,5},{8,14},{9,15},{10,... | collective-permute-start | bytes 811016 | tf_op jit(solution)/shard_map/ppermute | solution.py:418
  55.7 21.9 %collective-permute-start = (s16[1040,256]{1,0:T(8,128)(2,1)S(1)}, s16[1040,256]{1,0:T(8,128)(2,1)S(1)}, u32[]{:S(2)}, u32[]{:S(2)}) collective-permute-start(s16[1040,256]{1,0:T(8,128)(2,1)S(1)} %shard_map.55), channel_id=1, source_target_pairs={{0,1},{1,0},{2,3},{3,2},{4,5},{5,4},{6,7},{7,6},{8,9},{9,8},{10,11... | collective-permute-start | bytes 1597448 | tf_op jit(solution)/shard_map/ppermute | solution.py:429
  62.6 0.7 copy-start.6
  65.0 10.0 %copy-start.12 = (bf16[64,64]{1,0:T(8,128)(2,1)S(1)}, bf16[64,64]{1,0:T(8,128)(2,1)}, u32[]{:S(2)}) copy-start(bf16[64,64]{1,0:T(8,128)(2,1)} %get-tuple-element.113) | copy-start | bytes 24580
  65.0 10.0 %copy-start.13 = (bf16[64,64]{1,0:T(8,128)(2,1)S(1)}, bf16[64,64]{1,0:T(8,128)(2,1)}, u32[]{:S(2)}) copy-start(bf16[64,64]{1,0:T(8,128)(2,1)} %get-tuple-element.114) | copy-start | bytes 24580
  65.0 11.6 %copy-start.1 = (f32[32,256,64]{1,2,0:T(8,128)S(1)}, f32[32,256,64]{1,2,0:T(8,128)}, u32[]{:S(2)}) copy-start(f32[32,256,64]{1,2,0:T(8,128)} %copy-done) | copy-start | bytes 6291460
  65.0 11.6 %copy-start.7 = (s16[528,256]{1,0:T(8,128)(2,1)S(1)}, s16[528,256]{1,0:T(8,128)(2,1)}, u32[]{:S(2)}) copy-start(s16[528,256]{1,0:T(8,128)(2,1)} %copy-done.6) | copy-start | bytes 811012
  67.3 13.0 %copy-start.10 = (bf16[2,40,8]{2,1,0:T(8,128)(2,1)}, bf16[2,40,8]{2,1,0:T(8,128)(2,1)S(1)}, u32[]{:S(2)}) copy-start(bf16[2,40,8]{2,1,0:T(8,128)(2,1)S(1)} %get-tuple-element.85) | copy-start | bytes 3844
  67.3 13.0 %copy-start.11 = (bf16[2,40,8]{2,1,0:T(8,128)(2,1)}, bf16[2,40,8]{2,1,0:T(8,128)(2,1)S(1)}, u32[]{:S(2)}) copy-start(bf16[2,40,8]{2,1,0:T(8,128)(2,1)S(1)} %get-tuple-element.87) | copy-start | bytes 3844
  67.3 13.0 %collective-permute-start.16 = (bf16[2,40,8]{2,1,0:T(8,128)(2,1)S(1)}, bf16[2,40,8]{2,1,0:T(8,128)(2,1)S(1)}, u32[]{:S(2)}, u32[]{:S(2)}) collective-permute-start(bf16[2,40,8]{2,1,0:T(8,128)(2,1)S(1)} %get-tuple-element.85), channel_id=1, source_target_pairs={{1,0},{2,1},{3,2},{4,3},{5,4},{6,5},{7,6},{9,8},{10,9},{11,10},{12... | collective-permute-start | bytes 3848 | tf_op jit(solution)/shard_map/ppermute | solution.py:298
  69.6 15.9 %collective-permute-start.15 = (bf16[2,40,8]{2,1,0:T(8,128)(2,1)S(1)}, bf16[2,40,8]{2,1,0:T(8,128)(2,1)S(1)}, u32[]{:S(2)}, u32[]{:S(2)}) collective-permute-start(bf16[2,40,8]{2,1,0:T(8,128)(2,1)S(1)} %get-tuple-element.87), channel_id=1, source_target_pairs={{0,1},{1,2},{2,3},{3,4},{4,5},{5,6},{6,7},{8,9},{9,10},{10,11},{11... | collective-permute-start | bytes 3848 | tf_op jit(solution)/shard_map/ppermute | solution.py:298
  75.1 16.8 %collective-permute-start.8 = (s16[528,256]{1,0:T(8,128)(2,1)}, s16[528,256]{1,0:T(8,128)(2,1)}, u32[]{:S(2)}, u32[]{:S(2)}) collective-permute-start(s16[528,256]{1,0:T(8,128)(2,1)} %get-tuple-element.71), channel_id=1, source_target_pairs={{0,2},{1,3},{2,4},{3,5},{4,6},{5,7},{6,0},{7,1},{8,10},{9,11},{10,... | collective-permute-start | bytes 811016 | tf_op jit(solution)/shard_map/ppermute | solution.py:418
  75.7 16.2 %collective-permute-start.9 = (s16[528,256]{1,0:T(8,128)(2,1)}, s16[528,256]{1,0:T(8,128)(2,1)}, u32[]{:S(2)}, u32[]{:S(2)}) collective-permute-start(s16[528,256]{1,0:T(8,128)(2,1)} %get-tuple-element.72), channel_id=1, source_target_pairs={{0,4},{1,5},{2,6},{3,7},{4,0},{5,1},{6,2},{7,3},{8,12},{9,13},{10,... | collective-permute-start | bytes 811016 | tf_op jit(solution)/shard_map/ppermute | solution.py:418
  77.6 2.7 %copy-start.4 = (f32[8,64,256]{2,1,0:T(8,128)}, f32[8,64,256]{2,1,0:T(8,128)S(1)}, u32[]{:S(2)}) copy-start(f32[8,64,256]{2,1,0:T(8,128)S(1)} %get-tuple-element.77.late_ref) | copy-start | bytes 1572868
  77.6 14.3 %collective-permute-start.10 = (s16[528,256]{1,0:T(8,128)(2,1)}, s16[528,256]{1,0:T(8,128)(2,1)S(1)}, u32[]{:S(2)}, u32[]{:S(2)}) collective-permute-start(s16[528,256]{1,0:T(8,128)(2,1)} %get-tuple-element.73), channel_id=1, source_target_pairs={{0,6},{1,7},{2,0},{3,1},{4,2},{5,3},{6,4},{7,5},{8,14},{9,15},{10,... | collective-permute-start | bytes 811016 | tf_op jit(solution)/shard_map/ppermute | solution.py:418
  80.3 5.2 %copy-start.16 = (bf16[2,40,8]{2,1,0:T(8,128)(2,1)}, bf16[2,40,8]{2,1,0:T(8,128)(2,1)S(1)}, u32[]{:S(2)}) copy-start(bf16[2,40,8]{2,1,0:T(8,128)(2,1)S(1)} %collective-permute-done.16) | copy-start | bytes 3844
  80.3 11.5 %collective-permute-start.11 = (f32[4,64,256]{2,1,0:T(8,128)}, f32[4,64,256]{2,1,0:T(8,128)}, u32[]{:S(2)}, u32[]{:S(2)}) collective-permute-start(f32[4,64,256]{2,1,0:T(8,128)} %get-tuple-element.78), channel_id=1, source_target_pairs={{0,8},{8,16},{16,24},{24,32},{32,40},{40,48},{48,56},{56,64},{64,7... | collective-permute-start | bytes 786440 | tf_op jit(solution)/shard_map/ppermute | solution.py:298
  85.6 0.6 copy-start.17
  86.2 8.9 %collective-permute-start.12 = (f32[4,64,256]{2,1,0:T(8,128)}, f32[4,64,256]{2,1,0:T(8,128)}, u32[]{:S(2)}, u32[]{:S(2)}) collective-permute-start(f32[4,64,256]{2,1,0:T(8,128)} %get-tuple-element.79), channel_id=1, source_target_pairs={{8,0},{16,8},{24,16},{32,24},{40,32},{48,40},{56,48},{64,56},{72,6... | collective-permute-start | bytes 786440 | tf_op jit(solution)/shard_map/ppermute | solution.py:298
  90.3 15.9 %copy-start.2 = (f32[24,288,128]{2,1,0:T(8,128)S(1)}, f32[24,288,128]{2,1,0:T(8,128)}, u32[]{:S(2)}) copy-start(f32[24,288,128]{2,1,0:T(8,128)} %convolution_multiply_fusion.wv_ref) | copy-start | bytes 10616836
  95.0 1.0 copy-start.5
  99.4 17.0 %collective-permute-start.13 = (f32[24,8,128]{2,1,0:T(8,128)S(1)}, f32[24,8,128]{2,1,0:T(8,128)S(1)}, u32[]{:S(2)}, u32[]{:S(2)}) collective-permute-start(f32[24,8,128]{2,1,0:T(8,128)S(1)} %get-tuple-element.80.high_ref), channel_id=1, source_target_pairs={{0,1},{1,2},{2,3},{3,4},{4,5},{5,6},{6,7},{8,9},{9,10},{10,11},{11... | collective-permute-start | bytes 294920 | tf_op jit(solution)/shard_map/ppermute | solution.py:298
  101.8 14.6 %collective-permute-start.14 = (f32[24,8,128]{2,1,0:T(8,128)S(1)}, f32[24,8,128]{2,1,0:T(8,128)S(1)}, u32[]{:S(2)}, u32[]{:S(2)}) collective-permute-start(f32[24,8,128]{2,1,0:T(8,128)S(1)} %get-tuple-element.81.low_ref), channel_id=1, source_target_pairs={{1,0},{2,1},{3,2},{4,3},{5,4},{6,5},{7,6},{9,8},{10,9},{11,10},{12... | collective-permute-start | bytes 294920 | tf_op jit(solution)/shard_map/ppermute | solution.py:298
  106.2 2.0 %copy-start.3 = (f32[24,288,128]{2,1,0:T(8,128)S(1)}, f32[24,288,128]{2,1,0:T(8,128)}, u32[]{:S(2)}) copy-start(f32[24,288,128]{2,1,0:T(8,128)} %convolution_multiply_fusion.1.wh_ref) | copy-start | bytes 10616836

commit v6 on v5

--- a/solution.py
+++ b/solution.py
@@ -99,6 +99,7 @@
 
 def mix_kernel(
     which_ref, inv_ref, early_ref, late_ref, own_ref, a_ref, b_ref, c_ref, top_ref, bottom_ref,
+    weight_ref,
     mixed_ref, low_ref, high_ref, scale,
 ):
     half, count, width = early_ref.shape
@@ -109,6 +110,8 @@
     for s, ref in enumerate(parts):
         scale[s] = scales(ref[quarter * count :])
     clear_sides(mixed_ref)
+    low_ref[deep] = weight_ref[:8]
+    high_ref[deep] = weight_ref[width - 8 :]
 
     def third(r):
         x = own_ref[which_ref[0], r]
@@ -139,19 +142,19 @@
         )
 
 
-def mix(which, inv3, early, late, own, parts, top, bottom):
+def mix(which, inv3, early, late, own, parts, top, bottom, weights):
     half, count, width = early.shape
     deep = half + 2 * HALO
     vmem = pl.BlockSpec(memory_space=pltpu.VMEM)
-    shapes = [(deep, SPAN, 2 * count), (deep, 8, 2 * count), (deep, 8, 2 * count)]
+    shapes = [(deep, SPAN, 2 * count), (deep + 1, 8, 2 * count), (deep + 1, 8, 2 * count)]
     return pl.pallas_call(
         mix_kernel,
         out_shape=[jax.ShapeDtypeStruct(x, jnp.float32) for x in shapes],
-        in_specs=[pl.BlockSpec(memory_space=pltpu.SMEM)] + [vmem] * 9,
+        in_specs=[pl.BlockSpec(memory_space=pltpu.SMEM)] + [vmem] * 10,
         out_specs=[vmem] * 3,
         scratch_shapes=[pltpu.VMEM((3, 16, width), jnp.float32)],
         compiler_params=pltpu.CompilerParams(vmem_limit_bytes=10 * 2**20),
-    )(jnp.reshape(which, (1,)), inv3, early, late, own, *parts, top, bottom)
+    )(jnp.reshape(which, (1,)), inv3, early, late, own, *parts, top, bottom, weights)
 
 
 def diffuse(src, wh_ref, wv_ref, rows, columns, group, store):
@@ -231,22 +234,29 @@
 
 
 def sides_kernel(
-    invt_ref, left_ref, low_ref, high_ref, right_ref, wh_ref, wv_ref, inside_ref,
-    out_ref, mixed, y, z, turned,
+    invt_ref, left_ref, low_ref, high_ref, right_ref, inside_ref,
+    out_ref, mixed, y, z, wh, wv, turned,
 ):
     half, width, lanes = inside_ref.shape
     count = lanes // 2
     deep, span, _ = mixed.shape
-    for ref in (mixed, y, z):
+    for ref in (mixed, y, z, wh, wv):
         ref[...] = jnp.zeros(ref.shape, jnp.float32)
+    lower = lax.broadcasted_iota(jnp.int32, (8, lanes), 1) < count
     for at, ref in zip((8, 16, 32, 40), (left_ref, low_ref, high_ref, right_ref)):
-        mixed[:, at : at + 8] = ref[...]
+        mixed[:, at : at + 8] = ref[:deep]
+        packed = ref[deep]
+        for r in range(deep):
+            for weight, lane in ((wh, r), (wv, r + count)):
+                one = jnp.broadcast_to(packed[:, lane : lane + 1], (8, lanes))
+                two = jnp.broadcast_to(packed[:, lane + half : lane + half + 1], (8, lanes))
+                weight[r, at : at + 8] = jnp.where(lower, one, two)
 
     def store(i, c, value):
         z[i, pl.ds(c, span - 16)] = value
 
     iterate(
-        mixed, y, z, wh_ref, wv_ref, invt_ref, (8, span - 8), span - 16, deep - 4, store
+        mixed, y, z, wh, wv, invt_ref, (8, span - 8), span - 16, deep - 4, store
     )
     place = lax.broadcasted_iota(jnp.int32, (8, lanes), 0)
 
@@ -272,23 +282,25 @@
                 out_ref[e, :, t * 128 : (t + 1) * 128] = turned[t, pl.ds(e * 2 * half, 2 * half), :]
 
 
-def sides(inv3t, left, low, high, right, wh, wv, middle):
+def sides(inv3t, left, low, high, right, middle):
     half, width, lanes = middle.shape
     vmem = pl.BlockSpec(memory_space=pltpu.VMEM)
-    field = pltpu.VMEM(wh.shape, jnp.float32)
+    field = pltpu.VMEM((half + 2 * HALO, 56, lanes), jnp.float32)
     return pl.pallas_call(
         sides_kernel,
         out_shape=jax.ShapeDtypeStruct((lanes // 2, 2 * half, width), jnp.float32),
-        in_specs=[vmem] * 8,
+        in_specs=[vmem] * 6,
         out_specs=vmem,
         scratch_shapes=[
+            field,
+            field,
             field,
             field,
             field,
             pltpu.VMEM((width // 128, lanes * half, 128), jnp.float32),
         ],
         compiler_params=pltpu.CompilerParams(vmem_limit_bytes=14 * 2**20),
-    )(inv3t, left, low, high, right, wh, wv, middle)
+    )(inv3t, left, low, high, right, middle)
 
 
 def neighbours(axis, low_part, high_part):
@@ -320,11 +332,10 @@
     return jnp.pad(weights, ((0, 0), (0, 0), (LEAD, SPAN - LEAD - tile_w)))
 
 
-def side_parts(weights):
-    low, high = weights[..., :8], weights[..., -8:]
-    left, right = neighbours("col", low, high)
-    gap = jnp.zeros_like(low)
-    return [gap, left, low, gap, high, right, gap]
+def packed_weights(weights, count):
+    rows, width = weights.shape[1:]
+    packed = jnp.pad(weights.astype(jnp.float32), ((0, 0), (0, count - rows), (0, 0)))
+    return jnp.transpose(packed.reshape(2 * count, width)) * jnp.float32(KAPPA * EDGE_SCALE)
 
 
 def last_rows_kernel(which_ref, src_ref, out_ref):
@@ -429,15 +440,13 @@
     early_coded = lax.ppermute(early_coded, "col", swap)
     third = project(library_x, jnp.concatenate([third_own, third], axis=0), ys, quarter)
     third_coded = coded(third, order)
-    late_coded, weights, _ = barrier((late_coded, weights, third_coded))
-    weights_side = side_parts(weights)
+    late_coded, _ = barrier((late_coded, third_coded))
+    packed = packed_weights(weights, count)
     third_coded = over_y(third_coded)
     late, last = finished(late, y, late_coded, True)
     early, first = finished(early, x, [early_coded], False)
     top, bottom = neighbours("row", first, last)
 
-    weights_side, _, _ = barrier((weights_side, first, last))
-    wh_side, wv_side = held_weights(jnp.concatenate(weights_side, axis=2), count, half)
     inv_hi = lax.reduce_precision(inverse, 8, 7)
     inv3 = jnp.concatenate([inv_hi, inverse - inv_hi, inv_hi], axis=1).astype(jnp.bfloat16)
     block = lax.broadcasted_iota(jnp.int32, (2 * count, 2 * count), 0) // count
@@ -445,10 +454,10 @@
     twice = jnp.where(block, jnp.tile(inverse.T, (2, 2)), 0.0)
     twice_hi = lax.reduce_precision(twice, 8, 7)
     inv3t = jnp.concatenate([twice_hi, twice - twice_hi, twice_hi], axis=0).astype(jnp.bfloat16)
-    mixed, low, high = mix(y, inv3, early, late, third, third_coded, top, bottom)
+    mixed, low, high = mix(y, inv3, early, late, third, third_coded, top, bottom, packed)
     left, right = neighbours("col", low, high)
     middle = inside(inv3t, mixed, wh, wv, tile_w)
-    return sides(inv3t, left, low, high, right, wh_side, wv_side, middle)
+    return sides(inv3t, left, low, high, right, middle)
 
 
 def solution(mesh):

time: 122 us -> 121 us (level)
  the two profiles are of different devices: /device:TPU:39 before, /device:TPU:11 now
where the time goes in v6:
time: 121 us; the launch traced here: 120 us
  starting transfers between devices  37.5 us (31%)
  Pallas kernels  26.5 us (22%)
  local copies, waits for them, and re-layouts  24.3 us (20%)
  waiting for transfers between devices  15.9 us (13%)
  matrix products  10.3 us (9%)
  other arithmetic  5.37 us (4%)
    ppermute x3, waiting for transfers between devices, neighbours(): lax.ppermute(low_part, axis, backward)  11.4 us
    unnamed x40, local copies, waits for them, and re-layouts  10.6 us
    ppermute x3, starting transfers between devices, neighbours(): lax.ppermute(high_part, axis, forward)  10.5 us
    ppermute x3, starting transfers between devices, neighbours(): lax.ppermute(low_part, axis, backward)  9.36 us
    pallas_call x1, Pallas kernels, inside(): pl.pallas_call(inside_kernel, out_shape=jax.ShapeDtypeStruct((deep - 2 *...  8.15 us
    ppermute x6, starting transfers between devices, over_y(): return [lax.ppermute(p, 'col', turns[k + 1]) for k, p in enumerate(parts)]  7.76 us
    pallas_call x1, Pallas kernels, sides(): pl.pallas_call(sides_kernel, out_shape=jax.ShapeDtypeStruct((lanes // 2,...  5.28 us
    dot_general x2, matrix products, held_weights(): jnp.einsum('hrc,hl->rcl', x, spread, preferred_element_type=jnp.float32)  5.17 us
  transfers between devices with their start and end apart: 16, of which 5 were waited for; matrix products, arithmetic and copies ran while one was open for 21% of the time, Pallas kernels for 15%

profile of v6, /device:TPU:11, one launch (start us, length us, event | category | flops | bytes accessed | tf_op | source)
XLA Modules:
  0.0 120.4 jit_solution(3805202165390125964)
XLA Ops:
  0.0 2.3 %slice_bitcast_fusion = bf16[4,53,2,16,256]{4,3,1,2,0:T(8,128)(2,1)S(1)} fusion(bf16[4,2,53,32,256]{4,3,2,1,0:T(8,128)(2,1)} %bitcast.78), kind=kLoop, calls=%fused_computation.2 | loop fusion | bytes 6946816 | tf_op jit(solution)/shard_map/transpose | solution.py:406
  2.3 2.3 %copy.37 = bf16[4,53,2,16,256]{4,3,2,1,0:T(8,128)(2,1)} copy(bf16[4,53,2,16,256]{4,3,1,2,0:T(8,128)(2,1)S(1)} %slice_bitcast_fusion) | data formatting | bytes 6946816 | tf_op jit(solution)/shard_map/transpose | solution.py:406
  4.6 4.9 %all-to-all-start = ((bf16[4,53,32,256]{3,2,1,0:T(8,128)(2,1)}), bf16[4,53,32,256]{3,2,1,0:T(8,128)(2,1)}, u32[]{:S(2)}, u32[]{:S(2)}) async-start(bf16[4,53,32,256]{3,2,1,0:T(8,128)(2,1)} %bitcast.5), calls=%async_computation | async-start | bytes 6946816 | tf_op jit(solution)/shard_map/all_to_all | solution.py:412
  9.5 1.7 %copy_bitcast_fusion.3 = bf16[53,32,256]{2,1,0:T(8,128)(2,1)S(1)} fusion(bf16[4,2,53,32,256]{4,3,2,1,0:T(8,128)(2,1)} %bitcast.79, pred[]{:T(512)S(6)} %eq.17), kind=kLoop, calls=%fused_computation.16 | loop fusion | flops 434176 | bytes 2605057 | tf_op jit(solution)/shard_map/reshape | solution.py:395
  11.2 1.9 %collective-permute-start.1 = (bf16[53,32,256]{2,1,0:T(8,128)(2,1)S(1)}, bf16[53,32,256]{2,1,0:T(8,128)(2,1)S(1)}, u32[]{:S(2)}, u32[]{:S(2)}) collective-permute-start(bf16[53,32,256]{2,1,0:T(8,128)(2,1)S(1)} %copy_bitcast_fusion.3), channel_id=1, source_target_pairs={{0,1},{1,0},{2,3},{3,2},{4,5},{5,4},{6,7},{7,6},{8,9},{9,8},{10,11... | collective-permute-start | bytes 2605064 | tf_op jit(solution)/shard_map/ppermute | solution.py:415
  13.2 2.6 %copy_bitcast_fusion.2 = bf16[53,32,256]{2,1,0:T(8,128)(2,1)} fusion(bf16[4,2,53,32,256]{4,3,2,1,0:T(8,128)(2,1)} %bitcast.80, pred[]{:T(512)S(6)} %eq.17), kind=kLoop, calls=%fused_computation.15 | loop fusion | flops 434176 | bytes 2605057 | tf_op jit(solution)/shard_map/reshape | solution.py:395
  15.8 3.7 %shard_map.57 = bf16[4,53,16,256]{3,2,1,0:T(8,128)(2,1)} custom-call(s32[1]{0:T(128)} %bitcast.2.which_ref, bf16[4,2,53,32,256]{4,3,2,1,0:T(8,128)(2,1)} %bitcast.81), custom_call_target="tpu_custom_call" | custom-call | tf_op jit(solution)/shard_map/pallas_call | solution.py:349
  19.6 5.5 %collective-permute-start.3 = (bf16[2,4,256]{2,1,0:T(4,128)(2,1)S(1)}, bf16[2,4,256]{2,1,0:T(4,128)(2,1)S(1)}, u32[]{:S(2)}, u32[]{:S(2)}) collective-permute-start(bf16[2,4,256]{2,1,0:T(4,128)(2,1)S(1)} %get-tuple-element.93), channel_id=1, source_target_pairs={{0,8},{8,16},{16,24},{24,32},{32,40},{40,48},{48,56},{56,64},{64,7... | collective-permute-start | bytes 12296 | tf_op jit(solution)/shard_map/ppermute | solution.py:310
  25.1 1.9 %collective-permute-start.4 = (bf16[2,4,256]{2,1,0:T(4,128)(2,1)S(1)}, bf16[2,4,256]{2,1,0:T(4,128)(2,1)S(1)}, u32[]{:S(2)}, u32[]{:S(2)}) collective-permute-start(bf16[2,4,256]{2,1,0:T(4,128)(2,1)S(1)} %get-tuple-element.94), channel_id=1, source_target_pairs={{8,0},{16,8},{24,16},{32,24},{40,32},{48,40},{56,48},{64,56},{72,6... | collective-permute-start | bytes 12296 | tf_op jit(solution)/shard_map/ppermute | solution.py:310
  27.3 1.5 %slice_bitcast_fusion.1 = (bf16[53,4,8,256]{3,2,0,1:T(8,128)(2,1)S(1)}, bf16[53,4,8,256]{3,2,0,1:T(8,128)(2,1)S(1)}) fusion(bf16[4,53,16,256]{3,2,1,0:T(8,128)(2,1)} %shard_map.57), kind=kLoop, calls=%fused_computation.17 | loop fusion | bytes 3473408 | tf_op jit(solution)/shard_map/transpose | solution.py:422
  28.8 1.1 copy_bitcast_fusion
  30.9 4.8 %collective-permute-done.4 = bf16[2,4,256]{2,1,0:T(4,128)(2,1)S(1)} collective-permute-done((bf16[2,4,256]{2,1,0:T(4,128)(2,1)S(1)}, bf16[2,4,256]{2,1,0:T(4,128)(2,1)S(1)}, u32[]{:S(2)}, u32[]{:S(2)}) %collective-permute-start.4) | collective-permute-done | bytes 4128 | tf_op jit(solution)/shard_map/ppermute | solution.py:310
  36.0 2.6 %convolution_multiply_fusion.wv_ref = f32[24,288,128]{2,1,0:T(8,128)} fusion(bf16[1,2,24,288]{3,0,2,1:T(2,128)(2,1)S(1)} %copy.45, bf16[1,2,24,288]{3,0,2,1:T(2,128)(2,1)S(1)} %copy.44, pred[128]{0:T(512)(128)(4,1)S(1)} %compare_and_fusion, s32[128]{0:T(128)S(1)} %get-tuple-element.97, s32[128]{0:T(128)S(1)} %get-tuple-element.98), kind=kOutput, calls=%fused_computation.3 | convolution fusion | flops 4479488 | bytes 3595392 | tf_op jit(solution)/shard_map/hrc,hl->rcl/dot_general | solution.py:370
  38.6 2.6 %convolution_multiply_fusion.1.wh_ref = f32[24,288,128]{2,1,0:T(8,128)} fusion(bf16[1,2,24,288]{3,0,2,1:T(2,128)(2,1)S(1)} %copy.44, bf16[1,2,24,288]{3,0,2,1:T(2,128)(2,1)S(1)} %copy.45, pred[128]{0:T(512)(128)(4,1)S(1)} %compare_and_fusion, s32[128]{0:T(128)S(1)} %get-tuple-element.97, s32[128]{0:T(128)S(1)} %get-tuple-element.98), kind=kOutput, calls=%fused_computation.4 | convolution fusion | flops 4479488 | bytes 3595392 | tf_op jit(solution)/shard_map/hrc,hl->rcl/dot_general | solution.py:370
  42.2 1.7 %shard_map.58 = (s16[528,256]{1,0:T(8,128)(2,1)}, s16[528,256]{1,0:T(8,128)(2,1)}, s16[528,256]{1,0:T(8,128)(2,1)}) custom-call(s32[3]{0:T(128)S(1)} %pad_add_fusion.which_ref, f32[4,8,64,256]{3,2,1,0:T(8,128)S(1)} %bitcast.73), custom_call_target="tpu_custom_call" | custom-call | tf_op jit(solution)/shard_map/pallas_call | solution.py:46
  43.9 1.3 %copy-done = f32[32,256,64]{1,2,0:T(8,128)} copy-done((f32[32,256,64]{1,2,0:T(8,128)}, f32[32,256,64]{1,2,0:T(8,128)S(1)}, u32[]{:S(2)}) %copy-start) | copy-done | bytes 2097176
  45.2 1.2 collective-permute-start.5
  46.4 0.7 collective-permute-start.6
  47.1 2.0 %collective-permute-start.7 = (s16[528,256]{1,0:T(8,128)(2,1)}, s16[528,256]{1,0:T(8,128)(2,1)}, u32[]{:S(2)}, u32[]{:S(2)}) collective-permute-start(s16[528,256]{1,0:T(8,128)(2,1)} %get-tuple-element.58), channel_id=1, source_target_pairs={{0,6},{1,7},{2,0},{3,1},{4,2},{5,3},{6,4},{7,5},{8,14},{9,15},{10,... | collective-permute-start | bytes 811016 | tf_op jit(solution)/shard_map/ppermute | solution.py:429
  49.1 4.2 %fusion = f32[32,256,64]{1,2,0:T(8,128)S(1)} fusion(bf16[212,32,256]{2,1,0:T(8,128)(2,1)} %bitcast.6, bf16[64,53]{1,0:T(8,128)(2,1)S(1)} %get-tuple-element.86, bf16[64,53]{1,0:T(8,128)(2,1)S(1)} %get-tuple-element.87, bf16[64,53]{1,0:T(8,128)(2,1)S(1)} %get-tuple-element.88, bf16[64,53]{1,0:T(8,128)(2,1)S(1)} %get-tuple-element.89, ...), kind=kOutput, calls=%fused_computation | convolution fusion | flops 222528768 | bytes 5624833 | tf_op jit(solution)/shard_map/eb,bhw->hew/dot_general | solution.py:389
  53.5 3.0 %collective-permute-start = (s16[1040,256]{1,0:T(8,128)(2,1)S(1)}, s16[1040,256]{1,0:T(8,128)(2,1)S(1)}, u32[]{:S(2)}, u32[]{:S(2)}) collective-permute-start(s16[1040,256]{1,0:T(8,128)(2,1)S(1)} %shard_map.55), channel_id=1, source_target_pairs={{0,1},{1,0},{2,3},{3,2},{4,5},{5,4},{6,7},{7,6},{8,9},{9,8},{10,11... | collective-permute-start | bytes 1597448 | tf_op jit(solution)/shard_map/ppermute | solution.py:440
  57.2 0.7 tile.4
  57.9 1.0 tile.10
  59.0 1.7 %copy.47 = bf16[53,32,256]{2,0,1:T(8,128)(2,1)S(1)} copy(bf16[53,32,256]{2,1,0:T(8,128)(2,1)} %get-tuple-element.101) | data formatting | bytes 1736704 | tf_op jit(solution)/shard_map/reshape | solution.py:423
  60.8 0.8 collective-permute-done.7.refs_2_
  61.6 3.2 %collective-permute-done.2 = bf16[53,32,256]{2,1,0:T(8,128)(2,1)} collective-permute-done((bf16[53,32,256]{2,1,0:T(8,128)(2,1)}, bf16[53,32,256]{2,1,0:T(8,128)(2,1)}, u32[]{:S(2)}, u32[]{:S(2)}) %collective-permute-start.2) | collective-permute-done | bytes 868384 | tf_op jit(solution)/shard_map/ppermute | solution.py:432
  64.8 1.6 %copy.48 = bf16[53,32,256]{2,0,1:T(8,128)(2,1)S(1)} copy(bf16[53,32,256]{2,1,0:T(8,128)(2,1)} %collective-permute-done.2) | data formatting | bytes 1736704 | tf_op jit(solution)/shard_map/optimization_barrier | solution.py:439
  67.0 1.6 %shard_map.59 = (s16[528,256]{1,0:T(8,128)(2,1)}, s16[528,256]{1,0:T(8,128)(2,1)}, s16[528,256]{1,0:T(8,128)(2,1)}) custom-call(s32[3]{0:T(128)S(1)} %pad_add_fusion.which_ref, f32[4,8,64,256]{3,2,1,0:T(8,128)S(1)} %bitcast.75), custom_call_target="tpu_custom_call" | custom-call | tf_op jit(solution)/shard_map/pallas_call | solution.py:46
  68.6 1.2 collective-permute-start.8
  69.8 0.6 collective-permute-start.9
  70.4 2.1 %collective-permute-start.10 = (s16[528,256]{1,0:T(8,128)(2,1)}, s16[528,256]{1,0:T(8,128)(2,1)}, u32[]{:S(2)}, u32[]{:S(2)}) collective-permute-start(s16[528,256]{1,0:T(8,128)(2,1)} %get-tuple-element.65), channel_id=1, source_target_pairs={{0,6},{1,7},{2,0},{3,1},{4,2},{5,3},{6,4},{7,5},{8,14},{9,15},{10,... | collective-permute-start | bytes 811016 | tf_op jit(solution)/shard_map/ppermute | solution.py:429
  72.5 1.9 %shard_map.60 = (f32[8,64,256]{2,1,0:T(8,128)S(1)}, f32[4,64,256]{2,1,0:T(8,128)}) custom-call(s32[1]{0:T(128)} %bitcast.1.which_ref, f32[4,8,64,256]{3,2,1,0:T(8,128)S(1)} %bitcast.74, s16[528,256]{1,0:T(8,128)(2,1)S(1)} %collective-permute-done.5.refs_0_, s16[528,256]{1,0:T(8,128)(2,1)} %collective-permute-done.6.refs_1_, ...), custom_call_target="tpu_custom_call" | custom-call | tf_op jit(solution)/shard_map/pallas_call | solution.py:84
  74.4 0.8 copy-done.8
  75.2 2.8 %collective-permute-start.11 = (f32[4,64,256]{2,1,0:T(8,128)}, f32[4,64,256]{2,1,0:T(8,128)S(1)}, u32[]{:S(2)}, u32[]{:S(2)}) collective-permute-start(f32[4,64,256]{2,1,0:T(8,128)} %get-tuple-element.70), channel_id=1, source_target_pairs={{0,8},{8,16},{16,24},{24,32},{32,40},{40,48},{48,56},{56,64},{64,7... | collective-permute-start | bytes 786440 | tf_op jit(solution)/shard_map/ppermute | solution.py:310
  78.0 0.8 copy-done.6
  78.8 1.0 copy-done.7
  79.8 0.8 shard_map.56
  80.6 1.9 %collective-permute-start.12 = (f32[4,64,256]{2,1,0:T(8,128)}, f32[4,64,256]{2,1,0:T(8,128)S(1)}, u32[]{:S(2)}, u32[]{:S(2)}) collective-permute-start(f32[4,64,256]{2,1,0:T(8,128)} %get-tuple-element.71), channel_id=1, source_target_pairs={{8,0},{16,8},{24,16},{32,24},{40,32},{48,40},{56,48},{64,56},{72,6... | collective-permute-start | bytes 786440 | tf_op jit(solution)/shard_map/ppermute | solution.py:310
  82.8 6.6 %collective-permute-done.12.bottom_ref = f32[4,64,256]{2,1,0:T(8,128)S(1)} collective-permute-done((f32[4,64,256]{2,1,0:T(8,128)}, f32[4,64,256]{2,1,0:T(8,128)S(1)}, u32[]{:S(2)}, u32[]{:S(2)}) %collective-permute-start.12) | collective-permute-done | bytes 262176 | tf_op jit(solution)/shard_map/ppermute | solution.py:310
  89.4 1.6 %copy-done.3 = f32[32,256,64]{1,2,0:T(8,128)S(1)} copy-done((f32[32,256,64]{1,2,0:T(8,128)S(1)}, f32[32,256,64]{1,2,0:T(8,128)}, u32[]{:S(2)}) %copy-start.3) | copy-done | bytes 2097176
  91.0 1.0 copy-done.9
  92.0 3.2 %shard_map.61 = (f32[24,288,128]{2,1,0:T(8,128)S(1)}, f32[25,8,128]{2,1,0:T(8,128)S(1)}, f32[25,8,128]{2,1,0:T(8,128)S(1)}) custom-call(s32[1]{0:T(128)} %bitcast.1.which_ref, bf16[64,192]{1,0:T(8,128)(2,1)S(1)} %pad_maximum_fusion.3.inv_ref, f32[16,64,256]{2,1,0:T(8,128)S(1)} %get-tuple-element.42.early_ref, f32[8,64,256]{2,1,0:T(8,128)S(1)} %copy-done.9, ...), custom_call_target="tpu_custom_call" | custom-call | tf_op jit(solution)/shard_map/pallas_call | solution.py:150
  95.2 2.2 %collective-permute-start.13 = (f32[25,8,128]{2,1,0:T(8,128)S(1)}, f32[25,8,128]{2,1,0:T(8,128)S(1)}, u32[]{:S(2)}, u32[]{:S(2)}) collective-permute-start(f32[25,8,128]{2,1,0:T(8,128)S(1)} %get-tuple-element.72.high_ref), channel_id=1, source_target_pairs={{0,1},{1,2},{2,3},{3,4},{4,5},{5,6},{6,7},{8,9},{9,10},{10,11},{11... | collective-permute-start | bytes 307208 | tf_op jit(solution)/shard_map/ppermute | solution.py:310
  97.4 5.5 %collective-permute-start.14 = (f32[25,8,128]{2,1,0:T(8,128)S(1)}, f32[25,8,128]{2,1,0:T(8,128)S(1)}, u32[]{:S(2)}, u32[]{:S(2)}) collective-permute-start(f32[25,8,128]{2,1,0:T(8,128)S(1)} %get-tuple-element.73.low_ref), channel_id=1, source_target_pairs={{1,0},{2,1},{3,2},{4,3},{5,4},{6,5},{7,6},{9,8},{10,9},{11,10},{12... | collective-permute-start | bytes 307208 | tf_op jit(solution)/shard_map/ppermute | solution.py:310
  102.9 2.0 %copy-done.4 = f32[24,288,128]{2,1,0:T(8,128)S(1)} copy-done((f32[24,288,128]{2,1,0:T(8,128)S(1)}, f32[24,288,128]{2,1,0:T(8,128)}, u32[]{:S(2)}) %copy-start.4) | copy-done | bytes 3538968
  104.9 2.0 %copy-done.5 = f32[24,288,128]{2,1,0:T(8,128)S(1)} copy-done((f32[24,288,128]{2,1,0:T(8,128)S(1)}, f32[24,288,128]{2,1,0:T(8,128)}, u32[]{:S(2)}) %copy-start.5) | copy-done | bytes 3538968
  106.9 8.1 %shard_map.62.inside_ref = f32[16,256,128]{2,1,0:T(8,128)S(1)} custom-call(bf16[384,128]{1,0:T(8,128)(2,1)S(1)} %pad_maximum_fusion.invt_ref, f32[24,288,128]{2,1,0:T(8,128)S(1)} %get-tuple-element.74.mixed_ref, f32[24,288,128]{2,1,0:T(8,128)S(1)} %copy-done.5, f32[24,288,128]{2,1,0:T(8,128)S(1)} %copy-done.4), custom_call_target="tpu_custom_call" | custom-call | flops 3000000000 | bytes 25165824 | tf_op jit(solution)/shard_map/pallas_call | solution.py:223
  115.1 5.3 %shard_map.63 = f32[64,32,256]{2,1,0:T(8,128)} custom-call(bf16[384,128]{1,0:T(8,128)(2,1)S(1)} %pad_maximum_fusion.invt_ref, f32[25,8,128]{2,1,0:T(8,128)S(1)} %collective-permute-done.13.left_ref, f32[25,8,128]{2,1,0:T(8,128)S(1)} %get-tuple-element.73.low_ref, f32[25,8,128]{2,1,0:T(8,128)S(1)} %get-tuple-element.72.high_ref, ...), custom_call_target="tpu_custom_call" | custom-call | tf_op jit(solution)/shard_map/pallas_call | solution.py:289
  (69 shorter events, 4.4 us)
Async XLA Ops:
  4.6 44.5 %all-to-all-start = ((bf16[4,53,32,256]{3,2,1,0:T(8,128)(2,1)}), bf16[4,53,32,256]{3,2,1,0:T(8,128)(2,1)}, u32[]{:S(2)}, u32[]{:S(2)}) async-start(bf16[4,53,32,256]{3,2,1,0:T(8,128)(2,1)} %bitcast.5), calls=%async_computation | async-start | bytes 6946816 | tf_op jit(solution)/shard_map/all_to_all | solution.py:412
  11.2 29.9 %collective-permute-start.1 = (bf16[53,32,256]{2,1,0:T(8,128)(2,1)S(1)}, bf16[53,32,256]{2,1,0:T(8,128)(2,1)S(1)}, u32[]{:S(2)}, u32[]{:S(2)}) collective-permute-start(bf16[53,32,256]{2,1,0:T(8,128)(2,1)S(1)} %copy_bitcast_fusion.3), channel_id=1, source_target_pairs={{0,1},{1,0},{2,3},{3,2},{4,5},{5,4},{6,7},{7,6},{8,9},{9,8},{10,11... | collective-permute-start | bytes 2605064 | tf_op jit(solution)/shard_map/ppermute | solution.py:415
  15.8 3.7 %copy-start.18 = (s32[32,256]{1,0:T(8,128)S(1)}, s32[32,256]{1,0:T(8,128)}, u32[]{:S(2)}) copy-start(s32[32,256]{1,0:T(8,128)} %param.8) | copy-start | bytes 98308
  15.8 3.7 %copy-start.19 = (s32[32,256]{1,0:T(8,128)S(1)}, s32[32,256]{1,0:T(8,128)}, u32[]{:S(2)}) copy-start(s32[32,256]{1,0:T(8,128)} %param.9) | copy-start | bytes 98308
  15.8 11.3 %copy-start.10 = (bf16[64,424]{1,0:T(8,128)(2,1)S(1)}, bf16[64,424]{1,0:T(8,128)(2,1)}, u32[]{:S(2)}) copy-start(bf16[64,424]{1,0:T(8,128)(2,1)} %param.6) | copy-start | bytes 162820
  19.6 11.3 %collective-permute-start.3 = (bf16[2,4,256]{2,1,0:T(4,128)(2,1)S(1)}, bf16[2,4,256]{2,1,0:T(4,128)(2,1)S(1)}, u32[]{:S(2)}, u32[]{:S(2)}) collective-permute-start(bf16[2,4,256]{2,1,0:T(4,128)(2,1)S(1)} %get-tuple-element.93), channel_id=1, source_target_pairs={{0,8},{8,16},{16,24},{24,32},{32,40},{40,48},{48,56},{56,64},{64,7... | collective-permute-start | bytes 12296 | tf_op jit(solution)/shard_map/ppermute | solution.py:310
  25.1 10.6 %collective-permute-start.4 = (bf16[2,4,256]{2,1,0:T(4,128)(2,1)S(1)}, bf16[2,4,256]{2,1,0:T(4,128)(2,1)S(1)}, u32[]{:S(2)}, u32[]{:S(2)}) collective-permute-start(bf16[2,4,256]{2,1,0:T(4,128)(2,1)S(1)} %get-tuple-element.94), channel_id=1, source_target_pairs={{8,0},{16,8},{24,16},{32,24},{40,32},{48,40},{56,48},{64,56},{72,6... | collective-permute-start | bytes 12296 | tf_op jit(solution)/shard_map/ppermute | solution.py:310
  27.2 14.5 %copy-start.11 = (bf16[64,53]{1,0:T(8,128)(2,1)}, bf16[64,53]{1,0:T(8,128)(2,1)S(1)}, u32[]{:S(2)}) copy-start(bf16[64,53]{1,0:T(8,128)(2,1)S(1)} %get-tuple-element.81) | copy-start | bytes 20356
  27.3 14.5 %copy-start.13 = (bf16[64,53]{1,0:T(8,128)(2,1)}, bf16[64,53]{1,0:T(8,128)(2,1)S(1)}, u32[]{:S(2)}) copy-start(bf16[64,53]{1,0:T(8,128)(2,1)S(1)} %get-tuple-element.90) | copy-start | bytes 20356
  41.6 23.2 %collective-permute-start.2 = (bf16[53,32,256]{2,1,0:T(8,128)(2,1)}, bf16[53,32,256]{2,1,0:T(8,128)(2,1)}, u32[]{:S(2)}, u32[]{:S(2)}) collective-permute-start(bf16[53,32,256]{2,1,0:T(8,128)(2,1)} %copy_bitcast_fusion.2), channel_id=1, source_target_pairs={{0,1},{1,0},{2,3},{3,2},{4,5},{5,4},{6,7},{7,6},{8,9},{9,8},{10,11... | collective-permute-start | bytes 2605064 | tf_op jit(solution)/shard_map/ppermute | solution.py:432
  43.9 1.3 %copy-start = (f32[32,256,64]{1,2,0:T(8,128)}, f32[32,256,64]{1,2,0:T(8,128)S(1)}, u32[]{:S(2)}) copy-start(f32[32,256,64]{1,2,0:T(8,128)S(1)} %fusion.2) | copy-start | bytes 6291460
  45.2 15.6 %collective-permute-start.5 = (s16[528,256]{1,0:T(8,128)(2,1)}, s16[528,256]{1,0:T(8,128)(2,1)S(1)}, u32[]{:S(2)}, u32[]{:S(2)}) collective-permute-start(s16[528,256]{1,0:T(8,128)(2,1)} %get-tuple-element.56), channel_id=1, source_target_pairs={{0,2},{1,3},{2,4},{3,5},{4,6},{5,7},{6,0},{7,1},{8,10},{9,11},{10,... | collective-permute-start | bytes 811016 | tf_op jit(solution)/shard_map/ppermute | solution.py:429
  46.4 14.4 %collective-permute-start.6 = (s16[528,256]{1,0:T(8,128)(2,1)}, s16[528,256]{1,0:T(8,128)(2,1)}, u32[]{:S(2)}, u32[]{:S(2)}) collective-permute-start(s16[528,256]{1,0:T(8,128)(2,1)} %get-tuple-element.57), channel_id=1, source_target_pairs={{0,4},{1,5},{2,6},{3,7},{4,0},{5,1},{6,2},{7,3},{8,12},{9,13},{10,... | collective-permute-start | bytes 811016 | tf_op jit(solution)/shard_map/ppermute | solution.py:429
  47.1 14.6 %collective-permute-start.7 = (s16[528,256]{1,0:T(8,128)(2,1)}, s16[528,256]{1,0:T(8,128)(2,1)}, u32[]{:S(2)}, u32[]{:S(2)}) collective-permute-start(s16[528,256]{1,0:T(8,128)(2,1)} %get-tuple-element.58), channel_id=1, source_target_pairs={{0,6},{1,7},{2,0},{3,1},{4,2},{5,3},{6,4},{7,5},{8,14},{9,15},{10,... | collective-permute-start | bytes 811016 | tf_op jit(solution)/shard_map/ppermute | solution.py:429
  49.1 7.4 %copy-start.15 = (f32[64,64]{1,0:T(8,128)S(1)}, f32[64,64]{1,0:T(8,128)}, u32[]{:S(2)}) copy-start(f32[64,64]{1,0:T(8,128)} %param.7) | copy-start | bytes 49156
  53.5 24.5 %collective-permute-start = (s16[1040,256]{1,0:T(8,128)(2,1)S(1)}, s16[1040,256]{1,0:T(8,128)(2,1)S(1)}, u32[]{:S(2)}, u32[]{:S(2)}) collective-permute-start(s16[1040,256]{1,0:T(8,128)(2,1)S(1)} %shard_map.55), channel_id=1, source_target_pairs={{0,1},{1,0},{2,3},{3,2},{4,5},{5,4},{6,7},{7,6},{8,9},{9,8},{10,11... | collective-permute-start | bytes 1597448 | tf_op jit(solution)/shard_map/ppermute | solution.py:440
  59.0 7.5 %copy-start.12 = (bf16[64,53]{1,0:T(8,128)(2,1)S(1)}, bf16[64,53]{1,0:T(8,128)(2,1)}, u32[]{:S(2)}) copy-start(bf16[64,53]{1,0:T(8,128)(2,1)} %copy-done.11) | copy-start | bytes 20356
  59.0 7.5 %copy-start.14 = (bf16[64,53]{1,0:T(8,128)(2,1)S(1)}, bf16[64,53]{1,0:T(8,128)(2,1)}, u32[]{:S(2)}) copy-start(bf16[64,53]{1,0:T(8,128)(2,1)} %copy-done.13) | copy-start | bytes 20356
  66.5 6.0 %copy-start.1 = (f32[32,256,64]{1,2,0:T(8,128)S(1)}, f32[32,256,64]{1,2,0:T(8,128)}, u32[]{:S(2)}) copy-start(f32[32,256,64]{1,2,0:T(8,128)} %copy-done) | copy-start | bytes 6291460
  67.0 13.6 %copy-start.2 = (f32[32,256,64]{1,2,0:T(8,128)}, f32[32,256,64]{1,2,0:T(8,128)S(1)}, u32[]{:S(2)}) copy-start(f32[32,256,64]{1,2,0:T(8,128)S(1)} %fusion.6) | copy-start | bytes 6291460
  67.0 15.5 %copy-start.16 = (bf16[64,64]{1,0:T(8,128)(2,1)S(1)}, bf16[64,64]{1,0:T(8,128)(2,1)}, u32[]{:S(2)}) copy-start(bf16[64,64]{1,0:T(8,128)(2,1)} %get-tuple-element.95) | copy-start | bytes 24580
  67.0 15.5 %copy-start.17 = (bf16[64,64]{1,0:T(8,128)(2,1)S(1)}, bf16[64,64]{1,0:T(8,128)(2,1)}, u32[]{:S(2)}) copy-start(bf16[64,64]{1,0:T(8,128)(2,1)} %get-tuple-element.96) | copy-start | bytes 24580
  68.6 14.2 %collective-permute-start.8 = (s16[528,256]{1,0:T(8,128)(2,1)}, s16[528,256]{1,0:T(8,128)(2,1)}, u32[]{:S(2)}, u32[]{:S(2)}) collective-permute-start(s16[528,256]{1,0:T(8,128)(2,1)} %get-tuple-element.63), channel_id=1, source_target_pairs={{0,2},{1,3},{2,4},{3,5},{4,6},{5,7},{6,0},{7,1},{8,10},{9,11},{10,... | collective-permute-start | bytes 811016 | tf_op jit(solution)/shard_map/ppermute | solution.py:429
  69.8 13.0 %collective-permute-start.9 = (s16[528,256]{1,0:T(8,128)(2,1)}, s16[528,256]{1,0:T(8,128)(2,1)}, u32[]{:S(2)}, u32[]{:S(2)}) collective-permute-start(s16[528,256]{1,0:T(8,128)(2,1)} %get-tuple-element.64), channel_id=1, source_target_pairs={{0,4},{1,5},{2,6},{3,7},{4,0},{5,1},{6,2},{7,3},{8,12},{9,13},{10,... | collective-permute-start | bytes 811016 | tf_op jit(solution)/shard_map/ppermute | solution.py:429
  70.4 12.4 %collective-permute-start.10 = (s16[528,256]{1,0:T(8,128)(2,1)}, s16[528,256]{1,0:T(8,128)(2,1)}, u32[]{:S(2)}, u32[]{:S(2)}) collective-permute-start(s16[528,256]{1,0:T(8,128)(2,1)} %get-tuple-element.65), channel_id=1, source_target_pairs={{0,6},{1,7},{2,0},{3,1},{4,2},{5,3},{6,4},{7,5},{8,14},{9,15},{10,... | collective-permute-start | bytes 811016 | tf_op jit(solution)/shard_map/ppermute | solution.py:429
  74.4 0.8 copy-start.8
  75.2 7.6 %collective-permute-start.11 = (f32[4,64,256]{2,1,0:T(8,128)}, f32[4,64,256]{2,1,0:T(8,128)S(1)}, u32[]{:S(2)}, u32[]{:S(2)}) collective-permute-start(f32[4,64,256]{2,1,0:T(8,128)} %get-tuple-element.70), channel_id=1, source_target_pairs={{0,8},{8,16},{16,24},{24,32},{32,40},{40,48},{48,56},{56,64},{64,7... | collective-permute-start | bytes 786440 | tf_op jit(solution)/shard_map/ppermute | solution.py:310
  78.0 0.8 copy-start.6
  78.8 1.0 copy-start.7
  80.6 8.8 %collective-permute-start.12 = (f32[4,64,256]{2,1,0:T(8,128)}, f32[4,64,256]{2,1,0:T(8,128)S(1)}, u32[]{:S(2)}, u32[]{:S(2)}) collective-permute-start(f32[4,64,256]{2,1,0:T(8,128)} %get-tuple-element.71), channel_id=1, source_target_pairs={{8,0},{16,8},{24,16},{32,24},{40,32},{48,40},{56,48},{64,56},{72,6... | collective-permute-start | bytes 786440 | tf_op jit(solution)/shard_map/ppermute | solution.py:310
  89.4 1.6 %copy-start.3 = (f32[32,256,64]{1,2,0:T(8,128)S(1)}, f32[32,256,64]{1,2,0:T(8,128)}, u32[]{:S(2)}) copy-start(f32[32,256,64]{1,2,0:T(8,128)} %copy-done.2) | copy-start | bytes 6291460
  91.0 1.0 copy-start.9
  95.2 19.9 %collective-permute-start.13 = (f32[25,8,128]{2,1,0:T(8,128)S(1)}, f32[25,8,128]{2,1,0:T(8,128)S(1)}, u32[]{:S(2)}, u32[]{:S(2)}) collective-permute-start(f32[25,8,128]{2,1,0:T(8,128)S(1)} %get-tuple-element.72.high_ref), channel_id=1, source_target_pairs={{0,1},{1,2},{2,3},{3,4},{4,5},{5,6},{6,7},{8,9},{9,10},{10,11},{11... | collective-permute-start | bytes 307208 | tf_op jit(solution)/shard_map/ppermute | solution.py:310
  97.4 17.7 %collective-permute-start.14 = (f32[25,8,128]{2,1,0:T(8,128)S(1)}, f32[25,8,128]{2,1,0:T(8,128)S(1)}, u32[]{:S(2)}, u32[]{:S(2)}) collective-permute-start(f32[25,8,128]{2,1,0:T(8,128)S(1)} %get-tuple-element.73.low_ref), channel_id=1, source_target_pairs={{1,0},{2,1},{3,2},{4,3},{5,4},{6,5},{7,6},{9,8},{10,9},{11,10},{12... | collective-permute-start | bytes 307208 | tf_op jit(solution)/shard_map/ppermute | solution.py:310
  102.9 2.0 %copy-start.4 = (f32[24,288,128]{2,1,0:T(8,128)S(1)}, f32[24,288,128]{2,1,0:T(8,128)}, u32[]{:S(2)}) copy-start(f32[24,288,128]{2,1,0:T(8,128)} %convolution_multiply_fusion.wv_ref) | copy-start | bytes 10616836
  104.9 2.0 %copy-start.5 = (f32[24,288,128]{2,1,0:T(8,128)S(1)}, f32[24,288,128]{2,1,0:T(8,128)}, u32[]{:S(2)}) copy-start(f32[24,288,128]{2,1,0:T(8,128)} %convolution_multiply_fusion.1.wh_ref) | copy-start | bytes 10616836

commit v7 on v6

--- a/solution.py
+++ b/solution.py
@@ -456,6 +456,8 @@
     inv3t = jnp.concatenate([twice_hi, twice - twice_hi, twice_hi], axis=0).astype(jnp.bfloat16)
     mixed, low, high = mix(y, inv3, early, late, third, third_coded, top, bottom, packed)
     left, right = neighbours("col", low, high)
+    weights_in, _ = barrier((inside_weights(weights), low))
+    wv = held_weights(weights_in, count, half)[1]
     middle = inside(inv3t, mixed, wh, wv, tile_w)
     return sides(inv3t, left, low, high, right, middle)
 

time: 121 us -> 118 us (0.975)
  the two profiles are of different devices: /device:TPU:11 before, /device:TPU:39 now
where the time goes in v7:
time: 118 us; the launch traced here: 117 us
  starting transfers between devices  40 us (34%)
  Pallas kernels  26.7 us (23%)
  local copies, waits for them, and re-layouts  20.7 us (18%)
  waiting for transfers between devices  15.1 us (13%)
  matrix products  8.55 us (7%)
  other arithmetic  5.35 us (5%)
    ppermute x3, starting transfers between devices, neighbours(): lax.ppermute(high_part, axis, forward)  13.3 us
    ppermute x3, waiting for transfers between devices, neighbours(): lax.ppermute(low_part, axis, backward)  9.4 us
    ppermute x6, starting transfers between devices, over_y(): return [lax.ppermute(p, 'col', turns[k + 1]) for k, p in enumerate(parts)]  8.73 us
    pallas_call x1, Pallas kernels, inside(): pl.pallas_call(inside_kernel, out_shape=jax.ShapeDtypeStruct((deep - 2 *...  8.15 us
    ppermute x3, starting transfers between devices, neighbours(): lax.ppermute(low_part, axis, backward)  7.35 us
    unnamed x38, local copies, waits for them, and re-layouts  6.66 us
    pallas_call x1, Pallas kernels, sides(): pl.pallas_call(sides_kernel, out_shape=jax.ShapeDtypeStruct((lanes // 2,...  5.27 us
    dot_general x3, matrix products, project(): jnp.einsum('eb,bhw->hew', library, block, preferred_element_type=jnp.floa...  5.17 us
  transfers between devices with their start and end apart: 16, of which 5 were waited for; matrix products, arithmetic and copies ran while one was open for 20% of the time, Pallas kernels for 15%

profile of v7, /device:TPU:39, one launch (start us, length us, event | category | flops | bytes accessed | tf_op | source)
XLA Modules:
  0.0 116.8 jit_solution(6932889458759300537)
XLA Ops:
  0.0 2.3 %slice_bitcast_fusion = bf16[4,53,2,16,256]{4,3,1,2,0:T(8,128)(2,1)S(1)} fusion(bf16[4,2,53,32,256]{4,3,2,1,0:T(8,128)(2,1)} %bitcast.82), kind=kLoop, calls=%fused_computation.2 | loop fusion | bytes 6946816 | tf_op jit(solution)/shard_map/transpose | solution.py:406
  2.3 2.3 %copy.71 = bf16[4,53,2,16,256]{4,3,2,1,0:T(8,128)(2,1)} copy(bf16[4,53,2,16,256]{4,3,1,2,0:T(8,128)(2,1)S(1)} %slice_bitcast_fusion) | data formatting | bytes 6946816 | tf_op jit(solution)/shard_map/transpose | solution.py:406
  4.6 4.7 %all-to-all-start = ((bf16[4,53,32,256]{3,2,1,0:T(8,128)(2,1)}), bf16[4,53,32,256]{3,2,1,0:T(8,128)(2,1)}, u32[]{:S(2)}, u32[]{:S(2)}) async-start(bf16[4,53,32,256]{3,2,1,0:T(8,128)(2,1)} %bitcast.5), calls=%async_computation | async-start | bytes 6946816 | tf_op jit(solution)/shard_map/all_to_all | solution.py:412
  9.4 1.7 %copy_bitcast_fusion.3 = bf16[53,32,256]{2,1,0:T(8,128)(2,1)S(1)} fusion(bf16[4,2,53,32,256]{4,3,2,1,0:T(8,128)(2,1)} %bitcast.83, pred[]{:T(512)S(6)} %eq.18), kind=kLoop, calls=%fused_computation.16 | loop fusion | flops 434176 | bytes 2605057 | tf_op jit(solution)/shard_map/reshape | solution.py:395
  11.1 1.2 %collective-permute-start.1 = (bf16[53,32,256]{2,1,0:T(8,128)(2,1)S(1)}, bf16[53,32,256]{2,1,0:T(8,128)(2,1)S(1)}, u32[]{:S(2)}, u32[]{:S(2)}) collective-permute-start(bf16[53,32,256]{2,1,0:T(8,128)(2,1)S(1)} %copy_bitcast_fusion.3), channel_id=1, source_target_pairs={{0,1},{1,0},{2,3},{3,2},{4,5},{5,4},{6,7},{7,6},{8,9},{9,8},{10,11... | collective-permute-start | bytes 2605064 | tf_op jit(solution)/shard_map/ppermute | solution.py:415
  12.3 2.6 %copy_bitcast_fusion.2 = bf16[53,32,256]{2,1,0:T(8,128)(2,1)} fusion(bf16[4,2,53,32,256]{4,3,2,1,0:T(8,128)(2,1)} %bitcast.84, pred[]{:T(512)S(6)} %eq.18), kind=kLoop, calls=%fused_computation.15 | loop fusion | flops 434176 | bytes 2605057 | tf_op jit(solution)/shard_map/reshape | solution.py:395
  14.9 3.6 %shard_map.57 = bf16[4,53,16,256]{3,2,1,0:T(8,128)(2,1)} custom-call(s32[1]{0:T(128)} %bitcast.2.which_ref, bf16[4,2,53,32,256]{4,3,2,1,0:T(8,128)(2,1)} %bitcast.85), custom_call_target="tpu_custom_call" | custom-call | tf_op jit(solution)/shard_map/pallas_call | solution.py:349
  18.6 3.8 %collective-permute-start.3 = (bf16[2,4,256]{2,1,0:T(4,128)(2,1)S(1)}, bf16[2,4,256]{2,1,0:T(4,128)(2,1)S(1)}, u32[]{:S(2)}, u32[]{:S(2)}) collective-permute-start(bf16[2,4,256]{2,1,0:T(4,128)(2,1)S(1)} %get-tuple-element.95), channel_id=1, source_target_pairs={{0,8},{8,16},{16,24},{24,32},{32,40},{40,48},{48,56},{56,64},{64,7... | collective-permute-start | bytes 12296 | tf_op jit(solution)/shard_map/ppermute | solution.py:310
  22.4 1.9 %collective-permute-start.4 = (bf16[2,4,256]{2,1,0:T(4,128)(2,1)S(1)}, bf16[2,4,256]{2,1,0:T(4,128)(2,1)S(1)}, u32[]{:S(2)}, u32[]{:S(2)}) collective-permute-start(bf16[2,4,256]{2,1,0:T(4,128)(2,1)S(1)} %get-tuple-element.96), channel_id=1, source_target_pairs={{8,0},{16,8},{24,16},{32,24},{40,32},{48,40},{56,48},{64,56},{72,6... | collective-permute-start | bytes 12296 | tf_op jit(solution)/shard_map/ppermute | solution.py:310
  24.4 1.6 %slice_bitcast_fusion.1 = (bf16[53,4,8,256]{3,2,0,1:T(8,128)(2,1)S(1)}, bf16[53,4,8,256]{3,2,0,1:T(8,128)(2,1)S(1)}) fusion(bf16[4,53,16,256]{3,2,1,0:T(8,128)(2,1)} %shard_map.57), kind=kLoop, calls=%fused_computation.17 | loop fusion | bytes 3473408 | tf_op jit(solution)/shard_map/transpose | solution.py:422
  26.0 1.2 copy_bitcast_fusion
  27.8 2.5 %collective-permute-done.3 = bf16[2,4,256]{2,1,0:T(4,128)(2,1)S(1)} collective-permute-done((bf16[2,4,256]{2,1,0:T(4,128)(2,1)S(1)}, bf16[2,4,256]{2,1,0:T(4,128)(2,1)S(1)}, u32[]{:S(2)}, u32[]{:S(2)}) %collective-permute-start.3) | collective-permute-done | bytes 4128 | tf_op jit(solution)/shard_map/ppermute | solution.py:310
  30.3 2.9 %collective-permute-done.4 = bf16[2,4,256]{2,1,0:T(4,128)(2,1)S(1)} collective-permute-done((bf16[2,4,256]{2,1,0:T(4,128)(2,1)S(1)}, bf16[2,4,256]{2,1,0:T(4,128)(2,1)S(1)}, u32[]{:S(2)}, u32[]{:S(2)}) %collective-permute-start.4) | collective-permute-done | bytes 4128 | tf_op jit(solution)/shard_map/ppermute | solution.py:310
  33.5 2.6 %convolution_multiply_fusion.1.wh_ref = f32[24,288,128]{2,1,0:T(8,128)} fusion(bf16[1,2,24,288]{3,0,2,1:T(2,128)(2,1)S(1)} %copy.79, bf16[1,2,24,288]{3,0,2,1:T(2,128)(2,1)S(1)} %copy.78, pred[128]{0:T(512)(128)(4,1)S(1)} %compare_and_fusion, s32[128]{0:T(128)S(1)} %get-tuple-element.99, s32[128]{0:T(128)S(1)} %get-tuple-element.100), kind=kOutput, calls=%fused_computation.4 | convolution fusion | flops 4479488 | bytes 3595392 | tf_op jit(solution)/shard_map/hrc,hl->rcl/dot_general | solution.py:370
  36.5 3.5 %collective-permute-start.2 = (bf16[53,32,256]{2,1,0:T(8,128)(2,1)}, bf16[53,32,256]{2,1,0:T(8,128)(2,1)}, u32[]{:S(2)}, u32[]{:S(2)}) collective-permute-start(bf16[53,32,256]{2,1,0:T(8,128)(2,1)} %copy_bitcast_fusion.2), channel_id=1, source_target_pairs={{0,1},{1,0},{2,3},{3,2},{4,5},{5,4},{6,7},{7,6},{8,9},{9,8},{10,11... | collective-permute-start | bytes 2605064 | tf_op jit(solution)/shard_map/ppermute | solution.py:432
  40.6 1.6 %shard_map.58 = (s16[528,256]{1,0:T(8,128)(2,1)}, s16[528,256]{1,0:T(8,128)(2,1)}, s16[528,256]{1,0:T(8,128)(2,1)}) custom-call(s32[3]{0:T(128)S(1)} %pad_add_fusion.which_ref, f32[4,8,64,256]{3,2,1,0:T(8,128)S(1)} %bitcast.77), custom_call_target="tpu_custom_call" | custom-call | tf_op jit(solution)/shard_map/pallas_call | solution.py:46
  42.2 1.3 %copy-done = f32[32,256,64]{1,2,0:T(8,128)} copy-done((f32[32,256,64]{1,2,0:T(8,128)}, f32[32,256,64]{1,2,0:T(8,128)S(1)}, u32[]{:S(2)}) %copy-start) | copy-done | bytes 2097176
  43.5 1.4 %collective-permute-start.5 = (s16[528,256]{1,0:T(8,128)(2,1)}, s16[528,256]{1,0:T(8,128)(2,1)S(1)}, u32[]{:S(2)}, u32[]{:S(2)}) collective-permute-start(s16[528,256]{1,0:T(8,128)(2,1)} %get-tuple-element.56), channel_id=1, source_target_pairs={{0,2},{1,3},{2,4},{3,5},{4,6},{5,7},{6,0},{7,1},{8,10},{9,11},{10,... | collective-permute-start | bytes 811016 | tf_op jit(solution)/shard_map/ppermute | solution.py:429
  44.9 2.5 %collective-permute-start.6 = (s16[528,256]{1,0:T(8,128)(2,1)}, s16[528,256]{1,0:T(8,128)(2,1)}, u32[]{:S(2)}, u32[]{:S(2)}) collective-permute-start(s16[528,256]{1,0:T(8,128)(2,1)} %get-tuple-element.57), channel_id=1, source_target_pairs={{0,4},{1,5},{2,6},{3,7},{4,0},{5,1},{6,2},{7,3},{8,12},{9,13},{10,... | collective-permute-start | bytes 811016 | tf_op jit(solution)/shard_map/ppermute | solution.py:429
  47.4 1.1 collective-permute-start.7
  48.5 1.5 %all-to-all-done = bf16[4,53,32,256]{3,2,1,0:T(8,128)(2,1)} async-done(((bf16[4,53,32,256]{3,2,1,0:T(8,128)(2,1)}), bf16[4,53,32,256]{3,2,1,0:T(8,128)(2,1)}, u32[]{:S(2)}, u32[]{:S(2)}) %all-to-all-start) | async-done | bytes 3473440 | tf_op jit(solution)/shard_map/all_to_all | solution.py:412
  49.9 4.2 %fusion = f32[32,256,64]{1,2,0:T(8,128)S(1)} fusion(bf16[212,32,256]{2,1,0:T(8,128)(2,1)} %bitcast.6, bf16[64,53]{1,0:T(8,128)(2,1)S(1)} %get-tuple-element.86, bf16[64,53]{1,0:T(8,128)(2,1)S(1)} %get-tuple-element.87, bf16[64,53]{1,0:T(8,128)(2,1)S(1)} %get-tuple-element.88, bf16[64,53]{1,0:T(8,128)(2,1)S(1)} %get-tuple-element.89, ...), kind=kOutput, calls=%fused_computation | convolution fusion | flops 222528768 | bytes 5624833 | tf_op jit(solution)/shard_map/eb,bhw->hew/dot_general | solution.py:389
  54.4 1.2 %collective-permute-start = (s16[1040,256]{1,0:T(8,128)(2,1)S(1)}, s16[1040,256]{1,0:T(8,128)(2,1)S(1)}, u32[]{:S(2)}, u32[]{:S(2)}) collective-permute-start(s16[1040,256]{1,0:T(8,128)(2,1)S(1)} %shard_map.55), channel_id=1, source_target_pairs={{0,1},{1,0},{2,3},{3,2},{4,5},{5,4},{6,7},{7,6},{8,9},{9,8},{10,11... | collective-permute-start | bytes 1597448 | tf_op jit(solution)/shard_map/ppermute | solution.py:440
  56.3 0.7 tile.4
  57.0 1.0 tile.10
  58.0 1.7 %copy.81 = bf16[53,32,256]{2,0,1:T(8,128)(2,1)S(1)} copy(bf16[53,32,256]{2,1,0:T(8,128)(2,1)} %get-tuple-element.103) | data formatting | bytes 1736704 | tf_op jit(solution)/shard_map/reshape | solution.py:423
  59.8 1.7 %collective-permute-done.6.refs_1_ = s16[528,256]{1,0:T(8,128)(2,1)} collective-permute-done((s16[528,256]{1,0:T(8,128)(2,1)}, s16[528,256]{1,0:T(8,128)(2,1)}, u32[]{:S(2)}, u32[]{:S(2)}) %collective-permute-start.6) | collective-permute-done | bytes 270368 | tf_op jit(solution)/shard_map/ppermute | solution.py:429
  61.5 1.6 %copy.82 = bf16[53,32,256]{2,0,1:T(8,128)(2,1)S(1)} copy(bf16[53,32,256]{2,1,0:T(8,128)(2,1)} %collective-permute-done.2) | data formatting | bytes 1736704 | tf_op jit(solution)/shard_map/optimization_barrier | solution.py:439
  63.7 1.7 %shard_map.59 = (s16[528,256]{1,0:T(8,128)(2,1)}, s16[528,256]{1,0:T(8,128)(2,1)}, s16[528,256]{1,0:T(8,128)(2,1)}) custom-call(s32[3]{0:T(128)S(1)} %pad_add_fusion.which_ref, f32[4,8,64,256]{3,2,1,0:T(8,128)S(1)} %bitcast.79), custom_call_target="tpu_custom_call" | custom-call | tf_op jit(solution)/shard_map/pallas_call | solution.py:46
  65.4 1.3 %collective-permute-start.8 = (s16[528,256]{1,0:T(8,128)(2,1)}, s16[528,256]{1,0:T(8,128)(2,1)}, u32[]{:S(2)}, u32[]{:S(2)}) collective-permute-start(s16[528,256]{1,0:T(8,128)(2,1)} %get-tuple-element.63), channel_id=1, source_target_pairs={{0,2},{1,3},{2,4},{3,5},{4,6},{5,7},{6,0},{7,1},{8,10},{9,11},{10,... | collective-permute-start | bytes 811016 | tf_op jit(solution)/shard_map/ppermute | solution.py:429
  66.8 1.7 %collective-permute-start.9 = (s16[528,256]{1,0:T(8,128)(2,1)}, s16[528,256]{1,0:T(8,128)(2,1)}, u32[]{:S(2)}, u32[]{:S(2)}) collective-permute-start(s16[528,256]{1,0:T(8,128)(2,1)} %get-tuple-element.64), channel_id=1, source_target_pairs={{0,4},{1,5},{2,6},{3,7},{4,0},{5,1},{6,2},{7,3},{8,12},{9,13},{10,... | collective-permute-start | bytes 811016 | tf_op jit(solution)/shard_map/ppermute | solution.py:429
  68.5 0.7 collective-permute-start.10
  69.2 2.0 %shard_map.60 = (f32[8,64,256]{2,1,0:T(8,128)S(1)}, f32[4,64,256]{2,1,0:T(8,128)}) custom-call(s32[1]{0:T(128)} %bitcast.1.which_ref, f32[4,8,64,256]{3,2,1,0:T(8,128)S(1)} %bitcast.78, s16[528,256]{1,0:T(8,128)(2,1)S(1)} %collective-permute-done.5.refs_0_, s16[528,256]{1,0:T(8,128)(2,1)} %collective-permute-done.6.refs_1_, ...), custom_call_target="tpu_custom_call" | custom-call | tf_op jit(solution)/shard_map/pallas_call | solution.py:84
  71.1 0.8 copy-done.7
  71.9 5.3 %collective-permute-start.11 = (f32[4,64,256]{2,1,0:T(8,128)}, f32[4,64,256]{2,1,0:T(8,128)S(1)}, u32[]{:S(2)}, u32[]{:S(2)}) collective-permute-start(f32[4,64,256]{2,1,0:T(8,128)} %get-tuple-element.70), channel_id=1, source_target_pairs={{0,8},{8,16},{16,24},{24,32},{32,40},{40,48},{48,56},{56,64},{64,7... | collective-permute-start | bytes 786440 | tf_op jit(solution)/shard_map/ppermute | solution.py:310
  77.3 0.8 copy-done.5
  78.1 1.0 copy-done.6
  79.1 0.8 shard_map.56
  79.9 1.9 %collective-permute-start.12 = (f32[4,64,256]{2,1,0:T(8,128)}, f32[4,64,256]{2,1,0:T(8,128)S(1)}, u32[]{:S(2)}, u32[]{:S(2)}) collective-permute-start(f32[4,64,256]{2,1,0:T(8,128)} %get-tuple-element.71), channel_id=1, source_target_pairs={{8,0},{16,8},{24,16},{32,24},{40,32},{48,40},{56,48},{64,56},{72,6... | collective-permute-start | bytes 786440 | tf_op jit(solution)/shard_map/ppermute | solution.py:310
  82.2 6.5 %collective-permute-done.12.bottom_ref = f32[4,64,256]{2,1,0:T(8,128)S(1)} collective-permute-done((f32[4,64,256]{2,1,0:T(8,128)}, f32[4,64,256]{2,1,0:T(8,128)S(1)}, u32[]{:S(2)}, u32[]{:S(2)}) %collective-permute-start.12) | collective-permute-done | bytes 262176 | tf_op jit(solution)/shard_map/ppermute | solution.py:310
  88.7 1.6 %copy-done.3 = f32[32,256,64]{1,2,0:T(8,128)S(1)} copy-done((f32[32,256,64]{1,2,0:T(8,128)S(1)}, f32[32,256,64]{1,2,0:T(8,128)}, u32[]{:S(2)}) %copy-start.3) | copy-done | bytes 2097176
  90.3 1.0 copy-done.8
  91.3 3.3 %shard_map.61 = (f32[24,288,128]{2,1,0:T(8,128)S(1)}, f32[25,8,128]{2,1,0:T(8,128)S(1)}, f32[25,8,128]{2,1,0:T(8,128)S(1)}) custom-call(s32[1]{0:T(128)} %bitcast.1.which_ref, bf16[64,192]{1,0:T(8,128)(2,1)S(1)} %pad_maximum_fusion.4.inv_ref, f32[16,64,256]{2,1,0:T(8,128)S(1)} %get-tuple-element.42.early_ref, f32[8,64,256]{2,1,0:T(8,128)S(1)} %copy-done.8, ...), custom_call_target="tpu_custom_call" | custom-call | tf_op jit(solution)/shard_map/pallas_call | solution.py:150
  94.7 3.5 %collective-permute-start.14 = (f32[25,8,128]{2,1,0:T(8,128)S(1)}, f32[25,8,128]{2,1,0:T(8,128)S(1)}, u32[]{:S(2)}, u32[]{:S(2)}) collective-permute-start(f32[25,8,128]{2,1,0:T(8,128)S(1)} %get-tuple-element.73.low_ref), channel_id=1, source_target_pairs={{1,0},{2,1},{3,2},{4,3},{5,4},{6,5},{7,6},{9,8},{10,9},{11,10},{12... | collective-permute-start | bytes 307208 | tf_op jit(solution)/shard_map/ppermute | solution.py:310
  98.4 4.2 %collective-permute-start.13 = (f32[25,8,128]{2,1,0:T(8,128)S(1)}, f32[25,8,128]{2,1,0:T(8,128)S(1)}, u32[]{:S(2)}, u32[]{:S(2)}) collective-permute-start(f32[25,8,128]{2,1,0:T(8,128)S(1)} %get-tuple-element.72.high_ref), channel_id=1, source_target_pairs={{0,1},{1,2},{2,3},{3,4},{4,5},{5,6},{6,7},{8,9},{9,10},{10,11},{11... | collective-permute-start | bytes 307208 | tf_op jit(solution)/shard_map/ppermute | solution.py:310
  102.5 0.8 convolution_multiply_fusion.wv_ref
  103.4 8.2 %shard_map.62.inside_ref = f32[16,256,128]{2,1,0:T(8,128)S(1)} custom-call(bf16[384,128]{1,0:T(8,128)(2,1)S(1)} %pad_maximum_fusion.invt_ref, f32[24,288,128]{2,1,0:T(8,128)S(1)} %get-tuple-element.74.mixed_ref, f32[24,288,128]{2,1,0:T(8,128)S(1)} %copy-done.4, f32[24,288,128]{2,1,0:T(8,128)S(1)} %convolution_multiply_fusion.wv_ref), custom_call_target="tpu_custom_call" | custom-call | flops 3000000000 | bytes 25165824 | tf_op jit(solution)/shard_map/pallas_call | solution.py:223
  111.5 5.3 %shard_map.63 = f32[64,32,256]{2,1,0:T(8,128)} custom-call(bf16[384,128]{1,0:T(8,128)(2,1)S(1)} %pad_maximum_fusion.invt_ref, f32[25,8,128]{2,1,0:T(8,128)S(1)} %collective-permute-done.13.left_ref, f32[25,8,128]{2,1,0:T(8,128)S(1)} %get-tuple-element.73.low_ref, f32[25,8,128]{2,1,0:T(8,128)S(1)} %get-tuple-element.72.high_ref, ...), custom_call_target="tpu_custom_call" | custom-call | tf_op jit(solution)/shard_map/pallas_call | solution.py:289
  (71 shorter events, 4.0 us)
Async XLA Ops:
  4.6 45.3 %all-to-all-start = ((bf16[4,53,32,256]{3,2,1,0:T(8,128)(2,1)}), bf16[4,53,32,256]{3,2,1,0:T(8,128)(2,1)}, u32[]{:S(2)}, u32[]{:S(2)}) async-start(bf16[4,53,32,256]{3,2,1,0:T(8,128)(2,1)} %bitcast.5), calls=%async_computation | async-start | bytes 6946816 | tf_op jit(solution)/shard_map/all_to_all | solution.py:412
  11.1 25.0 %collective-permute-start.1 = (bf16[53,32,256]{2,1,0:T(8,128)(2,1)S(1)}, bf16[53,32,256]{2,1,0:T(8,128)(2,1)S(1)}, u32[]{:S(2)}, u32[]{:S(2)}) collective-permute-start(bf16[53,32,256]{2,1,0:T(8,128)(2,1)S(1)} %copy_bitcast_fusion.3), channel_id=1, source_target_pairs={{0,1},{1,0},{2,3},{3,2},{4,5},{5,4},{6,7},{7,6},{8,9},{9,8},{10,11... | collective-permute-start | bytes 2605064 | tf_op jit(solution)/shard_map/ppermute | solution.py:415
  14.9 3.7 %copy-start.17 = (s32[32,256]{1,0:T(8,128)S(1)}, s32[32,256]{1,0:T(8,128)}, u32[]{:S(2)}) copy-start(s32[32,256]{1,0:T(8,128)} %param.8) | copy-start | bytes 98308
  14.9 3.7 %copy-start.18 = (s32[32,256]{1,0:T(8,128)S(1)}, s32[32,256]{1,0:T(8,128)}, u32[]{:S(2)}) copy-start(s32[32,256]{1,0:T(8,128)} %param.9) | copy-start | bytes 98308
  18.6 11.7 %collective-permute-start.3 = (bf16[2,4,256]{2,1,0:T(4,128)(2,1)S(1)}, bf16[2,4,256]{2,1,0:T(4,128)(2,1)S(1)}, u32[]{:S(2)}, u32[]{:S(2)}) collective-permute-start(bf16[2,4,256]{2,1,0:T(4,128)(2,1)S(1)} %get-tuple-element.95), channel_id=1, source_target_pairs={{0,8},{8,16},{16,24},{24,32},{32,40},{40,48},{48,56},{56,64},{64,7... | collective-permute-start | bytes 12296 | tf_op jit(solution)/shard_map/ppermute | solution.py:310
  22.4 10.8 %collective-permute-start.4 = (bf16[2,4,256]{2,1,0:T(4,128)(2,1)S(1)}, bf16[2,4,256]{2,1,0:T(4,128)(2,1)S(1)}, u32[]{:S(2)}, u32[]{:S(2)}) collective-permute-start(bf16[2,4,256]{2,1,0:T(4,128)(2,1)S(1)} %get-tuple-element.96), channel_id=1, source_target_pairs={{8,0},{16,8},{24,16},{32,24},{40,32},{48,40},{56,48},{64,56},{72,6... | collective-permute-start | bytes 12296 | tf_op jit(solution)/shard_map/ppermute | solution.py:310
  24.4 2.7 %copy-start.9 = (bf16[64,424]{1,0:T(8,128)(2,1)S(1)}, bf16[64,424]{1,0:T(8,128)(2,1)}, u32[]{:S(2)}) copy-start(bf16[64,424]{1,0:T(8,128)(2,1)} %param.6) | copy-start | bytes 162820
  27.2 12.8 %copy-start.10 = (bf16[64,53]{1,0:T(8,128)(2,1)}, bf16[64,53]{1,0:T(8,128)(2,1)S(1)}, u32[]{:S(2)}) copy-start(bf16[64,53]{1,0:T(8,128)(2,1)S(1)} %get-tuple-element.81) | copy-start | bytes 20356
  27.3 12.8 %copy-start.12 = (bf16[64,53]{1,0:T(8,128)(2,1)}, bf16[64,53]{1,0:T(8,128)(2,1)S(1)}, u32[]{:S(2)}) copy-start(bf16[64,53]{1,0:T(8,128)(2,1)S(1)} %get-tuple-element.90) | copy-start | bytes 20356
  36.5 25.0 %collective-permute-start.2 = (bf16[53,32,256]{2,1,0:T(8,128)(2,1)}, bf16[53,32,256]{2,1,0:T(8,128)(2,1)}, u32[]{:S(2)}, u32[]{:S(2)}) collective-permute-start(bf16[53,32,256]{2,1,0:T(8,128)(2,1)} %copy_bitcast_fusion.2), channel_id=1, source_target_pairs={{0,1},{1,0},{2,3},{3,2},{4,5},{5,4},{6,7},{7,6},{8,9},{9,8},{10,11... | collective-permute-start | bytes 2605064 | tf_op jit(solution)/shard_map/ppermute | solution.py:432
  42.2 1.3 %copy-start = (f32[32,256,64]{1,2,0:T(8,128)}, f32[32,256,64]{1,2,0:T(8,128)S(1)}, u32[]{:S(2)}) copy-start(f32[32,256,64]{1,2,0:T(8,128)S(1)} %fusion.2) | copy-start | bytes 6291460
  43.5 16.3 %collective-permute-start.5 = (s16[528,256]{1,0:T(8,128)(2,1)}, s16[528,256]{1,0:T(8,128)(2,1)S(1)}, u32[]{:S(2)}, u32[]{:S(2)}) collective-permute-start(s16[528,256]{1,0:T(8,128)(2,1)} %get-tuple-element.56), channel_id=1, source_target_pairs={{0,2},{1,3},{2,4},{3,5},{4,6},{5,7},{6,0},{7,1},{8,10},{9,11},{10,... | collective-permute-start | bytes 811016 | tf_op jit(solution)/shard_map/ppermute | solution.py:429
  44.9 16.6 %collective-permute-start.6 = (s16[528,256]{1,0:T(8,128)(2,1)}, s16[528,256]{1,0:T(8,128)(2,1)}, u32[]{:S(2)}, u32[]{:S(2)}) collective-permute-start(s16[528,256]{1,0:T(8,128)(2,1)} %get-tuple-element.57), channel_id=1, source_target_pairs={{0,4},{1,5},{2,6},{3,7},{4,0},{5,1},{6,2},{7,3},{8,12},{9,13},{10,... | collective-permute-start | bytes 811016 | tf_op jit(solution)/shard_map/ppermute | solution.py:429
  47.4 14.2 %collective-permute-start.7 = (s16[528,256]{1,0:T(8,128)(2,1)}, s16[528,256]{1,0:T(8,128)(2,1)}, u32[]{:S(2)}, u32[]{:S(2)}) collective-permute-start(s16[528,256]{1,0:T(8,128)(2,1)} %get-tuple-element.58), channel_id=1, source_target_pairs={{0,6},{1,7},{2,0},{3,1},{4,2},{5,3},{6,4},{7,5},{8,14},{9,15},{10,... | collective-permute-start | bytes 811016 | tf_op jit(solution)/shard_map/ppermute | solution.py:429
  49.9 5.6 %copy-start.14 = (f32[64,64]{1,0:T(8,128)S(1)}, f32[64,64]{1,0:T(8,128)}, u32[]{:S(2)}) copy-start(f32[64,64]{1,0:T(8,128)} %param.7) | copy-start | bytes 49156
  54.4 22.9 %collective-permute-start = (s16[1040,256]{1,0:T(8,128)(2,1)S(1)}, s16[1040,256]{1,0:T(8,128)(2,1)S(1)}, u32[]{:S(2)}, u32[]{:S(2)}) collective-permute-start(s16[1040,256]{1,0:T(8,128)(2,1)S(1)} %shard_map.55), channel_id=1, source_target_pairs={{0,1},{1,0},{2,3},{3,2},{4,5},{5,4},{6,7},{7,6},{8,9},{9,8},{10,11... | collective-permute-start | bytes 1597448 | tf_op jit(solution)/shard_map/ppermute | solution.py:440
  58.0 5.2 %copy-start.11 = (bf16[64,53]{1,0:T(8,128)(2,1)S(1)}, bf16[64,53]{1,0:T(8,128)(2,1)}, u32[]{:S(2)}) copy-start(bf16[64,53]{1,0:T(8,128)(2,1)} %copy-done.10) | copy-start | bytes 20356
  58.0 5.2 %copy-start.13 = (bf16[64,53]{1,0:T(8,128)(2,1)S(1)}, bf16[64,53]{1,0:T(8,128)(2,1)}, u32[]{:S(2)}) copy-start(bf16[64,53]{1,0:T(8,128)(2,1)} %copy-done.12) | copy-start | bytes 20356
  63.2 6.0 %copy-start.1 = (f32[32,256,64]{1,2,0:T(8,128)S(1)}, f32[32,256,64]{1,2,0:T(8,128)}, u32[]{:S(2)}) copy-start(f32[32,256,64]{1,2,0:T(8,128)} %copy-done) | copy-start | bytes 6291460
  63.7 16.2 %copy-start.2 = (f32[32,256,64]{1,2,0:T(8,128)}, f32[32,256,64]{1,2,0:T(8,128)S(1)}, u32[]{:S(2)}) copy-start(f32[32,256,64]{1,2,0:T(8,128)S(1)} %fusion.6) | copy-start | bytes 6291460
  63.7 18.1 %copy-start.15 = (bf16[64,64]{1,0:T(8,128)(2,1)S(1)}, bf16[64,64]{1,0:T(8,128)(2,1)}, u32[]{:S(2)}) copy-start(bf16[64,64]{1,0:T(8,128)(2,1)} %get-tuple-element.97) | copy-start | bytes 24580
  63.7 18.1 %copy-start.16 = (bf16[64,64]{1,0:T(8,128)(2,1)S(1)}, bf16[64,64]{1,0:T(8,128)(2,1)}, u32[]{:S(2)}) copy-start(bf16[64,64]{1,0:T(8,128)(2,1)} %get-tuple-element.98) | copy-start | bytes 24580
  65.4 16.8 %collective-permute-start.8 = (s16[528,256]{1,0:T(8,128)(2,1)}, s16[528,256]{1,0:T(8,128)(2,1)}, u32[]{:S(2)}, u32[]{:S(2)}) collective-permute-start(s16[528,256]{1,0:T(8,128)(2,1)} %get-tuple-element.63), channel_id=1, source_target_pairs={{0,2},{1,3},{2,4},{3,5},{4,6},{5,7},{6,0},{7,1},{8,10},{9,11},{10,... | collective-permute-start | bytes 811016 | tf_op jit(solution)/shard_map/ppermute | solution.py:429
  66.8 15.4 %collective-permute-start.9 = (s16[528,256]{1,0:T(8,128)(2,1)}, s16[528,256]{1,0:T(8,128)(2,1)}, u32[]{:S(2)}, u32[]{:S(2)}) collective-permute-start(s16[528,256]{1,0:T(8,128)(2,1)} %get-tuple-element.64), channel_id=1, source_target_pairs={{0,4},{1,5},{2,6},{3,7},{4,0},{5,1},{6,2},{7,3},{8,12},{9,13},{10,... | collective-permute-start | bytes 811016 | tf_op jit(solution)/shard_map/ppermute | solution.py:429
  68.5 13.7 %collective-permute-start.10 = (s16[528,256]{1,0:T(8,128)(2,1)}, s16[528,256]{1,0:T(8,128)(2,1)}, u32[]{:S(2)}, u32[]{:S(2)}) collective-permute-start(s16[528,256]{1,0:T(8,128)(2,1)} %get-tuple-element.65), channel_id=1, source_target_pairs={{0,6},{1,7},{2,0},{3,1},{4,2},{5,3},{6,4},{7,5},{8,14},{9,15},{10,... | collective-permute-start | bytes 811016 | tf_op jit(solution)/shard_map/ppermute | solution.py:429
  71.1 0.8 copy-start.7
  71.9 10.2 %collective-permute-start.11 = (f32[4,64,256]{2,1,0:T(8,128)}, f32[4,64,256]{2,1,0:T(8,128)S(1)}, u32[]{:S(2)}, u32[]{:S(2)}) collective-permute-start(f32[4,64,256]{2,1,0:T(8,128)} %get-tuple-element.70), channel_id=1, source_target_pairs={{0,8},{8,16},{16,24},{24,32},{32,40},{40,48},{48,56},{56,64},{64,7... | collective-permute-start | bytes 786440 | tf_op jit(solution)/shard_map/ppermute | solution.py:310
  77.3 0.8 copy-start.5
  78.1 1.0 copy-start.6
  79.9 8.8 %collective-permute-start.12 = (f32[4,64,256]{2,1,0:T(8,128)}, f32[4,64,256]{2,1,0:T(8,128)S(1)}, u32[]{:S(2)}, u32[]{:S(2)}) collective-permute-start(f32[4,64,256]{2,1,0:T(8,128)} %get-tuple-element.71), channel_id=1, source_target_pairs={{8,0},{16,8},{24,16},{32,24},{40,32},{48,40},{56,48},{64,56},{72,6... | collective-permute-start | bytes 786440 | tf_op jit(solution)/shard_map/ppermute | solution.py:310
  88.7 1.6 %copy-start.3 = (f32[32,256,64]{1,2,0:T(8,128)S(1)}, f32[32,256,64]{1,2,0:T(8,128)}, u32[]{:S(2)}) copy-start(f32[32,256,64]{1,2,0:T(8,128)} %copy-done.2) | copy-start | bytes 6291460
  90.3 1.0 copy-start.8
  91.3 12.0 %copy-start.4 = (f32[24,288,128]{2,1,0:T(8,128)S(1)}, f32[24,288,128]{2,1,0:T(8,128)}, u32[]{:S(2)}) copy-start(f32[24,288,128]{2,1,0:T(8,128)} %convolution_multiply_fusion.1.wh_ref) | copy-start | bytes 10616836
  94.7 16.8 %collective-permute-start.14 = (f32[25,8,128]{2,1,0:T(8,128)S(1)}, f32[25,8,128]{2,1,0:T(8,128)S(1)}, u32[]{:S(2)}, u32[]{:S(2)}) collective-permute-start(f32[25,8,128]{2,1,0:T(8,128)S(1)} %get-tuple-element.73.low_ref), channel_id=1, source_target_pairs={{1,0},{2,1},{3,2},{4,3},{5,4},{6,5},{7,6},{9,8},{10,9},{11,10},{12... | collective-permute-start | bytes 307208 | tf_op jit(solution)/shard_map/ppermute | solution.py:310
  98.4 13.2 %collective-permute-start.13 = (f32[25,8,128]{2,1,0:T(8,128)S(1)}, f32[25,8,128]{2,1,0:T(8,128)S(1)}, u32[]{:S(2)}, u32[]{:S(2)}) collective-permute-start(f32[25,8,128]{2,1,0:T(8,128)S(1)} %get-tuple-element.72.high_ref), channel_id=1, source_target_pairs={{0,1},{1,2},{2,3},{3,4},{4,5},{5,6},{6,7},{8,9},{9,10},{10,11},{11... | collective-permute-start | bytes 307208 | tf_op jit(solution)/shard_map/ppermute | solution.py:310

commit v8 on v7

--- a/solution.py
+++ b/solution.py
@@ -12,7 +12,7 @@
 HALO = 4
 LEAD = 16
 SPAN = 288
-GROUP = 16
+GROUP = 128
 LEVELS = 256.0
 STEPS_MAX = 32000.0
 
@@ -213,7 +213,7 @@
         out_ref[i - HALO, pl.ds(pl.multiple_of(c - LEAD, 8), GROUP)] = value
 
     columns = (LEAD, LEAD + width)
-    iterate(mixed_ref, y, z, wh_ref, wv_ref, invt_ref, columns, GROUP, 2, store)
+    iterate(mixed_ref, y, z, wh_ref, wv_ref, invt_ref, columns, GROUP, 4, store)
 
 
 def inside(inv3t, mixed, wh, wv, width):

time: 118 us -> 116 us (0.983)
  Pallas kernels: 26.7 us -> 25.2 us
    pallas_call x1, Pallas kernels: 8.15 us -> 6.71 us  [inside(): pl.pallas_call(inside_kernel, out_shape=jax.ShapeDtypeStruct((deep - 2 *...]
  transfers between devices with their start and end apart: 16 -> 16, of which waited for: 5 -> 5; matrix products, arithmetic and copies ran while one was open for 20% -> 20% of each run, Pallas kernels for 15% -> 14%
where the time goes in v8:
time: 116 us; the launch traced here: 115 us
  starting transfers between devices  40 us (34%)
  Pallas kernels  25.2 us (22%)
  local copies, waits for them, and re-layouts  20.7 us (18%)
  waiting for transfers between devices  15.1 us (13%)
  matrix products  8.55 us (7%)
  other arithmetic  5.35 us (5%)
    ppermute x3, starting transfers between devices, neighbours(): lax.ppermute(high_part, axis, forward)  13.3 us
    ppermute x3, waiting for transfers between devices, neighbours(): lax.ppermute(low_part, axis, backward)  9.4 us
    ppermute x6, starting transfers between devices, over_y(): return [lax.ppermute(p, 'col', turns[k + 1]) for k, p in enumerate(parts)]  8.73 us
    ppermute x3, starting transfers between devices, neighbours(): lax.ppermute(low_part, axis, backward)  7.35 us
    pallas_call x1, Pallas kernels, inside(): pl.pallas_call(inside_kernel, out_shape=jax.ShapeDtypeStruct((deep - 2 *...  6.71 us
    unnamed x38, local copies, waits for them, and re-layouts  6.66 us
    pallas_call x1, Pallas kernels, sides(): pl.pallas_call(sides_kernel, out_shape=jax.ShapeDtypeStruct((lanes // 2,...  5.27 us
    dot_general x3, matrix products, project(): jnp.einsum('eb,bhw->hew', library, block, preferred_element_type=jnp.floa...  5.17 us
  transfers between devices with their start and end apart: 16, of which 5 were waited for; matrix products, arithmetic and copies ran while one was open for 20% of the time, Pallas kernels for 14%

profile of v8, /device:TPU:39, one launch (start us, length us, event | category | flops | bytes accessed | tf_op | source)
XLA Modules:
  0.0 115.4 jit_solution(14917092012023778677)
XLA Ops:
  0.0 2.3 %slice_bitcast_fusion = bf16[4,53,2,16,256]{4,3,1,2,0:T(8,128)(2,1)S(1)} fusion(bf16[4,2,53,32,256]{4,3,2,1,0:T(8,128)(2,1)} %bitcast.82), kind=kLoop, calls=%fused_computation.2 | loop fusion | bytes 6946816 | tf_op jit(solution)/shard_map/transpose | solution.py:406
  2.3 2.3 %copy.71 = bf16[4,53,2,16,256]{4,3,2,1,0:T(8,128)(2,1)} copy(bf16[4,53,2,16,256]{4,3,1,2,0:T(8,128)(2,1)S(1)} %slice_bitcast_fusion) | data formatting | bytes 6946816 | tf_op jit(solution)/shard_map/transpose | solution.py:406
  4.6 4.7 %all-to-all-start = ((bf16[4,53,32,256]{3,2,1,0:T(8,128)(2,1)}), bf16[4,53,32,256]{3,2,1,0:T(8,128)(2,1)}, u32[]{:S(2)}, u32[]{:S(2)}) async-start(bf16[4,53,32,256]{3,2,1,0:T(8,128)(2,1)} %bitcast.5), calls=%async_computation | async-start | bytes 6946816 | tf_op jit(solution)/shard_map/all_to_all | solution.py:412
  9.4 1.7 %copy_bitcast_fusion.3 = bf16[53,32,256]{2,1,0:T(8,128)(2,1)S(1)} fusion(bf16[4,2,53,32,256]{4,3,2,1,0:T(8,128)(2,1)} %bitcast.83, pred[]{:T(512)S(6)} %eq.18), kind=kLoop, calls=%fused_computation.16 | loop fusion | flops 434176 | bytes 2605057 | tf_op jit(solution)/shard_map/reshape | solution.py:395
  11.1 1.2 %collective-permute-start.1 = (bf16[53,32,256]{2,1,0:T(8,128)(2,1)S(1)}, bf16[53,32,256]{2,1,0:T(8,128)(2,1)S(1)}, u32[]{:S(2)}, u32[]{:S(2)}) collective-permute-start(bf16[53,32,256]{2,1,0:T(8,128)(2,1)S(1)} %copy_bitcast_fusion.3), channel_id=1, source_target_pairs={{0,1},{1,0},{2,3},{3,2},{4,5},{5,4},{6,7},{7,6},{8,9},{9,8},{10,11... | collective-permute-start | bytes 2605064 | tf_op jit(solution)/shard_map/ppermute | solution.py:415
  12.3 2.6 %copy_bitcast_fusion.2 = bf16[53,32,256]{2,1,0:T(8,128)(2,1)} fusion(bf16[4,2,53,32,256]{4,3,2,1,0:T(8,128)(2,1)} %bitcast.84, pred[]{:T(512)S(6)} %eq.18), kind=kLoop, calls=%fused_computation.15 | loop fusion | flops 434176 | bytes 2605057 | tf_op jit(solution)/shard_map/reshape | solution.py:395
  14.9 3.6 %shard_map.57 = bf16[4,53,16,256]{3,2,1,0:T(8,128)(2,1)} custom-call(s32[1]{0:T(128)} %bitcast.2.which_ref, bf16[4,2,53,32,256]{4,3,2,1,0:T(8,128)(2,1)} %bitcast.85), custom_call_target="tpu_custom_call" | custom-call | tf_op jit(solution)/shard_map/pallas_call | solution.py:349
  18.6 3.8 %collective-permute-start.3 = (bf16[2,4,256]{2,1,0:T(4,128)(2,1)S(1)}, bf16[2,4,256]{2,1,0:T(4,128)(2,1)S(1)}, u32[]{:S(2)}, u32[]{:S(2)}) collective-permute-start(bf16[2,4,256]{2,1,0:T(4,128)(2,1)S(1)} %get-tuple-element.95), channel_id=1, source_target_pairs={{0,8},{8,16},{16,24},{24,32},{32,40},{40,48},{48,56},{56,64},{64,7... | collective-permute-start | bytes 12296 | tf_op jit(solution)/shard_map/ppermute | solution.py:310
  22.4 1.9 %collective-permute-start.4 = (bf16[2,4,256]{2,1,0:T(4,128)(2,1)S(1)}, bf16[2,4,256]{2,1,0:T(4,128)(2,1)S(1)}, u32[]{:S(2)}, u32[]{:S(2)}) collective-permute-start(bf16[2,4,256]{2,1,0:T(4,128)(2,1)S(1)} %get-tuple-element.96), channel_id=1, source_target_pairs={{8,0},{16,8},{24,16},{32,24},{40,32},{48,40},{56,48},{64,56},{72,6... | collective-permute-start | bytes 12296 | tf_op jit(solution)/shard_map/ppermute | solution.py:310
  24.4 1.6 %slice_bitcast_fusion.1 = (bf16[53,4,8,256]{3,2,0,1:T(8,128)(2,1)S(1)}, bf16[53,4,8,256]{3,2,0,1:T(8,128)(2,1)S(1)}) fusion(bf16[4,53,16,256]{3,2,1,0:T(8,128)(2,1)} %shard_map.57), kind=kLoop, calls=%fused_computation.17 | loop fusion | bytes 3473408 | tf_op jit(solution)/shard_map/transpose | solution.py:422
  26.0 1.2 %copy_bitcast_fusion = (bf16[53,32,256]{2,1,0:T(8,128)(2,1)}, bf16[53,32,256]{2,1,0:T(8,128)(2,1)S(1)}) fusion(bf16[53,4,8,256]{3,2,0,1:T(8,128)(2,1)S(1)} %get-tuple-element.77, bf16[53,4,8,256]{3,2,0,1:T(8,128)(2,1)S(1)} %get-tuple-element.78), kind=kLoop, calls=%fused_computation.13 | loop fusion | bytes 3473408 | tf_op jit(solution)/shard_map/reshape | solution.py:423
  27.8 2.5 %collective-permute-done.3 = bf16[2,4,256]{2,1,0:T(4,128)(2,1)S(1)} collective-permute-done((bf16[2,4,256]{2,1,0:T(4,128)(2,1)S(1)}, bf16[2,4,256]{2,1,0:T(4,128)(2,1)S(1)}, u32[]{:S(2)}, u32[]{:S(2)}) %collective-permute-start.3) | collective-permute-done | bytes 4128 | tf_op jit(solution)/shard_map/ppermute | solution.py:310
  30.3 2.9 %collective-permute-done.4 = bf16[2,4,256]{2,1,0:T(4,128)(2,1)S(1)} collective-permute-done((bf16[2,4,256]{2,1,0:T(4,128)(2,1)S(1)}, bf16[2,4,256]{2,1,0:T(4,128)(2,1)S(1)}, u32[]{:S(2)}, u32[]{:S(2)}) %collective-permute-start.4) | collective-permute-done | bytes 4128 | tf_op jit(solution)/shard_map/ppermute | solution.py:310
  33.5 2.6 %convolution_multiply_fusion.1.wh_ref = f32[24,288,128]{2,1,0:T(8,128)} fusion(bf16[1,2,24,288]{3,0,2,1:T(2,128)(2,1)S(1)} %copy.79, bf16[1,2,24,288]{3,0,2,1:T(2,128)(2,1)S(1)} %copy.78, pred[128]{0:T(512)(128)(4,1)S(1)} %compare_and_fusion, s32[128]{0:T(128)S(1)} %get-tuple-element.99, s32[128]{0:T(128)S(1)} %get-tuple-element.100), kind=kOutput, calls=%fused_computation.4 | convolution fusion | flops 4479488 | bytes 3595392 | tf_op jit(solution)/shard_map/hrc,hl->rcl/dot_general | solution.py:370
  36.5 3.5 %collective-permute-start.2 = (bf16[53,32,256]{2,1,0:T(8,128)(2,1)}, bf16[53,32,256]{2,1,0:T(8,128)(2,1)}, u32[]{:S(2)}, u32[]{:S(2)}) collective-permute-start(bf16[53,32,256]{2,1,0:T(8,128)(2,1)} %copy_bitcast_fusion.2), channel_id=1, source_target_pairs={{0,1},{1,0},{2,3},{3,2},{4,5},{5,4},{6,7},{7,6},{8,9},{9,8},{10,11... | collective-permute-start | bytes 2605064 | tf_op jit(solution)/shard_map/ppermute | solution.py:432
  40.6 1.6 %shard_map.58 = (s16[528,256]{1,0:T(8,128)(2,1)}, s16[528,256]{1,0:T(8,128)(2,1)}, s16[528,256]{1,0:T(8,128)(2,1)}) custom-call(s32[3]{0:T(128)S(1)} %pad_add_fusion.which_ref, f32[4,8,64,256]{3,2,1,0:T(8,128)S(1)} %bitcast.77), custom_call_target="tpu_custom_call" | custom-call | tf_op jit(solution)/shard_map/pallas_call | solution.py:46
  42.2 1.3 %copy-done = f32[32,256,64]{1,2,0:T(8,128)} copy-done((f32[32,256,64]{1,2,0:T(8,128)}, f32[32,256,64]{1,2,0:T(8,128)S(1)}, u32[]{:S(2)}) %copy-start) | copy-done | bytes 2097176
  43.5 1.4 %collective-permute-start.5 = (s16[528,256]{1,0:T(8,128)(2,1)}, s16[528,256]{1,0:T(8,128)(2,1)S(1)}, u32[]{:S(2)}, u32[]{:S(2)}) collective-permute-start(s16[528,256]{1,0:T(8,128)(2,1)} %get-tuple-element.56), channel_id=1, source_target_pairs={{0,2},{1,3},{2,4},{3,5},{4,6},{5,7},{6,0},{7,1},{8,10},{9,11},{10,... | collective-permute-start | bytes 811016 | tf_op jit(solution)/shard_map/ppermute | solution.py:429
  44.9 2.5 %collective-permute-start.6 = (s16[528,256]{1,0:T(8,128)(2,1)}, s16[528,256]{1,0:T(8,128)(2,1)}, u32[]{:S(2)}, u32[]{:S(2)}) collective-permute-start(s16[528,256]{1,0:T(8,128)(2,1)} %get-tuple-element.57), channel_id=1, source_target_pairs={{0,4},{1,5},{2,6},{3,7},{4,0},{5,1},{6,2},{7,3},{8,12},{9,13},{10,... | collective-permute-start | bytes 811016 | tf_op jit(solution)/shard_map/ppermute | solution.py:429
  47.4 1.1 collective-permute-start.7
  48.5 1.5 %all-to-all-done = bf16[4,53,32,256]{3,2,1,0:T(8,128)(2,1)} async-done(((bf16[4,53,32,256]{3,2,1,0:T(8,128)(2,1)}), bf16[4,53,32,256]{3,2,1,0:T(8,128)(2,1)}, u32[]{:S(2)}, u32[]{:S(2)}) %all-to-all-start) | async-done | bytes 3473440 | tf_op jit(solution)/shard_map/all_to_all | solution.py:412
  49.9 4.2 %fusion = f32[32,256,64]{1,2,0:T(8,128)S(1)} fusion(bf16[212,32,256]{2,1,0:T(8,128)(2,1)} %bitcast.6, bf16[64,53]{1,0:T(8,128)(2,1)S(1)} %get-tuple-element.86, bf16[64,53]{1,0:T(8,128)(2,1)S(1)} %get-tuple-element.87, bf16[64,53]{1,0:T(8,128)(2,1)S(1)} %get-tuple-element.88, bf16[64,53]{1,0:T(8,128)(2,1)S(1)} %get-tuple-element.89, ...), kind=kOutput, calls=%fused_computation | convolution fusion | flops 222528768 | bytes 5624833 | tf_op jit(solution)/shard_map/eb,bhw->hew/dot_general | solution.py:389
  54.4 1.2 %collective-permute-start = (s16[1040,256]{1,0:T(8,128)(2,1)S(1)}, s16[1040,256]{1,0:T(8,128)(2,1)S(1)}, u32[]{:S(2)}, u32[]{:S(2)}) collective-permute-start(s16[1040,256]{1,0:T(8,128)(2,1)S(1)} %shard_map.55), channel_id=1, source_target_pairs={{0,1},{1,0},{2,3},{3,2},{4,5},{5,4},{6,7},{7,6},{8,9},{9,8},{10,11... | collective-permute-start | bytes 1597448 | tf_op jit(solution)/shard_map/ppermute | solution.py:440
  56.3 0.7 tile.4
  57.0 1.0 tile.10
  58.0 1.7 %copy.81 = bf16[53,32,256]{2,0,1:T(8,128)(2,1)S(1)} copy(bf16[53,32,256]{2,1,0:T(8,128)(2,1)} %get-tuple-element.103) | data formatting | bytes 1736704 | tf_op jit(solution)/shard_map/reshape | solution.py:423
  59.8 1.7 %collective-permute-done.6.refs_1_ = s16[528,256]{1,0:T(8,128)(2,1)} collective-permute-done((s16[528,256]{1,0:T(8,128)(2,1)}, s16[528,256]{1,0:T(8,128)(2,1)}, u32[]{:S(2)}, u32[]{:S(2)}) %collective-permute-start.6) | collective-permute-done | bytes 270368 | tf_op jit(solution)/shard_map/ppermute | solution.py:429
  61.5 1.6 %copy.82 = bf16[53,32,256]{2,0,1:T(8,128)(2,1)S(1)} copy(bf16[53,32,256]{2,1,0:T(8,128)(2,1)} %collective-permute-done.2) | data formatting | bytes 1736704 | tf_op jit(solution)/shard_map/optimization_barrier | solution.py:439
  63.7 1.7 %shard_map.59 = (s16[528,256]{1,0:T(8,128)(2,1)}, s16[528,256]{1,0:T(8,128)(2,1)}, s16[528,256]{1,0:T(8,128)(2,1)}) custom-call(s32[3]{0:T(128)S(1)} %pad_add_fusion.which_ref, f32[4,8,64,256]{3,2,1,0:T(8,128)S(1)} %bitcast.79), custom_call_target="tpu_custom_call" | custom-call | tf_op jit(solution)/shard_map/pallas_call | solution.py:46
  65.4 1.3 %collective-permute-start.8 = (s16[528,256]{1,0:T(8,128)(2,1)}, s16[528,256]{1,0:T(8,128)(2,1)}, u32[]{:S(2)}, u32[]{:S(2)}) collective-permute-start(s16[528,256]{1,0:T(8,128)(2,1)} %get-tuple-element.63), channel_id=1, source_target_pairs={{0,2},{1,3},{2,4},{3,5},{4,6},{5,7},{6,0},{7,1},{8,10},{9,11},{10,... | collective-permute-start | bytes 811016 | tf_op jit(solution)/shard_map/ppermute | solution.py:429
  66.8 1.7 %collective-permute-start.9 = (s16[528,256]{1,0:T(8,128)(2,1)}, s16[528,256]{1,0:T(8,128)(2,1)}, u32[]{:S(2)}, u32[]{:S(2)}) collective-permute-start(s16[528,256]{1,0:T(8,128)(2,1)} %get-tuple-element.64), channel_id=1, source_target_pairs={{0,4},{1,5},{2,6},{3,7},{4,0},{5,1},{6,2},{7,3},{8,12},{9,13},{10,... | collective-permute-start | bytes 811016 | tf_op jit(solution)/shard_map/ppermute | solution.py:429
  68.5 0.7 collective-permute-start.10
  69.2 2.0 %shard_map.60 = (f32[8,64,256]{2,1,0:T(8,128)S(1)}, f32[4,64,256]{2,1,0:T(8,128)}) custom-call(s32[1]{0:T(128)} %bitcast.1.which_ref, f32[4,8,64,256]{3,2,1,0:T(8,128)S(1)} %bitcast.78, s16[528,256]{1,0:T(8,128)(2,1)S(1)} %collective-permute-done.5.refs_0_, s16[528,256]{1,0:T(8,128)(2,1)} %collective-permute-done.6.refs_1_, ...), custom_call_target="tpu_custom_call" | custom-call | tf_op jit(solution)/shard_map/pallas_call | solution.py:84
  71.1 0.8 copy-done.7
  71.9 5.3 %collective-permute-start.11 = (f32[4,64,256]{2,1,0:T(8,128)}, f32[4,64,256]{2,1,0:T(8,128)S(1)}, u32[]{:S(2)}, u32[]{:S(2)}) collective-permute-start(f32[4,64,256]{2,1,0:T(8,128)} %get-tuple-element.70), channel_id=1, source_target_pairs={{0,8},{8,16},{16,24},{24,32},{32,40},{40,48},{48,56},{56,64},{64,7... | collective-permute-start | bytes 786440 | tf_op jit(solution)/shard_map/ppermute | solution.py:310
  77.3 0.8 copy-done.5
  78.1 1.0 copy-done.6
  79.1 0.8 shard_map.56
  79.9 1.9 %collective-permute-start.12 = (f32[4,64,256]{2,1,0:T(8,128)}, f32[4,64,256]{2,1,0:T(8,128)S(1)}, u32[]{:S(2)}, u32[]{:S(2)}) collective-permute-start(f32[4,64,256]{2,1,0:T(8,128)} %get-tuple-element.71), channel_id=1, source_target_pairs={{8,0},{16,8},{24,16},{32,24},{40,32},{48,40},{56,48},{64,56},{72,6... | collective-permute-start | bytes 786440 | tf_op jit(solution)/shard_map/ppermute | solution.py:310
  82.2 6.5 %collective-permute-done.12.bottom_ref = f32[4,64,256]{2,1,0:T(8,128)S(1)} collective-permute-done((f32[4,64,256]{2,1,0:T(8,128)}, f32[4,64,256]{2,1,0:T(8,128)S(1)}, u32[]{:S(2)}, u32[]{:S(2)}) %collective-permute-start.12) | collective-permute-done | bytes 262176 | tf_op jit(solution)/shard_map/ppermute | solution.py:310
  88.7 1.6 %copy-done.3 = f32[32,256,64]{1,2,0:T(8,128)S(1)} copy-done((f32[32,256,64]{1,2,0:T(8,128)S(1)}, f32[32,256,64]{1,2,0:T(8,128)}, u32[]{:S(2)}) %copy-start.3) | copy-done | bytes 2097176
  90.3 1.0 copy-done.8
  91.3 3.3 %shard_map.61 = (f32[24,288,128]{2,1,0:T(8,128)S(1)}, f32[25,8,128]{2,1,0:T(8,128)S(1)}, f32[25,8,128]{2,1,0:T(8,128)S(1)}) custom-call(s32[1]{0:T(128)} %bitcast.1.which_ref, bf16[64,192]{1,0:T(8,128)(2,1)S(1)} %pad_maximum_fusion.4.inv_ref, f32[16,64,256]{2,1,0:T(8,128)S(1)} %get-tuple-element.42.early_ref, f32[8,64,256]{2,1,0:T(8,128)S(1)} %copy-done.8, ...), custom_call_target="tpu_custom_call" | custom-call | tf_op jit(solution)/shard_map/pallas_call | solution.py:150
  94.7 3.5 %collective-permute-start.14 = (f32[25,8,128]{2,1,0:T(8,128)S(1)}, f32[25,8,128]{2,1,0:T(8,128)S(1)}, u32[]{:S(2)}, u32[]{:S(2)}) collective-permute-start(f32[25,8,128]{2,1,0:T(8,128)S(1)} %get-tuple-element.73.low_ref), channel_id=1, source_target_pairs={{1,0},{2,1},{3,2},{4,3},{5,4},{6,5},{7,6},{9,8},{10,9},{11,10},{12... | collective-permute-start | bytes 307208 | tf_op jit(solution)/shard_map/ppermute | solution.py:310
  98.4 4.2 %collective-permute-start.13 = (f32[25,8,128]{2,1,0:T(8,128)S(1)}, f32[25,8,128]{2,1,0:T(8,128)S(1)}, u32[]{:S(2)}, u32[]{:S(2)}) collective-permute-start(f32[25,8,128]{2,1,0:T(8,128)S(1)} %get-tuple-element.72.high_ref), channel_id=1, source_target_pairs={{0,1},{1,2},{2,3},{3,4},{4,5},{5,6},{6,7},{8,9},{9,10},{10,11},{11... | collective-permute-start | bytes 307208 | tf_op jit(solution)/shard_map/ppermute | solution.py:310
  102.5 0.8 convolution_multiply_fusion.wv_ref
  103.4 6.7 %shard_map.62.inside_ref = f32[16,256,128]{2,1,0:T(8,128)S(1)} custom-call(bf16[384,128]{1,0:T(8,128)(2,1)S(1)} %pad_maximum_fusion.invt_ref, f32[24,288,128]{2,1,0:T(8,128)S(1)} %get-tuple-element.74.mixed_ref, f32[24,288,128]{2,1,0:T(8,128)S(1)} %copy-done.4, f32[24,288,128]{2,1,0:T(8,128)S(1)} %convolution_multiply_fusion.wv_ref), custom_call_target="tpu_custom_call" | custom-call | flops 3000000000 | bytes 25165824 | tf_op jit(solution)/shard_map/pallas_call | solution.py:223
  110.1 5.3 %shard_map.63 = f32[64,32,256]{2,1,0:T(8,128)} custom-call(bf16[384,128]{1,0:T(8,128)(2,1)S(1)} %pad_maximum_fusion.invt_ref, f32[25,8,128]{2,1,0:T(8,128)S(1)} %collective-permute-done.13.left_ref, f32[25,8,128]{2,1,0:T(8,128)S(1)} %get-tuple-element.73.low_ref, f32[25,8,128]{2,1,0:T(8,128)S(1)} %get-tuple-element.72.high_ref, ...), custom_call_target="tpu_custom_call" | custom-call | tf_op jit(solution)/shard_map/pallas_call | solution.py:289
  (71 shorter events, 4.0 us)
Async XLA Ops:
  4.6 45.3 %all-to-all-start = ((bf16[4,53,32,256]{3,2,1,0:T(8,128)(2,1)}), bf16[4,53,32,256]{3,2,1,0:T(8,128)(2,1)}, u32[]{:S(2)}, u32[]{:S(2)}) async-start(bf16[4,53,32,256]{3,2,1,0:T(8,128)(2,1)} %bitcast.5), calls=%async_computation | async-start | bytes 6946816 | tf_op jit(solution)/shard_map/all_to_all | solution.py:412
  11.1 25.0 %collective-permute-start.1 = (bf16[53,32,256]{2,1,0:T(8,128)(2,1)S(1)}, bf16[53,32,256]{2,1,0:T(8,128)(2,1)S(1)}, u32[]{:S(2)}, u32[]{:S(2)}) collective-permute-start(bf16[53,32,256]{2,1,0:T(8,128)(2,1)S(1)} %copy_bitcast_fusion.3), channel_id=1, source_target_pairs={{0,1},{1,0},{2,3},{3,2},{4,5},{5,4},{6,7},{7,6},{8,9},{9,8},{10,11... | collective-permute-start | bytes 2605064 | tf_op jit(solution)/shard_map/ppermute | solution.py:415
  14.9 3.7 %copy-start.17 = (s32[32,256]{1,0:T(8,128)S(1)}, s32[32,256]{1,0:T(8,128)}, u32[]{:S(2)}) copy-start(s32[32,256]{1,0:T(8,128)} %param.8) | copy-start | bytes 98308
  14.9 3.7 %copy-start.18 = (s32[32,256]{1,0:T(8,128)S(1)}, s32[32,256]{1,0:T(8,128)}, u32[]{:S(2)}) copy-start(s32[32,256]{1,0:T(8,128)} %param.9) | copy-start | bytes 98308
  18.6 11.7 %collective-permute-start.3 = (bf16[2,4,256]{2,1,0:T(4,128)(2,1)S(1)}, bf16[2,4,256]{2,1,0:T(4,128)(2,1)S(1)}, u32[]{:S(2)}, u32[]{:S(2)}) collective-permute-start(bf16[2,4,256]{2,1,0:T(4,128)(2,1)S(1)} %get-tuple-element.95), channel_id=1, source_target_pairs={{0,8},{8,16},{16,24},{24,32},{32,40},{40,48},{48,56},{56,64},{64,7... | collective-permute-start | bytes 12296 | tf_op jit(solution)/shard_map/ppermute | solution.py:310
  22.4 10.8 %collective-permute-start.4 = (bf16[2,4,256]{2,1,0:T(4,128)(2,1)S(1)}, bf16[2,4,256]{2,1,0:T(4,128)(2,1)S(1)}, u32[]{:S(2)}, u32[]{:S(2)}) collective-permute-start(bf16[2,4,256]{2,1,0:T(4,128)(2,1)S(1)} %get-tuple-element.96), channel_id=1, source_target_pairs={{8,0},{16,8},{24,16},{32,24},{40,32},{48,40},{56,48},{64,56},{72,6... | collective-permute-start | bytes 12296 | tf_op jit(solution)/shard_map/ppermute | solution.py:310
  24.4 2.7 %copy-start.9 = (bf16[64,424]{1,0:T(8,128)(2,1)S(1)}, bf16[64,424]{1,0:T(8,128)(2,1)}, u32[]{:S(2)}) copy-start(bf16[64,424]{1,0:T(8,128)(2,1)} %param.6) | copy-start | bytes 162820
  27.2 12.8 %copy-start.10 = (bf16[64,53]{1,0:T(8,128)(2,1)}, bf16[64,53]{1,0:T(8,128)(2,1)S(1)}, u32[]{:S(2)}) copy-start(bf16[64,53]{1,0:T(8,128)(2,1)S(1)} %get-tuple-element.81) | copy-start | bytes 20356
  27.3 12.8 %copy-start.12 = (bf16[64,53]{1,0:T(8,128)(2,1)}, bf16[64,53]{1,0:T(8,128)(2,1)S(1)}, u32[]{:S(2)}) copy-start(bf16[64,53]{1,0:T(8,128)(2,1)S(1)} %get-tuple-element.90) | copy-start | bytes 20356
  36.5 25.0 %collective-permute-start.2 = (bf16[53,32,256]{2,1,0:T(8,128)(2,1)}, bf16[53,32,256]{2,1,0:T(8,128)(2,1)}, u32[]{:S(2)}, u32[]{:S(2)}) collective-permute-start(bf16[53,32,256]{2,1,0:T(8,128)(2,1)} %copy_bitcast_fusion.2), channel_id=1, source_target_pairs={{0,1},{1,0},{2,3},{3,2},{4,5},{5,4},{6,7},{7,6},{8,9},{9,8},{10,11... | collective-permute-start | bytes 2605064 | tf_op jit(solution)/shard_map/ppermute | solution.py:432
  42.2 1.3 %copy-start = (f32[32,256,64]{1,2,0:T(8,128)}, f32[32,256,64]{1,2,0:T(8,128)S(1)}, u32[]{:S(2)}) copy-start(f32[32,256,64]{1,2,0:T(8,128)S(1)} %fusion.2) | copy-start | bytes 6291460
  43.5 16.3 %collective-permute-start.5 = (s16[528,256]{1,0:T(8,128)(2,1)}, s16[528,256]{1,0:T(8,128)(2,1)S(1)}, u32[]{:S(2)}, u32[]{:S(2)}) collective-permute-start(s16[528,256]{1,0:T(8,128)(2,1)} %get-tuple-element.56), channel_id=1, source_target_pairs={{0,2},{1,3},{2,4},{3,5},{4,6},{5,7},{6,0},{7,1},{8,10},{9,11},{10,... | collective-permute-start | bytes 811016 | tf_op jit(solution)/shard_map/ppermute | solution.py:429
  44.9 16.6 %collective-permute-start.6 = (s16[528,256]{1,0:T(8,128)(2,1)}, s16[528,256]{1,0:T(8,128)(2,1)}, u32[]{:S(2)}, u32[]{:S(2)}) collective-permute-start(s16[528,256]{1,0:T(8,128)(2,1)} %get-tuple-element.57), channel_id=1, source_target_pairs={{0,4},{1,5},{2,6},{3,7},{4,0},{5,1},{6,2},{7,3},{8,12},{9,13},{10,... | collective-permute-start | bytes 811016 | tf_op jit(solution)/shard_map/ppermute | solution.py:429
  47.4 14.2 %collective-permute-start.7 = (s16[528,256]{1,0:T(8,128)(2,1)}, s16[528,256]{1,0:T(8,128)(2,1)}, u32[]{:S(2)}, u32[]{:S(2)}) collective-permute-start(s16[528,256]{1,0:T(8,128)(2,1)} %get-tuple-element.58), channel_id=1, source_target_pairs={{0,6},{1,7},{2,0},{3,1},{4,2},{5,3},{6,4},{7,5},{8,14},{9,15},{10,... | collective-permute-start | bytes 811016 | tf_op jit(solution)/shard_map/ppermute | solution.py:429
  49.9 5.6 %copy-start.14 = (f32[64,64]{1,0:T(8,128)S(1)}, f32[64,64]{1,0:T(8,128)}, u32[]{:S(2)}) copy-start(f32[64,64]{1,0:T(8,128)} %param.7) | copy-start | bytes 49156
  54.4 22.9 %collective-permute-start = (s16[1040,256]{1,0:T(8,128)(2,1)S(1)}, s16[1040,256]{1,0:T(8,128)(2,1)S(1)}, u32[]{:S(2)}, u32[]{:S(2)}) collective-permute-start(s16[1040,256]{1,0:T(8,128)(2,1)S(1)} %shard_map.55), channel_id=1, source_target_pairs={{0,1},{1,0},{2,3},{3,2},{4,5},{5,4},{6,7},{7,6},{8,9},{9,8},{10,11... | collective-permute-start | bytes 1597448 | tf_op jit(solution)/shard_map/ppermute | solution.py:440
  58.0 5.2 %copy-start.11 = (bf16[64,53]{1,0:T(8,128)(2,1)S(1)}, bf16[64,53]{1,0:T(8,128)(2,1)}, u32[]{:S(2)}) copy-start(bf16[64,53]{1,0:T(8,128)(2,1)} %copy-done.10) | copy-start | bytes 20356
  58.0 5.2 %copy-start.13 = (bf16[64,53]{1,0:T(8,128)(2,1)S(1)}, bf16[64,53]{1,0:T(8,128)(2,1)}, u32[]{:S(2)}) copy-start(bf16[64,53]{1,0:T(8,128)(2,1)} %copy-done.12) | copy-start | bytes 20356
  63.2 6.0 %copy-start.1 = (f32[32,256,64]{1,2,0:T(8,128)S(1)}, f32[32,256,64]{1,2,0:T(8,128)}, u32[]{:S(2)}) copy-start(f32[32,256,64]{1,2,0:T(8,128)} %copy-done) | copy-start | bytes 6291460
  63.7 16.2 %copy-start.2 = (f32[32,256,64]{1,2,0:T(8,128)}, f32[32,256,64]{1,2,0:T(8,128)S(1)}, u32[]{:S(2)}) copy-start(f32[32,256,64]{1,2,0:T(8,128)S(1)} %fusion.6) | copy-start | bytes 6291460
  63.7 18.1 %copy-start.15 = (bf16[64,64]{1,0:T(8,128)(2,1)S(1)}, bf16[64,64]{1,0:T(8,128)(2,1)}, u32[]{:S(2)}) copy-start(bf16[64,64]{1,0:T(8,128)(2,1)} %get-tuple-element.97) | copy-start | bytes 24580
  63.7 18.1 %copy-start.16 = (bf16[64,64]{1,0:T(8,128)(2,1)S(1)}, bf16[64,64]{1,0:T(8,128)(2,1)}, u32[]{:S(2)}) copy-start(bf16[64,64]{1,0:T(8,128)(2,1)} %get-tuple-element.98) | copy-start | bytes 24580
  65.4 16.8 %collective-permute-start.8 = (s16[528,256]{1,0:T(8,128)(2,1)}, s16[528,256]{1,0:T(8,128)(2,1)}, u32[]{:S(2)}, u32[]{:S(2)}) collective-permute-start(s16[528,256]{1,0:T(8,128)(2,1)} %get-tuple-element.63), channel_id=1, source_target_pairs={{0,2},{1,3},{2,4},{3,5},{4,6},{5,7},{6,0},{7,1},{8,10},{9,11},{10,... | collective-permute-start | bytes 811016 | tf_op jit(solution)/shard_map/ppermute | solution.py:429
  66.8 15.4 %collective-permute-start.9 = (s16[528,256]{1,0:T(8,128)(2,1)}, s16[528,256]{1,0:T(8,128)(2,1)}, u32[]{:S(2)}, u32[]{:S(2)}) collective-permute-start(s16[528,256]{1,0:T(8,128)(2,1)} %get-tuple-element.64), channel_id=1, source_target_pairs={{0,4},{1,5},{2,6},{3,7},{4,0},{5,1},{6,2},{7,3},{8,12},{9,13},{10,... | collective-permute-start | bytes 811016 | tf_op jit(solution)/shard_map/ppermute | solution.py:429
  68.5 13.7 %collective-permute-start.10 = (s16[528,256]{1,0:T(8,128)(2,1)}, s16[528,256]{1,0:T(8,128)(2,1)}, u32[]{:S(2)}, u32[]{:S(2)}) collective-permute-start(s16[528,256]{1,0:T(8,128)(2,1)} %get-tuple-element.65), channel_id=1, source_target_pairs={{0,6},{1,7},{2,0},{3,1},{4,2},{5,3},{6,4},{7,5},{8,14},{9,15},{10,... | collective-permute-start | bytes 811016 | tf_op jit(solution)/shard_map/ppermute | solution.py:429
  71.1 0.8 copy-start.7
  71.9 10.2 %collective-permute-start.11 = (f32[4,64,256]{2,1,0:T(8,128)}, f32[4,64,256]{2,1,0:T(8,128)S(1)}, u32[]{:S(2)}, u32[]{:S(2)}) collective-permute-start(f32[4,64,256]{2,1,0:T(8,128)} %get-tuple-element.70), channel_id=1, source_target_pairs={{0,8},{8,16},{16,24},{24,32},{32,40},{40,48},{48,56},{56,64},{64,7... | collective-permute-start | bytes 786440 | tf_op jit(solution)/shard_map/ppermute | solution.py:310
  77.3 0.8 copy-start.5
  78.1 1.0 copy-start.6
  79.9 8.8 %collective-permute-start.12 = (f32[4,64,256]{2,1,0:T(8,128)}, f32[4,64,256]{2,1,0:T(8,128)S(1)}, u32[]{:S(2)}, u32[]{:S(2)}) collective-permute-start(f32[4,64,256]{2,1,0:T(8,128)} %get-tuple-element.71), channel_id=1, source_target_pairs={{8,0},{16,8},{24,16},{32,24},{40,32},{48,40},{56,48},{64,56},{72,6... | collective-permute-start | bytes 786440 | tf_op jit(solution)/shard_map/ppermute | solution.py:310
  88.7 1.6 %copy-start.3 = (f32[32,256,64]{1,2,0:T(8,128)S(1)}, f32[32,256,64]{1,2,0:T(8,128)}, u32[]{:S(2)}) copy-start(f32[32,256,64]{1,2,0:T(8,128)} %copy-done.2) | copy-start | bytes 6291460
  90.3 1.0 copy-start.8
  91.3 12.0 %copy-start.4 = (f32[24,288,128]{2,1,0:T(8,128)S(1)}, f32[24,288,128]{2,1,0:T(8,128)}, u32[]{:S(2)}) copy-start(f32[24,288,128]{2,1,0:T(8,128)} %convolution_multiply_fusion.1.wh_ref) | copy-start | bytes 10616836
  94.7 15.4 %collective-permute-start.14 = (f32[25,8,128]{2,1,0:T(8,128)S(1)}, f32[25,8,128]{2,1,0:T(8,128)S(1)}, u32[]{:S(2)}, u32[]{:S(2)}) collective-permute-start(f32[25,8,128]{2,1,0:T(8,128)S(1)} %get-tuple-element.73.low_ref), channel_id=1, source_target_pairs={{1,0},{2,1},{3,2},{4,3},{5,4},{6,5},{7,6},{9,8},{10,9},{11,10},{12... | collective-permute-start | bytes 307208 | tf_op jit(solution)/shard_map/ppermute | solution.py:310
  98.4 11.7 %collective-permute-start.13 = (f32[25,8,128]{2,1,0:T(8,128)S(1)}, f32[25,8,128]{2,1,0:T(8,128)S(1)}, u32[]{:S(2)}, u32[]{:S(2)}) collective-permute-start(f32[25,8,128]{2,1,0:T(8,128)S(1)} %get-tuple-element.72.high_ref), channel_id=1, source_target_pairs={{0,1},{1,2},{2,3},{3,4},{4,5},{5,6},{6,7},{8,9},{9,10},{10,11},{11... | collective-permute-start | bytes 307208 | tf_op jit(solution)/shard_map/ppermute | solution.py:310

commit v9 on v8

--- a/solution.py
+++ b/solution.py
@@ -260,10 +260,10 @@
     )
     place = lax.broadcasted_iota(jnp.int32, (8, lanes), 0)
 
-    @pl.loop(0, half // 2)
+    @pl.loop(0, half // 4)
     def _(g):
-        for k in range(2):
-            r = g * 2 + k
+        for k in range(4):
+            r = g * 4 + k
             first = jnp.where(place < HALO, z[r + HALO, 16:24], inside_ref[r, :8])
             last = jnp.where(place < 8 - HALO, inside_ref[r, width - 8 :], z[r + HALO, 32:40])
             whole = jnp.concatenate([first, inside_ref[r, 8 : width - 8], last], axis=0)

time: 116 us -> 116 us (level)
  no operation moved by 1% of the time
where the time goes in v9:
time: 116 us; the launch traced here: 115 us
  starting transfers between devices  40 us (34%)
  Pallas kernels  25 us (22%)
  local copies, waits for them, and re-layouts  20.7 us (18%)
  waiting for transfers between devices  15.1 us (13%)
  matrix products  8.55 us (7%)
  other arithmetic  5.35 us (5%)
    ppermute x3, starting transfers between devices, neighbours(): lax.ppermute(high_part, axis, forward)  13.3 us
    ppermute x3, waiting for transfers between devices, neighbours(): lax.ppermute(low_part, axis, backward)  9.4 us
    ppermute x6, starting transfers between devices, over_y(): return [lax.ppermute(p, 'col', turns[k + 1]) for k, p in enumerate(parts)]  8.73 us
    ppermute x3, starting transfers between devices, neighbours(): lax.ppermute(low_part, axis, backward)  7.35 us
    pallas_call x1, Pallas kernels, inside(): pl.pallas_call(inside_kernel, out_shape=jax.ShapeDtypeStruct((deep - 2 *...  6.71 us
    unnamed x38, local copies, waits for them, and re-layouts  6.66 us
    dot_general x3, matrix products, project(): jnp.einsum('eb,bhw->hew', library, block, preferred_element_type=jnp.floa...  5.17 us
    pallas_call x1, Pallas kernels, sides(): pl.pallas_call(sides_kernel, out_shape=jax.ShapeDtypeStruct((lanes // 2,...  5.03 us
  transfers between devices with their start and end apart: 16, of which 5 were waited for; matrix products, arithmetic and copies ran while one was open for 20% of the time, Pallas kernels for 14%

profile of v9, /device:TPU:39, one launch (start us, length us, event | category | flops | bytes accessed | tf_op | source)
XLA Modules:
  0.0 115.1 jit_solution(7191943258352260706)
XLA Ops:
  0.0 2.3 %slice_bitcast_fusion = bf16[4,53,2,16,256]{4,3,1,2,0:T(8,128)(2,1)S(1)} fusion(bf16[4,2,53,32,256]{4,3,2,1,0:T(8,128)(2,1)} %bitcast.82), kind=kLoop, calls=%fused_computation.2 | loop fusion | bytes 6946816 | tf_op jit(solution)/shard_map/transpose | solution.py:406
  2.3 2.3 %copy.71 = bf16[4,53,2,16,256]{4,3,2,1,0:T(8,128)(2,1)} copy(bf16[4,53,2,16,256]{4,3,1,2,0:T(8,128)(2,1)S(1)} %slice_bitcast_fusion) | data formatting | bytes 6946816 | tf_op jit(solution)/shard_map/transpose | solution.py:406
  4.6 4.7 %all-to-all-start = ((bf16[4,53,32,256]{3,2,1,0:T(8,128)(2,1)}), bf16[4,53,32,256]{3,2,1,0:T(8,128)(2,1)}, u32[]{:S(2)}, u32[]{:S(2)}) async-start(bf16[4,53,32,256]{3,2,1,0:T(8,128)(2,1)} %bitcast.5), calls=%async_computation | async-start | bytes 6946816 | tf_op jit(solution)/shard_map/all_to_all | solution.py:412
  9.4 1.7 %copy_bitcast_fusion.3 = bf16[53,32,256]{2,1,0:T(8,128)(2,1)S(1)} fusion(bf16[4,2,53,32,256]{4,3,2,1,0:T(8,128)(2,1)} %bitcast.83, pred[]{:T(512)S(6)} %eq.18), kind=kLoop, calls=%fused_computation.16 | loop fusion | flops 434176 | bytes 2605057 | tf_op jit(solution)/shard_map/reshape | solution.py:395
  11.1 1.2 %collective-permute-start.1 = (bf16[53,32,256]{2,1,0:T(8,128)(2,1)S(1)}, bf16[53,32,256]{2,1,0:T(8,128)(2,1)S(1)}, u32[]{:S(2)}, u32[]{:S(2)}) collective-permute-start(bf16[53,32,256]{2,1,0:T(8,128)(2,1)S(1)} %copy_bitcast_fusion.3), channel_id=1, source_target_pairs={{0,1},{1,0},{2,3},{3,2},{4,5},{5,4},{6,7},{7,6},{8,9},{9,8},{10,11... | collective-permute-start | bytes 2605064 | tf_op jit(solution)/shard_map/ppermute | solution.py:415
  12.3 2.6 %copy_bitcast_fusion.2 = bf16[53,32,256]{2,1,0:T(8,128)(2,1)} fusion(bf16[4,2,53,32,256]{4,3,2,1,0:T(8,128)(2,1)} %bitcast.84, pred[]{:T(512)S(6)} %eq.18), kind=kLoop, calls=%fused_computation.15 | loop fusion | flops 434176 | bytes 2605057 | tf_op jit(solution)/shard_map/reshape | solution.py:395
  14.9 3.6 %shard_map.57 = bf16[4,53,16,256]{3,2,1,0:T(8,128)(2,1)} custom-call(s32[1]{0:T(128)} %bitcast.2.which_ref, bf16[4,2,53,32,256]{4,3,2,1,0:T(8,128)(2,1)} %bitcast.85), custom_call_target="tpu_custom_call" | custom-call | tf_op jit(solution)/shard_map/pallas_call | solution.py:349
  18.6 3.8 %collective-permute-start.3 = (bf16[2,4,256]{2,1,0:T(4,128)(2,1)S(1)}, bf16[2,4,256]{2,1,0:T(4,128)(2,1)S(1)}, u32[]{:S(2)}, u32[]{:S(2)}) collective-permute-start(bf16[2,4,256]{2,1,0:T(4,128)(2,1)S(1)} %get-tuple-element.95), channel_id=1, source_target_pairs={{0,8},{8,16},{16,24},{24,32},{32,40},{40,48},{48,56},{56,64},{64,7... | collective-permute-start | bytes 12296 | tf_op jit(solution)/shard_map/ppermute | solution.py:310
  22.4 1.9 %collective-permute-start.4 = (bf16[2,4,256]{2,1,0:T(4,128)(2,1)S(1)}, bf16[2,4,256]{2,1,0:T(4,128)(2,1)S(1)}, u32[]{:S(2)}, u32[]{:S(2)}) collective-permute-start(bf16[2,4,256]{2,1,0:T(4,128)(2,1)S(1)} %get-tuple-element.96), channel_id=1, source_target_pairs={{8,0},{16,8},{24,16},{32,24},{40,32},{48,40},{56,48},{64,56},{72,6... | collective-permute-start | bytes 12296 | tf_op jit(solution)/shard_map/ppermute | solution.py:310
  24.4 1.6 %slice_bitcast_fusion.1 = (bf16[53,4,8,256]{3,2,0,1:T(8,128)(2,1)S(1)}, bf16[53,4,8,256]{3,2,0,1:T(8,128)(2,1)S(1)}) fusion(bf16[4,53,16,256]{3,2,1,0:T(8,128)(2,1)} %shard_map.57), kind=kLoop, calls=%fused_computation.17 | loop fusion | bytes 3473408 | tf_op jit(solution)/shard_map/transpose | solution.py:422
  26.0 1.2 %copy_bitcast_fusion = (bf16[53,32,256]{2,1,0:T(8,128)(2,1)}, bf16[53,32,256]{2,1,0:T(8,128)(2,1)S(1)}) fusion(bf16[53,4,8,256]{3,2,0,1:T(8,128)(2,1)S(1)} %get-tuple-element.77, bf16[53,4,8,256]{3,2,0,1:T(8,128)(2,1)S(1)} %get-tuple-element.78), kind=kLoop, calls=%fused_computation.13 | loop fusion | bytes 3473408 | tf_op jit(solution)/shard_map/reshape | solution.py:423
  27.8 2.5 %collective-permute-done.3 = bf16[2,4,256]{2,1,0:T(4,128)(2,1)S(1)} collective-permute-done((bf16[2,4,256]{2,1,0:T(4,128)(2,1)S(1)}, bf16[2,4,256]{2,1,0:T(4,128)(2,1)S(1)}, u32[]{:S(2)}, u32[]{:S(2)}) %collective-permute-start.3) | collective-permute-done | bytes 4128 | tf_op jit(solution)/shard_map/ppermute | solution.py:310
  30.3 2.9 %collective-permute-done.4 = bf16[2,4,256]{2,1,0:T(4,128)(2,1)S(1)} collective-permute-done((bf16[2,4,256]{2,1,0:T(4,128)(2,1)S(1)}, bf16[2,4,256]{2,1,0:T(4,128)(2,1)S(1)}, u32[]{:S(2)}, u32[]{:S(2)}) %collective-permute-start.4) | collective-permute-done | bytes 4128 | tf_op jit(solution)/shard_map/ppermute | solution.py:310
  33.5 2.6 %convolution_multiply_fusion.1.wh_ref = f32[24,288,128]{2,1,0:T(8,128)} fusion(bf16[1,2,24,288]{3,0,2,1:T(2,128)(2,1)S(1)} %copy.79, bf16[1,2,24,288]{3,0,2,1:T(2,128)(2,1)S(1)} %copy.78, pred[128]{0:T(512)(128)(4,1)S(1)} %compare_and_fusion, s32[128]{0:T(128)S(1)} %get-tuple-element.99, s32[128]{0:T(128)S(1)} %get-tuple-element.100), kind=kOutput, calls=%fused_computation.4 | convolution fusion | flops 4479488 | bytes 3595392 | tf_op jit(solution)/shard_map/hrc,hl->rcl/dot_general | solution.py:370
  36.5 3.5 %collective-permute-start.2 = (bf16[53,32,256]{2,1,0:T(8,128)(2,1)}, bf16[53,32,256]{2,1,0:T(8,128)(2,1)}, u32[]{:S(2)}, u32[]{:S(2)}) collective-permute-start(bf16[53,32,256]{2,1,0:T(8,128)(2,1)} %copy_bitcast_fusion.2), channel_id=1, source_target_pairs={{0,1},{1,0},{2,3},{3,2},{4,5},{5,4},{6,7},{7,6},{8,9},{9,8},{10,11... | collective-permute-start | bytes 2605064 | tf_op jit(solution)/shard_map/ppermute | solution.py:432
  40.6 1.6 %shard_map.58 = (s16[528,256]{1,0:T(8,128)(2,1)}, s16[528,256]{1,0:T(8,128)(2,1)}, s16[528,256]{1,0:T(8,128)(2,1)}) custom-call(s32[3]{0:T(128)S(1)} %pad_add_fusion.which_ref, f32[4,8,64,256]{3,2,1,0:T(8,128)S(1)} %bitcast.77), custom_call_target="tpu_custom_call" | custom-call | tf_op jit(solution)/shard_map/pallas_call | solution.py:46
  42.2 1.3 %copy-done = f32[32,256,64]{1,2,0:T(8,128)} copy-done((f32[32,256,64]{1,2,0:T(8,128)}, f32[32,256,64]{1,2,0:T(8,128)S(1)}, u32[]{:S(2)}) %copy-start) | copy-done | bytes 2097176
  43.5 1.4 %collective-permute-start.5 = (s16[528,256]{1,0:T(8,128)(2,1)}, s16[528,256]{1,0:T(8,128)(2,1)S(1)}, u32[]{:S(2)}, u32[]{:S(2)}) collective-permute-start(s16[528,256]{1,0:T(8,128)(2,1)} %get-tuple-element.56), channel_id=1, source_target_pairs={{0,2},{1,3},{2,4},{3,5},{4,6},{5,7},{6,0},{7,1},{8,10},{9,11},{10,... | collective-permute-start | bytes 811016 | tf_op jit(solution)/shard_map/ppermute | solution.py:429
  44.9 2.5 %collective-permute-start.6 = (s16[528,256]{1,0:T(8,128)(2,1)}, s16[528,256]{1,0:T(8,128)(2,1)}, u32[]{:S(2)}, u32[]{:S(2)}) collective-permute-start(s16[528,256]{1,0:T(8,128)(2,1)} %get-tuple-element.57), channel_id=1, source_target_pairs={{0,4},{1,5},{2,6},{3,7},{4,0},{5,1},{6,2},{7,3},{8,12},{9,13},{10,... | collective-permute-start | bytes 811016 | tf_op jit(solution)/shard_map/ppermute | solution.py:429
  47.4 1.1 collective-permute-start.7
  48.5 1.5 %all-to-all-done = bf16[4,53,32,256]{3,2,1,0:T(8,128)(2,1)} async-done(((bf16[4,53,32,256]{3,2,1,0:T(8,128)(2,1)}), bf16[4,53,32,256]{3,2,1,0:T(8,128)(2,1)}, u32[]{:S(2)}, u32[]{:S(2)}) %all-to-all-start) | async-done | bytes 3473440 | tf_op jit(solution)/shard_map/all_to_all | solution.py:412
  49.9 4.2 %fusion = f32[32,256,64]{1,2,0:T(8,128)S(1)} fusion(bf16[212,32,256]{2,1,0:T(8,128)(2,1)} %bitcast.6, bf16[64,53]{1,0:T(8,128)(2,1)S(1)} %get-tuple-element.86, bf16[64,53]{1,0:T(8,128)(2,1)S(1)} %get-tuple-element.87, bf16[64,53]{1,0:T(8,128)(2,1)S(1)} %get-tuple-element.88, bf16[64,53]{1,0:T(8,128)(2,1)S(1)} %get-tuple-element.89, ...), kind=kOutput, calls=%fused_computation | convolution fusion | flops 222528768 | bytes 5624833 | tf_op jit(solution)/shard_map/eb,bhw->hew/dot_general | solution.py:389
  54.4 1.2 %collective-permute-start = (s16[1040,256]{1,0:T(8,128)(2,1)S(1)}, s16[1040,256]{1,0:T(8,128)(2,1)S(1)}, u32[]{:S(2)}, u32[]{:S(2)}) collective-permute-start(s16[1040,256]{1,0:T(8,128)(2,1)S(1)} %shard_map.55), channel_id=1, source_target_pairs={{0,1},{1,0},{2,3},{3,2},{4,5},{5,4},{6,7},{7,6},{8,9},{9,8},{10,11... | collective-permute-start | bytes 1597448 | tf_op jit(solution)/shard_map/ppermute | solution.py:440
  56.3 0.7 tile.4
  57.0 1.0 tile.10
  58.0 1.7 %copy.81 = bf16[53,32,256]{2,0,1:T(8,128)(2,1)S(1)} copy(bf16[53,32,256]{2,1,0:T(8,128)(2,1)} %get-tuple-element.103) | data formatting | bytes 1736704 | tf_op jit(solution)/shard_map/reshape | solution.py:423
  59.8 1.7 %collective-permute-done.6.refs_1_ = s16[528,256]{1,0:T(8,128)(2,1)} collective-permute-done((s16[528,256]{1,0:T(8,128)(2,1)}, s16[528,256]{1,0:T(8,128)(2,1)}, u32[]{:S(2)}, u32[]{:S(2)}) %collective-permute-start.6) | collective-permute-done | bytes 270368 | tf_op jit(solution)/shard_map/ppermute | solution.py:429
  61.5 1.6 %copy.82 = bf16[53,32,256]{2,0,1:T(8,128)(2,1)S(1)} copy(bf16[53,32,256]{2,1,0:T(8,128)(2,1)} %collective-permute-done.2) | data formatting | bytes 1736704 | tf_op jit(solution)/shard_map/optimization_barrier | solution.py:439
  63.7 1.7 %shard_map.59 = (s16[528,256]{1,0:T(8,128)(2,1)}, s16[528,256]{1,0:T(8,128)(2,1)}, s16[528,256]{1,0:T(8,128)(2,1)}) custom-call(s32[3]{0:T(128)S(1)} %pad_add_fusion.which_ref, f32[4,8,64,256]{3,2,1,0:T(8,128)S(1)} %bitcast.79), custom_call_target="tpu_custom_call" | custom-call | tf_op jit(solution)/shard_map/pallas_call | solution.py:46
  65.4 1.3 %collective-permute-start.8 = (s16[528,256]{1,0:T(8,128)(2,1)}, s16[528,256]{1,0:T(8,128)(2,1)}, u32[]{:S(2)}, u32[]{:S(2)}) collective-permute-start(s16[528,256]{1,0:T(8,128)(2,1)} %get-tuple-element.63), channel_id=1, source_target_pairs={{0,2},{1,3},{2,4},{3,5},{4,6},{5,7},{6,0},{7,1},{8,10},{9,11},{10,... | collective-permute-start | bytes 811016 | tf_op jit(solution)/shard_map/ppermute | solution.py:429
  66.8 1.7 %collective-permute-start.9 = (s16[528,256]{1,0:T(8,128)(2,1)}, s16[528,256]{1,0:T(8,128)(2,1)}, u32[]{:S(2)}, u32[]{:S(2)}) collective-permute-start(s16[528,256]{1,0:T(8,128)(2,1)} %get-tuple-element.64), channel_id=1, source_target_pairs={{0,4},{1,5},{2,6},{3,7},{4,0},{5,1},{6,2},{7,3},{8,12},{9,13},{10,... | collective-permute-start | bytes 811016 | tf_op jit(solution)/shard_map/ppermute | solution.py:429
  68.5 0.7 collective-permute-start.10
  69.2 2.0 %shard_map.60 = (f32[8,64,256]{2,1,0:T(8,128)S(1)}, f32[4,64,256]{2,1,0:T(8,128)}) custom-call(s32[1]{0:T(128)} %bitcast.1.which_ref, f32[4,8,64,256]{3,2,1,0:T(8,128)S(1)} %bitcast.78, s16[528,256]{1,0:T(8,128)(2,1)S(1)} %collective-permute-done.5.refs_0_, s16[528,256]{1,0:T(8,128)(2,1)} %collective-permute-done.6.refs_1_, ...), custom_call_target="tpu_custom_call" | custom-call | tf_op jit(solution)/shard_map/pallas_call | solution.py:84
  71.1 0.8 copy-done.7
  71.9 5.3 %collective-permute-start.11 = (f32[4,64,256]{2,1,0:T(8,128)}, f32[4,64,256]{2,1,0:T(8,128)S(1)}, u32[]{:S(2)}, u32[]{:S(2)}) collective-permute-start(f32[4,64,256]{2,1,0:T(8,128)} %get-tuple-element.70), channel_id=1, source_target_pairs={{0,8},{8,16},{16,24},{24,32},{32,40},{40,48},{48,56},{56,64},{64,7... | collective-permute-start | bytes 786440 | tf_op jit(solution)/shard_map/ppermute | solution.py:310
  77.3 0.8 copy-done.5
  78.1 1.0 copy-done.6
  79.1 0.8 shard_map.56
  79.9 1.9 %collective-permute-start.12 = (f32[4,64,256]{2,1,0:T(8,128)}, f32[4,64,256]{2,1,0:T(8,128)S(1)}, u32[]{:S(2)}, u32[]{:S(2)}) collective-permute-start(f32[4,64,256]{2,1,0:T(8,128)} %get-tuple-element.71), channel_id=1, source_target_pairs={{8,0},{16,8},{24,16},{32,24},{40,32},{48,40},{56,48},{64,56},{72,6... | collective-permute-start | bytes 786440 | tf_op jit(solution)/shard_map/ppermute | solution.py:310
  82.2 6.5 %collective-permute-done.12.bottom_ref = f32[4,64,256]{2,1,0:T(8,128)S(1)} collective-permute-done((f32[4,64,256]{2,1,0:T(8,128)}, f32[4,64,256]{2,1,0:T(8,128)S(1)}, u32[]{:S(2)}, u32[]{:S(2)}) %collective-permute-start.12) | collective-permute-done | bytes 262176 | tf_op jit(solution)/shard_map/ppermute | solution.py:310
  88.7 1.6 %copy-done.3 = f32[32,256,64]{1,2,0:T(8,128)S(1)} copy-done((f32[32,256,64]{1,2,0:T(8,128)S(1)}, f32[32,256,64]{1,2,0:T(8,128)}, u32[]{:S(2)}) %copy-start.3) | copy-done | bytes 2097176
  90.3 1.0 copy-done.8
  91.3 3.3 %shard_map.61 = (f32[24,288,128]{2,1,0:T(8,128)S(1)}, f32[25,8,128]{2,1,0:T(8,128)S(1)}, f32[25,8,128]{2,1,0:T(8,128)S(1)}) custom-call(s32[1]{0:T(128)} %bitcast.1.which_ref, bf16[64,192]{1,0:T(8,128)(2,1)S(1)} %pad_maximum_fusion.4.inv_ref, f32[16,64,256]{2,1,0:T(8,128)S(1)} %get-tuple-element.42.early_ref, f32[8,64,256]{2,1,0:T(8,128)S(1)} %copy-done.8, ...), custom_call_target="tpu_custom_call" | custom-call | tf_op jit(solution)/shard_map/pallas_call | solution.py:150
  94.7 3.5 %collective-permute-start.14 = (f32[25,8,128]{2,1,0:T(8,128)S(1)}, f32[25,8,128]{2,1,0:T(8,128)S(1)}, u32[]{:S(2)}, u32[]{:S(2)}) collective-permute-start(f32[25,8,128]{2,1,0:T(8,128)S(1)} %get-tuple-element.73.low_ref), channel_id=1, source_target_pairs={{1,0},{2,1},{3,2},{4,3},{5,4},{6,5},{7,6},{9,8},{10,9},{11,10},{12... | collective-permute-start | bytes 307208 | tf_op jit(solution)/shard_map/ppermute | solution.py:310
  98.4 4.2 %collective-permute-start.13 = (f32[25,8,128]{2,1,0:T(8,128)S(1)}, f32[25,8,128]{2,1,0:T(8,128)S(1)}, u32[]{:S(2)}, u32[]{:S(2)}) collective-permute-start(f32[25,8,128]{2,1,0:T(8,128)S(1)} %get-tuple-element.72.high_ref), channel_id=1, source_target_pairs={{0,1},{1,2},{2,3},{3,4},{4,5},{5,6},{6,7},{8,9},{9,10},{10,11},{11... | collective-permute-start | bytes 307208 | tf_op jit(solution)/shard_map/ppermute | solution.py:310
  102.5 0.8 convolution_multiply_fusion.wv_ref
  103.4 6.7 %shard_map.62.inside_ref = f32[16,256,128]{2,1,0:T(8,128)S(1)} custom-call(bf16[384,128]{1,0:T(8,128)(2,1)S(1)} %pad_maximum_fusion.invt_ref, f32[24,288,128]{2,1,0:T(8,128)S(1)} %get-tuple-element.74.mixed_ref, f32[24,288,128]{2,1,0:T(8,128)S(1)} %copy-done.4, f32[24,288,128]{2,1,0:T(8,128)S(1)} %convolution_multiply_fusion.wv_ref), custom_call_target="tpu_custom_call" | custom-call | flops 3000000000 | bytes 25165824 | tf_op jit(solution)/shard_map/pallas_call | solution.py:223
  110.1 5.0 %shard_map.63 = f32[64,32,256]{2,1,0:T(8,128)} custom-call(bf16[384,128]{1,0:T(8,128)(2,1)S(1)} %pad_maximum_fusion.invt_ref, f32[25,8,128]{2,1,0:T(8,128)S(1)} %collective-permute-done.13.left_ref, f32[25,8,128]{2,1,0:T(8,128)S(1)} %get-tuple-element.73.low_ref, f32[25,8,128]{2,1,0:T(8,128)S(1)} %get-tuple-element.72.high_ref, ...), custom_call_target="tpu_custom_call" | custom-call | tf_op jit(solution)/shard_map/pallas_call | solution.py:289
  (71 shorter events, 4.0 us)
Async XLA Ops:
  4.6 45.3 %all-to-all-start = ((bf16[4,53,32,256]{3,2,1,0:T(8,128)(2,1)}), bf16[4,53,32,256]{3,2,1,0:T(8,128)(2,1)}, u32[]{:S(2)}, u32[]{:S(2)}) async-start(bf16[4,53,32,256]{3,2,1,0:T(8,128)(2,1)} %bitcast.5), calls=%async_computation | async-start | bytes 6946816 | tf_op jit(solution)/shard_map/all_to_all | solution.py:412
  11.1 25.0 %collective-permute-start.1 = (bf16[53,32,256]{2,1,0:T(8,128)(2,1)S(1)}, bf16[53,32,256]{2,1,0:T(8,128)(2,1)S(1)}, u32[]{:S(2)}, u32[]{:S(2)}) collective-permute-start(bf16[53,32,256]{2,1,0:T(8,128)(2,1)S(1)} %copy_bitcast_fusion.3), channel_id=1, source_target_pairs={{0,1},{1,0},{2,3},{3,2},{4,5},{5,4},{6,7},{7,6},{8,9},{9,8},{10,11... | collective-permute-start | bytes 2605064 | tf_op jit(solution)/shard_map/ppermute | solution.py:415
  14.9 3.7 %copy-start.17 = (s32[32,256]{1,0:T(8,128)S(1)}, s32[32,256]{1,0:T(8,128)}, u32[]{:S(2)}) copy-start(s32[32,256]{1,0:T(8,128)} %param.8) | copy-start | bytes 98308
  14.9 3.7 %copy-start.18 = (s32[32,256]{1,0:T(8,128)S(1)}, s32[32,256]{1,0:T(8,128)}, u32[]{:S(2)}) copy-start(s32[32,256]{1,0:T(8,128)} %param.9) | copy-start | bytes 98308
  18.6 11.7 %collective-permute-start.3 = (bf16[2,4,256]{2,1,0:T(4,128)(2,1)S(1)}, bf16[2,4,256]{2,1,0:T(4,128)(2,1)S(1)}, u32[]{:S(2)}, u32[]{:S(2)}) collective-permute-start(bf16[2,4,256]{2,1,0:T(4,128)(2,1)S(1)} %get-tuple-element.95), channel_id=1, source_target_pairs={{0,8},{8,16},{16,24},{24,32},{32,40},{40,48},{48,56},{56,64},{64,7... | collective-permute-start | bytes 12296 | tf_op jit(solution)/shard_map/ppermute | solution.py:310
  22.4 10.8 %collective-permute-start.4 = (bf16[2,4,256]{2,1,0:T(4,128)(2,1)S(1)}, bf16[2,4,256]{2,1,0:T(4,128)(2,1)S(1)}, u32[]{:S(2)}, u32[]{:S(2)}) collective-permute-start(bf16[2,4,256]{2,1,0:T(4,128)(2,1)S(1)} %get-tuple-element.96), channel_id=1, source_target_pairs={{8,0},{16,8},{24,16},{32,24},{40,32},{48,40},{56,48},{64,56},{72,6... | collective-permute-start | bytes 12296 | tf_op jit(solution)/shard_map/ppermute | solution.py:310
  24.4 2.7 %copy-start.9 = (bf16[64,424]{1,0:T(8,128)(2,1)S(1)}, bf16[64,424]{1,0:T(8,128)(2,1)}, u32[]{:S(2)}) copy-start(bf16[64,424]{1,0:T(8,128)(2,1)} %param.6) | copy-start | bytes 162820
  27.2 12.8 %copy-start.10 = (bf16[64,53]{1,0:T(8,128)(2,1)}, bf16[64,53]{1,0:T(8,128)(2,1)S(1)}, u32[]{:S(2)}) copy-start(bf16[64,53]{1,0:T(8,128)(2,1)S(1)} %get-tuple-element.81) | copy-start | bytes 20356
  27.3 12.8 %copy-start.12 = (bf16[64,53]{1,0:T(8,128)(2,1)}, bf16[64,53]{1,0:T(8,128)(2,1)S(1)}, u32[]{:S(2)}) copy-start(bf16[64,53]{1,0:T(8,128)(2,1)S(1)} %get-tuple-element.90) | copy-start | bytes 20356
  36.5 25.0 %collective-permute-start.2 = (bf16[53,32,256]{2,1,0:T(8,128)(2,1)}, bf16[53,32,256]{2,1,0:T(8,128)(2,1)}, u32[]{:S(2)}, u32[]{:S(2)}) collective-permute-start(bf16[53,32,256]{2,1,0:T(8,128)(2,1)} %copy_bitcast_fusion.2), channel_id=1, source_target_pairs={{0,1},{1,0},{2,3},{3,2},{4,5},{5,4},{6,7},{7,6},{8,9},{9,8},{10,11... | collective-permute-start | bytes 2605064 | tf_op jit(solution)/shard_map/ppermute | solution.py:432
  42.2 1.3 %copy-start = (f32[32,256,64]{1,2,0:T(8,128)}, f32[32,256,64]{1,2,0:T(8,128)S(1)}, u32[]{:S(2)}) copy-start(f32[32,256,64]{1,2,0:T(8,128)S(1)} %fusion.2) | copy-start | bytes 6291460
  43.5 16.3 %collective-permute-start.5 = (s16[528,256]{1,0:T(8,128)(2,1)}, s16[528,256]{1,0:T(8,128)(2,1)S(1)}, u32[]{:S(2)}, u32[]{:S(2)}) collective-permute-start(s16[528,256]{1,0:T(8,128)(2,1)} %get-tuple-element.56), channel_id=1, source_target_pairs={{0,2},{1,3},{2,4},{3,5},{4,6},{5,7},{6,0},{7,1},{8,10},{9,11},{10,... | collective-permute-start | bytes 811016 | tf_op jit(solution)/shard_map/ppermute | solution.py:429
  44.9 16.6 %collective-permute-start.6 = (s16[528,256]{1,0:T(8,128)(2,1)}, s16[528,256]{1,0:T(8,128)(2,1)}, u32[]{:S(2)}, u32[]{:S(2)}) collective-permute-start(s16[528,256]{1,0:T(8,128)(2,1)} %get-tuple-element.57), channel_id=1, source_target_pairs={{0,4},{1,5},{2,6},{3,7},{4,0},{5,1},{6,2},{7,3},{8,12},{9,13},{10,... | collective-permute-start | bytes 811016 | tf_op jit(solution)/shard_map/ppermute | solution.py:429
  47.4 14.2 %collective-permute-start.7 = (s16[528,256]{1,0:T(8,128)(2,1)}, s16[528,256]{1,0:T(8,128)(2,1)}, u32[]{:S(2)}, u32[]{:S(2)}) collective-permute-start(s16[528,256]{1,0:T(8,128)(2,1)} %get-tuple-element.58), channel_id=1, source_target_pairs={{0,6},{1,7},{2,0},{3,1},{4,2},{5,3},{6,4},{7,5},{8,14},{9,15},{10,... | collective-permute-start | bytes 811016 | tf_op jit(solution)/shard_map/ppermute | solution.py:429
  49.9 5.6 %copy-start.14 = (f32[64,64]{1,0:T(8,128)S(1)}, f32[64,64]{1,0:T(8,128)}, u32[]{:S(2)}) copy-start(f32[64,64]{1,0:T(8,128)} %param.7) | copy-start | bytes 49156
  54.4 22.9 %collective-permute-start = (s16[1040,256]{1,0:T(8,128)(2,1)S(1)}, s16[1040,256]{1,0:T(8,128)(2,1)S(1)}, u32[]{:S(2)}, u32[]{:S(2)}) collective-permute-start(s16[1040,256]{1,0:T(8,128)(2,1)S(1)} %shard_map.55), channel_id=1, source_target_pairs={{0,1},{1,0},{2,3},{3,2},{4,5},{5,4},{6,7},{7,6},{8,9},{9,8},{10,11... | collective-permute-start | bytes 1597448 | tf_op jit(solution)/shard_map/ppermute | solution.py:440
  58.0 5.2 %copy-start.11 = (bf16[64,53]{1,0:T(8,128)(2,1)S(1)}, bf16[64,53]{1,0:T(8,128)(2,1)}, u32[]{:S(2)}) copy-start(bf16[64,53]{1,0:T(8,128)(2,1)} %copy-done.10) | copy-start | bytes 20356
  58.0 5.2 %copy-start.13 = (bf16[64,53]{1,0:T(8,128)(2,1)S(1)}, bf16[64,53]{1,0:T(8,128)(2,1)}, u32[]{:S(2)}) copy-start(bf16[64,53]{1,0:T(8,128)(2,1)} %copy-done.12) | copy-start | bytes 20356
  63.2 6.0 %copy-start.1 = (f32[32,256,64]{1,2,0:T(8,128)S(1)}, f32[32,256,64]{1,2,0:T(8,128)}, u32[]{:S(2)}) copy-start(f32[32,256,64]{1,2,0:T(8,128)} %copy-done) | copy-start | bytes 6291460
  63.7 16.2 %copy-start.2 = (f32[32,256,64]{1,2,0:T(8,128)}, f32[32,256,64]{1,2,0:T(8,128)S(1)}, u32[]{:S(2)}) copy-start(f32[32,256,64]{1,2,0:T(8,128)S(1)} %fusion.6) | copy-start | bytes 6291460
  63.7 18.1 %copy-start.15 = (bf16[64,64]{1,0:T(8,128)(2,1)S(1)}, bf16[64,64]{1,0:T(8,128)(2,1)}, u32[]{:S(2)}) copy-start(bf16[64,64]{1,0:T(8,128)(2,1)} %get-tuple-element.97) | copy-start | bytes 24580
  63.7 18.1 %copy-start.16 = (bf16[64,64]{1,0:T(8,128)(2,1)S(1)}, bf16[64,64]{1,0:T(8,128)(2,1)}, u32[]{:S(2)}) copy-start(bf16[64,64]{1,0:T(8,128)(2,1)} %get-tuple-element.98) | copy-start | bytes 24580
  65.4 16.8 %collective-permute-start.8 = (s16[528,256]{1,0:T(8,128)(2,1)}, s16[528,256]{1,0:T(8,128)(2,1)}, u32[]{:S(2)}, u32[]{:S(2)}) collective-permute-start(s16[528,256]{1,0:T(8,128)(2,1)} %get-tuple-element.63), channel_id=1, source_target_pairs={{0,2},{1,3},{2,4},{3,5},{4,6},{5,7},{6,0},{7,1},{8,10},{9,11},{10,... | collective-permute-start | bytes 811016 | tf_op jit(solution)/shard_map/ppermute | solution.py:429
  66.8 15.4 %collective-permute-start.9 = (s16[528,256]{1,0:T(8,128)(2,1)}, s16[528,256]{1,0:T(8,128)(2,1)}, u32[]{:S(2)}, u32[]{:S(2)}) collective-permute-start(s16[528,256]{1,0:T(8,128)(2,1)} %get-tuple-element.64), channel_id=1, source_target_pairs={{0,4},{1,5},{2,6},{3,7},{4,0},{5,1},{6,2},{7,3},{8,12},{9,13},{10,... | collective-permute-start | bytes 811016 | tf_op jit(solution)/shard_map/ppermute | solution.py:429
  68.5 13.7 %collective-permute-start.10 = (s16[528,256]{1,0:T(8,128)(2,1)}, s16[528,256]{1,0:T(8,128)(2,1)}, u32[]{:S(2)}, u32[]{:S(2)}) collective-permute-start(s16[528,256]{1,0:T(8,128)(2,1)} %get-tuple-element.65), channel_id=1, source_target_pairs={{0,6},{1,7},{2,0},{3,1},{4,2},{5,3},{6,4},{7,5},{8,14},{9,15},{10,... | collective-permute-start | bytes 811016 | tf_op jit(solution)/shard_map/ppermute | solution.py:429
  71.1 0.8 copy-start.7
  71.9 10.2 %collective-permute-start.11 = (f32[4,64,256]{2,1,0:T(8,128)}, f32[4,64,256]{2,1,0:T(8,128)S(1)}, u32[]{:S(2)}, u32[]{:S(2)}) collective-permute-start(f32[4,64,256]{2,1,0:T(8,128)} %get-tuple-element.70), channel_id=1, source_target_pairs={{0,8},{8,16},{16,24},{24,32},{32,40},{40,48},{48,56},{56,64},{64,7... | collective-permute-start | bytes 786440 | tf_op jit(solution)/shard_map/ppermute | solution.py:310
  77.3 0.8 copy-start.5
  78.1 1.0 copy-start.6
  79.9 8.8 %collective-permute-start.12 = (f32[4,64,256]{2,1,0:T(8,128)}, f32[4,64,256]{2,1,0:T(8,128)S(1)}, u32[]{:S(2)}, u32[]{:S(2)}) collective-permute-start(f32[4,64,256]{2,1,0:T(8,128)} %get-tuple-element.71), channel_id=1, source_target_pairs={{8,0},{16,8},{24,16},{32,24},{40,32},{48,40},{56,48},{64,56},{72,6... | collective-permute-start | bytes 786440 | tf_op jit(solution)/shard_map/ppermute | solution.py:310
  88.7 1.6 %copy-start.3 = (f32[32,256,64]{1,2,0:T(8,128)S(1)}, f32[32,256,64]{1,2,0:T(8,128)}, u32[]{:S(2)}) copy-start(f32[32,256,64]{1,2,0:T(8,128)} %copy-done.2) | copy-start | bytes 6291460
  90.3 1.0 copy-start.8
  91.3 12.0 %copy-start.4 = (f32[24,288,128]{2,1,0:T(8,128)S(1)}, f32[24,288,128]{2,1,0:T(8,128)}, u32[]{:S(2)}) copy-start(f32[24,288,128]{2,1,0:T(8,128)} %convolution_multiply_fusion.1.wh_ref) | copy-start | bytes 10616836
  94.7 15.4 %collective-permute-start.14 = (f32[25,8,128]{2,1,0:T(8,128)S(1)}, f32[25,8,128]{2,1,0:T(8,128)S(1)}, u32[]{:S(2)}, u32[]{:S(2)}) collective-permute-start(f32[25,8,128]{2,1,0:T(8,128)S(1)} %get-tuple-element.73.low_ref), channel_id=1, source_target_pairs={{1,0},{2,1},{3,2},{4,3},{5,4},{6,5},{7,6},{9,8},{10,9},{11,10},{12... | collective-permute-start | bytes 307208 | tf_op jit(solution)/shard_map/ppermute | solution.py:310
  98.4 11.7 %collective-permute-start.13 = (f32[25,8,128]{2,1,0:T(8,128)S(1)}, f32[25,8,128]{2,1,0:T(8,128)S(1)}, u32[]{:S(2)}, u32[]{:S(2)}) collective-permute-start(f32[25,8,128]{2,1,0:T(8,128)S(1)} %get-tuple-element.72.high_ref), channel_id=1, source_target_pairs={{0,1},{1,2},{2,3},{3,4},{4,5},{5,6},{6,7},{8,9},{9,10},{10,11},{11... | collective-permute-start | bytes 307208 | tf_op jit(solution)/shard_map/ppermute | solution.py:310
